TPU v7x, 512 devices: a whole 4x4x16 slice. The times are simulated.
512 devices in a mesh: gx: 16 (over z), gy: 4 (over x), gz: 8 (over y, core).
Axes of the slice: x: 4, y: 4, z: 16, core: 2. Of those that a mesh axis runs over, the one named last changes fastest.
Arguments:
- velocity: float32 [3, 128, 64, 1024], P(None, 'gx', 'gy', 'gz'), may hold values from -6 to 6
- density: float32 [128, 64, 1024], P('gx', 'gy', 'gz'), may hold values from 0 to 2
- offsets: int32 [3, 128, 64, 1024], P(None, 'gx', 'gy', 'gz'), may hold values from -4 to 3
- eighths: int32 [3, 128, 64, 1024], P(None, 'gx', 'gy', 'gz'), may hold values from 0 to 7
Outputs:
- new_velocity: float32 [3, 128, 64, 1024], P(None, 'gx', 'gy', 'gz')
- new_density: float32 [128, 64, 1024], P('gx', 'gy', 'gz')
- pressure: float32 [128, 64, 1024], P('gx', 'gy', 'gz')
All inputs are finite; a program needn't handle non-finite values.
Results may differ from a plain program's by a relative error of at most 0.00002.
Values sent between devices are 32-bit elements; how exact they have to be, the bound alone decides.
No kernel may reach another device: no remote copies, remote signals or barrier semaphores. Data moves between devices by JAX's collectives and lax.ppermute only.
A program may use at most 64 MiB of HBM per device.

v0:
```python
import jax
import jax.numpy as jnp
from jax import lax
from jax.sharding import PartitionSpec as P

RELAX_WEIGHT = 6.0 / 7.0


def padded_2(block, sides, width):
    for axis, dim in sides:
        count = lax.axis_size(axis)
        forward = [(i, i + 1) for i in range(count - 1)]
        backward = [(target, source) for source, target in forward]
        low = lax.ppermute(
            lax.slice_in_dim(block, block.shape[dim] - width, None, axis=dim), axis, forward
        )
        high = lax.ppermute(lax.slice_in_dim(block, 0, width, axis=dim), axis, backward)
        block = jnp.concatenate([low, block, high], axis=dim)
    return block


def with_halo(value, sides, width):
    edges = {}
    for axis, dim in sides:
        peers, length = (lax.axis_size(axis), value.shape[dim])
        up = [(i, (i + 1) % peers) for i in range(peers - 1)]
        last = lax.slice_in_dim(value, length - width, length, axis=dim)
        initial = lax.slice_in_dim(value, 0, width, axis=dim)
        edges[dim] = (
            lax.ppermute(last, axis, up),
            lax.ppermute(initial, axis, [(b, a) for a, b in up]),
        )
    done = []
    for _, dim in sides:
        low, high = edges[dim]
        around = [(width, width) if d in done else (0, 0) for d in range(value.ndim)]
        value = jnp.concatenate([jnp.pad(low, around), value, jnp.pad(high, around)], axis=dim)
        done.append(dim)
    return value


def neighbours(padded):
    summed = padded[2:, 1:-1, 1:-1] + padded[:-2, 1:-1, 1:-1]
    summed = summed + padded[1:-1, 2:, 1:-1] + padded[1:-1, :-2, 1:-1]
    summed = summed + padded[1:-1, 1:-1, 2:] + padded[1:-1, 1:-1, :-2]
    return summed


def operate(padded):
    return 6.0 * padded[1:-1, 1:-1, 1:-1] - neighbours(padded)


def axis_weights(offset_axis, fraction_axis):
    levels = lax.broadcasted_iota(jnp.int32, (9, 1, 1, 1), 0) - 4
    lower = jnp.where(offset_axis[None] == levels, 1.0 - fraction_axis[None], jnp.float32(0.0))
    upper = jnp.where(offset_axis[None] == levels - 1, fraction_axis[None], jnp.float32(0.0))
    return lower + upper


def advect_block(padded, offsets, eighths):
    field_count = padded.shape[0]
    box_shape = offsets.shape[1:]
    fraction = eighths.astype(jnp.float32) / 8.0
    weight_x = axis_weights(offsets[0], fraction[0])
    weight_y = axis_weights(offsets[1], fraction[1])
    weight_z = axis_weights(offsets[2], fraction[2])

    def one_plane(step_x, summed):
        slab = lax.dynamic_slice_in_dim(padded, step_x, box_shape[0], 1)
        plane_weight = lax.dynamic_index_in_dim(weight_x, step_x, 0, keepdims=False)
        for step_y in range(9):
            window = slab[:, :, step_y : step_y + box_shape[1], :]
            along_z = jnp.zeros((field_count,) + box_shape, jnp.float32)
            for step_z in range(9):
                along_z = (
                    along_z
                    + weight_z[step_z][None] * window[:, :, :, step_z : step_z + box_shape[2]]
                )
            summed = summed + (plane_weight * weight_y[step_y])[None] * along_z
        return summed

    summed = jnp.zeros((field_count,) + box_shape, jnp.float32)
    return lax.fori_loop(0, 9, one_plane, summed)


def divergence_of(velocity_pad):
    part_x = velocity_pad[0, 2:, 1:-1, 1:-1] - velocity_pad[0, :-2, 1:-1, 1:-1]
    part_y = velocity_pad[1, 1:-1, 2:, 1:-1] - velocity_pad[1, 1:-1, :-2, 1:-1]
    part_z = velocity_pad[2, 1:-1, 1:-1, 2:] - velocity_pad[2, 1:-1, 1:-1, :-2]
    return 0.5 * (part_x + part_y + part_z)


def gradient_of(pressure_pad):
    part_x = pressure_pad[2:, 1:-1, 1:-1] - pressure_pad[:-2, 1:-1, 1:-1]
    part_y = pressure_pad[1:-1, 2:, 1:-1] - pressure_pad[1:-1, :-2, 1:-1]
    part_z = pressure_pad[1:-1, 1:-1, 2:] - pressure_pad[1:-1, 1:-1, :-2]
    return 0.5 * jnp.stack([part_x, part_y, part_z], axis=0)


def restrict(field):
    return field.reshape(
        field.shape[0] // 2, 2, field.shape[1] // 2, 2, field.shape[2] // 2, 2
    ).mean(axis=(1, 3, 5))


def prolong(field):
    return jnp.repeat(jnp.repeat(jnp.repeat(field, 2, axis=0), 2, axis=1), 2, axis=2)


def inside_box(extents, margin):
    box_shape = (extents[0] + 2 * margin, extents[1] + 2 * margin, extents[2] + 2 * margin)
    coord_x = (
        lax.broadcasted_iota(jnp.int32, box_shape, 0) - margin + lax.axis_index("gx") * extents[0]
    )
    coord_y = (
        lax.broadcasted_iota(jnp.int32, box_shape, 1) - margin + lax.axis_index("gy") * extents[1]
    )
    coord_z = (
        lax.broadcasted_iota(jnp.int32, box_shape, 2) - margin + lax.axis_index("gz") * extents[2]
    )
    inside = (coord_x >= 0) & (coord_x < extents[0] * lax.axis_size("gx"))
    inside = inside & (coord_y >= 0) & (coord_y < extents[1] * lax.axis_size("gy"))
    inside = inside & (coord_z >= 0) & (coord_z < extents[2] * lax.axis_size("gz"))
    return inside


def smooth_level(source, spacing):
    relaxation = RELAX_WEIGHT / 6.0
    source_pad = padded_2(source, (("gx", 0), ("gy", 1), ("gz", 2)), 2)
    first_sweep = relaxation * spacing * source_pad
    second_wide = first_sweep[1:-1, 1:-1, 1:-1] + relaxation * (
        spacing * source_pad[1:-1, 1:-1, 1:-1] - operate(first_sweep)
    )
    second_wide = jnp.where(inside_box(source.shape, 1), second_wide, 0.0)
    residual = source - operate(second_wide) / spacing
    second_sweep = second_wide[1:-1, 1:-1, 1:-1]
    return (second_sweep, residual)


def solve_coarse(source):
    relaxation = RELAX_WEIGHT / 6.0
    spacing = 16.0
    first_sweep = relaxation * spacing * source
    first_pad = with_halo(first_sweep, (("gx", 0), ("gy", 1), ("gz", 2)), 1)
    return first_sweep + relaxation * (spacing * source - operate(first_pad))


def body(velocity, density, offsets, eighths):
    fields = jnp.concatenate([velocity, density[None]], axis=0)
    padded = padded_2(fields, (("gx", 1), ("gy", 2), ("gz", 3)), 4)
    advected = advect_block(padded, offsets, eighths)
    new_density = advected[3]
    moved_velocity = advected[:3]
    velocity_pad = with_halo(moved_velocity, (("gx", 1), ("gy", 2), ("gz", 3)), 1)
    divergence = divergence_of(velocity_pad)
    fine_sweep, fine_residual = smooth_level(-divergence, 1.0)
    middle_sweep, middle_residual = smooth_level(restrict(fine_residual), 4.0)
    coarse_sweep = solve_coarse(restrict(middle_residual))
    pressure = fine_sweep + prolong(middle_sweep + prolong(coarse_sweep))
    pressure_pad = with_halo(pressure, (("gx", 0), ("gy", 1), ("gz", 2)), 1)
    gradient = gradient_of(pressure_pad)
    return (moved_velocity - gradient, new_density, pressure)


def solution(mesh):
    return jax.shard_map(
        body,
        mesh=mesh,
        in_specs=(
            P(None, "gx", "gy", "gz"),
            P("gx", "gy", "gz"),
            P(None, "gx", "gy", "gz"),
            P(None, "gx", "gy", "gz"),
        ),
        out_specs=(P(None, "gx", "gy", "gz"), P("gx", "gy", "gz"), P("gx", "gy", "gz")),
        check_vma=False,
    )
```

profile of v0, /device:TPU:248, one launch (start us, length us, event | category | flops | bytes accessed | tf_op | source)
XLA Modules:
  0.0 281.0 jit_solution(1844982951480716901)
XLA Ops:
  1.6 5.0 %collective-permute-start = (f32[4,4,16,128]{3,2,1,0:T(8,128)S(1)}, f32[4,4,16,128]{3,2,1,0:T(8,128)S(1)}, u32[]{:S(2)}, u32[]{:S(2)}) collective-permute-start(f32[4,4,16,128]{3,2,1,0:T(8,128)S(1)} %get-tuple-element.197), channel_id=1, source_target_pairs={{0,32},{32,64},{64,96},{96,128},{128,160},{160,192},{192,224},{224... | collective-permute-start | bytes 393224 | tf_op jit(solution)/shard_map/ppermute | solution.py:14
  9.6 5.1 %collective-permute-done.1 = f32[4,4,16,128]{3,2,1,0:T(8,128)S(1)} collective-permute-done((f32[4,4,16,128]{3,2,1,0:T(8,128)S(1)}, f32[4,4,16,128]{3,2,1,0:T(8,128)S(1)}, u32[]{:S(2)}, u32[]{:S(2)}) %collective-permute-start.1) | collective-permute-done | bytes 131104 | tf_op jit(solution)/shard_map/ppermute | solution.py:17
  15.8 3.4 %collective-permute-start.2 = (f32[4,16,4,128]{3,1,2,0:T(8,128)S(1)}, f32[4,16,4,128]{3,1,2,0:T(8,128)S(1)}, u32[]{:S(2)}, u32[]{:S(2)}) collective-permute-start(f32[4,16,4,128]{3,1,2,0:T(8,128)S(1)} %copy.201), channel_id=1, source_target_pairs={{0,8},{8,16},{16,24},{1,9},{9,17},{17,25},{2,10},{10,18},{18,26},{... | collective-permute-start | bytes 393224 | tf_op jit(solution)/shard_map/ppermute | solution.py:14
  30.3 6.9 %pad_maximum_fusion = f32[4,16,24,128]{2,1,3,0:T(8,128)S(1)} fusion(f32[4,16,4,128]{2,1,3,0:T(8,128)} %copy.183, f32[4,16,16,128]{2,1,3,0:T(8,128)} %copy.182, f32[4,16,4,128]{2,1,3,0:T(8,128)} %copy.181), kind=kLoop, calls=%fused_computation.189 | loop fusion | flops 393216 | bytes 1572864 | tf_op jit(solution)/shard_map/concatenate | solution.py:18
  39.2 3.6 %collective-permute-start.5 = (f32[4,16,24,4]{2,1,3,0:T(8,128)S(1)}, f32[4,16,24,4]{2,1,3,0:T(8,128)S(1)}, u32[]{:S(2)}, u32[]{:S(2)}) collective-permute-start(f32[4,16,24,4]{2,1,3,0:T(8,128)S(1)} %get-tuple-element.188), channel_id=1, source_target_pairs={{1,0},{2,1},{3,2},{4,3},{5,4},{6,5},{7,6},{9,8},{10,9},{11,10},{12... | collective-permute-start | bytes 73736 | tf_op jit(solution)/shard_map/ppermute | solution.py:17
  44.0 3.8 %copy.185 = f32[4,16,24,128]{3,2,1,0:T(8,128)} copy(f32[4,16,24,128]{2,1,3,0:T(8,128)} %copy-done) | data formatting | bytes 1572864 | tf_op jit(solution)/shard_map/concatenate | solution.py:18
  52.8 99.9 %while.14 = (s32[]{:T(128)}, f32[4,8,16,128]{3,2,1,0:T(8,128)S(1)}, f32[9,8,16,128]{3,2,1,0:T(8,128)}, f32[9,8,16,128]{3,2,1,0:T(8,128)S(1)}, f32[9,8,16,128]{3,...) while((s32[]{:T(128)}, f32[4,8,16,128]{3,2,1,0:T(8,128)S(1)}, ...), condition=%wide.region_1.2_spmd.clone, body=%wide.region_0.1_spmd.clone.sunk | while | flops 11419659 | bytes 25362724 | solution.py:83
  55.1 8.7 %fusion.161 = f32[4,8,16,128]{3,2,1,0:T(8,128)S(1)} fusion(f32[4,16,24,136]{3,2,1,0:T(8,128)S(1)} %get-tuple-element.359, s32[]{:T(128)} %get-tuple-element.338, s32[]{:T(128)S(6)} %add.1693, s32[]{:T(128)S(6)} %add.1694, s32[]{:T(128)S(6)} %add.1695, s32[]{:T(128)S(6)} %add.1696, s32[]{:T(128)S(6)} %add.1697, s32[]{:T(128)S(6)} %add.1698, ...), kind=kLoop, calls=%fused_computation.3.clone.1 | loop fusion | flops 11272192 | bytes 22937636 | tf_op jit(solution)/shard_map/while/body/eval_jaxpr/add | solution.py:79
  66.2 8.8 %fusion.161 = f32[4,8,16,128]{3,2,1,0:T(8,128)S(1)} fusion(f32[4,16,24,136]{3,2,1,0:T(8,128)S(1)} %get-tuple-element.359, s32[]{:T(128)} %get-tuple-element.338, s32[]{:T(128)S(6)} %add.1693, s32[]{:T(128)S(6)} %add.1694, s32[]{:T(128)S(6)} %add.1695, s32[]{:T(128)S(6)} %add.1696, s32[]{:T(128)S(6)} %add.1697, s32[]{:T(128)S(6)} %add.1698, ...), kind=kLoop, calls=%fused_computation.3.clone.1 | loop fusion | flops 11272192 | bytes 22937636 | tf_op jit(solution)/shard_map/while/body/eval_jaxpr/add | solution.py:79
  77.3 8.7 %fusion.161 = f32[4,8,16,128]{3,2,1,0:T(8,128)S(1)} fusion(f32[4,16,24,136]{3,2,1,0:T(8,128)S(1)} %get-tuple-element.359, s32[]{:T(128)} %get-tuple-element.338, s32[]{:T(128)S(6)} %add.1693, s32[]{:T(128)S(6)} %add.1694, s32[]{:T(128)S(6)} %add.1695, s32[]{:T(128)S(6)} %add.1696, s32[]{:T(128)S(6)} %add.1697, s32[]{:T(128)S(6)} %add.1698, ...), kind=kLoop, calls=%fused_computation.3.clone.1 | loop fusion | flops 11272192 | bytes 22937636 | tf_op jit(solution)/shard_map/while/body/eval_jaxpr/add | solution.py:79
  88.4 8.8 %fusion.161 = f32[4,8,16,128]{3,2,1,0:T(8,128)S(1)} fusion(f32[4,16,24,136]{3,2,1,0:T(8,128)S(1)} %get-tuple-element.359, s32[]{:T(128)} %get-tuple-element.338, s32[]{:T(128)S(6)} %add.1693, s32[]{:T(128)S(6)} %add.1694, s32[]{:T(128)S(6)} %add.1695, s32[]{:T(128)S(6)} %add.1696, s32[]{:T(128)S(6)} %add.1697, s32[]{:T(128)S(6)} %add.1698, ...), kind=kLoop, calls=%fused_computation.3.clone.1 | loop fusion | flops 11272192 | bytes 22937636 | tf_op jit(solution)/shard_map/while/body/eval_jaxpr/add | solution.py:79
  99.6 8.7 %fusion.161 = f32[4,8,16,128]{3,2,1,0:T(8,128)S(1)} fusion(f32[4,16,24,136]{3,2,1,0:T(8,128)S(1)} %get-tuple-element.359, s32[]{:T(128)} %get-tuple-element.338, s32[]{:T(128)S(6)} %add.1693, s32[]{:T(128)S(6)} %add.1694, s32[]{:T(128)S(6)} %add.1695, s32[]{:T(128)S(6)} %add.1696, s32[]{:T(128)S(6)} %add.1697, s32[]{:T(128)S(6)} %add.1698, ...), kind=kLoop, calls=%fused_computation.3.clone.1 | loop fusion | flops 11272192 | bytes 22937636 | tf_op jit(solution)/shard_map/while/body/eval_jaxpr/add | solution.py:79
  110.6 8.8 %fusion.161 = f32[4,8,16,128]{3,2,1,0:T(8,128)S(1)} fusion(f32[4,16,24,136]{3,2,1,0:T(8,128)S(1)} %get-tuple-element.359, s32[]{:T(128)} %get-tuple-element.338, s32[]{:T(128)S(6)} %add.1693, s32[]{:T(128)S(6)} %add.1694, s32[]{:T(128)S(6)} %add.1695, s32[]{:T(128)S(6)} %add.1696, s32[]{:T(128)S(6)} %add.1697, s32[]{:T(128)S(6)} %add.1698, ...), kind=kLoop, calls=%fused_computation.3.clone.1 | loop fusion | flops 11272192 | bytes 22937636 | tf_op jit(solution)/shard_map/while/body/eval_jaxpr/add | solution.py:79
  121.8 8.7 %fusion.161 = f32[4,8,16,128]{3,2,1,0:T(8,128)S(1)} fusion(f32[4,16,24,136]{3,2,1,0:T(8,128)S(1)} %get-tuple-element.359, s32[]{:T(128)} %get-tuple-element.338, s32[]{:T(128)S(6)} %add.1693, s32[]{:T(128)S(6)} %add.1694, s32[]{:T(128)S(6)} %add.1695, s32[]{:T(128)S(6)} %add.1696, s32[]{:T(128)S(6)} %add.1697, s32[]{:T(128)S(6)} %add.1698, ...), kind=kLoop, calls=%fused_computation.3.clone.1 | loop fusion | flops 11272192 | bytes 22937636 | tf_op jit(solution)/shard_map/while/body/eval_jaxpr/add | solution.py:79
  132.8 8.8 %fusion.161 = f32[4,8,16,128]{3,2,1,0:T(8,128)S(1)} fusion(f32[4,16,24,136]{3,2,1,0:T(8,128)S(1)} %get-tuple-element.359, s32[]{:T(128)} %get-tuple-element.338, s32[]{:T(128)S(6)} %add.1693, s32[]{:T(128)S(6)} %add.1694, s32[]{:T(128)S(6)} %add.1695, s32[]{:T(128)S(6)} %add.1696, s32[]{:T(128)S(6)} %add.1697, s32[]{:T(128)S(6)} %add.1698, ...), kind=kLoop, calls=%fused_computation.3.clone.1 | loop fusion | flops 11272192 | bytes 22937636 | tf_op jit(solution)/shard_map/while/body/eval_jaxpr/add | solution.py:79
  144.0 8.7 %fusion.161 = f32[4,8,16,128]{3,2,1,0:T(8,128)S(1)} fusion(f32[4,16,24,136]{3,2,1,0:T(8,128)S(1)} %get-tuple-element.359, s32[]{:T(128)} %get-tuple-element.338, s32[]{:T(128)S(6)} %add.1693, s32[]{:T(128)S(6)} %add.1694, s32[]{:T(128)S(6)} %add.1695, s32[]{:T(128)S(6)} %add.1696, s32[]{:T(128)S(6)} %add.1697, s32[]{:T(128)S(6)} %add.1698, ...), kind=kLoop, calls=%fused_computation.3.clone.1 | loop fusion | flops 11272192 | bytes 22937636 | tf_op jit(solution)/shard_map/while/body/eval_jaxpr/add | solution.py:79
  158.6 5.4 %collective-permute-start.9 = (f32[3,8,1,128]{3,1,2,0:T(8,128)S(1)}, f32[3,8,1,128]{3,1,2,0:T(8,128)S(1)}, u32[]{:S(2)}, u32[]{:S(2)}) collective-permute-start(f32[3,8,1,128]{3,1,2,0:T(8,128)S(1)} %get-tuple-element.195), channel_id=1, source_target_pairs={{0,8},{8,16},{16,24},{1,9},{9,17},{17,25},{2,10},{10,18},{18,26},{... | collective-permute-start | bytes 36872 | tf_op jit(solution)/shard_map/ppermute | solution.py:30
  165.9 5.1 %collective-permute-start.7 = (f32[3,1,16,128]{3,2,1,0:T(8,128)S(1)}, f32[3,1,16,128]{3,2,1,0:T(8,128)S(1)}, u32[]{:S(2)}, u32[]{:S(2)}) collective-permute-start(f32[3,1,16,128]{3,2,1,0:T(8,128)S(1)} %get-tuple-element.193), channel_id=1, source_target_pairs={{0,32},{32,64},{64,96},{96,128},{128,160},{160,192},{192,224},{224... | collective-permute-start | bytes 73736 | tf_op jit(solution)/shard_map/ppermute | solution.py:30
  172.7 5.4 %collective-permute-start.12 = (f32[2,16,128]{2,1,0:T(8,128)S(1)}, f32[2,16,128]{2,1,0:T(8,128)S(1)}, u32[]{:S(2)}, u32[]{:S(2)}) collective-permute-start(f32[2,16,128]{2,1,0:T(8,128)S(1)} %get-tuple-element.220), channel_id=1, source_target_pairs={{0,32},{32,64},{64,96},{96,128},{128,160},{160,192},{192,224},{224... | collective-permute-start | bytes 49160 | tf_op jit(solution)/shard_map/ppermute | solution.py:14
  180.1 4.9 %collective-permute-done.13 = f32[2,16,128]{2,1,0:T(8,128)S(1)} collective-permute-done((f32[2,16,128]{2,1,0:T(8,128)S(1)}, f32[2,16,128]{2,1,0:T(8,128)S(1)}, u32[]{:S(2)}, u32[]{:S(2)}) %collective-permute-start.13) | collective-permute-done | bytes 16416 | tf_op jit(solution)/shard_map/ppermute | solution.py:17
  185.0 3.9 %collective-permute-start.14 = (f32[12,2,128]{2,1,0:T(2,128)S(1)}, f32[12,2,128]{2,1,0:T(2,128)S(1)}, u32[]{:S(2)}, u32[]{:S(2)}) collective-permute-start(f32[12,2,128]{2,1,0:T(2,128)S(1)} %get-tuple-element.210), channel_id=1, source_target_pairs={{0,8},{8,16},{16,24},{1,9},{9,17},{17,25},{2,10},{10,18},{18,26},{... | collective-permute-start | bytes 36872 | tf_op jit(solution)/shard_map/ppermute | solution.py:14
  190.3 4.2 %collective-permute-done.15 = f32[12,2,128]{2,1,0:T(2,128)S(1)} collective-permute-done((f32[12,2,128]{2,1,0:T(2,128)S(1)}, f32[12,2,128]{2,1,0:T(2,128)S(1)}, u32[]{:S(2)}, u32[]{:S(2)}) %collective-permute-start.15) | collective-permute-done | bytes 12320 | tf_op jit(solution)/shard_map/ppermute | solution.py:17
  196.6 3.6 %collective-permute-start.17 = (f32[12,20,2]{2,1,0:T(8,128)S(1)}, f32[12,20,2]{2,1,0:T(8,128)S(1)}, u32[]{:S(2)}, u32[]{:S(2)}) collective-permute-start(f32[12,20,2]{2,1,0:T(8,128)S(1)} %get-tuple-element.209), channel_id=1, source_target_pairs={{1,0},{2,1},{3,2},{4,3},{5,4},{6,5},{7,6},{9,8},{10,9},{11,10},{12... | collective-permute-start | bytes 5768 | tf_op jit(solution)/shard_map/ppermute | solution.py:17
  203.8 5.6 %reshape.46 = f32[4,2,8,2,64,2]{5,4,3,2,1,0:T(8,128)} reshape(f32[8,16,128]{2,1,0:T(8,128)S(1)} %fusion.106) | data formatting | bytes 131072 | tf_op jit(solution)/shard_map/reshape | solution.py:101
  213.9 3.9 %collective-permute-start.19 = (f32[2,8,64]{2,1,0:T(8,128)S(1)}, f32[2,8,64]{2,1,0:T(8,128)S(1)}, u32[]{:S(2)}, u32[]{:S(2)}) collective-permute-start(f32[2,8,64]{2,1,0:T(8,128)S(1)} %get-tuple-element.229), channel_id=1, source_target_pairs={{32,0},{64,32},{96,64},{128,96},{160,128},{192,160},{224,192},{256... | collective-permute-start | bytes 12296 | tf_op jit(solution)/shard_map/ppermute | solution.py:17
  220.7 3.4 %collective-permute-start.20 = (f32[8,2,64]{2,1,0:T(2,128)S(1)}, f32[8,2,64]{2,1,0:T(2,128)S(1)}, u32[]{:S(2)}, u32[]{:S(2)}) collective-permute-start(f32[8,2,64]{2,1,0:T(2,128)S(1)} %get-tuple-element.227), channel_id=1, source_target_pairs={{0,8},{8,16},{16,24},{1,9},{9,17},{17,25},{2,10},{10,18},{18,26},{... | collective-permute-start | bytes 12296 | tf_op jit(solution)/shard_map/ppermute | solution.py:14
  225.5 4.2 %collective-permute-done.21 = f32[8,2,64]{2,1,0:T(2,128)S(1)} collective-permute-done((f32[8,2,64]{2,1,0:T(2,128)S(1)}, f32[8,2,64]{2,1,0:T(2,128)S(1)}, u32[]{:S(2)}, u32[]{:S(2)}) %collective-permute-start.21) | collective-permute-done | bytes 4128 | tf_op jit(solution)/shard_map/ppermute | solution.py:17
  231.7 3.6 %collective-permute-start.23 = (f32[8,12,2]{2,0,1:T(8,128)S(1)}, f32[8,12,2]{2,0,1:T(8,128)S(1)}, u32[]{:S(2)}, u32[]{:S(2)}) collective-permute-start(f32[8,12,2]{2,0,1:T(8,128)S(1)} %get-tuple-element.225), channel_id=1, source_target_pairs={{1,0},{2,1},{3,2},{4,3},{5,4},{6,5},{7,6},{9,8},{10,9},{11,10},{12... | collective-permute-start | bytes 2312 | tf_op jit(solution)/shard_map/ppermute | solution.py:17
  242.2 4.3 %collective-permute-start.25 = (f32[1,4,32]{2,1,0:T(4,128)S(1)}, f32[1,4,32]{2,1,0:T(4,128)S(1)}, u32[]{:S(2)}, u32[]{:S(2)}) collective-permute-start(f32[1,4,32]{2,1,0:T(4,128)S(1)} %get-tuple-element.232), channel_id=1, source_target_pairs={{0,32},{32,64},{64,96},{96,128},{128,160},{160,192},{192,224},{224... | collective-permute-start | bytes 1544 | tf_op jit(solution)/shard_map/ppermute | solution.py:30
  246.6 4.5 %collective-permute-start.27 = (f32[2,1,32]{2,1,0:T(1,128)S(1)}, f32[2,1,32]{2,1,0:T(1,128)S(1)}, u32[]{:S(2)}, u32[]{:S(2)}) collective-permute-start(f32[2,1,32]{2,1,0:T(1,128)S(1)} %get-tuple-element.234), channel_id=1, source_target_pairs={{0,8},{8,16},{16,24},{1,9},{9,17},{17,25},{2,10},{10,18},{18,26},{... | collective-permute-start | bytes 776 | tf_op jit(solution)/shard_map/ppermute | solution.py:30
  261.6 5.1 %collective-permute-start.31 = (f32[1,16,128]{2,1,0:T(8,128)S(1)}, f32[1,16,128]{2,1,0:T(8,128)S(1)}, u32[]{:S(2)}, u32[]{:S(2)}) collective-permute-start(f32[1,16,128]{2,1,0:T(8,128)S(1)} %get-tuple-element.216), channel_id=1, source_target_pairs={{0,32},{32,64},{64,96},{96,128},{128,160},{160,192},{192,224},{224... | collective-permute-start | bytes 24584 | tf_op jit(solution)/shard_map/ppermute | solution.py:30
  268.0 4.5 %collective-permute-start.33 = (f32[8,1,128]{2,1,0:T(1,128)S(1)}, f32[8,1,128]{2,1,0:T(1,128)S(1)}, u32[]{:S(2)}, u32[]{:S(2)}) collective-permute-start(f32[8,1,128]{2,1,0:T(1,128)S(1)} %get-tuple-element.218), channel_id=1, source_target_pairs={{0,8},{8,16},{16,24},{1,9},{9,17},{17,25},{2,10},{10,18},{18,26},{... | collective-permute-start | bytes 12296 | tf_op jit(solution)/shard_map/ppermute | solution.py:30
  (158 shorter events, 100.7 us)
Async XLA Ops:
  1.6 8.0 %collective-permute-start = (f32[4,4,16,128]{3,2,1,0:T(8,128)S(1)}, f32[4,4,16,128]{3,2,1,0:T(8,128)S(1)}, u32[]{:S(2)}, u32[]{:S(2)}) collective-permute-start(f32[4,4,16,128]{3,2,1,0:T(8,128)S(1)} %get-tuple-element.197), channel_id=1, source_target_pairs={{0,32},{32,64},{64,96},{96,128},{128,160},{160,192},{192,224},{224... | collective-permute-start | bytes 393224 | tf_op jit(solution)/shard_map/ppermute | solution.py:14
  6.6 8.1 %collective-permute-start.1 = (f32[4,4,16,128]{3,2,1,0:T(8,128)S(1)}, f32[4,4,16,128]{3,2,1,0:T(8,128)S(1)}, u32[]{:S(2)}, u32[]{:S(2)}) collective-permute-start(f32[4,4,16,128]{3,2,1,0:T(8,128)S(1)} %get-tuple-element.198), channel_id=1, source_target_pairs={{32,0},{64,32},{96,64},{128,96},{160,128},{192,160},{224,192},{256... | collective-permute-start | bytes 393224 | tf_op jit(solution)/shard_map/ppermute | solution.py:17
  15.8 8.6 %collective-permute-start.2 = (f32[4,16,4,128]{3,1,2,0:T(8,128)S(1)}, f32[4,16,4,128]{3,1,2,0:T(8,128)S(1)}, u32[]{:S(2)}, u32[]{:S(2)}) collective-permute-start(f32[4,16,4,128]{3,1,2,0:T(8,128)S(1)} %copy.201), channel_id=1, source_target_pairs={{0,8},{8,16},{16,24},{1,9},{9,17},{17,25},{2,10},{10,18},{18,26},{... | collective-permute-start | bytes 393224 | tf_op jit(solution)/shard_map/ppermute | solution.py:14
  19.2 8.1 %collective-permute-start.3 = (f32[4,16,4,128]{3,1,2,0:T(8,128)S(1)}, f32[4,16,4,128]{3,1,2,0:T(8,128)S(1)}, u32[]{:S(2)}, u32[]{:S(2)}) collective-permute-start(f32[4,16,4,128]{3,1,2,0:T(8,128)S(1)} %copy.202), channel_id=1, source_target_pairs={{8,0},{16,8},{24,16},{9,1},{17,9},{25,17},{10,2},{18,10},{26,18},{... | collective-permute-start | bytes 393224 | tf_op jit(solution)/shard_map/ppermute | solution.py:17
  37.2 10.6 %collective-permute-start.4 = (f32[4,16,24,4]{2,1,3,0:T(8,128)S(1)}, f32[4,16,24,4]{2,1,3,0:T(8,128)S(1)}, u32[]{:S(2)}, u32[]{:S(2)}) collective-permute-start(f32[4,16,24,4]{2,1,3,0:T(8,128)S(1)} %get-tuple-element.187), channel_id=1, source_target_pairs={{0,1},{1,2},{2,3},{3,4},{4,5},{5,6},{6,7},{8,9},{9,10},{10,11},{11... | collective-permute-start | bytes 73736 | tf_op jit(solution)/shard_map/ppermute | solution.py:14
  39.2 10.0 %collective-permute-start.5 = (f32[4,16,24,4]{2,1,3,0:T(8,128)S(1)}, f32[4,16,24,4]{2,1,3,0:T(8,128)S(1)}, u32[]{:S(2)}, u32[]{:S(2)}) collective-permute-start(f32[4,16,24,4]{2,1,3,0:T(8,128)S(1)} %get-tuple-element.188), channel_id=1, source_target_pairs={{1,0},{2,1},{3,2},{4,3},{5,4},{6,5},{7,6},{9,8},{10,9},{11,10},{12... | collective-permute-start | bytes 73736 | tf_op jit(solution)/shard_map/ppermute | solution.py:17
  152.9 13.0 %collective-permute-start.8 = (f32[3,8,1,128]{3,1,2,0:T(8,128)S(1)}, f32[3,8,1,128]{3,1,2,0:T(8,128)S(1)}, u32[]{:S(2)}, u32[]{:S(2)}) collective-permute-start(f32[3,8,1,128]{3,1,2,0:T(8,128)S(1)} %get-tuple-element.196), channel_id=1, source_target_pairs={{8,0},{16,8},{24,16},{9,1},{17,9},{25,17},{10,2},{18,10},{26,18},{... | collective-permute-start | bytes 36872 | tf_op jit(solution)/shard_map/ppermute | solution.py:31
  154.3 16.9 %collective-permute-start.10 = (f32[3,8,16,1]{3,2,1,0:T(8,128)S(1)}, f32[3,8,16,1]{3,2,1,0:T(8,128)S(1)}, u32[]{:S(2)}, u32[]{:S(2)}) collective-permute-start(f32[3,8,16,1]{3,2,1,0:T(8,128)S(1)} %get-tuple-element.191), channel_id=1, source_target_pairs={{1,0},{2,1},{3,2},{4,3},{5,4},{6,5},{7,6},{9,8},{10,9},{11,10},{12... | collective-permute-start | bytes 4616 | tf_op jit(solution)/shard_map/ppermute | solution.py:31
  156.2 15.0 %collective-permute-start.11 = (f32[3,8,16,1]{3,2,1,0:T(8,128)S(1)}, f32[3,8,16,1]{3,2,1,0:T(8,128)S(1)}, u32[]{:S(2)}, u32[]{:S(2)}) collective-permute-start(f32[3,8,16,1]{3,2,1,0:T(8,128)S(1)} %get-tuple-element.192), channel_id=1, source_target_pairs={{0,1},{1,2},{2,3},{3,4},{4,5},{5,6},{6,7},{8,9},{9,10},{10,11},{11... | collective-permute-start | bytes 4616 | tf_op jit(solution)/shard_map/ppermute | solution.py:30
  158.6 12.5 %collective-permute-start.9 = (f32[3,8,1,128]{3,1,2,0:T(8,128)S(1)}, f32[3,8,1,128]{3,1,2,0:T(8,128)S(1)}, u32[]{:S(2)}, u32[]{:S(2)}) collective-permute-start(f32[3,8,1,128]{3,1,2,0:T(8,128)S(1)} %get-tuple-element.195), channel_id=1, source_target_pairs={{0,8},{8,16},{16,24},{1,9},{9,17},{17,25},{2,10},{10,18},{18,26},{... | collective-permute-start | bytes 36872 | tf_op jit(solution)/shard_map/ppermute | solution.py:30
  164.0 7.2 %collective-permute-start.6 = (f32[3,1,16,128]{3,2,1,0:T(8,128)S(1)}, f32[3,1,16,128]{3,2,1,0:T(8,128)S(1)}, u32[]{:S(2)}, u32[]{:S(2)}) collective-permute-start(f32[3,1,16,128]{3,2,1,0:T(8,128)S(1)} %get-tuple-element.194), channel_id=1, source_target_pairs={{32,0},{64,32},{96,64},{128,96},{160,128},{192,160},{224,192},{256... | collective-permute-start | bytes 73736 | tf_op jit(solution)/shard_map/ppermute | solution.py:31
  165.9 6.6 %collective-permute-start.7 = (f32[3,1,16,128]{3,2,1,0:T(8,128)S(1)}, f32[3,1,16,128]{3,2,1,0:T(8,128)S(1)}, u32[]{:S(2)}, u32[]{:S(2)}) collective-permute-start(f32[3,1,16,128]{3,2,1,0:T(8,128)S(1)} %get-tuple-element.193), channel_id=1, source_target_pairs={{0,32},{32,64},{64,96},{96,128},{128,160},{160,192},{192,224},{224... | collective-permute-start | bytes 73736 | tf_op jit(solution)/shard_map/ppermute | solution.py:30
  172.7 7.4 %collective-permute-start.12 = (f32[2,16,128]{2,1,0:T(8,128)S(1)}, f32[2,16,128]{2,1,0:T(8,128)S(1)}, u32[]{:S(2)}, u32[]{:S(2)}) collective-permute-start(f32[2,16,128]{2,1,0:T(8,128)S(1)} %get-tuple-element.220), channel_id=1, source_target_pairs={{0,32},{32,64},{64,96},{96,128},{128,160},{160,192},{192,224},{224... | collective-permute-start | bytes 49160 | tf_op jit(solution)/shard_map/ppermute | solution.py:14
  178.1 6.8 %collective-permute-start.13 = (f32[2,16,128]{2,1,0:T(8,128)S(1)}, f32[2,16,128]{2,1,0:T(8,128)S(1)}, u32[]{:S(2)}, u32[]{:S(2)}) collective-permute-start(f32[2,16,128]{2,1,0:T(8,128)S(1)} %get-tuple-element.221), channel_id=1, source_target_pairs={{32,0},{64,32},{96,64},{128,96},{160,128},{192,160},{224,192},{256... | collective-permute-start | bytes 49160 | tf_op jit(solution)/shard_map/ppermute | solution.py:17
  185.0 5.3 %collective-permute-start.14 = (f32[12,2,128]{2,1,0:T(2,128)S(1)}, f32[12,2,128]{2,1,0:T(2,128)S(1)}, u32[]{:S(2)}, u32[]{:S(2)}) collective-permute-start(f32[12,2,128]{2,1,0:T(2,128)S(1)} %get-tuple-element.210), channel_id=1, source_target_pairs={{0,8},{8,16},{16,24},{1,9},{9,17},{17,25},{2,10},{10,18},{18,26},{... | collective-permute-start | bytes 36872 | tf_op jit(solution)/shard_map/ppermute | solution.py:14
  188.9 5.6 %collective-permute-start.15 = (f32[12,2,128]{2,1,0:T(2,128)S(1)}, f32[12,2,128]{2,1,0:T(2,128)S(1)}, u32[]{:S(2)}, u32[]{:S(2)}) collective-permute-start(f32[12,2,128]{2,1,0:T(2,128)S(1)} %get-tuple-element.211), channel_id=1, source_target_pairs={{8,0},{16,8},{24,16},{9,1},{17,9},{25,17},{10,2},{18,10},{26,18},{... | collective-permute-start | bytes 36872 | tf_op jit(solution)/shard_map/ppermute | solution.py:17
  194.7 6.5 %collective-permute-start.16 = (f32[12,20,2]{2,1,0:T(8,128)S(1)}, f32[12,20,2]{2,1,0:T(8,128)S(1)}, u32[]{:S(2)}, u32[]{:S(2)}) collective-permute-start(f32[12,20,2]{2,1,0:T(8,128)S(1)} %get-tuple-element.208), channel_id=1, source_target_pairs={{0,1},{1,2},{2,3},{3,4},{4,5},{5,6},{6,7},{8,9},{9,10},{10,11},{11... | collective-permute-start | bytes 5768 | tf_op jit(solution)/shard_map/ppermute | solution.py:14
  196.6 6.3 %collective-permute-start.17 = (f32[12,20,2]{2,1,0:T(8,128)S(1)}, f32[12,20,2]{2,1,0:T(8,128)S(1)}, u32[]{:S(2)}, u32[]{:S(2)}) collective-permute-start(f32[12,20,2]{2,1,0:T(8,128)S(1)} %get-tuple-element.209), channel_id=1, source_target_pairs={{1,0},{2,1},{3,2},{4,3},{5,4},{6,5},{7,6},{9,8},{10,9},{11,10},{12... | collective-permute-start | bytes 5768 | tf_op jit(solution)/shard_map/ppermute | solution.py:17
  212.0 5.9 %collective-permute-start.18 = (f32[2,8,64]{2,1,0:T(8,128)S(1)}, f32[2,8,64]{2,1,0:T(8,128)S(1)}, u32[]{:S(2)}, u32[]{:S(2)}) collective-permute-start(f32[2,8,64]{2,1,0:T(8,128)S(1)} %get-tuple-element.228), channel_id=1, source_target_pairs={{0,32},{32,64},{64,96},{96,128},{128,160},{160,192},{192,224},{224... | collective-permute-start | bytes 12296 | tf_op jit(solution)/shard_map/ppermute | solution.py:14
  213.9 6.8 %collective-permute-start.19 = (f32[2,8,64]{2,1,0:T(8,128)S(1)}, f32[2,8,64]{2,1,0:T(8,128)S(1)}, u32[]{:S(2)}, u32[]{:S(2)}) collective-permute-start(f32[2,8,64]{2,1,0:T(8,128)S(1)} %get-tuple-element.229), channel_id=1, source_target_pairs={{32,0},{64,32},{96,64},{128,96},{160,128},{192,160},{224,192},{256... | collective-permute-start | bytes 12296 | tf_op jit(solution)/shard_map/ppermute | solution.py:17
  224.1 5.5 %collective-permute-start.21 = (f32[8,2,64]{2,1,0:T(2,128)S(1)}, f32[8,2,64]{2,1,0:T(2,128)S(1)}, u32[]{:S(2)}, u32[]{:S(2)}) collective-permute-start(f32[8,2,64]{2,1,0:T(2,128)S(1)} %get-tuple-element.226), channel_id=1, source_target_pairs={{8,0},{16,8},{24,16},{9,1},{17,9},{25,17},{10,2},{18,10},{26,18},{... | collective-permute-start | bytes 12296 | tf_op jit(solution)/shard_map/ppermute | solution.py:17
  229.7 6.2 %collective-permute-start.22 = (f32[8,12,2]{2,0,1:T(8,128)S(1)}, f32[8,12,2]{2,0,1:T(8,128)S(1)}, u32[]{:S(2)}, u32[]{:S(2)}) collective-permute-start(f32[8,12,2]{2,0,1:T(8,128)S(1)} %get-tuple-element.224), channel_id=1, source_target_pairs={{0,1},{1,2},{2,3},{3,4},{4,5},{5,6},{6,7},{8,9},{9,10},{10,11},{11... | collective-permute-start | bytes 2312 | tf_op jit(solution)/shard_map/ppermute | solution.py:14
  231.7 5.4 %collective-permute-start.23 = (f32[8,12,2]{2,0,1:T(8,128)S(1)}, f32[8,12,2]{2,0,1:T(8,128)S(1)}, u32[]{:S(2)}, u32[]{:S(2)}) collective-permute-start(f32[8,12,2]{2,0,1:T(8,128)S(1)} %get-tuple-element.225), channel_id=1, source_target_pairs={{1,0},{2,1},{3,2},{4,3},{5,4},{6,5},{7,6},{9,8},{10,9},{11,10},{12... | collective-permute-start | bytes 2312 | tf_op jit(solution)/shard_map/ppermute | solution.py:17
  238.2 20.4 %collective-permute-start.24 = (f32[1,4,32]{2,1,0:T(4,128)S(1)}, f32[1,4,32]{2,1,0:T(4,128)S(1)}, u32[]{:S(2)}, u32[]{:S(2)}) collective-permute-start(f32[1,4,32]{2,1,0:T(4,128)S(1)} %get-tuple-element.233), channel_id=1, source_target_pairs={{32,0},{64,32},{96,64},{128,96},{160,128},{192,160},{224,192},{256... | collective-permute-start | bytes 1544 | tf_op jit(solution)/shard_map/ppermute | solution.py:31
  240.9 12.8 %collective-permute-start.26 = (f32[2,1,32]{2,1,0:T(1,128)S(1)}, f32[2,1,32]{2,1,0:T(1,128)S(1)}, u32[]{:S(2)}, u32[]{:S(2)}) collective-permute-start(f32[2,1,32]{2,1,0:T(1,128)S(1)} %get-tuple-element.235), channel_id=1, source_target_pairs={{8,0},{16,8},{24,16},{9,1},{17,9},{25,17},{10,2},{18,10},{26,18},{... | collective-permute-start | bytes 776 | tf_op jit(solution)/shard_map/ppermute | solution.py:31
  242.2 16.4 %collective-permute-start.25 = (f32[1,4,32]{2,1,0:T(4,128)S(1)}, f32[1,4,32]{2,1,0:T(4,128)S(1)}, u32[]{:S(2)}, u32[]{:S(2)}) collective-permute-start(f32[1,4,32]{2,1,0:T(4,128)S(1)} %get-tuple-element.232), channel_id=1, source_target_pairs={{0,32},{32,64},{64,96},{96,128},{128,160},{160,192},{192,224},{224... | collective-permute-start | bytes 1544 | tf_op jit(solution)/shard_map/ppermute | solution.py:30
  246.6 9.1 %collective-permute-start.27 = (f32[2,1,32]{2,1,0:T(1,128)S(1)}, f32[2,1,32]{2,1,0:T(1,128)S(1)}, u32[]{:S(2)}, u32[]{:S(2)}) collective-permute-start(f32[2,1,32]{2,1,0:T(1,128)S(1)} %get-tuple-element.234), channel_id=1, source_target_pairs={{0,8},{8,16},{16,24},{1,9},{9,17},{17,25},{2,10},{10,18},{18,26},{... | collective-permute-start | bytes 776 | tf_op jit(solution)/shard_map/ppermute | solution.py:30
  259.6 17.4 %collective-permute-start.30 = (f32[1,16,128]{2,1,0:T(8,128)S(1)}, f32[1,16,128]{2,1,0:T(8,128)S(1)}, u32[]{:S(2)}, u32[]{:S(2)}) collective-permute-start(f32[1,16,128]{2,1,0:T(8,128)S(1)} %get-tuple-element.217), channel_id=1, source_target_pairs={{32,0},{64,32},{96,64},{128,96},{160,128},{192,160},{224,192},{256... | collective-permute-start | bytes 24584 | tf_op jit(solution)/shard_map/ppermute | solution.py:31
  261.6 15.5 %collective-permute-start.31 = (f32[1,16,128]{2,1,0:T(8,128)S(1)}, f32[1,16,128]{2,1,0:T(8,128)S(1)}, u32[]{:S(2)}, u32[]{:S(2)}) collective-permute-start(f32[1,16,128]{2,1,0:T(8,128)S(1)} %get-tuple-element.216), channel_id=1, source_target_pairs={{0,32},{32,64},{64,96},{96,128},{128,160},{160,192},{192,224},{224... | collective-permute-start | bytes 24584 | tf_op jit(solution)/shard_map/ppermute | solution.py:30
  266.7 7.9 %collective-permute-start.32 = (f32[8,1,128]{2,1,0:T(1,128)S(1)}, f32[8,1,128]{2,1,0:T(1,128)S(1)}, u32[]{:S(2)}, u32[]{:S(2)}) collective-permute-start(f32[8,1,128]{2,1,0:T(1,128)S(1)} %get-tuple-element.219), channel_id=1, source_target_pairs={{8,0},{16,8},{24,16},{9,1},{17,9},{25,17},{10,2},{18,10},{26,18},{... | collective-permute-start | bytes 12296 | tf_op jit(solution)/shard_map/ppermute | solution.py:31
  268.0 9.0 %collective-permute-start.33 = (f32[8,1,128]{2,1,0:T(1,128)S(1)}, f32[8,1,128]{2,1,0:T(1,128)S(1)}, u32[]{:S(2)}, u32[]{:S(2)}) collective-permute-start(f32[8,1,128]{2,1,0:T(1,128)S(1)} %get-tuple-element.218), channel_id=1, source_target_pairs={{0,8},{8,16},{16,24},{1,9},{9,17},{17,25},{2,10},{10,18},{18,26},{... | collective-permute-start | bytes 12296 | tf_op jit(solution)/shard_map/ppermute | solution.py:30
  274.6 5.6 %collective-permute-start.35 = (f32[8,16,1]{2,1,0:T(8,128)S(1)}, f32[8,16,1]{2,1,0:T(8,128)S(1)}, u32[]{:S(2)}, u32[]{:S(2)}) collective-permute-start(f32[8,16,1]{2,1,0:T(8,128)S(1)} %get-tuple-element.215), channel_id=1, source_target_pairs={{0,1},{1,2},{2,3},{3,4},{4,5},{5,6},{6,7},{8,9},{9,10},{10,11},{11... | collective-permute-start | bytes 1544 | tf_op jit(solution)/shard_map/ppermute | solution.py:30
  (6 other events, 45.7 us)
where the time goes:
time: 283 us; the launch traced here: 281 us
  other arithmetic  111 us (39%)
  starting transfers between devices  104 us (37%)
  waiting for transfers between devices  32.5 us (11%)
  local copies, waits for them, and re-layouts  31.6 us (11%)
    add x9, other arithmetic, one_plane(): summed = summed + (plane_weight * weight_y[step_y])[None] * along_z  78.8 us
    ppermute x9, starting transfers between devices, with_halo(): lax.ppermute(last, axis, up)  35.8 us
    ppermute x9, starting transfers between devices, padded_2(): lax.ppermute(lax.slice_in_dim(block, block.shape[dim] - width, None, axis...  28.9 us
    ppermute x9, waiting for transfers between devices, padded_2(): lax.ppermute(lax.slice_in_dim(block, 0, width, axis=dim), axis, backward)  24.1 us
    ppermute x9, starting transfers between devices, padded_2(): lax.ppermute(lax.slice_in_dim(block, 0, width, axis=dim), axis, backward)  22.6 us
    ppermute x9, starting transfers between devices, with_halo(): lax.ppermute(initial, axis, [(b, a) for a, b in up])  16.8 us
    mul x9, other arithmetic, one_plane(): summed = summed + (plane_weight * weight_y[step_y])[None] * along_z  13.7 us
    concatenate x7, other arithmetic, padded_2(): block = jnp.concatenate([low, block, high], axis=dim)  10.3 us
  transfers between devices with their start and end apart: 36, of which 12 were waited for; matrix products, arithmetic and copies ran while one was open for 5% of the time, Pallas kernels for 0%

commit v1 on v0

--- a/solution.py
+++ b/solution.py
@@ -1,9 +1,170 @@
+import functools
+
 import jax
 import jax.numpy as jnp
 from jax import lax
+from jax.experimental import pallas as pl
+from jax.experimental.pallas import tpu as pltpu
 from jax.sharding import PartitionSpec as P
 
 RELAX_WEIGHT = 6.0 / 7.0
+VMEM = pl.BlockSpec(memory_space=pltpu.VMEM)
+SMEM = pl.BlockSpec(memory_space=pltpu.SMEM)
+PARAMS = pltpu.CompilerParams(vmem_limit_bytes=48 * 1024 * 1024)
+
+
+def call(kernel, outs, scratch=(), scalars=0, inputs=0):
+    return pl.pallas_call(
+        kernel,
+        out_shape=[jax.ShapeDtypeStruct(shape, dtype) for shape, dtype in outs],
+        in_specs=[SMEM] * scalars + [VMEM] * inputs,
+        out_specs=[VMEM] * len(outs),
+        scratch_shapes=list(scratch),
+        compiler_params=PARAMS,
+    )
+
+
+def shift_ring(value, axis, step):
+    count = lax.axis_size(axis)
+    return lax.ppermute(value, axis, [(i, (i + step) % count) for i in range(count)])
+
+
+def own_kernel(velocity, density, offsets, eighths, fields_t, code_t):
+    for a in range(3):
+        fields_t[a] = velocity[a].reshape(128, 128).T
+    fields_t[3] = density[...].reshape(128, 128).T
+    code = (offsets[0] + 4) + (offsets[1] + 4) * 8 + (offsets[2] + 4) * 64
+    code = code + eighths[0] * 512 + eighths[1] * 4096 + eighths[2] * 32768
+    code_t[...] = code.astype(jnp.float32).reshape(128, 128).T.astype(jnp.int32)
+
+
+def rows_kernel(inside, velocity, density, low, high, to_low, to_high):
+    for f in range(4):
+        for pair in range(8):
+            for half in range(2):
+                plane = 2 * pair + half
+                if plane < 4:
+                    rows = low[f, plane] * inside[0]
+                elif plane >= 12:
+                    rows = high[f, plane - 12] * inside[1]
+                elif f < 3:
+                    rows = velocity[f, plane - 4]
+                else:
+                    rows = density[plane - 4]
+                to_low[f, pair, 4 * half : 4 * half + 4] = rows[0:4]
+                to_high[f, pair, 4 * half : 4 * half + 4] = rows[12:16]
+
+
+def planes_kernel(inside, low, high, planes_t):
+    for f in range(4):
+        both = jnp.concatenate(
+            [low[f].reshape(64, 128) * inside[0], high[f].reshape(64, 128) * inside[1]], axis=0
+        )
+        planes_t[f] = both.T
+
+
+def columns_kernel(inside, fields_t, planes_t, low, high, rows_t, to_low, to_high):
+    for f in range(4):
+        both = jnp.concatenate(
+            [low[f].reshape(64, 128) * inside[2], high[f].reshape(64, 128) * inside[3]], axis=0
+        )
+        turned = both.T
+        rows_t[f] = turned
+        for group, source in enumerate((fields_t[f], planes_t[f], turned)):
+            to_low[f, group] = source[0:8]
+            to_high[f, group] = source[120:128]
+
+
+def advect_kernel(inside, code_t, fields_t, planes_t, rows_t, low, high, moved_t, moved, padded):
+    for f in range(4):
+        for group, source in enumerate((fields_t, planes_t, rows_t)):
+            padded[f, group, 8:136] = source[f]
+            padded[f, group, 0:8] = low[f, group] * inside[4]
+            padded[f, group, 136:144] = high[f, group] * inside[5]
+
+    def tile(step, carry):
+        start = pl.multiple_of(step * 8, 8)
+        code = code_t[pl.ds(start, 8), :]
+        lane = lax.broadcasted_iota(jnp.int32, (8, 128), 1)
+        x = (lane >> 4) + (code & 7)
+        y = (lane & 15) + ((code >> 3) & 7)
+        level = (code >> 6) & 7
+        fx = ((code >> 9) & 7).astype(jnp.float32) / 8.0
+        fy = ((code >> 12) & 7).astype(jnp.float32) / 8.0
+        fz = ((code >> 15) & 7).astype(jnp.float32) / 8.0
+        corners = []
+        for cx in (0, 1):
+            for cy in (0, 1):
+                xc, yc = x + cx, y + cy
+                low_x, high_x = xc < 4, xc >= 12
+                in_rows = (yc < 4) | (yc >= 20)
+                in_planes = low_x | high_x
+                plane = xc - jnp.where(low_x, 0, jnp.where(high_x, 8, 4))
+                by_rows = xc * 4 + (yc & 3) + jnp.where(yc >= 20, 64, 0)
+                at = jnp.where(in_rows, by_rows, plane * 16 + yc - 4)
+                weight = (fx if cx else 1.0 - fx) * (fy if cy else 1.0 - fy)
+                corners.append((at, in_rows, in_planes, weight))
+        sums = [jnp.zeros((8, 128), jnp.float32) for _ in range(4)]
+        for dz in range(9):
+            weight_z = jnp.where(level == dz, 1.0 - fz, jnp.where(level == dz - 1, fz, 0.0))
+            for f in range(4):
+                groups = [padded[f, group, pl.ds(start + (4 + dz), 8), :] for group in range(3)]
+                total = None
+                for at, in_rows, in_planes, weight in corners:
+                    picked = [
+                        jnp.take_along_axis(group, at, axis=1, mode="promise_in_bounds")
+                        for group in groups
+                    ]
+                    value = jnp.where(
+                        in_rows, picked[2], jnp.where(in_planes, picked[1], picked[0])
+                    )
+                    total = weight * value if total is None else total + weight * value
+                sums[f] = sums[f] + weight_z * total
+        for f in range(4):
+            moved_t[f, pl.ds(start, 8), :] = sums[f]
+        return carry
+
+    lax.fori_loop(0, 16, tile, 0)
+    for f in range(4):
+        moved[f] = moved_t[f].T.reshape(8, 16, 128)
+
+
+def ends(axis):
+    place = lax.axis_index(axis)
+    return [place > 0, place < lax.axis_size(axis) - 1]
+
+
+def advect(inside, velocity, density, offsets, eighths):
+    f32 = jnp.float32
+    low_planes = jnp.concatenate([velocity[:, 0:4], density[None, 0:4]], axis=0)
+    high_planes = jnp.concatenate([velocity[:, 4:8], density[None, 4:8]], axis=0)
+    low = shift_ring(high_planes, "gx", 1)
+    high = shift_ring(low_planes, "gx", -1)
+    fields_t, code_t = call(
+        own_kernel, [((4, 128, 128), f32), ((128, 128), jnp.int32)], inputs=4
+    )(velocity, density, offsets, eighths)
+    strip = ((4, 8, 8, 128), f32)
+    to_low, to_high = call(rows_kernel, [strip, strip], scalars=1, inputs=4)(
+        inside, velocity, density, low, high
+    )
+    rows_low = shift_ring(to_high, "gy", 1)
+    rows_high = shift_ring(to_low, "gy", -1)
+    (planes_t,) = call(planes_kernel, [((4, 128, 128), f32)], scalars=1, inputs=2)(
+        inside, low, high
+    )
+    edge = ((4, 3, 8, 128), f32)
+    rows_t, to_low, to_high = call(
+        columns_kernel, [((4, 128, 128), f32), edge, edge], scalars=1, inputs=4
+    )(inside, fields_t, planes_t, rows_low, rows_high)
+    columns_low = shift_ring(to_high, "gz", 1)
+    columns_high = shift_ring(to_low, "gz", -1)
+    return call(
+        advect_kernel,
+        [((4, 128, 128), f32), ((4, 8, 16, 128), f32)],
+        scratch=[pltpu.VMEM((4, 3, 144, 128), f32)],
+        scalars=1,
+        inputs=6,
+    )(inside, code_t, fields_t, planes_t, rows_t, columns_low, columns_high)
 
 
 def padded_2(block, sides, width):
@@ -50,39 +211,6 @@
     return 6.0 * padded[1:-1, 1:-1, 1:-1] - neighbours(padded)
 
 
-def axis_weights(offset_axis, fraction_axis):
-    levels = lax.broadcasted_iota(jnp.int32, (9, 1, 1, 1), 0) - 4
-    lower = jnp.where(offset_axis[None] == levels, 1.0 - fraction_axis[None], jnp.float32(0.0))
-    upper = jnp.where(offset_axis[None] == levels - 1, fraction_axis[None], jnp.float32(0.0))
-    return lower + upper
-
-
-def advect_block(padded, offsets, eighths):
-    field_count = padded.shape[0]
-    box_shape = offsets.shape[1:]
-    fraction = eighths.astype(jnp.float32) / 8.0
-    weight_x = axis_weights(offsets[0], fraction[0])
-    weight_y = axis_weights(offsets[1], fraction[1])
-    weight_z = axis_weights(offsets[2], fraction[2])
-
-    def one_plane(step_x, summed):
-        slab = lax.dynamic_slice_in_dim(padded, step_x, box_shape[0], 1)
-        plane_weight = lax.dynamic_index_in_dim(weight_x, step_x, 0, keepdims=False)
-        for step_y in range(9):
-            window = slab[:, :, step_y : step_y + box_shape[1], :]
-            along_z = jnp.zeros((field_count,) + box_shape, jnp.float32)
-            for step_z in range(9):
-                along_z = (
-                    along_z
-                    + weight_z[step_z][None] * window[:, :, :, step_z : step_z + box_shape[2]]
-                )
-            summed = summed + (plane_weight * weight_y[step_y])[None] * along_z
-        return summed
-
-    summed = jnp.zeros((field_count,) + box_shape, jnp.float32)
-    return lax.fori_loop(0, 9, one_plane, summed)
-
-
 def divergence_of(velocity_pad):
     part_x = velocity_pad[0, 2:, 1:-1, 1:-1] - velocity_pad[0, :-2, 1:-1, 1:-1]
     part_y = velocity_pad[1, 1:-1, 2:, 1:-1] - velocity_pad[1, 1:-1, :-2, 1:-1]
@@ -146,9 +274,8 @@
 
 
 def body(velocity, density, offsets, eighths):
-    fields = jnp.concatenate([velocity, density[None]], axis=0)
-    padded = padded_2(fields, (("gx", 1), ("gy", 2), ("gz", 3)), 4)
-    advected = advect_block(padded, offsets, eighths)
+    inside = jnp.stack(ends("gx") + ends("gy") + ends("gz")).astype(jnp.float32)
+    _, advected = advect(inside, velocity, density, offsets, eighths)
     new_density = advected[3]
     moved_velocity = advected[:3]
     velocity_pad = with_halo(moved_velocity, (("gx", 1), ("gy", 2), ("gz", 3)), 1)

time: 283 us -> 178 us (0.63)
  the two profiles are of different devices: /device:TPU:248 before, /device:TPU:112 now
where the time goes in v1:
time: 178 us; the launch traced here: 177 us
  starting transfers between devices  102 us (57%)
  waiting for transfers between devices  35.6 us (20%)
  Pallas kernels  19.2 us (11%)
  local copies, waits for them, and re-layouts  13.4 us (8%)
  other arithmetic  5.41 us (3%)
    ppermute x9, starting transfers between devices, with_halo(): lax.ppermute(last, axis, up)  35 us
    ppermute x6, waiting for transfers between devices, padded_2(): lax.ppermute(lax.slice_in_dim(block, 0, width, axis=dim), axis, backward)  18.9 us
    ppermute x9, starting transfers between devices, with_halo(): lax.ppermute(initial, axis, [(b, a) for a, b in up])  17.7 us
    ppermute x6, starting transfers between devices, padded_2(): lax.ppermute(lax.slice_in_dim(block, block.shape[dim] - width, None, axis...  17.7 us
    pallas_call x1, Pallas kernels, advect(): call(advect_kernel, [((4, 128, 128), f32), ((4, 8, 16, 128), f32)], scrat...  17.1 us
    ppermute x6, starting transfers between devices, shift_ring(): lax.ppermute(value, axis, [(i, (i + step) % count) for i in range(count)])  15.8 us
    ppermute x6, starting transfers between devices, padded_2(): lax.ppermute(lax.slice_in_dim(block, 0, width, axis=dim), axis, backward)  15.7 us
    ppermute x6, waiting for transfers between devices, shift_ring(): lax.ppermute(value, axis, [(i, (i + step) % count) for i in range(count)])  8.28 us
  transfers between devices with their start and end apart: 36, of which 15 were waited for; matrix products, arithmetic and copies ran while one was open for 1% of the time, Pallas kernels for 0%

profile of v1, /device:TPU:112, one launch (start us, length us, event | category | flops | bytes accessed | tf_op | source)
XLA Modules:
  0.0 176.9 jit_solution(3019304954836509043)
XLA Ops:
  2.4 5.0 %collective-permute-start = (f32[4,4,16,128]{3,2,1,0:T(8,128)S(1)}, f32[4,4,16,128]{3,2,1,0:T(8,128)S(1)}, u32[]{:S(2)}, u32[]{:S(2)}) collective-permute-start(f32[4,4,16,128]{3,2,1,0:T(8,128)S(1)} %pad_maximum_fusion.2), channel_id=1, source_target_pairs={{0,32},{32,64},{64,96},{96,128},{128,160},{160,192},{192,224},{224... | collective-permute-start | bytes 393224 | tf_op jit(solution)/shard_map/ppermute | solution.py:29
  10.2 5.4 %collective-permute-done.1.high = f32[4,4,16,128]{3,2,1,0:T(8,128)S(1)} collective-permute-done((f32[4,4,16,128]{3,2,1,0:T(8,128)S(1)}, f32[4,4,16,128]{3,2,1,0:T(8,128)S(1)}, u32[]{:S(2)}, u32[]{:S(2)}) %collective-permute-start.1) | collective-permute-done | bytes 131104 | tf_op jit(solution)/shard_map/ppermute | solution.py:29
  17.9 3.4 %collective-permute-start.2 = (f32[4,8,8,128]{3,2,1,0:T(8,128)S(1)}, f32[4,8,8,128]{3,2,1,0:T(8,128)S(1)}, u32[]{:S(2)}, u32[]{:S(2)}) collective-permute-start(f32[4,8,8,128]{3,2,1,0:T(8,128)S(1)} %get-tuple-element.13), channel_id=1, source_target_pairs={{0,8},{8,16},{16,24},{24,0},{1,9},{9,17},{17,25},{25,1},{2,10},{10... | collective-permute-start | bytes 393224 | tf_op jit(solution)/shard_map/ppermute | solution.py:29
  21.3 3.7 %collective-permute-start.3 = (f32[4,8,8,128]{3,2,1,0:T(8,128)S(1)}, f32[4,8,8,128]{3,2,1,0:T(8,128)S(1)}, u32[]{:S(2)}, u32[]{:S(2)}) collective-permute-start(f32[4,8,8,128]{3,2,1,0:T(8,128)S(1)} %get-tuple-element.14), channel_id=1, source_target_pairs={{0,24},{8,0},{16,8},{24,16},{1,25},{9,1},{17,9},{25,17},{2,26},{10... | collective-permute-start | bytes 393224 | tf_op jit(solution)/shard_map/ppermute | solution.py:29
  32.4 17.1 %shard_map.71 = (f32[4,128,128]{2,1,0:T(8,128)}, f32[4,8,16,128]{3,2,1,0:T(8,128)S(1)}) custom-call(f32[6]{0:T(128)S(1)} %convert_element_type.21.inside, s32[128,128]{1,0:T(8,128)S(1)} %get-tuple-element.11.code_t, f32[4,128,128]{2,1,0:T(8,128)S(1)} %get-tuple-element.12.fields_t, f32[4,128,128]{2,1,0:T(8,128)S(1)} %shard_map.68.planes_t, ...), custom_call_target="tpu_custom_call" | custom-call | tf_op jit(solution)/shard_map/pallas_call | solution.py:161
  50.9 3.7 %collective-permute-start.10 = (f32[3,8,16,1]{3,2,1,0:T(8,128)S(1)}, f32[3,8,16,1]{3,2,1,0:T(8,128)S(1)}, u32[]{:S(2)}, u32[]{:S(2)}) collective-permute-start(f32[3,8,16,1]{3,2,1,0:T(8,128)S(1)} %get-tuple-element.21), channel_id=1, source_target_pairs={{1,0},{2,1},{3,2},{4,3},{5,4},{6,5},{7,6},{9,8},{10,9},{11,10},{12... | collective-permute-start | bytes 4616 | tf_op jit(solution)/shard_map/ppermute | solution.py:192
  54.6 1.9 %collective-permute-start.11 = (f32[3,8,16,1]{3,2,1,0:T(8,128)S(1)}, f32[3,8,16,1]{3,2,1,0:T(8,128)S(1)}, u32[]{:S(2)}, u32[]{:S(2)}) collective-permute-start(f32[3,8,16,1]{3,2,1,0:T(8,128)S(1)} %get-tuple-element.22), channel_id=1, source_target_pairs={{0,1},{1,2},{2,3},{3,4},{4,5},{5,6},{6,7},{8,9},{9,10},{10,11},{11... | collective-permute-start | bytes 4616 | tf_op jit(solution)/shard_map/ppermute | solution.py:191
  56.5 1.9 %collective-permute-start.6 = (f32[3,1,16,128]{3,2,1,0:T(8,128)S(1)}, f32[3,1,16,128]{3,2,1,0:T(8,128)S(1)}, u32[]{:S(2)}, u32[]{:S(2)}) collective-permute-start(f32[3,1,16,128]{3,2,1,0:T(8,128)S(1)} %get-tuple-element.24), channel_id=1, source_target_pairs={{32,0},{64,32},{96,64},{128,96},{160,128},{192,160},{224,192},{256... | collective-permute-start | bytes 73736 | tf_op jit(solution)/shard_map/ppermute | solution.py:192
  58.4 5.1 %collective-permute-start.7 = (f32[3,1,16,128]{3,2,1,0:T(8,128)S(1)}, f32[3,1,16,128]{3,2,1,0:T(8,128)S(1)}, u32[]{:S(2)}, u32[]{:S(2)}) collective-permute-start(f32[3,1,16,128]{3,2,1,0:T(8,128)S(1)} %get-tuple-element.23), channel_id=1, source_target_pairs={{0,32},{32,64},{64,96},{96,128},{128,160},{160,192},{192,224},{224... | collective-permute-start | bytes 73736 | tf_op jit(solution)/shard_map/ppermute | solution.py:191
  63.6 4.3 %collective-permute-start.9 = (f32[3,8,1,128]{3,2,1,0:T(1,128)S(1)}, f32[3,8,1,128]{3,2,1,0:T(1,128)S(1)}, u32[]{:S(2)}, u32[]{:S(2)}) collective-permute-start(f32[3,8,1,128]{3,2,1,0:T(1,128)S(1)} %get-tuple-element.25), channel_id=1, source_target_pairs={{0,8},{8,16},{16,24},{1,9},{9,17},{17,25},{2,10},{10,18},{18,26},{... | collective-permute-start | bytes 36872 | tf_op jit(solution)/shard_map/ppermute | solution.py:191
  69.5 1.9 %collective-permute-start.12 = (f32[2,16,128]{2,1,0:T(8,128)S(1)}, f32[2,16,128]{2,1,0:T(8,128)S(1)}, u32[]{:S(2)}, u32[]{:S(2)}) collective-permute-start(f32[2,16,128]{2,1,0:T(8,128)S(1)} %get-tuple-element.41), channel_id=1, source_target_pairs={{0,32},{32,64},{64,96},{96,128},{128,160},{160,192},{192,224},{224... | collective-permute-start | bytes 49160 | tf_op jit(solution)/shard_map/ppermute | solution.py:175
  71.4 3.9 %collective-permute-start.13 = (f32[2,16,128]{2,1,0:T(8,128)S(1)}, f32[2,16,128]{2,1,0:T(8,128)S(1)}, u32[]{:S(2)}, u32[]{:S(2)}) collective-permute-start(f32[2,16,128]{2,1,0:T(8,128)S(1)} %get-tuple-element.42), channel_id=1, source_target_pairs={{32,0},{64,32},{96,64},{128,96},{160,128},{192,160},{224,192},{256... | collective-permute-start | bytes 49160 | tf_op jit(solution)/shard_map/ppermute | solution.py:178
  75.3 2.9 %collective-permute-done.13 = f32[2,16,128]{2,1,0:T(8,128)S(1)} collective-permute-done((f32[2,16,128]{2,1,0:T(8,128)S(1)}, f32[2,16,128]{2,1,0:T(8,128)S(1)}, u32[]{:S(2)}, u32[]{:S(2)}) %collective-permute-start.13) | collective-permute-done | bytes 16416 | tf_op jit(solution)/shard_map/ppermute | solution.py:178
  78.2 4.2 %collective-permute-start.14 = (f32[12,2,128]{2,1,0:T(2,128)S(1)}, f32[12,2,128]{2,1,0:T(2,128)S(1)}, u32[]{:S(2)}, u32[]{:S(2)}) collective-permute-start(f32[12,2,128]{2,1,0:T(2,128)S(1)} %get-tuple-element.31), channel_id=1, source_target_pairs={{0,8},{8,16},{16,24},{1,9},{9,17},{17,25},{2,10},{10,18},{18,26},{... | collective-permute-start | bytes 36872 | tf_op jit(solution)/shard_map/ppermute | solution.py:175
  83.8 4.2 %collective-permute-done.15 = f32[12,2,128]{2,1,0:T(2,128)S(1)} collective-permute-done((f32[12,2,128]{2,1,0:T(2,128)S(1)}, f32[12,2,128]{2,1,0:T(2,128)S(1)}, u32[]{:S(2)}, u32[]{:S(2)}) %collective-permute-start.15) | collective-permute-done | bytes 12320 | tf_op jit(solution)/shard_map/ppermute | solution.py:178
  90.1 3.6 %collective-permute-start.17 = (f32[12,20,2]{2,1,0:T(8,128)S(1)}, f32[12,20,2]{2,1,0:T(8,128)S(1)}, u32[]{:S(2)}, u32[]{:S(2)}) collective-permute-start(f32[12,20,2]{2,1,0:T(8,128)S(1)} %get-tuple-element.30), channel_id=1, source_target_pairs={{1,0},{2,1},{3,2},{4,3},{5,4},{6,5},{7,6},{9,8},{10,9},{11,10},{12... | collective-permute-start | bytes 5768 | tf_op jit(solution)/shard_map/ppermute | solution.py:178
  97.4 5.6 %reshape.37 = f32[4,2,8,2,64,2]{5,4,3,2,1,0:T(8,128)} reshape(f32[8,16,128]{2,1,0:T(8,128)S(1)} %fusion.15) | data formatting | bytes 131072 | tf_op jit(solution)/shard_map/reshape | solution.py:229
  102.9 2.5 %reduce_sum.18 = f32[4,8,64]{2,1,0:T(8,128)S(1)} reduce(f32[4,2,8,2,64,2]{5,4,3,2,1,0:T(8,128)} %reshape.37, f32[]{:T(128)} %constant.42.clone.1), dimensions={1,3,5}, to_apply=%region_0.1 | reduce | flops 14336 | bytes 73732 | tf_op jit(solution)/shard_map/reduce_sum | solution.py:231
  105.5 4.3 %collective-permute-start.18 = (f32[2,8,64]{2,1,0:T(8,128)S(1)}, f32[2,8,64]{2,1,0:T(8,128)S(1)}, u32[]{:S(2)}, u32[]{:S(2)}) collective-permute-start(f32[2,8,64]{2,1,0:T(8,128)S(1)} %get-tuple-element.51), channel_id=1, source_target_pairs={{0,32},{32,64},{64,96},{96,128},{128,160},{160,192},{192,224},{224... | collective-permute-start | bytes 12296 | tf_op jit(solution)/shard_map/ppermute | solution.py:175
  111.8 4.8 %collective-permute-done.19 = f32[2,8,64]{2,1,0:T(8,128)S(1)} collective-permute-done((f32[2,8,64]{2,1,0:T(8,128)S(1)}, f32[2,8,64]{2,1,0:T(8,128)S(1)}, u32[]{:S(2)}, u32[]{:S(2)}) %collective-permute-start.19) | collective-permute-done | bytes 4128 | tf_op jit(solution)/shard_map/ppermute | solution.py:178
  116.6 3.4 %collective-permute-start.20 = (f32[8,2,64]{2,1,0:T(2,128)S(1)}, f32[8,2,64]{2,1,0:T(2,128)S(1)}, u32[]{:S(2)}, u32[]{:S(2)}) collective-permute-start(f32[8,2,64]{2,1,0:T(2,128)S(1)} %get-tuple-element.50), channel_id=1, source_target_pairs={{0,8},{8,16},{16,24},{1,9},{9,17},{17,25},{2,10},{10,18},{18,26},{... | collective-permute-start | bytes 12296 | tf_op jit(solution)/shard_map/ppermute | solution.py:175
  121.4 4.2 %collective-permute-done.21 = f32[8,2,64]{2,1,0:T(2,128)S(1)} collective-permute-done((f32[8,2,64]{2,1,0:T(2,128)S(1)}, f32[8,2,64]{2,1,0:T(2,128)S(1)}, u32[]{:S(2)}, u32[]{:S(2)}) %collective-permute-start.21) | collective-permute-done | bytes 4128 | tf_op jit(solution)/shard_map/ppermute | solution.py:178
  127.6 3.6 %collective-permute-start.23 = (f32[8,12,2]{2,0,1:T(8,128)S(1)}, f32[8,12,2]{2,0,1:T(8,128)S(1)}, u32[]{:S(2)}, u32[]{:S(2)}) collective-permute-start(f32[8,12,2]{2,0,1:T(8,128)S(1)} %get-tuple-element.48), channel_id=1, source_target_pairs={{1,0},{2,1},{3,2},{4,3},{5,4},{6,5},{7,6},{9,8},{10,9},{11,10},{12... | collective-permute-start | bytes 2312 | tf_op jit(solution)/shard_map/ppermute | solution.py:178
  137.3 5.1 %collective-permute-start.25 = (f32[1,4,32]{2,1,0:T(4,128)S(1)}, f32[1,4,32]{2,1,0:T(4,128)S(1)}, u32[]{:S(2)}, u32[]{:S(2)}) collective-permute-start(f32[1,4,32]{2,1,0:T(4,128)S(1)} %get-tuple-element.55), channel_id=1, source_target_pairs={{0,32},{32,64},{64,96},{96,128},{128,160},{160,192},{192,224},{224... | collective-permute-start | bytes 1544 | tf_op jit(solution)/shard_map/ppermute | solution.py:191
  142.5 4.5 %collective-permute-start.27 = (f32[2,1,32]{2,1,0:T(1,128)S(1)}, f32[2,1,32]{2,1,0:T(1,128)S(1)}, u32[]{:S(2)}, u32[]{:S(2)}) collective-permute-start(f32[2,1,32]{2,1,0:T(1,128)S(1)} %get-tuple-element.57), channel_id=1, source_target_pairs={{0,8},{8,16},{16,24},{1,9},{9,17},{17,25},{2,10},{10,18},{18,26},{... | collective-permute-start | bytes 776 | tf_op jit(solution)/shard_map/ppermute | solution.py:191
  147.0 2.6 %collective-permute-start.28 = (f32[2,4,1]{2,1,0:T(4,128)S(1)}, f32[2,4,1]{2,1,0:T(4,128)S(1)}, u32[]{:S(2)}, u32[]{:S(2)}) collective-permute-start(f32[2,4,1]{2,1,0:T(4,128)S(1)} %get-tuple-element.53), channel_id=1, source_target_pairs={{1,0},{2,1},{3,2},{4,3},{5,4},{6,5},{7,6},{9,8},{10,9},{11,10},{12... | collective-permute-start | bytes 104 | tf_op jit(solution)/shard_map/ppermute | solution.py:192
  149.6 1.9 %collective-permute-start.29 = (f32[2,4,1]{2,1,0:T(4,128)S(1)}, f32[2,4,1]{2,1,0:T(4,128)S(1)}, u32[]{:S(2)}, u32[]{:S(2)}) collective-permute-start(f32[2,4,1]{2,1,0:T(4,128)S(1)} %get-tuple-element.54), channel_id=1, source_target_pairs={{0,1},{1,2},{2,3},{3,4},{4,5},{5,6},{6,7},{8,9},{9,10},{10,11},{11... | collective-permute-start | bytes 104 | tf_op jit(solution)/shard_map/ppermute | solution.py:191
  151.6 3.0 %collective-permute-done.29 = f32[2,4,1]{2,1,0:T(4,128)S(1)} collective-permute-done((f32[2,4,1]{2,1,0:T(4,128)S(1)}, f32[2,4,1]{2,1,0:T(4,128)S(1)}, u32[]{:S(2)}, u32[]{:S(2)}) %collective-permute-start.29) | collective-permute-done | bytes 64 | tf_op jit(solution)/shard_map/ppermute | solution.py:191
  157.5 5.1 %collective-permute-start.31 = (f32[1,16,128]{2,1,0:T(8,128)S(1)}, f32[1,16,128]{2,1,0:T(8,128)S(1)}, u32[]{:S(2)}, u32[]{:S(2)}) collective-permute-start(f32[1,16,128]{2,1,0:T(8,128)S(1)} %get-tuple-element.37), channel_id=1, source_target_pairs={{0,32},{32,64},{64,96},{96,128},{128,160},{160,192},{192,224},{224... | collective-permute-start | bytes 24584 | tf_op jit(solution)/shard_map/ppermute | solution.py:191
  163.9 4.5 %collective-permute-start.33 = (f32[8,1,128]{2,1,0:T(1,128)S(1)}, f32[8,1,128]{2,1,0:T(1,128)S(1)}, u32[]{:S(2)}, u32[]{:S(2)}) collective-permute-start(f32[8,1,128]{2,1,0:T(1,128)S(1)} %get-tuple-element.39), channel_id=1, source_target_pairs={{0,8},{8,16},{16,24},{1,9},{9,17},{17,25},{2,10},{10,18},{18,26},{... | collective-permute-start | bytes 12296 | tf_op jit(solution)/shard_map/ppermute | solution.py:191
  170.5 2.4 %collective-permute-start.35 = (f32[8,16,1]{2,1,0:T(8,128)S(1)}, f32[8,16,1]{2,1,0:T(8,128)S(1)}, u32[]{:S(2)}, u32[]{:S(2)}) collective-permute-start(f32[8,16,1]{2,1,0:T(8,128)S(1)} %get-tuple-element.36), channel_id=1, source_target_pairs={{0,1},{1,2},{2,3},{3,4},{4,5},{5,6},{6,7},{8,9},{9,10},{10,11},{11... | collective-permute-start | bytes 1544 | tf_op jit(solution)/shard_map/ppermute | solution.py:191
  173.0 3.1 %collective-permute-done.35 = f32[8,16,1]{2,1,0:T(8,128)S(1)} collective-permute-done((f32[8,16,1]{2,1,0:T(8,128)S(1)}, f32[8,16,1]{2,1,0:T(8,128)S(1)}, u32[]{:S(2)}, u32[]{:S(2)}) %collective-permute-start.35) | collective-permute-done | bytes 544 | tf_op jit(solution)/shard_map/ppermute | solution.py:191
  (126 shorter events, 42.5 us)
Async XLA Ops:
  2.4 7.8 %collective-permute-start = (f32[4,4,16,128]{3,2,1,0:T(8,128)S(1)}, f32[4,4,16,128]{3,2,1,0:T(8,128)S(1)}, u32[]{:S(2)}, u32[]{:S(2)}) collective-permute-start(f32[4,4,16,128]{3,2,1,0:T(8,128)S(1)} %pad_maximum_fusion.2), channel_id=1, source_target_pairs={{0,32},{32,64},{64,96},{96,128},{128,160},{160,192},{192,224},{224... | collective-permute-start | bytes 393224 | tf_op jit(solution)/shard_map/ppermute | solution.py:29
  7.5 8.1 %collective-permute-start.1 = (f32[4,4,16,128]{3,2,1,0:T(8,128)S(1)}, f32[4,4,16,128]{3,2,1,0:T(8,128)S(1)}, u32[]{:S(2)}, u32[]{:S(2)}) collective-permute-start(f32[4,4,16,128]{3,2,1,0:T(8,128)S(1)} %pad_maximum_fusion.3), channel_id=1, source_target_pairs={{0,480},{32,0},{64,32},{96,64},{128,96},{160,128},{192,160},{224,1... | collective-permute-start | bytes 393224 | tf_op jit(solution)/shard_map/ppermute | solution.py:29
  17.9 9.8 %collective-permute-start.2 = (f32[4,8,8,128]{3,2,1,0:T(8,128)S(1)}, f32[4,8,8,128]{3,2,1,0:T(8,128)S(1)}, u32[]{:S(2)}, u32[]{:S(2)}) collective-permute-start(f32[4,8,8,128]{3,2,1,0:T(8,128)S(1)} %get-tuple-element.13), channel_id=1, source_target_pairs={{0,8},{8,16},{16,24},{24,0},{1,9},{9,17},{17,25},{25,1},{2,10},{10... | collective-permute-start | bytes 393224 | tf_op jit(solution)/shard_map/ppermute | solution.py:29
  21.3 6.9 %collective-permute-start.3 = (f32[4,8,8,128]{3,2,1,0:T(8,128)S(1)}, f32[4,8,8,128]{3,2,1,0:T(8,128)S(1)}, u32[]{:S(2)}, u32[]{:S(2)}) collective-permute-start(f32[4,8,8,128]{3,2,1,0:T(8,128)S(1)} %get-tuple-element.14), channel_id=1, source_target_pairs={{0,24},{8,0},{16,8},{24,16},{1,25},{9,1},{17,9},{25,17},{2,26},{10... | collective-permute-start | bytes 393224 | tf_op jit(solution)/shard_map/ppermute | solution.py:29
  49.6 14.0 %collective-permute-start.8 = (f32[3,8,1,128]{3,2,1,0:T(1,128)S(1)}, f32[3,8,1,128]{3,2,1,0:T(1,128)S(1)}, u32[]{:S(2)}, u32[]{:S(2)}) collective-permute-start(f32[3,8,1,128]{3,2,1,0:T(1,128)S(1)} %get-tuple-element.26), channel_id=1, source_target_pairs={{8,0},{16,8},{24,16},{9,1},{17,9},{25,17},{10,2},{18,10},{26,18},{... | collective-permute-start | bytes 36872 | tf_op jit(solution)/shard_map/ppermute | solution.py:192
  50.9 18.3 %collective-permute-start.10 = (f32[3,8,16,1]{3,2,1,0:T(8,128)S(1)}, f32[3,8,16,1]{3,2,1,0:T(8,128)S(1)}, u32[]{:S(2)}, u32[]{:S(2)}) collective-permute-start(f32[3,8,16,1]{3,2,1,0:T(8,128)S(1)} %get-tuple-element.21), channel_id=1, source_target_pairs={{1,0},{2,1},{3,2},{4,3},{5,4},{6,5},{7,6},{9,8},{10,9},{11,10},{12... | collective-permute-start | bytes 4616 | tf_op jit(solution)/shard_map/ppermute | solution.py:192
  54.6 14.7 %collective-permute-start.11 = (f32[3,8,16,1]{3,2,1,0:T(8,128)S(1)}, f32[3,8,16,1]{3,2,1,0:T(8,128)S(1)}, u32[]{:S(2)}, u32[]{:S(2)}) collective-permute-start(f32[3,8,16,1]{3,2,1,0:T(8,128)S(1)} %get-tuple-element.22), channel_id=1, source_target_pairs={{0,1},{1,2},{2,3},{3,4},{4,5},{5,6},{6,7},{8,9},{9,10},{10,11},{11... | collective-permute-start | bytes 4616 | tf_op jit(solution)/shard_map/ppermute | solution.py:191
  56.5 12.8 %collective-permute-start.6 = (f32[3,1,16,128]{3,2,1,0:T(8,128)S(1)}, f32[3,1,16,128]{3,2,1,0:T(8,128)S(1)}, u32[]{:S(2)}, u32[]{:S(2)}) collective-permute-start(f32[3,1,16,128]{3,2,1,0:T(8,128)S(1)} %get-tuple-element.24), channel_id=1, source_target_pairs={{32,0},{64,32},{96,64},{128,96},{160,128},{192,160},{224,192},{256... | collective-permute-start | bytes 73736 | tf_op jit(solution)/shard_map/ppermute | solution.py:192
  58.4 10.9 %collective-permute-start.7 = (f32[3,1,16,128]{3,2,1,0:T(8,128)S(1)}, f32[3,1,16,128]{3,2,1,0:T(8,128)S(1)}, u32[]{:S(2)}, u32[]{:S(2)}) collective-permute-start(f32[3,1,16,128]{3,2,1,0:T(8,128)S(1)} %get-tuple-element.23), channel_id=1, source_target_pairs={{0,32},{32,64},{64,96},{96,128},{128,160},{160,192},{192,224},{224... | collective-permute-start | bytes 73736 | tf_op jit(solution)/shard_map/ppermute | solution.py:191
  63.6 5.7 %collective-permute-start.9 = (f32[3,8,1,128]{3,2,1,0:T(1,128)S(1)}, f32[3,8,1,128]{3,2,1,0:T(1,128)S(1)}, u32[]{:S(2)}, u32[]{:S(2)}) collective-permute-start(f32[3,8,1,128]{3,2,1,0:T(1,128)S(1)} %get-tuple-element.25), channel_id=1, source_target_pairs={{0,8},{8,16},{16,24},{1,9},{9,17},{17,25},{2,10},{10,18},{18,26},{... | collective-permute-start | bytes 36872 | tf_op jit(solution)/shard_map/ppermute | solution.py:191
  69.5 5.9 %collective-permute-start.12 = (f32[2,16,128]{2,1,0:T(8,128)S(1)}, f32[2,16,128]{2,1,0:T(8,128)S(1)}, u32[]{:S(2)}, u32[]{:S(2)}) collective-permute-start(f32[2,16,128]{2,1,0:T(8,128)S(1)} %get-tuple-element.41), channel_id=1, source_target_pairs={{0,32},{32,64},{64,96},{96,128},{128,160},{160,192},{192,224},{224... | collective-permute-start | bytes 49160 | tf_op jit(solution)/shard_map/ppermute | solution.py:175
  71.4 6.8 %collective-permute-start.13 = (f32[2,16,128]{2,1,0:T(8,128)S(1)}, f32[2,16,128]{2,1,0:T(8,128)S(1)}, u32[]{:S(2)}, u32[]{:S(2)}) collective-permute-start(f32[2,16,128]{2,1,0:T(8,128)S(1)} %get-tuple-element.42), channel_id=1, source_target_pairs={{32,0},{64,32},{96,64},{128,96},{160,128},{192,160},{224,192},{256... | collective-permute-start | bytes 49160 | tf_op jit(solution)/shard_map/ppermute | solution.py:178
  78.2 5.6 %collective-permute-start.14 = (f32[12,2,128]{2,1,0:T(2,128)S(1)}, f32[12,2,128]{2,1,0:T(2,128)S(1)}, u32[]{:S(2)}, u32[]{:S(2)}) collective-permute-start(f32[12,2,128]{2,1,0:T(2,128)S(1)} %get-tuple-element.31), channel_id=1, source_target_pairs={{0,8},{8,16},{16,24},{1,9},{9,17},{17,25},{2,10},{10,18},{18,26},{... | collective-permute-start | bytes 36872 | tf_op jit(solution)/shard_map/ppermute | solution.py:175
  82.4 5.6 %collective-permute-start.15 = (f32[12,2,128]{2,1,0:T(2,128)S(1)}, f32[12,2,128]{2,1,0:T(2,128)S(1)}, u32[]{:S(2)}, u32[]{:S(2)}) collective-permute-start(f32[12,2,128]{2,1,0:T(2,128)S(1)} %get-tuple-element.32), channel_id=1, source_target_pairs={{8,0},{16,8},{24,16},{9,1},{17,9},{25,17},{10,2},{18,10},{26,18},{... | collective-permute-start | bytes 36872 | tf_op jit(solution)/shard_map/ppermute | solution.py:178
  88.2 6.5 %collective-permute-start.16 = (f32[12,20,2]{2,1,0:T(8,128)S(1)}, f32[12,20,2]{2,1,0:T(8,128)S(1)}, u32[]{:S(2)}, u32[]{:S(2)}) collective-permute-start(f32[12,20,2]{2,1,0:T(8,128)S(1)} %get-tuple-element.29), channel_id=1, source_target_pairs={{0,1},{1,2},{2,3},{3,4},{4,5},{5,6},{6,7},{8,9},{9,10},{10,11},{11... | collective-permute-start | bytes 5768 | tf_op jit(solution)/shard_map/ppermute | solution.py:175
  90.1 6.3 %collective-permute-start.17 = (f32[12,20,2]{2,1,0:T(8,128)S(1)}, f32[12,20,2]{2,1,0:T(8,128)S(1)}, u32[]{:S(2)}, u32[]{:S(2)}) collective-permute-start(f32[12,20,2]{2,1,0:T(8,128)S(1)} %get-tuple-element.30), channel_id=1, source_target_pairs={{1,0},{2,1},{3,2},{4,3},{5,4},{6,5},{7,6},{9,8},{10,9},{11,10},{12... | collective-permute-start | bytes 5768 | tf_op jit(solution)/shard_map/ppermute | solution.py:178
  105.5 6.3 %collective-permute-start.18 = (f32[2,8,64]{2,1,0:T(8,128)S(1)}, f32[2,8,64]{2,1,0:T(8,128)S(1)}, u32[]{:S(2)}, u32[]{:S(2)}) collective-permute-start(f32[2,8,64]{2,1,0:T(8,128)S(1)} %get-tuple-element.51), channel_id=1, source_target_pairs={{0,32},{32,64},{64,96},{96,128},{128,160},{160,192},{192,224},{224... | collective-permute-start | bytes 12296 | tf_op jit(solution)/shard_map/ppermute | solution.py:175
  109.8 6.8 %collective-permute-start.19 = (f32[2,8,64]{2,1,0:T(8,128)S(1)}, f32[2,8,64]{2,1,0:T(8,128)S(1)}, u32[]{:S(2)}, u32[]{:S(2)}) collective-permute-start(f32[2,8,64]{2,1,0:T(8,128)S(1)} %get-tuple-element.52), channel_id=1, source_target_pairs={{32,0},{64,32},{96,64},{128,96},{160,128},{192,160},{224,192},{256... | collective-permute-start | bytes 12296 | tf_op jit(solution)/shard_map/ppermute | solution.py:178
  116.6 4.8 %collective-permute-start.20 = (f32[8,2,64]{2,1,0:T(2,128)S(1)}, f32[8,2,64]{2,1,0:T(2,128)S(1)}, u32[]{:S(2)}, u32[]{:S(2)}) collective-permute-start(f32[8,2,64]{2,1,0:T(2,128)S(1)} %get-tuple-element.50), channel_id=1, source_target_pairs={{0,8},{8,16},{16,24},{1,9},{9,17},{17,25},{2,10},{10,18},{18,26},{... | collective-permute-start | bytes 12296 | tf_op jit(solution)/shard_map/ppermute | solution.py:175
  120.0 5.5 %collective-permute-start.21 = (f32[8,2,64]{2,1,0:T(2,128)S(1)}, f32[8,2,64]{2,1,0:T(2,128)S(1)}, u32[]{:S(2)}, u32[]{:S(2)}) collective-permute-start(f32[8,2,64]{2,1,0:T(2,128)S(1)} %get-tuple-element.49), channel_id=1, source_target_pairs={{8,0},{16,8},{24,16},{9,1},{17,9},{25,17},{10,2},{18,10},{26,18},{... | collective-permute-start | bytes 12296 | tf_op jit(solution)/shard_map/ppermute | solution.py:178
  125.7 6.2 %collective-permute-start.22 = (f32[8,12,2]{2,0,1:T(8,128)S(1)}, f32[8,12,2]{2,0,1:T(8,128)S(1)}, u32[]{:S(2)}, u32[]{:S(2)}) collective-permute-start(f32[8,12,2]{2,0,1:T(8,128)S(1)} %get-tuple-element.47), channel_id=1, source_target_pairs={{0,1},{1,2},{2,3},{3,4},{4,5},{5,6},{6,7},{8,9},{9,10},{10,11},{11... | collective-permute-start | bytes 2312 | tf_op jit(solution)/shard_map/ppermute | solution.py:175
  127.6 5.4 %collective-permute-start.23 = (f32[8,12,2]{2,0,1:T(8,128)S(1)}, f32[8,12,2]{2,0,1:T(8,128)S(1)}, u32[]{:S(2)}, u32[]{:S(2)}) collective-permute-start(f32[8,12,2]{2,0,1:T(8,128)S(1)} %get-tuple-element.48), channel_id=1, source_target_pairs={{1,0},{2,1},{3,2},{4,3},{5,4},{6,5},{7,6},{9,8},{10,9},{11,10},{12... | collective-permute-start | bytes 2312 | tf_op jit(solution)/shard_map/ppermute | solution.py:178
  134.1 20.4 %collective-permute-start.24 = (f32[1,4,32]{2,1,0:T(4,128)S(1)}, f32[1,4,32]{2,1,0:T(4,128)S(1)}, u32[]{:S(2)}, u32[]{:S(2)}) collective-permute-start(f32[1,4,32]{2,1,0:T(4,128)S(1)} %get-tuple-element.56), channel_id=1, source_target_pairs={{32,0},{64,32},{96,64},{128,96},{160,128},{192,160},{224,192},{256... | collective-permute-start | bytes 1544 | tf_op jit(solution)/shard_map/ppermute | solution.py:192
  136.0 13.6 %collective-permute-start.26 = (f32[2,1,32]{2,1,0:T(1,128)S(1)}, f32[2,1,32]{2,1,0:T(1,128)S(1)}, u32[]{:S(2)}, u32[]{:S(2)}) collective-permute-start(f32[2,1,32]{2,1,0:T(1,128)S(1)} %get-tuple-element.58), channel_id=1, source_target_pairs={{8,0},{16,8},{24,16},{9,1},{17,9},{25,17},{10,2},{18,10},{26,18},{... | collective-permute-start | bytes 776 | tf_op jit(solution)/shard_map/ppermute | solution.py:192
  137.3 17.2 %collective-permute-start.25 = (f32[1,4,32]{2,1,0:T(4,128)S(1)}, f32[1,4,32]{2,1,0:T(4,128)S(1)}, u32[]{:S(2)}, u32[]{:S(2)}) collective-permute-start(f32[1,4,32]{2,1,0:T(4,128)S(1)} %get-tuple-element.55), channel_id=1, source_target_pairs={{0,32},{32,64},{64,96},{96,128},{128,160},{160,192},{192,224},{224... | collective-permute-start | bytes 1544 | tf_op jit(solution)/shard_map/ppermute | solution.py:191
  142.5 9.1 %collective-permute-start.27 = (f32[2,1,32]{2,1,0:T(1,128)S(1)}, f32[2,1,32]{2,1,0:T(1,128)S(1)}, u32[]{:S(2)}, u32[]{:S(2)}) collective-permute-start(f32[2,1,32]{2,1,0:T(1,128)S(1)} %get-tuple-element.57), channel_id=1, source_target_pairs={{0,8},{8,16},{16,24},{1,9},{9,17},{17,25},{2,10},{10,18},{18,26},{... | collective-permute-start | bytes 776 | tf_op jit(solution)/shard_map/ppermute | solution.py:191
  149.6 4.9 %collective-permute-start.29 = (f32[2,4,1]{2,1,0:T(4,128)S(1)}, f32[2,4,1]{2,1,0:T(4,128)S(1)}, u32[]{:S(2)}, u32[]{:S(2)}) collective-permute-start(f32[2,4,1]{2,1,0:T(4,128)S(1)} %get-tuple-element.54), channel_id=1, source_target_pairs={{0,1},{1,2},{2,3},{3,4},{4,5},{5,6},{6,7},{8,9},{9,10},{10,11},{11... | collective-permute-start | bytes 104 | tf_op jit(solution)/shard_map/ppermute | solution.py:191
  155.6 17.4 %collective-permute-start.30 = (f32[1,16,128]{2,1,0:T(8,128)S(1)}, f32[1,16,128]{2,1,0:T(8,128)S(1)}, u32[]{:S(2)}, u32[]{:S(2)}) collective-permute-start(f32[1,16,128]{2,1,0:T(8,128)S(1)} %get-tuple-element.38), channel_id=1, source_target_pairs={{32,0},{64,32},{96,64},{128,96},{160,128},{192,160},{224,192},{256... | collective-permute-start | bytes 24584 | tf_op jit(solution)/shard_map/ppermute | solution.py:192
  157.5 15.5 %collective-permute-start.31 = (f32[1,16,128]{2,1,0:T(8,128)S(1)}, f32[1,16,128]{2,1,0:T(8,128)S(1)}, u32[]{:S(2)}, u32[]{:S(2)}) collective-permute-start(f32[1,16,128]{2,1,0:T(8,128)S(1)} %get-tuple-element.37), channel_id=1, source_target_pairs={{0,32},{32,64},{64,96},{96,128},{128,160},{160,192},{192,224},{224... | collective-permute-start | bytes 24584 | tf_op jit(solution)/shard_map/ppermute | solution.py:191
  162.6 7.9 %collective-permute-start.32 = (f32[8,1,128]{2,1,0:T(1,128)S(1)}, f32[8,1,128]{2,1,0:T(1,128)S(1)}, u32[]{:S(2)}, u32[]{:S(2)}) collective-permute-start(f32[8,1,128]{2,1,0:T(1,128)S(1)} %get-tuple-element.40), channel_id=1, source_target_pairs={{8,0},{16,8},{24,16},{9,1},{17,9},{25,17},{10,2},{18,10},{26,18},{... | collective-permute-start | bytes 12296 | tf_op jit(solution)/shard_map/ppermute | solution.py:192
  163.9 9.0 %collective-permute-start.33 = (f32[8,1,128]{2,1,0:T(1,128)S(1)}, f32[8,1,128]{2,1,0:T(1,128)S(1)}, u32[]{:S(2)}, u32[]{:S(2)}) collective-permute-start(f32[8,1,128]{2,1,0:T(1,128)S(1)} %get-tuple-element.39), channel_id=1, source_target_pairs={{0,8},{8,16},{16,24},{1,9},{9,17},{17,25},{2,10},{10,18},{18,26},{... | collective-permute-start | bytes 12296 | tf_op jit(solution)/shard_map/ppermute | solution.py:191
  170.5 5.6 %collective-permute-start.35 = (f32[8,16,1]{2,1,0:T(8,128)S(1)}, f32[8,16,1]{2,1,0:T(8,128)S(1)}, u32[]{:S(2)}, u32[]{:S(2)}) collective-permute-start(f32[8,16,1]{2,1,0:T(8,128)S(1)} %get-tuple-element.36), channel_id=1, source_target_pairs={{0,1},{1,2},{2,3},{3,4},{4,5},{5,6},{6,7},{8,9},{9,10},{10,11},{11... | collective-permute-start | bytes 1544 | tf_op jit(solution)/shard_map/ppermute | solution.py:191
  (9 other events, 41.1 us)

commit v2 on v1

--- a/solution.py
+++ b/solution.py
@@ -167,126 +167,368 @@
     )(inside, code_t, fields_t, planes_t, rows_t, columns_low, columns_high)
 
 
-def padded_2(block, sides, width):
-    for axis, dim in sides:
-        count = lax.axis_size(axis)
-        forward = [(i, i + 1) for i in range(count - 1)]
-        backward = [(target, source) for source, target in forward]
-        low = lax.ppermute(
-            lax.slice_in_dim(block, block.shape[dim] - width, None, axis=dim), axis, forward
-        )
-        high = lax.ppermute(lax.slice_in_dim(block, 0, width, axis=dim), axis, backward)
-        block = jnp.concatenate([low, block, high], axis=dim)
-    return block
-
-
-def with_halo(value, sides, width):
-    edges = {}
-    for axis, dim in sides:
-        peers, length = (lax.axis_size(axis), value.shape[dim])
-        up = [(i, (i + 1) % peers) for i in range(peers - 1)]
-        last = lax.slice_in_dim(value, length - width, length, axis=dim)
-        initial = lax.slice_in_dim(value, 0, width, axis=dim)
-        edges[dim] = (
-            lax.ppermute(last, axis, up),
-            lax.ppermute(initial, axis, [(b, a) for a, b in up]),
-        )
-    done = []
-    for _, dim in sides:
-        low, high = edges[dim]
-        around = [(width, width) if d in done else (0, 0) for d in range(value.ndim)]
-        value = jnp.concatenate([jnp.pad(low, around), value, jnp.pad(high, around)], axis=dim)
-        done.append(dim)
-    return value
-
-
-def neighbours(padded):
-    summed = padded[2:, 1:-1, 1:-1] + padded[:-2, 1:-1, 1:-1]
-    summed = summed + padded[1:-1, 2:, 1:-1] + padded[1:-1, :-2, 1:-1]
-    summed = summed + padded[1:-1, 1:-1, 2:] + padded[1:-1, 1:-1, :-2]
-    return summed
-
-
-def operate(padded):
-    return 6.0 * padded[1:-1, 1:-1, 1:-1] - neighbours(padded)
-
-
-def divergence_of(velocity_pad):
-    part_x = velocity_pad[0, 2:, 1:-1, 1:-1] - velocity_pad[0, :-2, 1:-1, 1:-1]
-    part_y = velocity_pad[1, 1:-1, 2:, 1:-1] - velocity_pad[1, 1:-1, :-2, 1:-1]
-    part_z = velocity_pad[2, 1:-1, 1:-1, 2:] - velocity_pad[2, 1:-1, 1:-1, :-2]
-    return 0.5 * (part_x + part_y + part_z)
-
-
-def gradient_of(pressure_pad):
-    part_x = pressure_pad[2:, 1:-1, 1:-1] - pressure_pad[:-2, 1:-1, 1:-1]
-    part_y = pressure_pad[1:-1, 2:, 1:-1] - pressure_pad[1:-1, :-2, 1:-1]
-    part_z = pressure_pad[1:-1, 1:-1, 2:] - pressure_pad[1:-1, 1:-1, :-2]
-    return 0.5 * jnp.stack([part_x, part_y, part_z], axis=0)
-
-
-def restrict(field):
-    return field.reshape(
-        field.shape[0] // 2, 2, field.shape[1] // 2, 2, field.shape[2] // 2, 2
-    ).mean(axis=(1, 3, 5))
-
-
-def prolong(field):
-    return jnp.repeat(jnp.repeat(jnp.repeat(field, 2, axis=0), 2, axis=1), 2, axis=2)
-
-
-def inside_box(extents, margin):
-    box_shape = (extents[0] + 2 * margin, extents[1] + 2 * margin, extents[2] + 2 * margin)
-    coord_x = (
-        lax.broadcasted_iota(jnp.int32, box_shape, 0) - margin + lax.axis_index("gx") * extents[0]
-    )
-    coord_y = (
-        lax.broadcasted_iota(jnp.int32, box_shape, 1) - margin + lax.axis_index("gy") * extents[1]
-    )
-    coord_z = (
-        lax.broadcasted_iota(jnp.int32, box_shape, 2) - margin + lax.axis_index("gz") * extents[2]
-    )
-    inside = (coord_x >= 0) & (coord_x < extents[0] * lax.axis_size("gx"))
-    inside = inside & (coord_y >= 0) & (coord_y < extents[1] * lax.axis_size("gy"))
-    inside = inside & (coord_z >= 0) & (coord_z < extents[2] * lax.axis_size("gz"))
-    return inside
-
-
-def smooth_level(source, spacing):
+def roll(value, shift, dim):
+    return pltpu.roll(value, shift % value.shape[dim], dim)
+
+
+def neighbours(value):
+    none = jnp.zeros_like(value[:1])
+    summed = jnp.concatenate([value[1:], none], axis=0) + jnp.concatenate([none, value[:-1]], axis=0)
+    summed = summed + roll(value, -1, 1) + roll(value, 1, 1)
+    return summed + roll(value, -1, 2) + roll(value, 1, 2)
+
+
+def grid_mask(inside, planes, rows, lanes):
+    shape = (rows[0], lanes[0])
+    row = lax.broadcasted_iota(jnp.int32, shape, 0)
+    lane = lax.broadcasted_iota(jnp.int32, shape, 1)
+    by_row = jnp.where(
+        row < rows[1], 1.0, jnp.where(row < (rows[0] + rows[1]) // 2, inside[3], inside[2])
+    )
+    by_lane = jnp.where(
+        lane < lanes[1], 1.0, jnp.where(lane < (lanes[0] + lanes[1]) // 2, inside[5], inside[4])
+    )
+    both = by_row * by_lane
+    first, count, block = planes
+    parts = [
+        both * inside[0] if x < 0 else (both * inside[1] if x >= block else both)
+        for x in range(first, first + count)
+    ]
+    return jnp.stack(parts, axis=0)
+
+
+def smooth(source, spacing, mask, want_residual):
     relaxation = RELAX_WEIGHT / 6.0
-    source_pad = padded_2(source, (("gx", 0), ("gy", 1), ("gz", 2)), 2)
-    first_sweep = relaxation * spacing * source_pad
-    second_wide = first_sweep[1:-1, 1:-1, 1:-1] + relaxation * (
-        spacing * source_pad[1:-1, 1:-1, 1:-1] - operate(first_sweep)
-    )
-    second_wide = jnp.where(inside_box(source.shape, 1), second_wide, 0.0)
-    residual = source - operate(second_wide) / spacing
-    second_sweep = second_wide[1:-1, 1:-1, 1:-1]
-    return (second_sweep, residual)
-
-
-def solve_coarse(source):
-    relaxation = RELAX_WEIGHT / 6.0
-    spacing = 16.0
-    first_sweep = relaxation * spacing * source
-    first_pad = with_halo(first_sweep, (("gx", 0), ("gy", 1), ("gz", 2)), 1)
-    return first_sweep + relaxation * (spacing * source - operate(first_pad))
+    first = relaxation * spacing * source
+    second = first + relaxation * (spacing * source - (6.0 * first - neighbours(first)))
+    second = second * mask
+    if not want_residual:
+        return second
+    residual = source - (6.0 * second - neighbours(second)) / spacing
+    return second, residual * mask
+
+
+def pick_lanes(value, index):
+    parts = [
+        jnp.take_along_axis(value[r : r + 8], index, axis=1, mode="promise_in_bounds")
+        for r in range(0, value.shape[0], 8)
+    ]
+    return jnp.concatenate(parts, axis=0)
+
+
+def lane_numbers(rows):
+    return lax.broadcasted_iota(jnp.int32, (rows, 128), 1)
+
+
+def row_numbers(rows):
+    return lax.broadcasted_iota(jnp.int32, (rows, 128), 0)
+
+
+def pair_sum(value):
+    value = value + roll(value, -1, 1)
+    return value + roll(value, -1, 2)
+
+
+def restrict_fine(residual, halves):
+    lane = lane_numbers(8)
+    index = (lane * 2) & 127
+    left = lane_numbers(16) < 64
+    row = row_numbers(8)
+    planes = []
+    pairs = pair_sum(
+        jnp.stack([residual[2 * p] + residual[2 * p + 1] for p in range(8)], axis=0)
+    )
+    for p in range(8):
+        even = []
+        for side in range(2):
+            both = pairs[p, :, 128 * side : 128 * side + 128]
+            halves[side, p, 0:16] = both[0:16]
+            halves[side, p, 16:24] = jnp.where(row < 4, both[16:24], 0.0)
+            halves[side, p, 24:32] = jnp.where(row >= 4, both[16:24], 0.0)
+            even.append(pick_lanes(halves[side, p, pl.ds(0, 16, stride=2), :], index))
+        planes.append(jnp.where(left, even[0], even[1]))
+    return jnp.stack(planes, axis=0) * 0.125
+
+
+def restrict_middle(residual, halves):
+    index = (lane_numbers(8) * 2) & 127
+    row, lane = row_numbers(16), lane_numbers(16)
+    valid = ((row < 6) | (row >= 14)) & ((lane < 36) | (lane >= 124))
+    pairs = pair_sum(
+        jnp.stack([residual[2 * p] + residual[2 * p + 1] for p in range(6)], axis=0)
+    )
+    planes = []
+    for p in range(6):
+        halves[0, p, 0:16] = pairs[p]
+        even = pick_lanes(halves[0, p, pl.ds(0, 8, stride=2), :], index)
+        planes.append(jnp.where(valid, jnp.concatenate([even, even], axis=0), 0.0))
+    return jnp.stack(planes, axis=0) * 0.125
+
+
+def with_planes(value, count):
+    none = jnp.zeros((count,) + value.shape[1:], value.dtype)
+    return jnp.concatenate([none, value, none], axis=0)
+
+
+def levels_kernel(
+    inside, moved, to_low, to_high, to_low_2, to_high_2, fine, middle, coarse, halves
+):
+    def spread(a):
+        block = jnp.concatenate([moved[a], jnp.zeros((8, 8, 128), jnp.float32)], axis=1)
+        block = jnp.concatenate([block, jnp.zeros((8, 24, 128), jnp.float32)], axis=2)
+        return with_planes(block, 4)
+
+    u = spread(0)
+    none = jnp.zeros_like(u[:1])
+    slope = jnp.concatenate([u[1:], none], axis=0) - jnp.concatenate([none, u[:-1]], axis=0)
+    u = spread(1)
+    slope = slope + (roll(u, -1, 1) - roll(u, 1, 1))
+    u = spread(2)
+    slope = slope + (roll(u, -1, 2) - roll(u, 1, 2))
+    mask = grid_mask(inside, (-4, 16, 8), (24, 16), (256, 128))
+    second, residual = smooth(slope * mask * -0.5, 1.0, mask, True)
+    mask = grid_mask(inside, (-4, 12, 4), (16, 8), (128, 64))
+    source = with_planes(restrict_fine(residual, halves), 2)
+    second_1, residual = smooth(source, 4.0, mask, True)
+    mask = grid_mask(inside, (-3, 8, 2), (16, 4), (128, 32))
+    source = with_planes(restrict_middle(residual, halves), 1)
+    second_2 = smooth(source, 16.0, mask, False)
+    fine[...] = second[3:13]
+    middle[...] = second_1[3:9]
+    coarse[...] = second_2[2:6]
+    for out, at_0, at_1, at_2 in ((to_high, 11, 7, 4), (to_low, 2, 1, 0)):
+        sides = None
+        for k in range(3):
+            out[24 * k : 24 * k + 24] = second[at_0 + k][:, 0:128]
+            side = roll(second[at_0 + k][:, 128:256], 16 * k, 1)
+            sides = side if sides is None else sides + side
+        out[72:96] = sides
+        for k in range(4):
+            out[96 + 16 * k : 112 + 16 * k] = second_1[at_1 + k] + roll(second_2[at_2 + k], 80, 1)
+    for k in range(2):
+        to_high_2[16 * k : 16 * k + 16] = second_2[6 + k]
+        to_low_2[16 * k : 16 * k + 16] = second_2[k]
+
+
+def near_end(lane):
+    return (lane < 8) | (lane >= 120)
+
+
+def split_levels(both):
+    lane = lane_numbers(both.shape[0])
+    middle = jnp.where((lane < 72) | (lane >= 120), both, 0.0)
+    coarse = jnp.where((lane >= 72) & (lane < 120), both, 0.0)
+    return middle, roll(coarse, -80, 1)
+
+
+def planes_sum_kernel(
+    inside, fine, middle, coarse, low, high, low_2, high_2, to_low, to_high, fine_o, middle_o, coarse_o
+):
+    f = [fine[k] for k in range(10)]
+    m = [middle[k] for k in range(6)]
+    c = [coarse[k] for k in range(4)]
+    lane = lane_numbers(24)
+    for got, flag, at_0, at_1 in ((low, inside[0], 0, 0), (high, inside[1], 7, 2)):
+        sides = got[72:96] * flag
+        for k in range(3):
+            side = jnp.where(near_end(lane), roll(sides, -16 * k, 1), 0.0)
+            centre = got[24 * k : 24 * k + 24] * flag
+            f[at_0 + k] = f[at_0 + k] + jnp.concatenate([centre, side], axis=1)
+        for k in range(4):
+            add_m, add_c = split_levels(got[96 + 16 * k : 112 + 16 * k] * flag)
+            m[at_1 + k] = m[at_1 + k] + add_m
+            c[k] = c[k] + add_c
+    for k in range(2):
+        c[k] = c[k] + low_2[16 * k : 16 * k + 16] * inside[6]
+        c[2 + k] = c[2 + k] + high_2[16 * k : 16 * k + 16] * inside[7]
+    c[0], c[3] = c[0] * inside[0], c[3] * inside[1]
+    for k in range(10):
+        fine_o[k] = f[k]
+    for k in range(6):
+        middle_o[k] = m[k]
+    for k in range(4):
+        coarse_o[k] = c[k]
+    for out, at_0, at_1, at_2 in ((to_high, 15, 7, 3), (to_low, -2, -3, -3)):
+        sides = None
+        for k in range(10):
+            rows = roll(f[k], -at_0, 0)[0:8]
+            out[4 * k : 4 * k + 4] = rows[0:4, 0:128]
+            side = roll(jnp.where(near_end(lane_numbers(8)), rows[:, 128:256], 0.0), 8 + 12 * k, 1)
+            sides = side if sides is None else sides + side
+        out[40:48] = sides
+        for k in range(6):
+            rows = roll(m[k], -at_1, 0)[0:8]
+            if k < 4:
+                rows = rows + roll(roll(c[k], -at_2, 0)[0:8], 80, 1)
+            out[48 + 4 * k : 52 + 4 * k] = rows[0:4]
+
+
+def rows_sum_kernel(
+    inside, fine, middle, coarse, low, high, to_low, to_high, fine_o, middle_o, coarse_o
+):
+    f = [fine[k] for k in range(10)]
+    m = [middle[k] for k in range(6)]
+    c = [coarse[k] for k in range(4)]
+    row = row_numbers(8)
+
+    def place(rows, count, first):
+        none = jnp.zeros((count - 8,) + rows.shape[1:], jnp.float32)
+        return roll(jnp.concatenate([rows, none], axis=0), first, 0)
+
+    def four(got, at, flag):
+        tile = got[at - at % 8 : at - at % 8 + 8] * flag
+        tile = roll(tile, -4, 0) if at % 8 else tile
+        return jnp.where(row < 4, tile, 0.0)
+
+    for got, flag, at_0, at_1, at_2 in (
+        (low, inside[2], -1, -1, -1),
+        (high, inside[3], 14, 5, 1),
+    ):
+        sides = jnp.where(row < 3, got[40:48] * flag, 0.0)
+        for k in range(10):
+            side = jnp.where(four_lanes(8), roll(sides, -(8 + 12 * k), 1), 0.0)
+            rows = jnp.where(row < 3, four(got, 4 * k, flag), 0.0)
+            f[k] = f[k] + place(jnp.concatenate([rows, side], axis=1), 24, at_0)
+        for k in range(6):
+            add_m, add_c = split_levels(four(got, 48 + 4 * k, flag))
+            m[k] = m[k] + place(add_m, 16, at_1)
+            if k < 4:
+                c[k] = c[k] + place(add_c, 16, at_2)
+    for k in range(10):
+        fine_o[k] = f[k]
+    for k in range(6):
+        middle_o[k] = m[k]
+    for k in range(4):
+        coarse_o[k] = c[k]
+    lane = lane_numbers(24)
+    lane_16 = lane_numbers(16)
+    none = jnp.zeros((8, 128), jnp.float32)
+
+    def strip(value, first, count, at):
+        lanes = lane_numbers(value.shape[0])
+        moved = roll(value, at - first, 1)
+        return jnp.where((lanes >= at) & (lanes < at + count), moved, 0.0)
+
+    for out, at_0, at_1, at_2 in ((to_high, 127, 63, 31), (to_low, 126, 125, 125)):
+        total = jnp.zeros((24, 128), jnp.float32)
+        for k in range(10):
+            own = lane == 127 if at_0 == 127 else lane == 0
+            total = total + strip(jnp.where(own, f[k][:, 0:128], f[k][:, 128:256]), at_0, 3, 4 * k)
+        part = jnp.zeros((16, 128), jnp.float32)
+        for k in range(6):
+            part = part + strip(m[k], at_1, 4, 40 + 4 * k)
+        for k in range(4):
+            part = part + strip(c[k], at_2, 4, 64 + 4 * k)
+        out[...] = total + jnp.concatenate([part, none], axis=0)
+
+
+def four_lanes(rows):
+    lane = lane_numbers(rows)
+    return (lane < 4) | (lane >= 124)
+
+
+def pressure_kernel(inside, moved, fine, middle, coarse, low, high, velocity, pressure, halves):
+    f = [fine[k] for k in range(10)]
+    m = [middle[k] for k in range(6)]
+    c = [coarse[k] for k in range(4)]
+
+    def strip(value, at, count, first):
+        lanes = lane_numbers(value.shape[0])
+        kept = jnp.where((lanes >= at) & (lanes < at + count), value, 0.0)
+        return roll(kept, first - at, 1)
+
+    lane = lane_numbers(24)
+    for got, flag, at_0, at_1, at_2 in (
+        (low, inside[4], -1, -1, -1),
+        (high, inside[5], 126, 61, 29),
+    ):
+        whole = got[...] * flag
+        part = whole[0:16]
+        for k in range(10):
+            add = strip(whole, 4 * k, 3, at_0)
+            own = (lane < 64) if at_0 < 0 else (lane >= 64)
+            add = jnp.concatenate([jnp.where(own, add, 0.0), jnp.where(own, 0.0, add)], axis=1)
+            f[k] = f[k] + add
+        for k in range(6):
+            m[k] = m[k] + strip(part, 40 + 4 * k, 4, at_1)
+        for k in range(4):
+            c[k] = c[k] + strip(part, 64 + 4 * k, 4, at_2)
+    row = row_numbers(8)
+    lane = lane_numbers(8)
+    to_middle = (lane >> 1) + jnp.where(lane < 96, 0, 64)
+    for k in range(4):
+        wide = pick_lanes(c[k], to_middle)
+        halves[0, k, pl.ds(0, 16, stride=2), :] = wide
+        halves[0, k, pl.ds(1, 16, stride=2), :] = wide
+    for k in range(6):
+        at = (k + 1) // 2
+        tail = jnp.where(row < 4, halves[0, at, 8:16], halves[0, at, 24:32])
+        m[k] = m[k] + jnp.concatenate([halves[0, at, 0:8], tail], axis=0)
+    to_centre = lane >> 1
+    to_side = to_centre + 64
+    for k in range(6):
+        for side, index in enumerate((to_centre, to_side)):
+            wide = pick_lanes(m[k], index)
+            halves[side, k, pl.ds(0, 16, stride=2), :] = wide
+            halves[side, k, pl.ds(1, 16, stride=2), :] = wide
+    for k in range(10):
+        at = (k + 1) // 2
+        sides = []
+        for side in range(2):
+            tail = jnp.where(row < 4, halves[side, at, 16:24], halves[side, at, 24:32])
+            sides.append(jnp.concatenate([halves[side, at, 0:16], tail], axis=0))
+        f[k] = f[k] + jnp.concatenate(sides, axis=1)
+    for k in range(8):
+        here = f[k + 1]
+        pressure[k] = here[0:16, 0:128]
+        velocity[0, k] = moved[0, k] - 0.5 * (f[k + 2][0:16, 0:128] - f[k][0:16, 0:128])
+        slope = roll(here, -1, 0) - roll(here, 1, 0)
+        velocity[1, k] = moved[1, k] - 0.5 * slope[0:16, 0:128]
+        here = here[0:16]
+        slope = roll(here, -1, 1) - roll(here, 1, 1)
+        velocity[2, k] = moved[2, k] - 0.5 * slope[:, 0:128]
+
+
+def project(inside, moved):
+    f32 = jnp.float32
+    held = [((10, 24, 256), f32), ((6, 16, 128), f32), ((4, 16, 128), f32)]
+    halves = [pltpu.VMEM((2, 8, 32, 128), f32)]
+    side, side_2 = ((160, 128), f32), ((32, 128), f32)
+    to_low, to_high, to_low_2, to_high_2, *sums = call(
+        levels_kernel, [side, side, side_2, side_2] + held, halves, scalars=1, inputs=1
+    )(inside, moved)
+    low = shift_ring(to_high, "gx", 1)
+    high = shift_ring(to_low, "gx", -1)
+    low_2 = shift_ring(to_high_2, "gx", 2)
+    high_2 = shift_ring(to_low_2, "gx", -2)
+    side = ((72, 128), f32)
+    to_low, to_high, *sums = call(
+        planes_sum_kernel, [side, side] + held, scalars=1, inputs=7
+    )(inside, *sums, low, high, low_2, high_2)
+    low = shift_ring(to_high, "gy", 1)
+    high = shift_ring(to_low, "gy", -1)
+    side = ((24, 128), f32)
+    to_low, to_high, *sums = call(rows_sum_kernel, [side, side] + held, scalars=1, inputs=5)(
+        inside, *sums, low, high
+    )
+    low = shift_ring(to_high, "gz", 1)
+    high = shift_ring(to_low, "gz", -1)
+    return call(
+        pressure_kernel,
+        [((3, 8, 16, 128), f32), ((8, 16, 128), f32)],
+        halves,
+        scalars=1,
+        inputs=6,
+    )(inside, moved, *sums, low, high)
 
 
 def body(velocity, density, offsets, eighths):
-    inside = jnp.stack(ends("gx") + ends("gy") + ends("gz")).astype(jnp.float32)
-    _, advected = advect(inside, velocity, density, offsets, eighths)
-    new_density = advected[3]
-    moved_velocity = advected[:3]
-    velocity_pad = with_halo(moved_velocity, (("gx", 1), ("gy", 2), ("gz", 3)), 1)
-    divergence = divergence_of(velocity_pad)
-    fine_sweep, fine_residual = smooth_level(-divergence, 1.0)
-    middle_sweep, middle_residual = smooth_level(restrict(fine_residual), 4.0)
-    coarse_sweep = solve_coarse(restrict(middle_residual))
-    pressure = fine_sweep + prolong(middle_sweep + prolong(coarse_sweep))
-    pressure_pad = with_halo(pressure, (("gx", 0), ("gy", 1), ("gz", 2)), 1)
-    gradient = gradient_of(pressure_pad)
-    return (moved_velocity - gradient, new_density, pressure)
+    place = lax.axis_index("gx")
+    beyond = [place > 1, place < lax.axis_size("gx") - 2]
+    inside = jnp.stack(ends("gx") + ends("gy") + ends("gz") + beyond).astype(jnp.float32)
+    _, moved = advect(inside, velocity, density, offsets, eighths)
+    new_velocity, pressure = project(inside, moved)
+    return new_velocity, moved[3], pressure
 
 
 def solution(mesh):

time: 178 us -> 88.9 us (0.50)
  the two profiles are of different devices: /device:TPU:112 before, /device:TPU:6 now
where the time goes in v2:
time: 88.9 us; the launch traced here: 87.9 us
  starting transfers between devices  46.5 us (52%)
  Pallas kernels  24.3 us (27%)
  waiting for transfers between devices  13.7 us (15%)
  local copies, waits for them, and re-layouts  2.5 us (3%)
    ppermute x14, starting transfers between devices, shift_ring(): lax.ppermute(value, axis, [(i, (i + step) % count) for i in range(count)])  46.5 us
    pallas_call x1, Pallas kernels, advect(): call(advect_kernel, [((4, 128, 128), f32), ((4, 8, 16, 128), f32)], scrat...  17.1 us
    ppermute x14, waiting for transfers between devices, shift_ring(): lax.ppermute(value, axis, [(i, (i + step) % count) for i in range(count)])  13.7 us
    pallas_call x1, Pallas kernels, project(): call(levels_kernel, [side, side, side_2, side_2] + held, halves, scalars=...  1.94 us
  transfers between devices with their start and end apart: 14, of which 8 were waited for; matrix products, arithmetic and copies ran while one was open for 1% of the time, Pallas kernels for 1%

profile of v2, /device:TPU:6, one launch (start us, length us, event | category | flops | bytes accessed | tf_op | source)
XLA Modules:
  0.0 87.9 jit_solution(1212073780363251768)
XLA Ops:
  0.6 0.8 slice_bitcast_fusion.1
  1.4 1.0 %fusion = (f32[3,4,16,128]{3,2,1,0:T(8,128)S(1)}, f32[3,4,16,128]{3,2,1,0:T(8,128)S(1)}) fusion(f32[3,8,16,128]{3,2,1,0:T(8,128)} %velocity.3), kind=kLoop, calls=%fused_computation.5 | loop fusion | bytes 393216 | tf_op jit(solution)/shard_map/slice | solution.py:139
  2.4 4.0 %collective-permute-start = (f32[4,4,16,128]{3,2,1,0:T(8,128)S(1)}, f32[4,4,16,128]{3,2,1,0:T(8,128)S(1)}, u32[]{:S(2)}, u32[]{:S(2)}) collective-permute-start(f32[4,4,16,128]{3,2,1,0:T(8,128)S(1)} %pad_maximum_fusion), channel_id=1, source_target_pairs={{0,32},{32,64},{64,96},{96,128},{128,160},{160,192},{192,224},{224... | collective-permute-start | bytes 393224 | tf_op jit(solution)/shard_map/ppermute | solution.py:29
  6.4 9.5 %collective-permute-start.1 = (f32[4,4,16,128]{3,2,1,0:T(8,128)S(1)}, f32[4,4,16,128]{3,2,1,0:T(8,128)S(1)}, u32[]{:S(2)}, u32[]{:S(2)}) collective-permute-start(f32[4,4,16,128]{3,2,1,0:T(8,128)S(1)} %pad_maximum_fusion.1), channel_id=1, source_target_pairs={{0,480},{32,0},{64,32},{96,64},{128,96},{160,128},{192,160},{224,1... | collective-permute-start | bytes 393224 | tf_op jit(solution)/shard_map/ppermute | solution.py:29
  16.1 1.4 %collective-permute-done.low = f32[4,4,16,128]{3,2,1,0:T(8,128)S(1)} collective-permute-done((f32[4,4,16,128]{3,2,1,0:T(8,128)S(1)}, f32[4,4,16,128]{3,2,1,0:T(8,128)S(1)}, u32[]{:S(2)}, u32[]{:S(2)}) %collective-permute-start) | collective-permute-done | bytes 131104 | tf_op jit(solution)/shard_map/ppermute | solution.py:29
  17.4 1.2 %collective-permute-done.1.high = f32[4,4,16,128]{3,2,1,0:T(8,128)S(1)} collective-permute-done((f32[4,4,16,128]{3,2,1,0:T(8,128)S(1)}, f32[4,4,16,128]{3,2,1,0:T(8,128)S(1)}, u32[]{:S(2)}, u32[]{:S(2)}) %collective-permute-start.1) | collective-permute-done | bytes 131104 | tf_op jit(solution)/shard_map/ppermute | solution.py:29
  18.6 0.6 shard_map.69
  19.2 2.4 %collective-permute-start.2 = (f32[4,8,8,128]{3,2,1,0:T(8,128)S(1)}, f32[4,8,8,128]{3,2,1,0:T(8,128)S(1)}, u32[]{:S(2)}, u32[]{:S(2)}) collective-permute-start(f32[4,8,8,128]{3,2,1,0:T(8,128)S(1)} %get-tuple-element.32), channel_id=1, source_target_pairs={{0,8},{8,16},{16,24},{24,0},{1,9},{9,17},{17,25},{25,1},{2,10},{10... | collective-permute-start | bytes 393224 | tf_op jit(solution)/shard_map/ppermute | solution.py:29
  21.6 3.5 %collective-permute-start.3 = (f32[4,8,8,128]{3,2,1,0:T(8,128)S(1)}, f32[4,8,8,128]{3,2,1,0:T(8,128)S(1)}, u32[]{:S(2)}, u32[]{:S(2)}) collective-permute-start(f32[4,8,8,128]{3,2,1,0:T(8,128)S(1)} %get-tuple-element.33), channel_id=1, source_target_pairs={{0,24},{8,0},{16,8},{24,16},{1,25},{9,1},{17,9},{25,17},{2,26},{10... | collective-permute-start | bytes 393224 | tf_op jit(solution)/shard_map/ppermute | solution.py:29
  25.1 0.2 shard_map.67
  25.3 0.7 shard_map.68.planes_t
  26.0 0.1 collective-permute-done.2.low
  26.1 3.6 %collective-permute-done.3.high = f32[4,8,8,128]{3,2,1,0:T(8,128)S(1)} collective-permute-done((f32[4,8,8,128]{3,2,1,0:T(8,128)S(1)}, f32[4,8,8,128]{3,2,1,0:T(8,128)S(1)}, u32[]{:S(2)}, u32[]{:S(2)}) %collective-permute-start.3) | collective-permute-done | bytes 131104 | tf_op jit(solution)/shard_map/ppermute | solution.py:29
  29.7 0.7 shard_map.70
  30.4 2.9 %collective-permute-start.5 = (f32[4,3,8,128]{3,2,1,0:T(8,128)S(1)}, f32[4,3,8,128]{3,2,1,0:T(8,128)S(1)}, u32[]{:S(2)}, u32[]{:S(2)}) collective-permute-start(f32[4,3,8,128]{3,2,1,0:T(8,128)S(1)} %get-tuple-element.36), channel_id=1, source_target_pairs={{0,7},{1,0},{2,1},{3,2},{4,3},{5,4},{6,5},{7,6},{8,15},{9,8},{10,9... | collective-permute-start | bytes 147464 | tf_op jit(solution)/shard_map/ppermute | solution.py:29
  33.3 1.8 %collective-permute-done.4.low = f32[4,3,8,128]{3,2,1,0:T(8,128)S(1)} collective-permute-done((f32[4,3,8,128]{3,2,1,0:T(8,128)S(1)}, f32[4,3,8,128]{3,2,1,0:T(8,128)S(1)}, u32[]{:S(2)}, u32[]{:S(2)}) %collective-permute-start.4) | collective-permute-done | bytes 49184 | tf_op jit(solution)/shard_map/ppermute | solution.py:29
  35.1 17.1 %shard_map.71 = (f32[4,128,128]{2,1,0:T(8,128)}, f32[4,8,16,128]{3,2,1,0:T(8,128)S(1)}) custom-call(f32[8]{0:T(128)S(1)} %convert_element_type.3.inside, s32[128,128]{1,0:T(8,128)S(1)} %get-tuple-element.30.code_t, f32[4,128,128]{2,1,0:T(8,128)S(1)} %get-tuple-element.31.fields_t, f32[4,128,128]{2,1,0:T(8,128)S(1)} %shard_map.68.planes_t, ...), custom_call_target="tpu_custom_call" | custom-call | tf_op jit(solution)/shard_map/pallas_call | solution.py:161
  52.2 1.9 %shard_map.72 = (f32[160,128]{1,0:T(8,128)S(1)}, f32[160,128]{1,0:T(8,128)S(1)}, f32[32,128]{1,0:T(8,128)S(1)}, f32[32,128]{1,0:T(8,128)S(1)}, f32[10,24,256]{2,...) custom-call(f32[8]{0:T(128)S(1)} %convert_element_type.3.inside, ...), custom_call_target="tpu_custom_call" | custom-call | tf_op jit(solution)/shard_map/pallas_call | solution.py:497
  54.1 1.9 %collective-permute-start.6 = (f32[160,128]{1,0:T(8,128)S(1)}, f32[160,128]{1,0:T(8,128)S(1)}, u32[]{:S(2)}, u32[]{:S(2)}) collective-permute-start(f32[160,128]{1,0:T(8,128)S(1)} %get-tuple-element.41), channel_id=1, source_target_pairs={{0,32},{32,64},{64,96},{96,128},{128,160},{160,192},{192,224},{224... | collective-permute-start | bytes 245768 | tf_op jit(solution)/shard_map/ppermute | solution.py:29
  56.1 5.6 %collective-permute-start.7 = (f32[160,128]{1,0:T(8,128)S(1)}, f32[160,128]{1,0:T(8,128)S(1)}, u32[]{:S(2)}, u32[]{:S(2)}) collective-permute-start(f32[160,128]{1,0:T(8,128)S(1)} %get-tuple-element.42), channel_id=1, source_target_pairs={{0,480},{32,0},{64,32},{96,64},{128,96},{160,128},{192,160},{224,1... | collective-permute-start | bytes 245768 | tf_op jit(solution)/shard_map/ppermute | solution.py:29
  61.7 1.9 %collective-permute-start.8 = (f32[32,128]{1,0:T(8,128)S(1)}, f32[32,128]{1,0:T(8,128)S(1)}, u32[]{:S(2)}, u32[]{:S(2)}) collective-permute-start(f32[32,128]{1,0:T(8,128)S(1)} %get-tuple-element.43), channel_id=1, source_target_pairs={{0,64},{32,96},{64,128},{96,160},{128,192},{160,224},{192,256},{22... | collective-permute-start | bytes 49160 | tf_op jit(solution)/shard_map/ppermute | solution.py:29
  63.6 6.0 %collective-permute-start.9 = (f32[32,128]{1,0:T(8,128)S(1)}, f32[32,128]{1,0:T(8,128)S(1)}, u32[]{:S(2)}, u32[]{:S(2)}) collective-permute-start(f32[32,128]{1,0:T(8,128)S(1)} %get-tuple-element.44), channel_id=1, source_target_pairs={{0,448},{32,480},{64,0},{96,32},{128,64},{160,96},{192,128},{224,1... | collective-permute-start | bytes 49160 | tf_op jit(solution)/shard_map/ppermute | solution.py:29
  69.7 1.4 %collective-permute-done.9.high_2 = f32[32,128]{1,0:T(8,128)S(1)} collective-permute-done((f32[32,128]{1,0:T(8,128)S(1)}, f32[32,128]{1,0:T(8,128)S(1)}, u32[]{:S(2)}, u32[]{:S(2)}) %collective-permute-start.9) | collective-permute-done | bytes 16416 | tf_op jit(solution)/shard_map/ppermute | solution.py:29
  71.1 0.7 shard_map.73
  71.8 2.2 %collective-permute-start.10 = (f32[72,128]{1,0:T(8,128)S(1)}, f32[72,128]{1,0:T(8,128)S(1)}, u32[]{:S(2)}, u32[]{:S(2)}) collective-permute-start(f32[72,128]{1,0:T(8,128)S(1)} %get-tuple-element.48), channel_id=1, source_target_pairs={{0,8},{8,16},{16,24},{24,0},{1,9},{9,17},{17,25},{25,1},{2,10},{10... | collective-permute-start | bytes 110600 | tf_op jit(solution)/shard_map/ppermute | solution.py:29
  74.0 3.7 %collective-permute-start.11 = (f32[72,128]{1,0:T(8,128)S(1)}, f32[72,128]{1,0:T(8,128)S(1)}, u32[]{:S(2)}, u32[]{:S(2)}) collective-permute-start(f32[72,128]{1,0:T(8,128)S(1)} %get-tuple-element.49), channel_id=1, source_target_pairs={{0,24},{8,0},{16,8},{24,16},{1,25},{9,1},{17,9},{25,17},{2,26},{10... | collective-permute-start | bytes 110600 | tf_op jit(solution)/shard_map/ppermute | solution.py:29
  77.7 3.4 %collective-permute-done.11.high = f32[72,128]{1,0:T(8,128)S(1)} collective-permute-done((f32[72,128]{1,0:T(8,128)S(1)}, f32[72,128]{1,0:T(8,128)S(1)}, u32[]{:S(2)}, u32[]{:S(2)}) %collective-permute-start.11) | collective-permute-done | bytes 36896 | tf_op jit(solution)/shard_map/ppermute | solution.py:29
  81.1 0.8 shard_map.74
  81.9 2.9 %collective-permute-start.13 = (f32[24,128]{1,0:T(8,128)S(1)}, f32[24,128]{1,0:T(8,128)S(1)}, u32[]{:S(2)}, u32[]{:S(2)}) collective-permute-start(f32[24,128]{1,0:T(8,128)S(1)} %get-tuple-element.54), channel_id=1, source_target_pairs={{0,7},{1,0},{2,1},{3,2},{4,3},{5,4},{6,5},{7,6},{8,15},{9,8},{10,9... | collective-permute-start | bytes 36872 | tf_op jit(solution)/shard_map/ppermute | solution.py:29
  84.8 0.6 slice_bitcast_fusion
  85.5 0.7 collective-permute-done.12.low
  86.2 1.7 %shard_map.75 = (f32[3,8,16,128]{3,2,1,0:T(8,128)}, f32[8,16,128]{2,1,0:T(8,128)}) custom-call(f32[8]{0:T(128)S(1)} %convert_element_type.3.inside, f32[4,8,16,128]{3,2,1,0:T(8,128)S(1)} %get-tuple-element.37.moved, f32[10,24,256]{2,1,0:T(8,128)S(1)} %get-tuple-element.50.fine, f32[6,16,128]{2,1,0:T(8,128)S(1)} %get-tuple-element.51.middle, ...), custom_call_target="tpu_custom_call" | custom-call | tf_op jit(solution)/shard_map/pallas_call | solution.py:516
  (20 shorter events, 0.2 us)
Async XLA Ops:
  2.4 16.2 %copy-start = (f32[3,8,16,128]{3,2,1,0:T(8,128)S(1)}, f32[3,8,16,128]{3,2,1,0:T(8,128)}, u32[]{:S(2)}) copy-start(f32[3,8,16,128]{3,2,1,0:T(8,128)} %velocity.3) | copy-start | bytes 589828
  2.4 15.0 %collective-permute-start = (f32[4,4,16,128]{3,2,1,0:T(8,128)S(1)}, f32[4,4,16,128]{3,2,1,0:T(8,128)S(1)}, u32[]{:S(2)}, u32[]{:S(2)}) collective-permute-start(f32[4,4,16,128]{3,2,1,0:T(8,128)S(1)} %pad_maximum_fusion), channel_id=1, source_target_pairs={{0,32},{32,64},{64,96},{96,128},{128,160},{160,192},{192,224},{224... | collective-permute-start | bytes 393224 | tf_op jit(solution)/shard_map/ppermute | solution.py:29
  6.4 12.3 %copy-start.1 = (f32[8,16,128]{2,1,0:T(8,128)S(1)}, f32[8,16,128]{2,1,0:T(8,128)}, u32[]{:S(2)}) copy-start(f32[8,16,128]{2,1,0:T(8,128)} %density.3) | copy-start | bytes 196612
  6.4 12.2 %collective-permute-start.1 = (f32[4,4,16,128]{3,2,1,0:T(8,128)S(1)}, f32[4,4,16,128]{3,2,1,0:T(8,128)S(1)}, u32[]{:S(2)}, u32[]{:S(2)}) collective-permute-start(f32[4,4,16,128]{3,2,1,0:T(8,128)S(1)} %pad_maximum_fusion.1), channel_id=1, source_target_pairs={{0,480},{32,0},{64,32},{96,64},{128,96},{160,128},{192,160},{224,1... | collective-permute-start | bytes 393224 | tf_op jit(solution)/shard_map/ppermute | solution.py:29
  16.0 9.1 %copy-start.2 = (s32[3,8,16,128]{3,2,1,0:T(8,128)S(1)}, s32[3,8,16,128]{3,2,1,0:T(8,128)}, u32[]{:S(2)}) copy-start(s32[3,8,16,128]{3,2,1,0:T(8,128)} %offsets.1) | copy-start | bytes 589828
  16.0 9.1 %copy-start.3 = (s32[3,8,16,128]{3,2,1,0:T(8,128)S(1)}, s32[3,8,16,128]{3,2,1,0:T(8,128)}, u32[]{:S(2)}) copy-start(s32[3,8,16,128]{3,2,1,0:T(8,128)} %eighths.1) | copy-start | bytes 589828
  19.2 6.9 %collective-permute-start.2 = (f32[4,8,8,128]{3,2,1,0:T(8,128)S(1)}, f32[4,8,8,128]{3,2,1,0:T(8,128)S(1)}, u32[]{:S(2)}, u32[]{:S(2)}) collective-permute-start(f32[4,8,8,128]{3,2,1,0:T(8,128)S(1)} %get-tuple-element.32), channel_id=1, source_target_pairs={{0,8},{8,16},{16,24},{24,0},{1,9},{9,17},{17,25},{25,1},{2,10},{10... | collective-permute-start | bytes 393224 | tf_op jit(solution)/shard_map/ppermute | solution.py:29
  21.6 8.1 %collective-permute-start.3 = (f32[4,8,8,128]{3,2,1,0:T(8,128)S(1)}, f32[4,8,8,128]{3,2,1,0:T(8,128)S(1)}, u32[]{:S(2)}, u32[]{:S(2)}) collective-permute-start(f32[4,8,8,128]{3,2,1,0:T(8,128)S(1)} %get-tuple-element.33), channel_id=1, source_target_pairs={{0,24},{8,0},{16,8},{24,16},{1,25},{9,1},{17,9},{25,17},{2,26},{10... | collective-permute-start | bytes 393224 | tf_op jit(solution)/shard_map/ppermute | solution.py:29
  30.4 4.7 %collective-permute-start.4 = (f32[4,3,8,128]{3,2,1,0:T(8,128)S(1)}, f32[4,3,8,128]{3,2,1,0:T(8,128)S(1)}, u32[]{:S(2)}, u32[]{:S(2)}) collective-permute-start(f32[4,3,8,128]{3,2,1,0:T(8,128)S(1)} %get-tuple-element.35), channel_id=1, source_target_pairs={{0,1},{1,2},{2,3},{3,4},{4,5},{5,6},{6,7},{7,0},{8,9},{9,10},{10,1... | collective-permute-start | bytes 147464 | tf_op jit(solution)/shard_map/ppermute | solution.py:29
  30.4 4.7 %collective-permute-start.5 = (f32[4,3,8,128]{3,2,1,0:T(8,128)S(1)}, f32[4,3,8,128]{3,2,1,0:T(8,128)S(1)}, u32[]{:S(2)}, u32[]{:S(2)}) collective-permute-start(f32[4,3,8,128]{3,2,1,0:T(8,128)S(1)} %get-tuple-element.36), channel_id=1, source_target_pairs={{0,7},{1,0},{2,1},{3,2},{4,3},{5,4},{6,5},{7,6},{8,15},{9,8},{10,9... | collective-permute-start | bytes 147464 | tf_op jit(solution)/shard_map/ppermute | solution.py:29
  54.1 16.9 %collective-permute-start.6 = (f32[160,128]{1,0:T(8,128)S(1)}, f32[160,128]{1,0:T(8,128)S(1)}, u32[]{:S(2)}, u32[]{:S(2)}) collective-permute-start(f32[160,128]{1,0:T(8,128)S(1)} %get-tuple-element.41), channel_id=1, source_target_pairs={{0,32},{32,64},{64,96},{96,128},{128,160},{160,192},{192,224},{224... | collective-permute-start | bytes 245768 | tf_op jit(solution)/shard_map/ppermute | solution.py:29
  56.1 15.0 %collective-permute-start.7 = (f32[160,128]{1,0:T(8,128)S(1)}, f32[160,128]{1,0:T(8,128)S(1)}, u32[]{:S(2)}, u32[]{:S(2)}) collective-permute-start(f32[160,128]{1,0:T(8,128)S(1)} %get-tuple-element.42), channel_id=1, source_target_pairs={{0,480},{32,0},{64,32},{96,64},{128,96},{160,128},{192,160},{224,1... | collective-permute-start | bytes 245768 | tf_op jit(solution)/shard_map/ppermute | solution.py:29
  61.7 8.0 %collective-permute-start.8 = (f32[32,128]{1,0:T(8,128)S(1)}, f32[32,128]{1,0:T(8,128)S(1)}, u32[]{:S(2)}, u32[]{:S(2)}) collective-permute-start(f32[32,128]{1,0:T(8,128)S(1)} %get-tuple-element.43), channel_id=1, source_target_pairs={{0,64},{32,96},{64,128},{96,160},{128,192},{160,224},{192,256},{22... | collective-permute-start | bytes 49160 | tf_op jit(solution)/shard_map/ppermute | solution.py:29
  63.6 7.5 %collective-permute-start.9 = (f32[32,128]{1,0:T(8,128)S(1)}, f32[32,128]{1,0:T(8,128)S(1)}, u32[]{:S(2)}, u32[]{:S(2)}) collective-permute-start(f32[32,128]{1,0:T(8,128)S(1)} %get-tuple-element.44), channel_id=1, source_target_pairs={{0,448},{32,480},{64,0},{96,32},{128,64},{160,96},{192,128},{224,1... | collective-permute-start | bytes 49160 | tf_op jit(solution)/shard_map/ppermute | solution.py:29
  71.8 5.9 %collective-permute-start.10 = (f32[72,128]{1,0:T(8,128)S(1)}, f32[72,128]{1,0:T(8,128)S(1)}, u32[]{:S(2)}, u32[]{:S(2)}) collective-permute-start(f32[72,128]{1,0:T(8,128)S(1)} %get-tuple-element.48), channel_id=1, source_target_pairs={{0,8},{8,16},{16,24},{24,0},{1,9},{9,17},{17,25},{25,1},{2,10},{10... | collective-permute-start | bytes 110600 | tf_op jit(solution)/shard_map/ppermute | solution.py:29
  74.0 7.1 %collective-permute-start.11 = (f32[72,128]{1,0:T(8,128)S(1)}, f32[72,128]{1,0:T(8,128)S(1)}, u32[]{:S(2)}, u32[]{:S(2)}) collective-permute-start(f32[72,128]{1,0:T(8,128)S(1)} %get-tuple-element.49), channel_id=1, source_target_pairs={{0,24},{8,0},{16,8},{24,16},{1,25},{9,1},{17,9},{25,17},{2,26},{10... | collective-permute-start | bytes 110600 | tf_op jit(solution)/shard_map/ppermute | solution.py:29
  81.9 4.3 %collective-permute-start.12 = (f32[24,128]{1,0:T(8,128)S(1)}, f32[24,128]{1,0:T(8,128)S(1)}, u32[]{:S(2)}, u32[]{:S(2)}) collective-permute-start(f32[24,128]{1,0:T(8,128)S(1)} %get-tuple-element.53), channel_id=1, source_target_pairs={{0,1},{1,2},{2,3},{3,4},{4,5},{5,6},{6,7},{7,0},{8,9},{9,10},{10,1... | collective-permute-start | bytes 36872 | tf_op jit(solution)/shard_map/ppermute | solution.py:29
  81.9 4.3 %collective-permute-start.13 = (f32[24,128]{1,0:T(8,128)S(1)}, f32[24,128]{1,0:T(8,128)S(1)}, u32[]{:S(2)}, u32[]{:S(2)}) collective-permute-start(f32[24,128]{1,0:T(8,128)S(1)} %get-tuple-element.54), channel_id=1, source_target_pairs={{0,7},{1,0},{2,1},{3,2},{4,3},{5,4},{6,5},{7,6},{8,15},{9,8},{10,9... | collective-permute-start | bytes 36872 | tf_op jit(solution)/shard_map/ppermute | solution.py:29

commit v3 on v2

--- a/solution.py
+++ b/solution.py
@@ -29,6 +29,13 @@
     return lax.ppermute(value, axis, [(i, (i + step) % count) for i in range(count)])
 
 
+def pack_kernel(velocity, density, low_planes, high_planes):
+    for f in range(4):
+        field = velocity[f] if f < 3 else density[...]
+        low_planes[f] = field[0:4]
+        high_planes[f] = field[4:8]
+
+
 def own_kernel(velocity, density, offsets, eighths, fields_t, code_t):
     for a in range(3):
         fields_t[a] = velocity[a].reshape(128, 128).T
@@ -38,7 +45,7 @@
     code_t[...] = code.astype(jnp.float32).reshape(128, 128).T.astype(jnp.int32)
 
 
-def rows_kernel(inside, velocity, density, low, high, to_low, to_high):
+def rows_kernel(inside, velocity, density, low, high, after, to_low, to_high):
     for f in range(4):
         for pair in range(8):
             for half in range(2):
@@ -63,7 +70,7 @@
         planes_t[f] = both.T
 
 
-def columns_kernel(inside, fields_t, planes_t, low, high, rows_t, to_low, to_high):
+def columns_kernel(inside, fields_t, planes_t, low, high, after, rows_t, to_low, to_high):
     for f in range(4):
         both = jnp.concatenate(
             [low[f].reshape(64, 128) * inside[2], high[f].reshape(64, 128) * inside[3]], axis=0
@@ -75,56 +82,98 @@
             to_high[f, group] = source[120:128]
 
 
-def advect_kernel(inside, code_t, fields_t, planes_t, rows_t, low, high, moved_t, moved, padded):
+def corners_of(code):
+    lane = lax.broadcasted_iota(jnp.int32, (8, 128), 1)
+    x = (lane >> 4) + (code & 7)
+    y = (lane & 15) + ((code >> 3) & 7)
+    fx = ((code >> 9) & 7).astype(jnp.float32) / 8.0
+    fy = ((code >> 12) & 7).astype(jnp.float32) / 8.0
+    corners = []
+    for cx in (0, 1):
+        for cy in (0, 1):
+            xc, yc = x + cx, y + cy
+            low_x, high_x = xc < 4, xc >= 12
+            in_rows = (yc < 4) | (yc >= 20)
+            in_planes = low_x | high_x
+            plane = xc - jnp.where(low_x, 0, jnp.where(high_x, 8, 4))
+            by_rows = xc * 4 + (yc & 3) + jnp.where(yc >= 20, 64, 0)
+            at = jnp.where(in_rows, by_rows, plane * 16 + yc - 4)
+            weight = (fx if cx else 1.0 - fx) * (fy if cy else 1.0 - fy)
+            in_block = jnp.where(in_rows, 0.0, weight)
+            weights = (
+                jnp.where(in_planes, 0.0, in_block),
+                jnp.where(in_planes, in_block, 0.0),
+                jnp.where(in_rows, weight, 0.0),
+            )
+            corners.append((at, weights))
+    return corners
+
+
+def weights_z(code, shifts):
+    level = (code >> 6) & 7
+    fz = ((code >> 15) & 7).astype(jnp.float32) / 8.0
+    return [
+        jnp.where(level == dz, 1.0 - fz, jnp.where(level == dz - 1, fz, 0.0)) for dz in shifts
+    ]
+
+
+def gathered(at, weights, rows_of):
+    parts = [None] * 4
+    for shift, weight in enumerate(weights):
+        for f in range(4):
+            taken = jnp.take_along_axis(
+                rows_of(f, shift), at, axis=1, mode="promise_in_bounds"
+            )
+            parts[f] = weight * taken if shift == 0 else parts[f] + weight * taken
+    return parts
+
+
+def group_kernel(group, code_t, source_t, *refs):
+    before, (after, padded) = refs[:-2], refs[-2:]
+    none = jnp.zeros((8, 128), jnp.float32)
     for f in range(4):
-        for group, source in enumerate((fields_t, planes_t, rows_t)):
-            padded[f, group, 8:136] = source[f]
-            padded[f, group, 0:8] = low[f, group] * inside[4]
-            padded[f, group, 136:144] = high[f, group] * inside[5]
+        padded[f, 8:136] = source_t[f]
+        padded[f, 0:8] = none
+        padded[f, 136:144] = none
 
     def tile(step, carry):
         start = pl.multiple_of(step * 8, 8)
         code = code_t[pl.ds(start, 8), :]
-        lane = lax.broadcasted_iota(jnp.int32, (8, 128), 1)
-        x = (lane >> 4) + (code & 7)
-        y = (lane & 15) + ((code >> 3) & 7)
-        level = (code >> 6) & 7
-        fx = ((code >> 9) & 7).astype(jnp.float32) / 8.0
-        fy = ((code >> 12) & 7).astype(jnp.float32) / 8.0
-        fz = ((code >> 15) & 7).astype(jnp.float32) / 8.0
-        corners = []
-        for cx in (0, 1):
-            for cy in (0, 1):
-                xc, yc = x + cx, y + cy
-                low_x, high_x = xc < 4, xc >= 12
-                in_rows = (yc < 4) | (yc >= 20)
-                in_planes = low_x | high_x
-                plane = xc - jnp.where(low_x, 0, jnp.where(high_x, 8, 4))
-                by_rows = xc * 4 + (yc & 3) + jnp.where(yc >= 20, 64, 0)
-                at = jnp.where(in_rows, by_rows, plane * 16 + yc - 4)
-                weight = (fx if cx else 1.0 - fx) * (fy if cy else 1.0 - fy)
-                corners.append((at, in_rows, in_planes, weight))
-        sums = [jnp.zeros((8, 128), jnp.float32) for _ in range(4)]
-        for dz in range(9):
-            weight_z = jnp.where(level == dz, 1.0 - fz, jnp.where(level == dz - 1, fz, 0.0))
+        by_shift = weights_z(code, range(9))
+        sums = [before[0][f, pl.ds(start, 8), :] if before else none for f in range(4)]
+        for at, weights in corners_of(code):
+            parts = gathered(at, by_shift, lambda f, dz: padded[f, pl.ds(start + (4 + dz), 8), :])
             for f in range(4):
-                groups = [padded[f, group, pl.ds(start + (4 + dz), 8), :] for group in range(3)]
-                total = None
-                for at, in_rows, in_planes, weight in corners:
-                    picked = [
-                        jnp.take_along_axis(group, at, axis=1, mode="promise_in_bounds")
-                        for group in groups
-                    ]
-                    value = jnp.where(
-                        in_rows, picked[2], jnp.where(in_planes, picked[1], picked[0])
-                    )
-                    total = weight * value if total is None else total + weight * value
-                sums[f] = sums[f] + weight_z * total
+                sums[f] = sums[f] + weights[group] * parts[f]
         for f in range(4):
-            moved_t[f, pl.ds(start, 8), :] = sums[f]
+            after[f, pl.ds(start, 8), :] = sums[f]
         return carry
 
     lax.fori_loop(0, 16, tile, 0)
+
+
+def edges_kernel(inside, code_t, sums_t, low, high, moved, moved_t, padded):
+    none = jnp.zeros((8, 128), jnp.float32)
+    for f in range(4):
+        moved_t[f] = sums_t[f]
+        for group in range(3):
+            padded[0, f, group, 0:8] = low[f, group] * inside[4]
+            padded[0, f, group, 8:16] = none
+            padded[1, f, group, 0:8] = none
+            padded[1, f, group, 8:16] = high[f, group] * inside[5]
+    for end, start, first, shifts in ((0, 0, 4, range(0, 4)), (1, 120, 1, range(5, 9))):
+        code = code_t[start : start + 8]
+        by_shift = weights_z(code, shifts)
+        sums = [sums_t[f, start : start + 8] for f in range(4)]
+        for at, weights in corners_of(code):
+            for group in range(3):
+                parts = gathered(
+                    at, by_shift, lambda f, k: padded[end, f, group, first + k : first + k + 8]
+                )
+                for f in range(4):
+                    sums[f] = sums[f] + weights[group] * parts[f]
+        for f in range(4):
+            moved_t[f, start : start + 8] = sums[f]
     for f in range(4):
         moved[f] = moved_t[f].T.reshape(8, 16, 128)
 
@@ -136,35 +185,40 @@
 
 def advect(inside, velocity, density, offsets, eighths):
     f32 = jnp.float32
-    low_planes = jnp.concatenate([velocity[:, 0:4], density[None, 0:4]], axis=0)
-    high_planes = jnp.concatenate([velocity[:, 4:8], density[None, 4:8]], axis=0)
+    turned = ((4, 128, 128), f32)
+
+    def gather(group, *values):
+        padded = [pltpu.VMEM((4, 144, 128), f32)]
+        kernel = functools.partial(group_kernel, group)
+        return call(kernel, [turned], padded, inputs=len(values))(*values)[0]
+
+    planes = ((4, 4, 16, 128), f32)
+    low_planes, high_planes = call(pack_kernel, [planes, planes], inputs=2)(velocity, density)
     low = shift_ring(high_planes, "gx", 1)
     high = shift_ring(low_planes, "gx", -1)
-    fields_t, code_t = call(
-        own_kernel, [((4, 128, 128), f32), ((128, 128), jnp.int32)], inputs=4
-    )(velocity, density, offsets, eighths)
+    fields_t, code_t = call(own_kernel, [turned, ((128, 128), jnp.int32)], inputs=4)(
+        velocity, density, offsets, eighths
+    )
+    sums_t = gather(0, code_t, fields_t)
     strip = ((4, 8, 8, 128), f32)
-    to_low, to_high = call(rows_kernel, [strip, strip], scalars=1, inputs=4)(
-        inside, velocity, density, low, high
+    to_low, to_high = call(rows_kernel, [strip, strip], scalars=1, inputs=5)(
+        inside, velocity, density, low, high, sums_t
     )
     rows_low = shift_ring(to_high, "gy", 1)
     rows_high = shift_ring(to_low, "gy", -1)
-    (planes_t,) = call(planes_kernel, [((4, 128, 128), f32)], scalars=1, inputs=2)(
-        inside, low, high
-    )
+    (planes_t,) = call(planes_kernel, [turned], scalars=1, inputs=2)(inside, low, high)
+    sums_t = gather(1, code_t, planes_t, sums_t)
     edge = ((4, 3, 8, 128), f32)
     rows_t, to_low, to_high = call(
-        columns_kernel, [((4, 128, 128), f32), edge, edge], scalars=1, inputs=4
-    )(inside, fields_t, planes_t, rows_low, rows_high)
+        columns_kernel, [turned, edge, edge], scalars=1, inputs=5
+    )(inside, fields_t, planes_t, rows_low, rows_high, sums_t)
     columns_low = shift_ring(to_high, "gz", 1)
     columns_high = shift_ring(to_low, "gz", -1)
-    return call(
-        advect_kernel,
-        [((4, 128, 128), f32), ((4, 8, 16, 128), f32)],
-        scratch=[pltpu.VMEM((4, 3, 144, 128), f32)],
-        scalars=1,
-        inputs=6,
-    )(inside, code_t, fields_t, planes_t, rows_t, columns_low, columns_high)
+    sums_t = gather(2, code_t, rows_t, sums_t)
+    scratch = [pltpu.VMEM((4, 128, 128), f32), pltpu.VMEM((2, 4, 3, 16, 128), f32)]
+    return call(edges_kernel, [((4, 8, 16, 128), f32)], scratch, scalars=1, inputs=4)(
+        inside, code_t, sums_t, columns_low, columns_high
+    )[0]
 
 
 def roll(value, shift, dim):
@@ -526,7 +580,7 @@
     place = lax.axis_index("gx")
     beyond = [place > 1, place < lax.axis_size("gx") - 2]
     inside = jnp.stack(ends("gx") + ends("gy") + ends("gz") + beyond).astype(jnp.float32)
-    _, moved = advect(inside, velocity, density, offsets, eighths)
+    moved = advect(inside, velocity, density, offsets, eighths)
     new_velocity, pressure = project(inside, moved)
     return new_velocity, moved[3], pressure
 

time: 88.9 us -> 79.5 us (0.89)
  waiting for transfers between devices: 13.7 us -> 7.01 us
  Pallas kernels: 24.3 us -> 20.2 us
  local copies, waits for them, and re-layouts: 2.5 us -> 4.35 us
    ppermute x14, waiting for transfers between devices: 13.7 us -> 7.01 us  [shift_ring(): lax.ppermute(value, axis, [(i, (i + step) % count) for i in range(count)])]
    pallas_call x5 -> x9, Pallas kernels: 19.2 us -> 15 us  [the longest x3 11.8 us: gather(): return call(kernel, [turned], padded, inputs=len(values))(*values)[0]]
    unnamed x8 -> x12, local copies, waits for them, and re-layouts: 0.02 us -> 3.61 us
    slice x1 -> x0, local copies, waits for them, and re-layouts: 0.95 us -> none  [advect(): low_planes = jnp.concatenate([velocity[:, 0:4], density[None, 0:4]], axis=0)]
  transfers between devices with their start and end apart: 14 -> 14, of which waited for: 8 -> 3; matrix products, arithmetic and copies ran while one was open for 1% -> 1% of each run, Pallas kernels for 1% -> 16%
where the time goes in v3:
time: 79.5 us; the launch traced here: 78.5 us
  starting transfers between devices  46.1 us (58%)
  Pallas kernels  20.2 us (25%)
  waiting for transfers between devices  7.01 us (9%)
  local copies, waits for them, and re-layouts  4.35 us (5%)
  between operations  0.91 us (1%)
    ppermute x14, starting transfers between devices, shift_ring(): lax.ppermute(value, axis, [(i, (i + step) % count) for i in range(count)])  46.1 us
    pallas_call x3, Pallas kernels, gather(): return call(kernel, [turned], padded, inputs=len(values))(*values)[0]  11.8 us
    ppermute x14, waiting for transfers between devices, shift_ring(): lax.ppermute(value, axis, [(i, (i + step) % count) for i in range(count)])  7.01 us
    unnamed x12, local copies, waits for them, and re-layouts  3.61 us
    pallas_call x1, Pallas kernels, project(): call(levels_kernel, [side, side, side_2, side_2] + held, halves, scalars=...  1.94 us
    pallas_call x1, Pallas kernels, project(): call(pressure_kernel, [((3, 8, 16, 128), f32), ((8, 16, 128), f32)], halv...  1.69 us
  transfers between devices with their start and end apart: 14, of which 3 were waited for; matrix products, arithmetic and copies ran while one was open for 1% of the time, Pallas kernels for 16%

profile of v3, /device:TPU:6, one launch (start us, length us, event | category | flops | bytes accessed | tf_op | source)
XLA Modules:
  0.0 78.5 jit_solution(5035602176684395217)
XLA Ops:
  0.6 0.9 %copy-done = f32[3,8,16,128]{3,2,1,0:T(8,128)S(1)} copy-done((f32[3,8,16,128]{3,2,1,0:T(8,128)S(1)}, f32[3,8,16,128]{3,2,1,0:T(8,128)}, u32[]{:S(2)}) %copy-start) | copy-done | bytes 196632
  1.6 0.8 %copy-done.2 = f32[8,16,128]{2,1,0:T(8,128)S(1)} copy-done((f32[8,16,128]{2,1,0:T(8,128)S(1)}, f32[8,16,128]{2,1,0:T(8,128)}, u32[]{:S(2)}) %copy-start.2) | copy-done | bytes 65560
  2.4 4.0 %collective-permute-start = (f32[4,4,16,128]{3,2,1,0:T(8,128)S(1)}, f32[4,4,16,128]{3,2,1,0:T(8,128)S(1)}, u32[]{:S(2)}, u32[]{:S(2)}) collective-permute-start(f32[4,4,16,128]{3,2,1,0:T(8,128)S(1)} %get-tuple-element.33), channel_id=1, source_target_pairs={{0,32},{32,64},{64,96},{96,128},{128,160},{160,192},{192,224},{224... | collective-permute-start | bytes 393224 | tf_op jit(solution)/shard_map/ppermute | solution.py:29
  6.4 9.5 %collective-permute-start.1 = (f32[4,4,16,128]{3,2,1,0:T(8,128)S(1)}, f32[4,4,16,128]{3,2,1,0:T(8,128)S(1)}, u32[]{:S(2)}, u32[]{:S(2)}) collective-permute-start(f32[4,4,16,128]{3,2,1,0:T(8,128)S(1)} %get-tuple-element.34), channel_id=1, source_target_pairs={{0,480},{32,0},{64,32},{96,64},{128,96},{160,128},{192,160},{224,1... | collective-permute-start | bytes 393224 | tf_op jit(solution)/shard_map/ppermute | solution.py:29
  16.1 0.9 %copy-done.4 = s32[3,8,16,128]{3,2,1,0:T(8,128)S(1)} copy-done((s32[3,8,16,128]{3,2,1,0:T(8,128)S(1)}, s32[3,8,16,128]{3,2,1,0:T(8,128)}, u32[]{:S(2)}) %copy-start.4) | copy-done | bytes 196632
  17.0 0.9 %copy-done.5 = s32[3,8,16,128]{3,2,1,0:T(8,128)S(1)} copy-done((s32[3,8,16,128]{3,2,1,0:T(8,128)S(1)}, s32[3,8,16,128]{3,2,1,0:T(8,128)}, u32[]{:S(2)}) %copy-start.5) | copy-done | bytes 196632
  17.9 0.2 shard_map.67
  18.1 3.9 %shard_map.70.after.refs_0_ = f32[4,128,128]{2,1,0:T(8,128)S(1)} custom-call(s32[128,128]{1,0:T(8,128)S(1)} %get-tuple-element.31.code_t, f32[4,128,128]{2,1,0:T(8,128)S(1)} %get-tuple-element.32.source_t.fields_t), custom_call_target="tpu_custom_call" | custom-call | tf_op jit(solution)/shard_map/pallas_call | solution.py:193
  22.0 0.6 shard_map.71
  22.6 2.4 %collective-permute-start.2 = (f32[4,8,8,128]{3,2,1,0:T(8,128)S(1)}, f32[4,8,8,128]{3,2,1,0:T(8,128)S(1)}, u32[]{:S(2)}, u32[]{:S(2)}) collective-permute-start(f32[4,8,8,128]{3,2,1,0:T(8,128)S(1)} %get-tuple-element.35), channel_id=1, source_target_pairs={{0,8},{8,16},{16,24},{24,0},{1,9},{9,17},{17,25},{25,1},{2,10},{10... | collective-permute-start | bytes 393224 | tf_op jit(solution)/shard_map/ppermute | solution.py:29
  25.0 3.5 %collective-permute-start.3 = (f32[4,8,8,128]{3,2,1,0:T(8,128)S(1)}, f32[4,8,8,128]{3,2,1,0:T(8,128)S(1)}, u32[]{:S(2)}, u32[]{:S(2)}) collective-permute-start(f32[4,8,8,128]{3,2,1,0:T(8,128)S(1)} %get-tuple-element.36), channel_id=1, source_target_pairs={{0,24},{8,0},{16,8},{24,16},{1,25},{9,1},{17,9},{25,17},{2,26},{10... | collective-permute-start | bytes 393224 | tf_op jit(solution)/shard_map/ppermute | solution.py:29
  28.5 0.7 shard_map.69.source_t.planes_t
  29.1 3.9 %shard_map.72.after.refs_0_ = f32[4,128,128]{2,1,0:T(8,128)S(1)} custom-call(s32[128,128]{1,0:T(8,128)S(1)} %get-tuple-element.31.code_t, f32[4,128,128]{2,1,0:T(8,128)S(1)} %shard_map.69.source_t.planes_t, f32[4,128,128]{2,1,0:T(8,128)S(1)} %shard_map.70.after.refs_0_), custom_call_target="tpu_custom_call" | custom-call | tf_op jit(solution)/shard_map/pallas_call | solution.py:193
  33.1 0.7 shard_map.73
  33.8 2.9 %collective-permute-start.5 = (f32[4,3,8,128]{3,2,1,0:T(8,128)S(1)}, f32[4,3,8,128]{3,2,1,0:T(8,128)S(1)}, u32[]{:S(2)}, u32[]{:S(2)}) collective-permute-start(f32[4,3,8,128]{3,2,1,0:T(8,128)S(1)} %get-tuple-element.39), channel_id=1, source_target_pairs={{0,7},{1,0},{2,1},{3,2},{4,3},{5,4},{6,5},{7,6},{8,15},{9,8},{10,9... | collective-permute-start | bytes 147464 | tf_op jit(solution)/shard_map/ppermute | solution.py:29
  36.7 3.9 %shard_map.74.sums_t = f32[4,128,128]{2,1,0:T(8,128)S(1)} custom-call(s32[128,128]{1,0:T(8,128)S(1)} %get-tuple-element.31.code_t, f32[4,128,128]{2,1,0:T(8,128)S(1)} %get-tuple-element.37.source_t, f32[4,128,128]{2,1,0:T(8,128)S(1)} %shard_map.72.after.refs_0_), custom_call_target="tpu_custom_call" | custom-call | tf_op jit(solution)/shard_map/pallas_call | solution.py:193
  40.7 1.2 %shard_map.75.moved = f32[4,8,16,128]{3,2,1,0:T(8,128)S(1)} custom-call(f32[8]{0:T(128)S(1)} %convert_element_type.3.inside, s32[128,128]{1,0:T(8,128)S(1)} %get-tuple-element.31.code_t, f32[4,128,128]{2,1,0:T(8,128)S(1)} %shard_map.74.sums_t, f32[4,3,8,128]{3,2,1,0:T(8,128)S(1)} %collective-permute-done.4.low, f32[4,3,8,128]{3,2,1,0:T(8,128)S(1)} %collective-permute-done.5.high), custom_call_target="tpu_custom_call" | custom-call | tf_op jit(solution)/shard_map/pallas_call | solution.py:219
  41.8 1.9 %shard_map.76 = (f32[160,128]{1,0:T(8,128)S(1)}, f32[160,128]{1,0:T(8,128)S(1)}, f32[32,128]{1,0:T(8,128)S(1)}, f32[32,128]{1,0:T(8,128)S(1)}, f32[10,24,256]{2,...) custom-call(f32[8]{0:T(128)S(1)} %convert_element_type.3.inside, ...), custom_call_target="tpu_custom_call" | custom-call | tf_op jit(solution)/shard_map/pallas_call | solution.py:551
  43.8 1.9 %collective-permute-start.6 = (f32[160,128]{1,0:T(8,128)S(1)}, f32[160,128]{1,0:T(8,128)S(1)}, u32[]{:S(2)}, u32[]{:S(2)}) collective-permute-start(f32[160,128]{1,0:T(8,128)S(1)} %get-tuple-element.43), channel_id=1, source_target_pairs={{0,32},{32,64},{64,96},{96,128},{128,160},{160,192},{192,224},{224... | collective-permute-start | bytes 245768 | tf_op jit(solution)/shard_map/ppermute | solution.py:29
  45.7 5.1 %collective-permute-start.7 = (f32[160,128]{1,0:T(8,128)S(1)}, f32[160,128]{1,0:T(8,128)S(1)}, u32[]{:S(2)}, u32[]{:S(2)}) collective-permute-start(f32[160,128]{1,0:T(8,128)S(1)} %get-tuple-element.44), channel_id=1, source_target_pairs={{0,480},{32,0},{64,32},{96,64},{128,96},{160,128},{192,160},{224,1... | collective-permute-start | bytes 245768 | tf_op jit(solution)/shard_map/ppermute | solution.py:29
  50.9 1.9 %collective-permute-start.8 = (f32[32,128]{1,0:T(8,128)S(1)}, f32[32,128]{1,0:T(8,128)S(1)}, u32[]{:S(2)}, u32[]{:S(2)}) collective-permute-start(f32[32,128]{1,0:T(8,128)S(1)} %get-tuple-element.45), channel_id=1, source_target_pairs={{0,64},{32,96},{64,128},{96,160},{128,192},{160,224},{192,256},{22... | collective-permute-start | bytes 49160 | tf_op jit(solution)/shard_map/ppermute | solution.py:29
  52.8 6.0 %collective-permute-start.9 = (f32[32,128]{1,0:T(8,128)S(1)}, f32[32,128]{1,0:T(8,128)S(1)}, u32[]{:S(2)}, u32[]{:S(2)}) collective-permute-start(f32[32,128]{1,0:T(8,128)S(1)} %get-tuple-element.46), channel_id=1, source_target_pairs={{0,448},{32,480},{64,0},{96,32},{128,64},{160,96},{192,128},{224,1... | collective-permute-start | bytes 49160 | tf_op jit(solution)/shard_map/ppermute | solution.py:29
  58.8 1.4 %collective-permute-done.9.high_2 = f32[32,128]{1,0:T(8,128)S(1)} collective-permute-done((f32[32,128]{1,0:T(8,128)S(1)}, f32[32,128]{1,0:T(8,128)S(1)}, u32[]{:S(2)}, u32[]{:S(2)}) %collective-permute-start.9) | collective-permute-done | bytes 16416 | tf_op jit(solution)/shard_map/ppermute | solution.py:29
  60.3 0.7 shard_map.77
  61.0 3.6 %collective-permute-start.10 = (f32[72,128]{1,0:T(8,128)S(1)}, f32[72,128]{1,0:T(8,128)S(1)}, u32[]{:S(2)}, u32[]{:S(2)}) collective-permute-start(f32[72,128]{1,0:T(8,128)S(1)} %get-tuple-element.50), channel_id=1, source_target_pairs={{0,8},{8,16},{16,24},{24,0},{1,9},{9,17},{17,25},{25,1},{2,10},{10... | collective-permute-start | bytes 110600 | tf_op jit(solution)/shard_map/ppermute | solution.py:29
  64.6 2.2 %collective-permute-start.11 = (f32[72,128]{1,0:T(8,128)S(1)}, f32[72,128]{1,0:T(8,128)S(1)}, u32[]{:S(2)}, u32[]{:S(2)}) collective-permute-start(f32[72,128]{1,0:T(8,128)S(1)} %get-tuple-element.51), channel_id=1, source_target_pairs={{0,24},{8,0},{16,8},{24,16},{1,25},{9,1},{17,9},{25,17},{2,26},{10... | collective-permute-start | bytes 110600 | tf_op jit(solution)/shard_map/ppermute | solution.py:29
  66.9 4.8 %collective-permute-done.11.high = f32[72,128]{1,0:T(8,128)S(1)} collective-permute-done((f32[72,128]{1,0:T(8,128)S(1)}, f32[72,128]{1,0:T(8,128)S(1)}, u32[]{:S(2)}, u32[]{:S(2)}) %collective-permute-start.11) | collective-permute-done | bytes 36896 | tf_op jit(solution)/shard_map/ppermute | solution.py:29
  71.7 0.8 %shard_map.78 = (f32[24,128]{1,0:T(8,128)S(1)}, f32[24,128]{1,0:T(8,128)S(1)}, f32[10,24,256]{2,1,0:T(8,128)S(1)}, f32[6,16,128]{2,1,0:T(8,128)S(1)}, f32[4,16,128]{2,1,0:T(8,128)S(1)}) custom-call(f32[8]{0:T(128)S(1)} %convert_element_type.3.inside, f32[10,24,256]{2,1,0:T(8,128)S(1)} %get-tuple-element.47.fine, f32[6,16,128]{2,1,0:T(8,128)S(1)} %get-tuple-element.48.middle, ...), custom_call_target="tpu_custom_call" | custom-call | tf_op jit(solution)/shard_map/pallas_call | solution.py:565
  72.5 2.9 %collective-permute-start.13 = (f32[24,128]{1,0:T(8,128)S(1)}, f32[24,128]{1,0:T(8,128)S(1)}, u32[]{:S(2)}, u32[]{:S(2)}) collective-permute-start(f32[24,128]{1,0:T(8,128)S(1)} %get-tuple-element.56), channel_id=1, source_target_pairs={{0,7},{1,0},{2,1},{3,2},{4,3},{5,4},{6,5},{7,6},{8,15},{9,8},{10,9... | collective-permute-start | bytes 36872 | tf_op jit(solution)/shard_map/ppermute | solution.py:29
  75.4 0.6 slice_bitcast_fusion
  76.1 0.7 collective-permute-done.12.low
  76.8 1.7 %shard_map.79 = (f32[3,8,16,128]{3,2,1,0:T(8,128)}, f32[8,16,128]{2,1,0:T(8,128)}) custom-call(f32[8]{0:T(128)S(1)} %convert_element_type.3.inside, f32[4,8,16,128]{3,2,1,0:T(8,128)S(1)} %shard_map.75.moved, f32[10,24,256]{2,1,0:T(8,128)S(1)} %get-tuple-element.52.fine, f32[6,16,128]{2,1,0:T(8,128)S(1)} %get-tuple-element.53.middle, ...), custom_call_target="tpu_custom_call" | custom-call | tf_op jit(solution)/shard_map/pallas_call | solution.py:570
  (24 shorter events, 0.2 us)
Async XLA Ops:
  0.6 0.9 %copy-start = (f32[3,8,16,128]{3,2,1,0:T(8,128)S(1)}, f32[3,8,16,128]{3,2,1,0:T(8,128)}, u32[]{:S(2)}) copy-start(f32[3,8,16,128]{3,2,1,0:T(8,128)} %velocity.5) | copy-start | bytes 589828
  1.6 0.8 %copy-start.2 = (f32[8,16,128]{2,1,0:T(8,128)S(1)}, f32[8,16,128]{2,1,0:T(8,128)}, u32[]{:S(2)}) copy-start(f32[8,16,128]{2,1,0:T(8,128)} %density.5) | copy-start | bytes 196612
  2.4 13.6 %copy-start.1 = (f32[3,8,16,128]{3,2,1,0:T(8,128)S(1)}, f32[3,8,16,128]{3,2,1,0:T(8,128)}, u32[]{:S(2)}) copy-start(f32[3,8,16,128]{3,2,1,0:T(8,128)} %velocity.5) | copy-start | bytes 589828
  2.4 13.6 %copy-start.3 = (f32[8,16,128]{2,1,0:T(8,128)S(1)}, f32[8,16,128]{2,1,0:T(8,128)}, u32[]{:S(2)}) copy-start(f32[8,16,128]{2,1,0:T(8,128)} %density.5) | copy-start | bytes 196612
  2.4 19.6 %collective-permute-start = (f32[4,4,16,128]{3,2,1,0:T(8,128)S(1)}, f32[4,4,16,128]{3,2,1,0:T(8,128)S(1)}, u32[]{:S(2)}, u32[]{:S(2)}) collective-permute-start(f32[4,4,16,128]{3,2,1,0:T(8,128)S(1)} %get-tuple-element.33), channel_id=1, source_target_pairs={{0,32},{32,64},{64,96},{96,128},{128,160},{160,192},{192,224},{224... | collective-permute-start | bytes 393224 | tf_op jit(solution)/shard_map/ppermute | solution.py:29
  6.4 15.6 %collective-permute-start.1 = (f32[4,4,16,128]{3,2,1,0:T(8,128)S(1)}, f32[4,4,16,128]{3,2,1,0:T(8,128)S(1)}, u32[]{:S(2)}, u32[]{:S(2)}) collective-permute-start(f32[4,4,16,128]{3,2,1,0:T(8,128)S(1)} %get-tuple-element.34), channel_id=1, source_target_pairs={{0,480},{32,0},{64,32},{96,64},{128,96},{160,128},{192,160},{224,1... | collective-permute-start | bytes 393224 | tf_op jit(solution)/shard_map/ppermute | solution.py:29
  16.0 0.9 %copy-start.4 = (s32[3,8,16,128]{3,2,1,0:T(8,128)S(1)}, s32[3,8,16,128]{3,2,1,0:T(8,128)}, u32[]{:S(2)}) copy-start(s32[3,8,16,128]{3,2,1,0:T(8,128)} %offsets.1) | copy-start | bytes 589828
  17.0 0.9 %copy-start.5 = (s32[3,8,16,128]{3,2,1,0:T(8,128)S(1)}, s32[3,8,16,128]{3,2,1,0:T(8,128)}, u32[]{:S(2)}) copy-start(s32[3,8,16,128]{3,2,1,0:T(8,128)} %eighths.1) | copy-start | bytes 589828
  22.6 10.5 %collective-permute-start.2 = (f32[4,8,8,128]{3,2,1,0:T(8,128)S(1)}, f32[4,8,8,128]{3,2,1,0:T(8,128)S(1)}, u32[]{:S(2)}, u32[]{:S(2)}) collective-permute-start(f32[4,8,8,128]{3,2,1,0:T(8,128)S(1)} %get-tuple-element.35), channel_id=1, source_target_pairs={{0,8},{8,16},{16,24},{24,0},{1,9},{9,17},{17,25},{25,1},{2,10},{10... | collective-permute-start | bytes 393224 | tf_op jit(solution)/shard_map/ppermute | solution.py:29
  25.0 8.1 %collective-permute-start.3 = (f32[4,8,8,128]{3,2,1,0:T(8,128)S(1)}, f32[4,8,8,128]{3,2,1,0:T(8,128)S(1)}, u32[]{:S(2)}, u32[]{:S(2)}) collective-permute-start(f32[4,8,8,128]{3,2,1,0:T(8,128)S(1)} %get-tuple-element.36), channel_id=1, source_target_pairs={{0,24},{8,0},{16,8},{24,16},{1,25},{9,1},{17,9},{25,17},{2,26},{10... | collective-permute-start | bytes 393224 | tf_op jit(solution)/shard_map/ppermute | solution.py:29
  33.8 6.9 %collective-permute-start.4 = (f32[4,3,8,128]{3,2,1,0:T(8,128)S(1)}, f32[4,3,8,128]{3,2,1,0:T(8,128)S(1)}, u32[]{:S(2)}, u32[]{:S(2)}) collective-permute-start(f32[4,3,8,128]{3,2,1,0:T(8,128)S(1)} %get-tuple-element.38), channel_id=1, source_target_pairs={{0,1},{1,2},{2,3},{3,4},{4,5},{5,6},{6,7},{7,0},{8,9},{9,10},{10,1... | collective-permute-start | bytes 147464 | tf_op jit(solution)/shard_map/ppermute | solution.py:29
  33.8 6.9 %collective-permute-start.5 = (f32[4,3,8,128]{3,2,1,0:T(8,128)S(1)}, f32[4,3,8,128]{3,2,1,0:T(8,128)S(1)}, u32[]{:S(2)}, u32[]{:S(2)}) collective-permute-start(f32[4,3,8,128]{3,2,1,0:T(8,128)S(1)} %get-tuple-element.39), channel_id=1, source_target_pairs={{0,7},{1,0},{2,1},{3,2},{4,3},{5,4},{6,5},{7,6},{8,15},{9,8},{10,9... | collective-permute-start | bytes 147464 | tf_op jit(solution)/shard_map/ppermute | solution.py:29
  43.8 16.5 %collective-permute-start.6 = (f32[160,128]{1,0:T(8,128)S(1)}, f32[160,128]{1,0:T(8,128)S(1)}, u32[]{:S(2)}, u32[]{:S(2)}) collective-permute-start(f32[160,128]{1,0:T(8,128)S(1)} %get-tuple-element.43), channel_id=1, source_target_pairs={{0,32},{32,64},{64,96},{96,128},{128,160},{160,192},{192,224},{224... | collective-permute-start | bytes 245768 | tf_op jit(solution)/shard_map/ppermute | solution.py:29
  45.7 14.5 %collective-permute-start.7 = (f32[160,128]{1,0:T(8,128)S(1)}, f32[160,128]{1,0:T(8,128)S(1)}, u32[]{:S(2)}, u32[]{:S(2)}) collective-permute-start(f32[160,128]{1,0:T(8,128)S(1)} %get-tuple-element.44), channel_id=1, source_target_pairs={{0,480},{32,0},{64,32},{96,64},{128,96},{160,128},{192,160},{224,1... | collective-permute-start | bytes 245768 | tf_op jit(solution)/shard_map/ppermute | solution.py:29
  50.9 8.0 %collective-permute-start.8 = (f32[32,128]{1,0:T(8,128)S(1)}, f32[32,128]{1,0:T(8,128)S(1)}, u32[]{:S(2)}, u32[]{:S(2)}) collective-permute-start(f32[32,128]{1,0:T(8,128)S(1)} %get-tuple-element.45), channel_id=1, source_target_pairs={{0,64},{32,96},{64,128},{96,160},{128,192},{160,224},{192,256},{22... | collective-permute-start | bytes 49160 | tf_op jit(solution)/shard_map/ppermute | solution.py:29
  52.8 7.5 %collective-permute-start.9 = (f32[32,128]{1,0:T(8,128)S(1)}, f32[32,128]{1,0:T(8,128)S(1)}, u32[]{:S(2)}, u32[]{:S(2)}) collective-permute-start(f32[32,128]{1,0:T(8,128)S(1)} %get-tuple-element.46), channel_id=1, source_target_pairs={{0,448},{32,480},{64,0},{96,32},{128,64},{160,96},{192,128},{224,1... | collective-permute-start | bytes 49160 | tf_op jit(solution)/shard_map/ppermute | solution.py:29
  61.0 5.9 %collective-permute-start.10 = (f32[72,128]{1,0:T(8,128)S(1)}, f32[72,128]{1,0:T(8,128)S(1)}, u32[]{:S(2)}, u32[]{:S(2)}) collective-permute-start(f32[72,128]{1,0:T(8,128)S(1)} %get-tuple-element.50), channel_id=1, source_target_pairs={{0,8},{8,16},{16,24},{24,0},{1,9},{9,17},{17,25},{25,1},{2,10},{10... | collective-permute-start | bytes 110600 | tf_op jit(solution)/shard_map/ppermute | solution.py:29
  64.6 7.1 %collective-permute-start.11 = (f32[72,128]{1,0:T(8,128)S(1)}, f32[72,128]{1,0:T(8,128)S(1)}, u32[]{:S(2)}, u32[]{:S(2)}) collective-permute-start(f32[72,128]{1,0:T(8,128)S(1)} %get-tuple-element.51), channel_id=1, source_target_pairs={{0,24},{8,0},{16,8},{24,16},{1,25},{9,1},{17,9},{25,17},{2,26},{10... | collective-permute-start | bytes 110600 | tf_op jit(solution)/shard_map/ppermute | solution.py:29
  72.5 4.3 %collective-permute-start.12 = (f32[24,128]{1,0:T(8,128)S(1)}, f32[24,128]{1,0:T(8,128)S(1)}, u32[]{:S(2)}, u32[]{:S(2)}) collective-permute-start(f32[24,128]{1,0:T(8,128)S(1)} %get-tuple-element.55), channel_id=1, source_target_pairs={{0,1},{1,2},{2,3},{3,4},{4,5},{5,6},{6,7},{7,0},{8,9},{9,10},{10,1... | collective-permute-start | bytes 36872 | tf_op jit(solution)/shard_map/ppermute | solution.py:29
  72.5 4.3 %collective-permute-start.13 = (f32[24,128]{1,0:T(8,128)S(1)}, f32[24,128]{1,0:T(8,128)S(1)}, u32[]{:S(2)}, u32[]{:S(2)}) collective-permute-start(f32[24,128]{1,0:T(8,128)S(1)} %get-tuple-element.56), channel_id=1, source_target_pairs={{0,7},{1,0},{2,1},{3,2},{4,3},{5,4},{6,5},{7,6},{8,15},{9,8},{10,9... | collective-permute-start | bytes 36872 | tf_op jit(solution)/shard_map/ppermute | solution.py:29

commit v4 on v3

--- a/solution.py
+++ b/solution.py
@@ -10,14 +10,15 @@
 RELAX_WEIGHT = 6.0 / 7.0
 VMEM = pl.BlockSpec(memory_space=pltpu.VMEM)
 SMEM = pl.BlockSpec(memory_space=pltpu.SMEM)
+FAR = pl.BlockSpec(memory_space=pl.ANY)
 PARAMS = pltpu.CompilerParams(vmem_limit_bytes=48 * 1024 * 1024)
 
 
-def call(kernel, outs, scratch=(), scalars=0, inputs=0):
+def call(kernel, outs, scratch=(), scalars=0, inputs=0, far=0):
     return pl.pallas_call(
         kernel,
         out_shape=[jax.ShapeDtypeStruct(shape, dtype) for shape, dtype in outs],
-        in_specs=[SMEM] * scalars + [VMEM] * inputs,
+        in_specs=[SMEM] * scalars + [VMEM] * inputs + [FAR] * far,
         out_specs=[VMEM] * len(outs),
         scratch_shapes=list(scratch),
         compiler_params=PARAMS,
@@ -29,19 +30,35 @@
     return lax.ppermute(value, axis, [(i, (i + step) % count) for i in range(count)])
 
 
-def pack_kernel(velocity, density, low_planes, high_planes):
+def pack_kernel(velocity, density, low_planes, high_planes, arrived):
+    copies = []
+    for k, (out, first) in enumerate(((low_planes, 0), (high_planes, 4))):
+        planes = pl.ds(first, 4)
+        copies.append(
+            pltpu.make_async_copy(velocity.at[:, planes], out.at[pl.ds(0, 3)], arrived.at[2 * k])
+        )
+        copies.append(pltpu.make_async_copy(density.at[planes], out.at[3], arrived.at[2 * k + 1]))
+    for copy in copies:
+        copy.start()
+    for copy in copies:
+        copy.wait()
+
+
+def own_kernel(velocity, density, offsets, eighths, fields_t, code_t, own, whole, parts, arrived):
+    copies = [
+        pltpu.make_async_copy(velocity, own.at[pl.ds(0, 3)], arrived.at[0]),
+        pltpu.make_async_copy(density, own.at[3], arrived.at[1]),
+        pltpu.make_async_copy(offsets, whole, arrived.at[2]),
+        pltpu.make_async_copy(eighths, parts, arrived.at[3]),
+    ]
+    for copy in copies:
+        copy.start()
+    for copy in copies:
+        copy.wait()
     for f in range(4):
-        field = velocity[f] if f < 3 else density[...]
-        low_planes[f] = field[0:4]
-        high_planes[f] = field[4:8]
-
-
-def own_kernel(velocity, density, offsets, eighths, fields_t, code_t):
-    for a in range(3):
-        fields_t[a] = velocity[a].reshape(128, 128).T
-    fields_t[3] = density[...].reshape(128, 128).T
-    code = (offsets[0] + 4) + (offsets[1] + 4) * 8 + (offsets[2] + 4) * 64
-    code = code + eighths[0] * 512 + eighths[1] * 4096 + eighths[2] * 32768
+        fields_t[f] = own[f].reshape(128, 128).T
+    code = (whole[0] + 4) + (whole[1] + 4) * 8 + (whole[2] + 4) * 64
+    code = code + parts[0] * 512 + parts[1] * 4096 + parts[2] * 32768
     code_t[...] = code.astype(jnp.float32).reshape(128, 128).T.astype(jnp.int32)
 
 
@@ -70,7 +87,7 @@
         planes_t[f] = both.T
 
 
-def columns_kernel(inside, fields_t, planes_t, low, high, after, rows_t, to_low, to_high):
+def columns_kernel(inside, fields_t, planes_t, code_t, low, high, after, rows_t, to_low, to_high):
     for f in range(4):
         both = jnp.concatenate(
             [low[f].reshape(64, 128) * inside[2], high[f].reshape(64, 128) * inside[3]], axis=0
@@ -78,8 +95,13 @@
         turned = both.T
         rows_t[f] = turned
         for group, source in enumerate((fields_t[f], planes_t[f], turned)):
-            to_low[f, group] = source[0:8]
-            to_high[f, group] = source[120:128]
+            at = 24 * (3 * f + group)
+            to_low[at : at + 24] = source[0:24]
+            to_high[at : at + 24] = source[104:128]
+    for out, first in ((to_low, 0), (to_high, 112)):
+        code = code_t[first : first + 16]
+        for k in range(6):
+            out[288 + 16 * k : 304 + 16 * k] = ((code >> (3 * k)) & 7).astype(jnp.float32)
 
 
 def corners_of(code):
@@ -117,10 +139,10 @@
     ]
 
 
-def gathered(at, weights, rows_of):
-    parts = [None] * 4
+def gathered(at, weights, rows_of, count=4):
+    parts = [None] * count
     for shift, weight in enumerate(weights):
-        for f in range(4):
+        for f in range(count):
             taken = jnp.take_along_axis(
                 rows_of(f, shift), at, axis=1, mode="promise_in_bounds"
             )
@@ -129,12 +151,8 @@
 
 
 def group_kernel(group, code_t, source_t, *refs):
-    before, (after, padded) = refs[:-2], refs[-2:]
+    before, after = refs[:-1], refs[-1]
     none = jnp.zeros((8, 128), jnp.float32)
-    for f in range(4):
-        padded[f, 8:136] = source_t[f]
-        padded[f, 0:8] = none
-        padded[f, 136:144] = none
 
     def tile(step, carry):
         start = pl.multiple_of(step * 8, 8)
@@ -142,40 +160,80 @@
         by_shift = weights_z(code, range(9))
         sums = [before[0][f, pl.ds(start, 8), :] if before else none for f in range(4)]
         for at, weights in corners_of(code):
-            parts = gathered(at, by_shift, lambda f, dz: padded[f, pl.ds(start + (4 + dz), 8), :])
+            parts = gathered(
+                at, by_shift, lambda f, dz: source_t[f, pl.ds(start + (dz - 4), 8), :]
+            )
             for f in range(4):
                 sums[f] = sums[f] + weights[group] * parts[f]
         for f in range(4):
             after[f, pl.ds(start, 8), :] = sums[f]
         return carry
 
-    lax.fori_loop(0, 16, tile, 0)
-
-
-def edges_kernel(inside, code_t, sums_t, low, high, moved, moved_t, padded):
-    none = jnp.zeros((8, 128), jnp.float32)
+    lax.fori_loop(1, 15, tile, 0, unroll=7)
+
+
+def edges_kernel(
+    inside, code_t, sums_t, fields_t, planes_t, rows_t, low, high,
+    moved, density, beyond, moved_t, beyond_t, padded, codes,
+):
+    for f in range(4):
+        for group, source in enumerate((fields_t, planes_t, rows_t)):
+            at = 24 * (3 * f + group)
+            padded[0, f, group, 0:24] = low[at : at + 24] * inside[4]
+            padded[0, f, group, 24:40] = source[f, 0:16]
+            padded[1, f, group, 0:16] = source[f, 112:128]
+            padded[1, f, group, 16:40] = high[at : at + 24] * inside[5]
+    for end, got in ((0, low), (1, high)):
+        code = jnp.zeros((16, 128), jnp.int32)
+        for k in range(6):
+            code = code + (got[288 + 16 * k : 304 + 16 * k].astype(jnp.int32) << (3 * k))
+        if end == 0:
+            codes[0, 0:16] = code
+            codes[0, 16:24] = code_t[0:8]
+        else:
+            codes[1, 0:8] = code_t[120:128]
+            codes[1, 8:24] = code
     for f in range(4):
         moved_t[f] = sums_t[f]
-        for group in range(3):
-            padded[0, f, group, 0:8] = low[f, group] * inside[4]
-            padded[0, f, group, 8:16] = none
-            padded[1, f, group, 0:8] = none
-            padded[1, f, group, 8:16] = high[f, group] * inside[5]
-    for end, start, first, shifts in ((0, 0, 4, range(0, 4)), (1, 120, 1, range(5, 9))):
-        code = code_t[start : start + 8]
-        by_shift = weights_z(code, shifts)
-        sums = [sums_t[f, start : start + 8] for f in range(4)]
+
+    def moved_tile(end, start, count):
+        code = codes[end, pl.ds(start, 8), :]
+        by_shift = weights_z(code, range(9))
+        sums = [jnp.zeros((8, 128), jnp.float32)] * count
         for at, weights in corners_of(code):
             for group in range(3):
                 parts = gathered(
-                    at, by_shift, lambda f, k: padded[end, f, group, first + k : first + k + 8]
+                    at,
+                    by_shift,
+                    lambda f, dz: padded[end, f, group, pl.ds(start + (4 + dz), 8), :],
+                    count,
                 )
-                for f in range(4):
+                for f in range(count):
                     sums[f] = sums[f] + weights[group] * parts[f]
+        return sums
+
+    def inner(end, carry):
+        sums = moved_tile(end, pl.multiple_of(16 * (1 - end), 8), 4)
         for f in range(4):
-            moved_t[f, start : start + 8] = sums[f]
-    for f in range(4):
+            moved_t[f, pl.ds(pl.multiple_of(120 * end, 8), 8), :] = sums[f]
+        return carry
+
+    def outer(step, carry):
+        end, half = step // 2, step % 2
+        sums = moved_tile(end, pl.multiple_of(8 * (end + half), 8), 3)
+        flag = jnp.where(end == 0, inside[4], inside[5])
+        for f in range(3):
+            beyond_t[f, pl.ds(pl.multiple_of(112 * (1 - end) + 8 * half, 8), 8), :] = sums[f] * flag
+        return carry
+
+    lax.fori_loop(0, 2, inner, 0, unroll=2)
+    for f in range(3):
+        beyond_t[f] = jnp.zeros((128, 128), jnp.float32)
+    lax.fori_loop(0, 4, outer, 0, unroll=2)
+    for f in range(3):
         moved[f] = moved_t[f].T.reshape(8, 16, 128)
+        beyond[f] = beyond_t[f].T.reshape(8, 16, 128)
+    density[...] = moved_t[3].T.reshape(8, 16, 128)
 
 
 def ends(axis):
@@ -186,17 +244,21 @@
 def advect(inside, velocity, density, offsets, eighths):
     f32 = jnp.float32
     turned = ((4, 128, 128), f32)
+    arrived = pltpu.SemaphoreType.DMA((4,))
 
     def gather(group, *values):
-        padded = [pltpu.VMEM((4, 144, 128), f32)]
         kernel = functools.partial(group_kernel, group)
-        return call(kernel, [turned], padded, inputs=len(values))(*values)[0]
+        return call(kernel, [turned], inputs=len(values))(*values)[0]
 
     planes = ((4, 4, 16, 128), f32)
-    low_planes, high_planes = call(pack_kernel, [planes, planes], inputs=2)(velocity, density)
+    low_planes, high_planes = call(pack_kernel, [planes, planes], [arrived], far=2)(
+        velocity, density
+    )
     low = shift_ring(high_planes, "gx", 1)
     high = shift_ring(low_planes, "gx", -1)
-    fields_t, code_t = call(own_kernel, [turned, ((128, 128), jnp.int32)], inputs=4)(
+    whole = pltpu.VMEM((3, 8, 16, 128), jnp.int32)
+    scratch = [pltpu.VMEM((4, 8, 16, 128), f32), whole, whole, arrived]
+    fields_t, code_t = call(own_kernel, [turned, ((128, 128), jnp.int32)], scratch, far=4)(
         velocity, density, offsets, eighths
     )
     sums_t = gather(0, code_t, fields_t)
@@ -208,17 +270,23 @@
     rows_high = shift_ring(to_low, "gy", -1)
     (planes_t,) = call(planes_kernel, [turned], scalars=1, inputs=2)(inside, low, high)
     sums_t = gather(1, code_t, planes_t, sums_t)
-    edge = ((4, 3, 8, 128), f32)
+    edge = ((384, 128), f32)
     rows_t, to_low, to_high = call(
-        columns_kernel, [turned, edge, edge], scalars=1, inputs=5
-    )(inside, fields_t, planes_t, rows_low, rows_high, sums_t)
+        columns_kernel, [turned, edge, edge], scalars=1, inputs=6
+    )(inside, fields_t, planes_t, code_t, rows_low, rows_high, sums_t)
     columns_low = shift_ring(to_high, "gz", 1)
     columns_high = shift_ring(to_low, "gz", -1)
     sums_t = gather(2, code_t, rows_t, sums_t)
-    scratch = [pltpu.VMEM((4, 128, 128), f32), pltpu.VMEM((2, 4, 3, 16, 128), f32)]
-    return call(edges_kernel, [((4, 8, 16, 128), f32)], scratch, scalars=1, inputs=4)(
-        inside, code_t, sums_t, columns_low, columns_high
-    )[0]
+    scratch = [
+        pltpu.VMEM((4, 128, 128), f32),
+        pltpu.VMEM((3, 128, 128), f32),
+        pltpu.VMEM((2, 4, 3, 40, 128), f32),
+        pltpu.VMEM((2, 24, 128), jnp.int32),
+    ]
+    block = ((3, 8, 16, 128), f32)
+    return call(
+        edges_kernel, [block, ((8, 16, 128), f32), block], scratch, scalars=1, inputs=7
+    )(inside, code_t, sums_t, fields_t, planes_t, rows_t, columns_low, columns_high)
 
 
 def roll(value, shift, dim):
@@ -325,11 +393,11 @@
 
 
 def levels_kernel(
-    inside, moved, to_low, to_high, to_low_2, to_high_2, fine, middle, coarse, halves
+    inside, moved, beyond, to_low, to_high, to_low_2, to_high_2, fine, middle, coarse, halves
 ):
     def spread(a):
-        block = jnp.concatenate([moved[a], jnp.zeros((8, 8, 128), jnp.float32)], axis=1)
-        block = jnp.concatenate([block, jnp.zeros((8, 24, 128), jnp.float32)], axis=2)
+        block = jnp.concatenate([moved[a], beyond[a]], axis=2)
+        block = jnp.concatenate([block, jnp.zeros((8, 8, 256), jnp.float32)], axis=1)
         return with_planes(block, 4)
 
     u = spread(0)
@@ -347,6 +415,11 @@
     mask = grid_mask(inside, (-3, 8, 2), (16, 4), (128, 32))
     source = with_planes(restrict_middle(residual, halves), 1)
     second_2 = smooth(source, 16.0, mask, False)
+    lane = lax.broadcasted_iota(jnp.int32, (1, 24, 256), 2)
+    second = jnp.where((lane < 132) | (lane >= 252), second, 0.0)
+    lane = lane_numbers(16)[None]
+    second_1 = jnp.where((lane < 72) | (lane >= 120), second_1, 0.0)
+    second_2 = jnp.where((lane < 40) | (lane >= 120), second_2, 0.0)
     fine[...] = second[3:13]
     middle[...] = second_1[3:9]
     coarse[...] = second_2[2:6]
@@ -417,8 +490,13 @@
             out[48 + 4 * k : 52 + 4 * k] = rows[0:4]
 
 
-def rows_sum_kernel(
-    inside, fine, middle, coarse, low, high, to_low, to_high, fine_o, middle_o, coarse_o
+def four_lanes(rows):
+    lane = lane_numbers(rows)
+    return (lane < 4) | (lane >= 124)
+
+
+def pressure_kernel(
+    inside, moved, fine, middle, coarse, low, high, velocity, pressure, halves
 ):
     f = [fine[k] for k in range(10)]
     m = [middle[k] for k in range(6)]
@@ -448,66 +526,6 @@
             m[k] = m[k] + place(add_m, 16, at_1)
             if k < 4:
                 c[k] = c[k] + place(add_c, 16, at_2)
-    for k in range(10):
-        fine_o[k] = f[k]
-    for k in range(6):
-        middle_o[k] = m[k]
-    for k in range(4):
-        coarse_o[k] = c[k]
-    lane = lane_numbers(24)
-    lane_16 = lane_numbers(16)
-    none = jnp.zeros((8, 128), jnp.float32)
-
-    def strip(value, first, count, at):
-        lanes = lane_numbers(value.shape[0])
-        moved = roll(value, at - first, 1)
-        return jnp.where((lanes >= at) & (lanes < at + count), moved, 0.0)
-
-    for out, at_0, at_1, at_2 in ((to_high, 127, 63, 31), (to_low, 126, 125, 125)):
-        total = jnp.zeros((24, 128), jnp.float32)
-        for k in range(10):
-            own = lane == 127 if at_0 == 127 else lane == 0
-            total = total + strip(jnp.where(own, f[k][:, 0:128], f[k][:, 128:256]), at_0, 3, 4 * k)
-        part = jnp.zeros((16, 128), jnp.float32)
-        for k in range(6):
-            part = part + strip(m[k], at_1, 4, 40 + 4 * k)
-        for k in range(4):
-            part = part + strip(c[k], at_2, 4, 64 + 4 * k)
-        out[...] = total + jnp.concatenate([part, none], axis=0)
-
-
-def four_lanes(rows):
-    lane = lane_numbers(rows)
-    return (lane < 4) | (lane >= 124)
-
-
-def pressure_kernel(inside, moved, fine, middle, coarse, low, high, velocity, pressure, halves):
-    f = [fine[k] for k in range(10)]
-    m = [middle[k] for k in range(6)]
-    c = [coarse[k] for k in range(4)]
-
-    def strip(value, at, count, first):
-        lanes = lane_numbers(value.shape[0])
-        kept = jnp.where((lanes >= at) & (lanes < at + count), value, 0.0)
-        return roll(kept, first - at, 1)
-
-    lane = lane_numbers(24)
-    for got, flag, at_0, at_1, at_2 in (
-        (low, inside[4], -1, -1, -1),
-        (high, inside[5], 126, 61, 29),
-    ):
-        whole = got[...] * flag
-        part = whole[0:16]
-        for k in range(10):
-            add = strip(whole, 4 * k, 3, at_0)
-            own = (lane < 64) if at_0 < 0 else (lane >= 64)
-            add = jnp.concatenate([jnp.where(own, add, 0.0), jnp.where(own, 0.0, add)], axis=1)
-            f[k] = f[k] + add
-        for k in range(6):
-            m[k] = m[k] + strip(part, 40 + 4 * k, 4, at_1)
-        for k in range(4):
-            c[k] = c[k] + strip(part, 64 + 4 * k, 4, at_2)
-    row = row_numbers(8)
     lane = lane_numbers(8)
     to_middle = (lane >> 1) + jnp.where(lane < 96, 0, 64)
     for k in range(4):
@@ -543,14 +561,14 @@
         velocity[2, k] = moved[2, k] - 0.5 * slope[:, 0:128]
 
 
-def project(inside, moved):
+def project(inside, moved, beyond):
     f32 = jnp.float32
     held = [((10, 24, 256), f32), ((6, 16, 128), f32), ((4, 16, 128), f32)]
     halves = [pltpu.VMEM((2, 8, 32, 128), f32)]
     side, side_2 = ((160, 128), f32), ((32, 128), f32)
     to_low, to_high, to_low_2, to_high_2, *sums = call(
-        levels_kernel, [side, side, side_2, side_2] + held, halves, scalars=1, inputs=1
-    )(inside, moved)
+        levels_kernel, [side, side, side_2, side_2] + held, halves, scalars=1, inputs=2
+    )(inside, moved, beyond)
     low = shift_ring(to_high, "gx", 1)
     high = shift_ring(to_low, "gx", -1)
     low_2 = shift_ring(to_high_2, "gx", 2)
@@ -561,12 +579,6 @@
     )(inside, *sums, low, high, low_2, high_2)
     low = shift_ring(to_high, "gy", 1)
     high = shift_ring(to_low, "gy", -1)
-    side = ((24, 128), f32)
-    to_low, to_high, *sums = call(rows_sum_kernel, [side, side] + held, scalars=1, inputs=5)(
-        inside, *sums, low, high
-    )
-    low = shift_ring(to_high, "gz", 1)
-    high = shift_ring(to_low, "gz", -1)
     return call(
         pressure_kernel,
         [((3, 8, 16, 128), f32), ((8, 16, 128), f32)],
@@ -580,9 +592,9 @@
     place = lax.axis_index("gx")
     beyond = [place > 1, place < lax.axis_size("gx") - 2]
     inside = jnp.stack(ends("gx") + ends("gy") + ends("gz") + beyond).astype(jnp.float32)
-    moved = advect(inside, velocity, density, offsets, eighths)
-    new_velocity, pressure = project(inside, moved)
-    return new_velocity, moved[3], pressure
+    moved, new_density, past = advect(inside, velocity, density, offsets, eighths)
+    new_velocity, pressure = project(inside, moved, past)
+    return new_velocity, new_density, pressure
 
 
 def solution(mesh):

time: 79.5 us -> 74.1 us (0.932)
  starting transfers between devices: 46.1 us -> 43 us
  Pallas kernels: 20.2 us -> 18.9 us
    ppermute x14 -> x12, starting transfers between devices: 46.1 us -> 43 us  [shift_ring(): lax.ppermute(value, axis, [(i, (i + step) % count) for i in range(count)])]
    pallas_call x8 -> x7, Pallas kernels: 14.6 us -> 13.4 us  [the longest x3 7.47 us: gather(): return call(kernel, [turned], inputs=len(values))(*values)[0]]
    ppermute x14 -> x12, waiting for transfers between devices: 7.01 us -> 7.11 us  [shift_ring(): lax.ppermute(value, axis, [(i, (i + step) % count) for i in range(count)])]
  transfers between devices with their start and end apart: 14 -> 12, of which waited for: 3 -> 4; matrix products, arithmetic and copies ran while one was open for 1% -> 0% of each run, Pallas kernels for 16% -> 12%
where the time goes in v4:
time: 74.1 us; the launch traced here: 73.6 us
  starting transfers between devices  43 us (58%)
  Pallas kernels  18.9 us (26%)
  waiting for transfers between devices  7.11 us (10%)
  local copies, waits for them, and re-layouts  3.72 us (5%)
  between operations  0.87 us (1%)
    ppermute x12, starting transfers between devices, shift_ring(): lax.ppermute(value, axis, [(i, (i + step) % count) for i in range(count)])  43 us
    pallas_call x3, Pallas kernels, gather(): return call(kernel, [turned], inputs=len(values))(*values)[0]  7.47 us
    ppermute x12, waiting for transfers between devices, shift_ring(): lax.ppermute(value, axis, [(i, (i + step) % count) for i in range(count)])  7.11 us
    pallas_call x1, Pallas kernels, advect(): call(edges_kernel, [block, ((8, 16, 128), f32), block], scratch, scalars=...  4.01 us
    unnamed x12, local copies, waits for them, and re-layouts  3.61 us
    pallas_call x1, Pallas kernels, project(): call(levels_kernel, [side, side, side_2, side_2] + held, halves, scalars=...  1.97 us
    pallas_call x1, Pallas kernels, project(): call(pressure_kernel, [((3, 8, 16, 128), f32), ((8, 16, 128), f32)], halv...  1.62 us
  transfers between devices with their start and end apart: 12, of which 4 were waited for; matrix products, arithmetic and copies ran while one was open for 0% of the time, Pallas kernels for 12%

profile of v4, /device:TPU:6, one launch (start us, length us, event | category | flops | bytes accessed | tf_op | source)
XLA Modules:
  0.0 73.6 jit_solution(5974014836313597088)
XLA Ops:
  0.6 0.9 %copy-done = f32[3,8,16,128]{3,2,1,0:T(8,128)S(1)} copy-done((f32[3,8,16,128]{3,2,1,0:T(8,128)S(1)}, f32[3,8,16,128]{3,2,1,0:T(8,128)}, u32[]{:S(2)}) %copy-start) | copy-done | bytes 196632
  1.6 0.8 %copy-done.2 = f32[8,16,128]{2,1,0:T(8,128)S(1)} copy-done((f32[8,16,128]{2,1,0:T(8,128)S(1)}, f32[8,16,128]{2,1,0:T(8,128)}, u32[]{:S(2)}) %copy-start.2) | copy-done | bytes 65560
  2.4 0.2 shard_map.68
  2.6 3.8 %collective-permute-start = (f32[4,4,16,128]{3,2,1,0:T(8,128)S(1)}, f32[4,4,16,128]{3,2,1,0:T(8,128)S(1)}, u32[]{:S(2)}, u32[]{:S(2)}) collective-permute-start(f32[4,4,16,128]{3,2,1,0:T(8,128)S(1)} %get-tuple-element.31), channel_id=1, source_target_pairs={{0,32},{32,64},{64,96},{96,128},{128,160},{160,192},{192,224},{224... | collective-permute-start | bytes 393224 | tf_op jit(solution)/shard_map/ppermute | solution.py:30
  6.4 9.5 %collective-permute-start.1 = (f32[4,4,16,128]{3,2,1,0:T(8,128)S(1)}, f32[4,4,16,128]{3,2,1,0:T(8,128)S(1)}, u32[]{:S(2)}, u32[]{:S(2)}) collective-permute-start(f32[4,4,16,128]{3,2,1,0:T(8,128)S(1)} %get-tuple-element.32), channel_id=1, source_target_pairs={{0,480},{32,0},{64,32},{96,64},{128,96},{160,128},{192,160},{224,1... | collective-permute-start | bytes 393224 | tf_op jit(solution)/shard_map/ppermute | solution.py:30
  16.0 0.1 stack.35
  16.1 0.9 %copy-done.4 = s32[3,8,16,128]{3,2,1,0:T(8,128)S(1)} copy-done((s32[3,8,16,128]{3,2,1,0:T(8,128)S(1)}, s32[3,8,16,128]{3,2,1,0:T(8,128)}, u32[]{:S(2)}) %copy-start.4) | copy-done | bytes 196632
  17.0 0.9 %copy-done.5 = s32[3,8,16,128]{3,2,1,0:T(8,128)S(1)} copy-done((s32[3,8,16,128]{3,2,1,0:T(8,128)S(1)}, s32[3,8,16,128]{3,2,1,0:T(8,128)}, u32[]{:S(2)}) %copy-start.5) | copy-done | bytes 196632
  18.0 1.0 %shard_map.67 = (f32[4,128,128]{2,1,0:T(8,128)S(1)}, s32[128,128]{1,0:T(8,128)S(1)}) custom-call(f32[3,8,16,128]{3,2,1,0:T(8,128)S(1)} %copy-done.1, f32[8,16,128]{2,1,0:T(8,128)S(1)} %copy-done.3, s32[3,8,16,128]{3,2,1,0:T(8,128)S(1)} %copy-done.4, s32[3,8,16,128]{3,2,1,0:T(8,128)S(1)} %copy-done.5), custom_call_target="tpu_custom_call" | custom-call | tf_op jit(solution)/shard_map/pallas_call | solution.py:261
  19.0 2.5 %shard_map.70.after.refs_0_ = f32[4,128,128]{2,1,0:T(8,128)S(1)} custom-call(s32[128,128]{1,0:T(8,128)S(1)} %get-tuple-element.29.code_t, f32[4,128,128]{2,1,0:T(8,128)S(1)} %get-tuple-element.30.source_t.fields_t), custom_call_target="tpu_custom_call" | custom-call | tf_op jit(solution)/shard_map/pallas_call | solution.py:251
  21.5 0.6 shard_map.71
  22.1 2.4 %collective-permute-start.2 = (f32[4,8,8,128]{3,2,1,0:T(8,128)S(1)}, f32[4,8,8,128]{3,2,1,0:T(8,128)S(1)}, u32[]{:S(2)}, u32[]{:S(2)}) collective-permute-start(f32[4,8,8,128]{3,2,1,0:T(8,128)S(1)} %get-tuple-element.33), channel_id=1, source_target_pairs={{0,8},{8,16},{16,24},{24,0},{1,9},{9,17},{17,25},{25,1},{2,10},{10... | collective-permute-start | bytes 393224 | tf_op jit(solution)/shard_map/ppermute | solution.py:30
  24.5 3.5 %collective-permute-start.3 = (f32[4,8,8,128]{3,2,1,0:T(8,128)S(1)}, f32[4,8,8,128]{3,2,1,0:T(8,128)S(1)}, u32[]{:S(2)}, u32[]{:S(2)}) collective-permute-start(f32[4,8,8,128]{3,2,1,0:T(8,128)S(1)} %get-tuple-element.34), channel_id=1, source_target_pairs={{0,24},{8,0},{16,8},{24,16},{1,25},{9,1},{17,9},{25,17},{2,26},{10... | collective-permute-start | bytes 393224 | tf_op jit(solution)/shard_map/ppermute | solution.py:30
  27.9 0.7 shard_map.69.source_t.planes_t
  28.6 2.5 %shard_map.72.after.refs_0_ = f32[4,128,128]{2,1,0:T(8,128)S(1)} custom-call(s32[128,128]{1,0:T(8,128)S(1)} %get-tuple-element.29.code_t, f32[4,128,128]{2,1,0:T(8,128)S(1)} %shard_map.69.source_t.planes_t, f32[4,128,128]{2,1,0:T(8,128)S(1)} %shard_map.70.after.refs_0_), custom_call_target="tpu_custom_call" | custom-call | tf_op jit(solution)/shard_map/pallas_call | solution.py:251
  31.1 1.4 %collective-permute-done.3.high = f32[4,8,8,128]{3,2,1,0:T(8,128)S(1)} collective-permute-done((f32[4,8,8,128]{3,2,1,0:T(8,128)S(1)}, f32[4,8,8,128]{3,2,1,0:T(8,128)S(1)}, u32[]{:S(2)}, u32[]{:S(2)}) %collective-permute-start.3) | collective-permute-done | bytes 131104 | tf_op jit(solution)/shard_map/ppermute | solution.py:30
  32.6 0.7 shard_map.73
  33.3 2.9 %collective-permute-start.5 = (f32[384,128]{1,0:T(8,128)S(1)}, f32[384,128]{1,0:T(8,128)S(1)}, u32[]{:S(2)}, u32[]{:S(2)}) collective-permute-start(f32[384,128]{1,0:T(8,128)S(1)} %get-tuple-element.37), channel_id=1, source_target_pairs={{0,7},{1,0},{2,1},{3,2},{4,3},{5,4},{6,5},{7,6},{8,15},{9,8},{10,9... | collective-permute-start | bytes 589832 | tf_op jit(solution)/shard_map/ppermute | solution.py:30
  36.2 2.5 %shard_map.74.sums_t = f32[4,128,128]{2,1,0:T(8,128)S(1)} custom-call(s32[128,128]{1,0:T(8,128)S(1)} %get-tuple-element.29.code_t, f32[4,128,128]{2,1,0:T(8,128)S(1)} %get-tuple-element.35.source_t.rows_t, f32[4,128,128]{2,1,0:T(8,128)S(1)} %shard_map.72.after.refs_0_), custom_call_target="tpu_custom_call" | custom-call | tf_op jit(solution)/shard_map/pallas_call | solution.py:251
  38.7 0.9 %collective-permute-done.4.low = f32[384,128]{1,0:T(8,128)S(1)} collective-permute-done((f32[384,128]{1,0:T(8,128)S(1)}, f32[384,128]{1,0:T(8,128)S(1)}, u32[]{:S(2)}, u32[]{:S(2)}) %collective-permute-start.4) | collective-permute-done | bytes 196640 | tf_op jit(solution)/shard_map/ppermute | solution.py:30
  39.6 4.0 %shard_map.75 = (f32[3,8,16,128]{3,2,1,0:T(8,128)S(1)}, f32[8,16,128]{2,1,0:T(8,128)}, f32[3,8,16,128]{3,2,1,0:T(8,128)S(1)}) custom-call(f32[8]{0:T(128)S(1)} %convert_element_type.3.inside, s32[128,128]{1,0:T(8,128)S(1)} %get-tuple-element.29.code_t, f32[4,128,128]{2,1,0:T(8,128)S(1)} %shard_map.74.sums_t, ...), custom_call_target="tpu_custom_call" | custom-call | tf_op jit(solution)/shard_map/pallas_call | solution.py:287
  43.6 2.0 %shard_map.76 = (f32[160,128]{1,0:T(8,128)S(1)}, f32[160,128]{1,0:T(8,128)S(1)}, f32[32,128]{1,0:T(8,128)S(1)}, f32[32,128]{1,0:T(8,128)S(1)}, f32[10,24,256]{2,...) custom-call(f32[8]{0:T(128)S(1)} %convert_element_type.3.inside, ...), custom_call_target="tpu_custom_call" | custom-call | tf_op jit(solution)/shard_map/pallas_call | solution.py:569
  45.5 1.9 %collective-permute-start.6 = (f32[160,128]{1,0:T(8,128)S(1)}, f32[160,128]{1,0:T(8,128)S(1)}, u32[]{:S(2)}, u32[]{:S(2)}) collective-permute-start(f32[160,128]{1,0:T(8,128)S(1)} %get-tuple-element.43), channel_id=1, source_target_pairs={{0,32},{32,64},{64,96},{96,128},{128,160},{160,192},{192,224},{224... | collective-permute-start | bytes 245768 | tf_op jit(solution)/shard_map/ppermute | solution.py:30
  47.5 5.1 %collective-permute-start.7 = (f32[160,128]{1,0:T(8,128)S(1)}, f32[160,128]{1,0:T(8,128)S(1)}, u32[]{:S(2)}, u32[]{:S(2)}) collective-permute-start(f32[160,128]{1,0:T(8,128)S(1)} %get-tuple-element.44), channel_id=1, source_target_pairs={{0,480},{32,0},{64,32},{96,64},{128,96},{160,128},{192,160},{224,1... | collective-permute-start | bytes 245768 | tf_op jit(solution)/shard_map/ppermute | solution.py:30
  52.6 1.9 %collective-permute-start.8 = (f32[32,128]{1,0:T(8,128)S(1)}, f32[32,128]{1,0:T(8,128)S(1)}, u32[]{:S(2)}, u32[]{:S(2)}) collective-permute-start(f32[32,128]{1,0:T(8,128)S(1)} %get-tuple-element.45), channel_id=1, source_target_pairs={{0,64},{32,96},{64,128},{96,160},{128,192},{160,224},{192,256},{22... | collective-permute-start | bytes 49160 | tf_op jit(solution)/shard_map/ppermute | solution.py:30
  54.5 6.0 %collective-permute-start.9 = (f32[32,128]{1,0:T(8,128)S(1)}, f32[32,128]{1,0:T(8,128)S(1)}, u32[]{:S(2)}, u32[]{:S(2)}) collective-permute-start(f32[32,128]{1,0:T(8,128)S(1)} %get-tuple-element.46), channel_id=1, source_target_pairs={{0,448},{32,480},{64,0},{96,32},{128,64},{160,96},{192,128},{224,1... | collective-permute-start | bytes 49160 | tf_op jit(solution)/shard_map/ppermute | solution.py:30
  60.6 1.4 %collective-permute-done.9.high_2 = f32[32,128]{1,0:T(8,128)S(1)} collective-permute-done((f32[32,128]{1,0:T(8,128)S(1)}, f32[32,128]{1,0:T(8,128)S(1)}, u32[]{:S(2)}, u32[]{:S(2)}) %collective-permute-start.9) | collective-permute-done | bytes 16416 | tf_op jit(solution)/shard_map/ppermute | solution.py:30
  62.0 0.7 shard_map.77
  62.7 2.2 %collective-permute-start.10 = (f32[72,128]{1,0:T(8,128)S(1)}, f32[72,128]{1,0:T(8,128)S(1)}, u32[]{:S(2)}, u32[]{:S(2)}) collective-permute-start(f32[72,128]{1,0:T(8,128)S(1)} %get-tuple-element.50), channel_id=1, source_target_pairs={{0,8},{8,16},{16,24},{24,0},{1,9},{9,17},{17,25},{25,1},{2,10},{10... | collective-permute-start | bytes 110600 | tf_op jit(solution)/shard_map/ppermute | solution.py:30
  64.9 3.7 %collective-permute-start.11 = (f32[72,128]{1,0:T(8,128)S(1)}, f32[72,128]{1,0:T(8,128)S(1)}, u32[]{:S(2)}, u32[]{:S(2)}) collective-permute-start(f32[72,128]{1,0:T(8,128)S(1)} %get-tuple-element.51), channel_id=1, source_target_pairs={{0,24},{8,0},{16,8},{24,16},{1,25},{9,1},{17,9},{25,17},{2,26},{10... | collective-permute-start | bytes 110600 | tf_op jit(solution)/shard_map/ppermute | solution.py:30
  68.6 3.4 %collective-permute-done.11.high = f32[72,128]{1,0:T(8,128)S(1)} collective-permute-done((f32[72,128]{1,0:T(8,128)S(1)}, f32[72,128]{1,0:T(8,128)S(1)}, u32[]{:S(2)}, u32[]{:S(2)}) %collective-permute-start.11) | collective-permute-done | bytes 36896 | tf_op jit(solution)/shard_map/ppermute | solution.py:30
  72.0 1.6 %shard_map.78 = (f32[3,8,16,128]{3,2,1,0:T(8,128)}, f32[8,16,128]{2,1,0:T(8,128)}) custom-call(f32[8]{0:T(128)S(1)} %convert_element_type.3.inside, f32[3,8,16,128]{3,2,1,0:T(8,128)S(1)} %get-tuple-element.38.moved, f32[10,24,256]{2,1,0:T(8,128)S(1)} %get-tuple-element.47.fine, f32[6,16,128]{2,1,0:T(8,128)S(1)} %get-tuple-element.48.middle, ...), custom_call_target="tpu_custom_call" | custom-call | tf_op jit(solution)/shard_map/pallas_call | solution.py:582
  (18 shorter events, 0.1 us)
Async XLA Ops:
  0.6 0.9 %copy-start = (f32[3,8,16,128]{3,2,1,0:T(8,128)S(1)}, f32[3,8,16,128]{3,2,1,0:T(8,128)}, u32[]{:S(2)}) copy-start(f32[3,8,16,128]{3,2,1,0:T(8,128)} %velocity.5) | copy-start | bytes 589828
  1.6 0.8 %copy-start.2 = (f32[8,16,128]{2,1,0:T(8,128)S(1)}, f32[8,16,128]{2,1,0:T(8,128)}, u32[]{:S(2)}) copy-start(f32[8,16,128]{2,1,0:T(8,128)} %density.5) | copy-start | bytes 196612
  2.4 13.7 %copy-start.1 = (f32[3,8,16,128]{3,2,1,0:T(8,128)S(1)}, f32[3,8,16,128]{3,2,1,0:T(8,128)}, u32[]{:S(2)}) copy-start(f32[3,8,16,128]{3,2,1,0:T(8,128)} %velocity.5) | copy-start | bytes 589828
  2.4 13.7 %copy-start.3 = (f32[8,16,128]{2,1,0:T(8,128)S(1)}, f32[8,16,128]{2,1,0:T(8,128)}, u32[]{:S(2)}) copy-start(f32[8,16,128]{2,1,0:T(8,128)} %density.5) | copy-start | bytes 196612
  2.6 18.9 %collective-permute-start = (f32[4,4,16,128]{3,2,1,0:T(8,128)S(1)}, f32[4,4,16,128]{3,2,1,0:T(8,128)S(1)}, u32[]{:S(2)}, u32[]{:S(2)}) collective-permute-start(f32[4,4,16,128]{3,2,1,0:T(8,128)S(1)} %get-tuple-element.31), channel_id=1, source_target_pairs={{0,32},{32,64},{64,96},{96,128},{128,160},{160,192},{192,224},{224... | collective-permute-start | bytes 393224 | tf_op jit(solution)/shard_map/ppermute | solution.py:30
  6.4 15.0 %collective-permute-start.1 = (f32[4,4,16,128]{3,2,1,0:T(8,128)S(1)}, f32[4,4,16,128]{3,2,1,0:T(8,128)S(1)}, u32[]{:S(2)}, u32[]{:S(2)}) collective-permute-start(f32[4,4,16,128]{3,2,1,0:T(8,128)S(1)} %get-tuple-element.32), channel_id=1, source_target_pairs={{0,480},{32,0},{64,32},{96,64},{128,96},{160,128},{192,160},{224,1... | collective-permute-start | bytes 393224 | tf_op jit(solution)/shard_map/ppermute | solution.py:30
  16.1 0.9 %copy-start.4 = (s32[3,8,16,128]{3,2,1,0:T(8,128)S(1)}, s32[3,8,16,128]{3,2,1,0:T(8,128)}, u32[]{:S(2)}) copy-start(s32[3,8,16,128]{3,2,1,0:T(8,128)} %offsets.1) | copy-start | bytes 589828
  17.0 0.9 %copy-start.5 = (s32[3,8,16,128]{3,2,1,0:T(8,128)S(1)}, s32[3,8,16,128]{3,2,1,0:T(8,128)}, u32[]{:S(2)}) copy-start(s32[3,8,16,128]{3,2,1,0:T(8,128)} %eighths.1) | copy-start | bytes 589828
  22.1 9.0 %collective-permute-start.2 = (f32[4,8,8,128]{3,2,1,0:T(8,128)S(1)}, f32[4,8,8,128]{3,2,1,0:T(8,128)S(1)}, u32[]{:S(2)}, u32[]{:S(2)}) collective-permute-start(f32[4,8,8,128]{3,2,1,0:T(8,128)S(1)} %get-tuple-element.33), channel_id=1, source_target_pairs={{0,8},{8,16},{16,24},{24,0},{1,9},{9,17},{17,25},{25,1},{2,10},{10... | collective-permute-start | bytes 393224 | tf_op jit(solution)/shard_map/ppermute | solution.py:30
  24.5 8.1 %collective-permute-start.3 = (f32[4,8,8,128]{3,2,1,0:T(8,128)S(1)}, f32[4,8,8,128]{3,2,1,0:T(8,128)S(1)}, u32[]{:S(2)}, u32[]{:S(2)}) collective-permute-start(f32[4,8,8,128]{3,2,1,0:T(8,128)S(1)} %get-tuple-element.34), channel_id=1, source_target_pairs={{0,24},{8,0},{16,8},{24,16},{1,25},{9,1},{17,9},{25,17},{2,26},{10... | collective-permute-start | bytes 393224 | tf_op jit(solution)/shard_map/ppermute | solution.py:30
  33.2 6.3 %collective-permute-start.4 = (f32[384,128]{1,0:T(8,128)S(1)}, f32[384,128]{1,0:T(8,128)S(1)}, u32[]{:S(2)}, u32[]{:S(2)}) collective-permute-start(f32[384,128]{1,0:T(8,128)S(1)} %get-tuple-element.36), channel_id=1, source_target_pairs={{0,1},{1,2},{2,3},{3,4},{4,5},{5,6},{6,7},{7,0},{8,9},{9,10},{10,1... | collective-permute-start | bytes 589832 | tf_op jit(solution)/shard_map/ppermute | solution.py:30
  33.3 6.3 %collective-permute-start.5 = (f32[384,128]{1,0:T(8,128)S(1)}, f32[384,128]{1,0:T(8,128)S(1)}, u32[]{:S(2)}, u32[]{:S(2)}) collective-permute-start(f32[384,128]{1,0:T(8,128)S(1)} %get-tuple-element.37), channel_id=1, source_target_pairs={{0,7},{1,0},{2,1},{3,2},{4,3},{5,4},{6,5},{7,6},{8,15},{9,8},{10,9... | collective-permute-start | bytes 589832 | tf_op jit(solution)/shard_map/ppermute | solution.py:30
  45.5 16.5 %collective-permute-start.6 = (f32[160,128]{1,0:T(8,128)S(1)}, f32[160,128]{1,0:T(8,128)S(1)}, u32[]{:S(2)}, u32[]{:S(2)}) collective-permute-start(f32[160,128]{1,0:T(8,128)S(1)} %get-tuple-element.43), channel_id=1, source_target_pairs={{0,32},{32,64},{64,96},{96,128},{128,160},{160,192},{192,224},{224... | collective-permute-start | bytes 245768 | tf_op jit(solution)/shard_map/ppermute | solution.py:30
  47.5 14.5 %collective-permute-start.7 = (f32[160,128]{1,0:T(8,128)S(1)}, f32[160,128]{1,0:T(8,128)S(1)}, u32[]{:S(2)}, u32[]{:S(2)}) collective-permute-start(f32[160,128]{1,0:T(8,128)S(1)} %get-tuple-element.44), channel_id=1, source_target_pairs={{0,480},{32,0},{64,32},{96,64},{128,96},{160,128},{192,160},{224,1... | collective-permute-start | bytes 245768 | tf_op jit(solution)/shard_map/ppermute | solution.py:30
  52.6 8.0 %collective-permute-start.8 = (f32[32,128]{1,0:T(8,128)S(1)}, f32[32,128]{1,0:T(8,128)S(1)}, u32[]{:S(2)}, u32[]{:S(2)}) collective-permute-start(f32[32,128]{1,0:T(8,128)S(1)} %get-tuple-element.45), channel_id=1, source_target_pairs={{0,64},{32,96},{64,128},{96,160},{128,192},{160,224},{192,256},{22... | collective-permute-start | bytes 49160 | tf_op jit(solution)/shard_map/ppermute | solution.py:30
  54.5 7.5 %collective-permute-start.9 = (f32[32,128]{1,0:T(8,128)S(1)}, f32[32,128]{1,0:T(8,128)S(1)}, u32[]{:S(2)}, u32[]{:S(2)}) collective-permute-start(f32[32,128]{1,0:T(8,128)S(1)} %get-tuple-element.46), channel_id=1, source_target_pairs={{0,448},{32,480},{64,0},{96,32},{128,64},{160,96},{192,128},{224,1... | collective-permute-start | bytes 49160 | tf_op jit(solution)/shard_map/ppermute | solution.py:30
  62.7 5.9 %collective-permute-start.10 = (f32[72,128]{1,0:T(8,128)S(1)}, f32[72,128]{1,0:T(8,128)S(1)}, u32[]{:S(2)}, u32[]{:S(2)}) collective-permute-start(f32[72,128]{1,0:T(8,128)S(1)} %get-tuple-element.50), channel_id=1, source_target_pairs={{0,8},{8,16},{16,24},{24,0},{1,9},{9,17},{17,25},{25,1},{2,10},{10... | collective-permute-start | bytes 110600 | tf_op jit(solution)/shard_map/ppermute | solution.py:30
  64.9 7.1 %collective-permute-start.11 = (f32[72,128]{1,0:T(8,128)S(1)}, f32[72,128]{1,0:T(8,128)S(1)}, u32[]{:S(2)}, u32[]{:S(2)}) collective-permute-start(f32[72,128]{1,0:T(8,128)S(1)} %get-tuple-element.51), channel_id=1, source_target_pairs={{0,24},{8,0},{16,8},{24,16},{1,25},{9,1},{17,9},{25,17},{2,26},{10... | collective-permute-start | bytes 110600 | tf_op jit(solution)/shard_map/ppermute | solution.py:30

commit v5 on v4

--- a/solution.py
+++ b/solution.py
@@ -9,60 +9,50 @@
 
 RELAX_WEIGHT = 6.0 / 7.0
 VMEM = pl.BlockSpec(memory_space=pltpu.VMEM)
-SMEM = pl.BlockSpec(memory_space=pltpu.SMEM)
-FAR = pl.BlockSpec(memory_space=pl.ANY)
 PARAMS = pltpu.CompilerParams(vmem_limit_bytes=48 * 1024 * 1024)
 
 
-def call(kernel, outs, scratch=(), scalars=0, inputs=0, far=0):
+def call(kernel, outs, scratch=(), inputs=0):
     return pl.pallas_call(
         kernel,
         out_shape=[jax.ShapeDtypeStruct(shape, dtype) for shape, dtype in outs],
-        in_specs=[SMEM] * scalars + [VMEM] * inputs + [FAR] * far,
+        in_specs=[VMEM] * inputs,
         out_specs=[VMEM] * len(outs),
         scratch_shapes=list(scratch),
         compiler_params=PARAMS,
     )
 
 
+def inside_grid():
+    found = []
+    for axis, step in (("gx", 1), ("gy", 1), ("gz", 1), ("gx", 2)):
+        place, count = lax.axis_index(axis), lax.axis_size(axis)
+        found.append(jnp.where(place >= step, 1.0, 0.0))
+        found.append(jnp.where(place < count - step, 1.0, 0.0))
+    return found
+
+
 def shift_ring(value, axis, step):
     count = lax.axis_size(axis)
     return lax.ppermute(value, axis, [(i, (i + step) % count) for i in range(count)])
 
 
-def pack_kernel(velocity, density, low_planes, high_planes, arrived):
-    copies = []
-    for k, (out, first) in enumerate(((low_planes, 0), (high_planes, 4))):
-        planes = pl.ds(first, 4)
-        copies.append(
-            pltpu.make_async_copy(velocity.at[:, planes], out.at[pl.ds(0, 3)], arrived.at[2 * k])
-        )
-        copies.append(pltpu.make_async_copy(density.at[planes], out.at[3], arrived.at[2 * k + 1]))
-    for copy in copies:
-        copy.start()
-    for copy in copies:
-        copy.wait()
-
-
-def own_kernel(velocity, density, offsets, eighths, fields_t, code_t, own, whole, parts, arrived):
-    copies = [
-        pltpu.make_async_copy(velocity, own.at[pl.ds(0, 3)], arrived.at[0]),
-        pltpu.make_async_copy(density, own.at[3], arrived.at[1]),
-        pltpu.make_async_copy(offsets, whole, arrived.at[2]),
-        pltpu.make_async_copy(eighths, parts, arrived.at[3]),
-    ]
-    for copy in copies:
-        copy.start()
-    for copy in copies:
-        copy.wait()
+def pack_kernel(velocity, density, low_planes, high_planes):
     for f in range(4):
-        fields_t[f] = own[f].reshape(128, 128).T
-    code = (whole[0] + 4) + (whole[1] + 4) * 8 + (whole[2] + 4) * 64
-    code = code + parts[0] * 512 + parts[1] * 4096 + parts[2] * 32768
-    code_t[...] = code.astype(jnp.float32).reshape(128, 128).T.astype(jnp.int32)
-
-
-def rows_kernel(inside, velocity, density, low, high, after, to_low, to_high):
+        field = velocity[f] if f < 3 else density[...]
+        low_planes[f] = field[0:4]
+        high_planes[f] = field[4:8]
+
+
+def own_kernel(velocity, density, code, fields_t, code_t):
+    for a in range(3):
+        fields_t[a] = velocity[a].reshape(128, 128).T
+    fields_t[3] = density[...].reshape(128, 128).T
+    code_t[...] = code[...].reshape(128, 128).T.astype(jnp.int32)
+
+
+def rows_kernel(velocity, density, low, high, after, to_low, to_high):
+    inside = inside_grid()
     for f in range(4):
         for pair in range(8):
             for half in range(2):
@@ -79,7 +69,8 @@
                 to_high[f, pair, 4 * half : 4 * half + 4] = rows[12:16]
 
 
-def planes_kernel(inside, low, high, planes_t):
+def planes_kernel(low, high, planes_t):
+    inside = inside_grid()
     for f in range(4):
         both = jnp.concatenate(
             [low[f].reshape(64, 128) * inside[0], high[f].reshape(64, 128) * inside[1]], axis=0
@@ -87,7 +78,8 @@
         planes_t[f] = both.T
 
 
-def columns_kernel(inside, fields_t, planes_t, code_t, low, high, after, rows_t, to_low, to_high):
+def columns_kernel(fields_t, planes_t, code_t, low, high, after, rows_t, to_low, to_high):
+    inside = inside_grid()
     for f in range(4):
         both = jnp.concatenate(
             [low[f].reshape(64, 128) * inside[2], high[f].reshape(64, 128) * inside[3]], axis=0
@@ -173,9 +165,10 @@
 
 
 def edges_kernel(
-    inside, code_t, sums_t, fields_t, planes_t, rows_t, low, high,
+    code_t, sums_t, fields_t, planes_t, rows_t, low, high,
     moved, density, beyond, moved_t, beyond_t, padded, codes,
 ):
+    inside = inside_grid()
     for f in range(4):
         for group, source in enumerate((fields_t, planes_t, rows_t)):
             at = 24 * (3 * f + group)
@@ -236,44 +229,38 @@
     density[...] = moved_t[3].T.reshape(8, 16, 128)
 
 
-def ends(axis):
-    place = lax.axis_index(axis)
-    return [place > 0, place < lax.axis_size(axis) - 1]
-
-
-def advect(inside, velocity, density, offsets, eighths):
+def advect(velocity, density, offsets, eighths):
     f32 = jnp.float32
     turned = ((4, 128, 128), f32)
-    arrived = pltpu.SemaphoreType.DMA((4,))
 
     def gather(group, *values):
         kernel = functools.partial(group_kernel, group)
         return call(kernel, [turned], inputs=len(values))(*values)[0]
 
     planes = ((4, 4, 16, 128), f32)
-    low_planes, high_planes = call(pack_kernel, [planes, planes], [arrived], far=2)(
+    low_planes, high_planes = call(pack_kernel, [planes, planes], inputs=2)(
         velocity, density
     )
     low = shift_ring(high_planes, "gx", 1)
     high = shift_ring(low_planes, "gx", -1)
-    whole = pltpu.VMEM((3, 8, 16, 128), jnp.int32)
-    scratch = [pltpu.VMEM((4, 8, 16, 128), f32), whole, whole, arrived]
-    fields_t, code_t = call(own_kernel, [turned, ((128, 128), jnp.int32)], scratch, far=4)(
-        velocity, density, offsets, eighths
+    code = (offsets[0] + 4) + (offsets[1] + 4) * 8 + (offsets[2] + 4) * 64
+    code = code + eighths[0] * 512 + eighths[1] * 4096 + eighths[2] * 32768
+    fields_t, code_t = call(own_kernel, [turned, ((128, 128), jnp.int32)], inputs=3)(
+        velocity, density, code.astype(f32)
     )
     sums_t = gather(0, code_t, fields_t)
     strip = ((4, 8, 8, 128), f32)
-    to_low, to_high = call(rows_kernel, [strip, strip], scalars=1, inputs=5)(
-        inside, velocity, density, low, high, sums_t
+    to_low, to_high = call(rows_kernel, [strip, strip], inputs=5)(
+        velocity, density, low, high, sums_t
     )
     rows_low = shift_ring(to_high, "gy", 1)
     rows_high = shift_ring(to_low, "gy", -1)
-    (planes_t,) = call(planes_kernel, [turned], scalars=1, inputs=2)(inside, low, high)
+    (planes_t,) = call(planes_kernel, [turned], inputs=2)(low, high)
     sums_t = gather(1, code_t, planes_t, sums_t)
     edge = ((384, 128), f32)
     rows_t, to_low, to_high = call(
-        columns_kernel, [turned, edge, edge], scalars=1, inputs=6
-    )(inside, fields_t, planes_t, code_t, rows_low, rows_high, sums_t)
+        columns_kernel, [turned, edge, edge], inputs=6
+    )(fields_t, planes_t, code_t, rows_low, rows_high, sums_t)
     columns_low = shift_ring(to_high, "gz", 1)
     columns_high = shift_ring(to_low, "gz", -1)
     sums_t = gather(2, code_t, rows_t, sums_t)
@@ -285,8 +272,8 @@
     ]
     block = ((3, 8, 16, 128), f32)
     return call(
-        edges_kernel, [block, ((8, 16, 128), f32), block], scratch, scalars=1, inputs=7
-    )(inside, code_t, sums_t, fields_t, planes_t, rows_t, columns_low, columns_high)
+        edges_kernel, [block, ((8, 16, 128), f32), block], scratch, inputs=7
+    )(code_t, sums_t, fields_t, planes_t, rows_t, columns_low, columns_high)
 
 
 def roll(value, shift, dim):
@@ -393,8 +380,9 @@
 
 
 def levels_kernel(
-    inside, moved, beyond, to_low, to_high, to_low_2, to_high_2, fine, middle, coarse, halves
+    moved, beyond, to_low, to_high, to_low_2, to_high_2, fine, middle, coarse, halves
 ):
+    inside = inside_grid()
     def spread(a):
         block = jnp.concatenate([moved[a], beyond[a]], axis=2)
         block = jnp.concatenate([block, jnp.zeros((8, 8, 256), jnp.float32)], axis=1)
@@ -449,8 +437,9 @@
 
 
 def planes_sum_kernel(
-    inside, fine, middle, coarse, low, high, low_2, high_2, to_low, to_high, fine_o, middle_o, coarse_o
+    fine, middle, coarse, low, high, low_2, high_2, to_low, to_high, fine_o, middle_o, coarse_o
 ):
+    inside = inside_grid()
     f = [fine[k] for k in range(10)]
     m = [middle[k] for k in range(6)]
     c = [coarse[k] for k in range(4)]
@@ -496,8 +485,9 @@
 
 
 def pressure_kernel(
-    inside, moved, fine, middle, coarse, low, high, velocity, pressure, halves
+    moved, fine, middle, coarse, low, high, velocity, pressure, halves
 ):
+    inside = inside_grid()
     f = [fine[k] for k in range(10)]
     m = [middle[k] for k in range(6)]
     c = [coarse[k] for k in range(4)]
@@ -561,39 +551,35 @@
         velocity[2, k] = moved[2, k] - 0.5 * slope[:, 0:128]
 
 
-def project(inside, moved, beyond):
+def project(moved, beyond):
     f32 = jnp.float32
     held = [((10, 24, 256), f32), ((6, 16, 128), f32), ((4, 16, 128), f32)]
     halves = [pltpu.VMEM((2, 8, 32, 128), f32)]
     side, side_2 = ((160, 128), f32), ((32, 128), f32)
     to_low, to_high, to_low_2, to_high_2, *sums = call(
-        levels_kernel, [side, side, side_2, side_2] + held, halves, scalars=1, inputs=2
-    )(inside, moved, beyond)
+        levels_kernel, [side, side, side_2, side_2] + held, halves, inputs=2
+    )(moved, beyond)
     low = shift_ring(to_high, "gx", 1)
     high = shift_ring(to_low, "gx", -1)
     low_2 = shift_ring(to_high_2, "gx", 2)
     high_2 = shift_ring(to_low_2, "gx", -2)
     side = ((72, 128), f32)
     to_low, to_high, *sums = call(
-        planes_sum_kernel, [side, side] + held, scalars=1, inputs=7
-    )(inside, *sums, low, high, low_2, high_2)
+        planes_sum_kernel, [side, side] + held, inputs=7
+    )(*sums, low, high, low_2, high_2)
     low = shift_ring(to_high, "gy", 1)
     high = shift_ring(to_low, "gy", -1)
     return call(
         pressure_kernel,
         [((3, 8, 16, 128), f32), ((8, 16, 128), f32)],
         halves,
-        scalars=1,
         inputs=6,
-    )(inside, moved, *sums, low, high)
+    )(moved, *sums, low, high)
 
 
 def body(velocity, density, offsets, eighths):
-    place = lax.axis_index("gx")
-    beyond = [place > 1, place < lax.axis_size("gx") - 2]
-    inside = jnp.stack(ends("gx") + ends("gy") + ends("gz") + beyond).astype(jnp.float32)
-    moved, new_density, past = advect(inside, velocity, density, offsets, eighths)
-    new_velocity, pressure = project(inside, moved, past)
+    moved, new_density, past = advect(velocity, density, offsets, eighths)
+    new_velocity, pressure = project(moved, past)
     return new_velocity, new_density, pressure
 
 

time: 74.1 us -> 68.9 us (0.930)
  Pallas kernels: 18.9 us -> 14.1 us
  local copies, waits for them, and re-layouts: 3.72 us -> 1.76 us
  other arithmetic: 0.01 us -> 0.94 us
    pallas_call x8, Pallas kernels: 9.84 us -> 5.57 us  [the longest x1 3.45 us: advect(): call(edges_kernel, [block, ((8, 16, 128), f32), block], scratch, inputs=7)]
    unnamed x12 -> x6, local copies, waits for them, and re-layouts: 3.61 us -> 1.76 us
    convert_element_type x1, other arithmetic: 0.01 us -> 0.94 us  [advect(): code.astype(f32)]
  transfers between devices with their start and end apart: 12 -> 12, of which waited for: 4 -> 4; matrix products, arithmetic and copies ran while one was open for 0% -> 1% of each run, Pallas kernels for 12% -> 11%
where the time goes in v5:
time: 68.9 us; the launch traced here: 68.4 us
  starting transfers between devices  43.1 us (63%)
  Pallas kernels  14.1 us (20%)
  waiting for transfers between devices  7.67 us (11%)
  local copies, waits for them, and re-layouts  1.76 us (3%)
  other arithmetic  0.94 us (1%)
  between operations  0.83 us (1%)
    ppermute x12, starting transfers between devices, shift_ring(): lax.ppermute(value, axis, [(i, (i + step) % count) for i in range(count)])  43.1 us
    ppermute x12, waiting for transfers between devices, shift_ring(): lax.ppermute(value, axis, [(i, (i + step) % count) for i in range(count)])  7.67 us
    pallas_call x3, Pallas kernels, gather(): return call(kernel, [turned], inputs=len(values))(*values)[0]  7.42 us
    pallas_call x1, Pallas kernels, advect(): call(edges_kernel, [block, ((8, 16, 128), f32), block], scratch, inputs=7)  3.45 us
    unnamed x6, local copies, waits for them, and re-layouts  1.76 us
    pallas_call x1, Pallas kernels, project(): call(levels_kernel, [side, side, side_2, side_2] + held, halves, inputs=2)  1.43 us
  transfers between devices with their start and end apart: 12, of which 4 were waited for; matrix products, arithmetic and copies ran while one was open for 1% of the time, Pallas kernels for 11%

profile of v5, /device:TPU:6, one launch (start us, length us, event | category | flops | bytes accessed | tf_op | source)
XLA Modules:
  0.0 68.4 jit_solution(991998447390527591)
XLA Ops:
  0.6 0.9 %copy-done = f32[3,8,16,128]{3,2,1,0:T(8,128)S(1)} copy-done((f32[3,8,16,128]{3,2,1,0:T(8,128)S(1)}, f32[3,8,16,128]{3,2,1,0:T(8,128)}, u32[]{:S(2)}) %copy-start) | copy-done | bytes 196632
  1.6 0.8 %copy-done.1 = f32[8,16,128]{2,1,0:T(8,128)S(1)} copy-done((f32[8,16,128]{2,1,0:T(8,128)S(1)}, f32[8,16,128]{2,1,0:T(8,128)}, u32[]{:S(2)}) %copy-start.1) | copy-done | bytes 65560
  2.4 4.0 %collective-permute-start = (f32[4,4,16,128]{3,2,1,0:T(8,128)S(1)}, f32[4,4,16,128]{3,2,1,0:T(8,128)S(1)}, u32[]{:S(2)}, u32[]{:S(2)}) collective-permute-start(f32[4,4,16,128]{3,2,1,0:T(8,128)S(1)} %get-tuple-element.31), channel_id=1, source_target_pairs={{0,32},{32,64},{64,96},{96,128},{128,160},{160,192},{192,224},{224... | collective-permute-start | bytes 393224 | tf_op jit(solution)/shard_map/ppermute | solution.py:37
  6.4 9.5 %collective-permute-start.1 = (f32[4,4,16,128]{3,2,1,0:T(8,128)S(1)}, f32[4,4,16,128]{3,2,1,0:T(8,128)S(1)}, u32[]{:S(2)}, u32[]{:S(2)}) collective-permute-start(f32[4,4,16,128]{3,2,1,0:T(8,128)S(1)} %get-tuple-element.32), channel_id=1, source_target_pairs={{0,480},{32,0},{64,32},{96,64},{128,96},{160,128},{192,160},{224,1... | collective-permute-start | bytes 393224 | tf_op jit(solution)/shard_map/ppermute | solution.py:37
  15.9 0.9 %convert_bitcast_fusion.code = f32[8,16,128]{2,1,0:T(8,128)S(1)} fusion(s32[3,8,16,128]{3,2,1,0:T(8,128)S(1)} %copy-done.2, s32[3,8,16,128]{3,2,1,0:T(8,128)} %param.6), kind=kLoop, calls=%fused_computation | loop fusion | flops 229376 | bytes 458752 | tf_op jit(solution)/shard_map/convert_element_type | solution.py:249
  16.8 0.2 shard_map.67
  17.0 2.5 %shard_map.70.after.refs_0_ = f32[4,128,128]{2,1,0:T(8,128)S(1)} custom-call(s32[128,128]{1,0:T(8,128)S(1)} %get-tuple-element.29.code_t, f32[4,128,128]{2,1,0:T(8,128)S(1)} %get-tuple-element.30.source_t.fields_t), custom_call_target="tpu_custom_call" | custom-call | tf_op jit(solution)/shard_map/pallas_call | solution.py:238
  19.5 0.0 collective-permute-done.low
  19.5 0.0 collective-permute-done.1.high
  19.6 2.4 %collective-permute-start.2 = (f32[4,8,8,128]{3,2,1,0:T(8,128)S(1)}, f32[4,8,8,128]{3,2,1,0:T(8,128)S(1)}, u32[]{:S(2)}, u32[]{:S(2)}) collective-permute-start(f32[4,8,8,128]{3,2,1,0:T(8,128)S(1)} %get-tuple-element.33), channel_id=1, source_target_pairs={{0,8},{8,16},{16,24},{24,0},{1,9},{9,17},{17,25},{25,1},{2,10},{10... | collective-permute-start | bytes 393224 | tf_op jit(solution)/shard_map/ppermute | solution.py:37
  22.0 3.5 %collective-permute-start.3 = (f32[4,8,8,128]{3,2,1,0:T(8,128)S(1)}, f32[4,8,8,128]{3,2,1,0:T(8,128)S(1)}, u32[]{:S(2)}, u32[]{:S(2)}) collective-permute-start(f32[4,8,8,128]{3,2,1,0:T(8,128)S(1)} %get-tuple-element.34), channel_id=1, source_target_pairs={{0,24},{8,0},{16,8},{24,16},{1,25},{9,1},{17,9},{25,17},{2,26},{10... | collective-permute-start | bytes 393224 | tf_op jit(solution)/shard_map/ppermute | solution.py:37
  25.4 0.1 shard_map.69.source_t.planes_t
  25.6 2.5 %shard_map.72.after.refs_0_ = f32[4,128,128]{2,1,0:T(8,128)S(1)} custom-call(s32[128,128]{1,0:T(8,128)S(1)} %get-tuple-element.29.code_t, f32[4,128,128]{2,1,0:T(8,128)S(1)} %shard_map.69.source_t.planes_t, f32[4,128,128]{2,1,0:T(8,128)S(1)} %shard_map.70.after.refs_0_), custom_call_target="tpu_custom_call" | custom-call | tf_op jit(solution)/shard_map/pallas_call | solution.py:238
  28.0 0.0 collective-permute-done.2.low
  28.1 2.0 %collective-permute-done.3.high = f32[4,8,8,128]{3,2,1,0:T(8,128)S(1)} collective-permute-done((f32[4,8,8,128]{3,2,1,0:T(8,128)S(1)}, f32[4,8,8,128]{3,2,1,0:T(8,128)S(1)}, u32[]{:S(2)}, u32[]{:S(2)}) %collective-permute-start.3) | collective-permute-done | bytes 131104 | tf_op jit(solution)/shard_map/ppermute | solution.py:37
  30.0 0.1 shard_map.73
  30.2 0.0 collective-permute-start.4
  30.2 2.9 %collective-permute-start.5 = (f32[384,128]{1,0:T(8,128)S(1)}, f32[384,128]{1,0:T(8,128)S(1)}, u32[]{:S(2)}, u32[]{:S(2)}) collective-permute-start(f32[384,128]{1,0:T(8,128)S(1)} %get-tuple-element.37), channel_id=1, source_target_pairs={{0,7},{1,0},{2,1},{3,2},{4,3},{5,4},{6,5},{7,6},{8,15},{9,8},{10,9... | collective-permute-start | bytes 589832 | tf_op jit(solution)/shard_map/ppermute | solution.py:37
  33.1 2.5 %shard_map.74.sums_t = f32[4,128,128]{2,1,0:T(8,128)S(1)} custom-call(s32[128,128]{1,0:T(8,128)S(1)} %get-tuple-element.29.code_t, f32[4,128,128]{2,1,0:T(8,128)S(1)} %get-tuple-element.35.source_t.rows_t, f32[4,128,128]{2,1,0:T(8,128)S(1)} %shard_map.72.after.refs_0_), custom_call_target="tpu_custom_call" | custom-call | tf_op jit(solution)/shard_map/pallas_call | solution.py:238
  35.6 0.9 %collective-permute-done.4.low = f32[384,128]{1,0:T(8,128)S(1)} collective-permute-done((f32[384,128]{1,0:T(8,128)S(1)}, f32[384,128]{1,0:T(8,128)S(1)}, u32[]{:S(2)}, u32[]{:S(2)}) %collective-permute-start.4) | collective-permute-done | bytes 196640 | tf_op jit(solution)/shard_map/ppermute | solution.py:37
  36.5 3.5 %shard_map.75 = (f32[3,8,16,128]{3,2,1,0:T(8,128)S(1)}, f32[8,16,128]{2,1,0:T(8,128)}, f32[3,8,16,128]{3,2,1,0:T(8,128)S(1)}) custom-call(s32[128,128]{1,0:T(8,128)S(1)} %get-tuple-element.29.code_t, f32[4,128,128]{2,1,0:T(8,128)S(1)} %shard_map.74.sums_t, f32[4,128,128]{2,1,0:T(8,128)S(1)} %get-tuple-element.30.source_t.fields_t, ...), custom_call_target="tpu_custom_call" | custom-call | tf_op jit(solution)/shard_map/pallas_call | solution.py:274
  39.9 1.4 %shard_map.76 = (f32[160,128]{1,0:T(8,128)S(1)}, f32[160,128]{1,0:T(8,128)S(1)}, f32[32,128]{1,0:T(8,128)S(1)}, f32[32,128]{1,0:T(8,128)S(1)}, f32[10,24,256]{2,...) custom-call(f32[3,8,16,128]{3,2,1,0:T(8,128)S(1)} %get-tuple-element.38.moved, ...), custom_call_target="tpu_custom_call" | custom-call | tf_op jit(solution)/shard_map/pallas_call | solution.py:559
  41.4 1.9 %collective-permute-start.6 = (f32[160,128]{1,0:T(8,128)S(1)}, f32[160,128]{1,0:T(8,128)S(1)}, u32[]{:S(2)}, u32[]{:S(2)}) collective-permute-start(f32[160,128]{1,0:T(8,128)S(1)} %get-tuple-element.43), channel_id=1, source_target_pairs={{0,32},{32,64},{64,96},{96,128},{128,160},{160,192},{192,224},{224... | collective-permute-start | bytes 245768 | tf_op jit(solution)/shard_map/ppermute | solution.py:37
  43.3 5.1 %collective-permute-start.7 = (f32[160,128]{1,0:T(8,128)S(1)}, f32[160,128]{1,0:T(8,128)S(1)}, u32[]{:S(2)}, u32[]{:S(2)}) collective-permute-start(f32[160,128]{1,0:T(8,128)S(1)} %get-tuple-element.44), channel_id=1, source_target_pairs={{0,480},{32,0},{64,32},{96,64},{128,96},{160,128},{192,160},{224,1... | collective-permute-start | bytes 245768 | tf_op jit(solution)/shard_map/ppermute | solution.py:37
  48.4 1.9 %collective-permute-start.8 = (f32[32,128]{1,0:T(8,128)S(1)}, f32[32,128]{1,0:T(8,128)S(1)}, u32[]{:S(2)}, u32[]{:S(2)}) collective-permute-start(f32[32,128]{1,0:T(8,128)S(1)} %get-tuple-element.45), channel_id=1, source_target_pairs={{0,64},{32,96},{64,128},{96,160},{128,192},{160,224},{192,256},{22... | collective-permute-start | bytes 49160 | tf_op jit(solution)/shard_map/ppermute | solution.py:37
  50.4 6.0 %collective-permute-start.9 = (f32[32,128]{1,0:T(8,128)S(1)}, f32[32,128]{1,0:T(8,128)S(1)}, u32[]{:S(2)}, u32[]{:S(2)}) collective-permute-start(f32[32,128]{1,0:T(8,128)S(1)} %get-tuple-element.46), channel_id=1, source_target_pairs={{0,448},{32,480},{64,0},{96,32},{128,64},{160,96},{192,128},{224,1... | collective-permute-start | bytes 49160 | tf_op jit(solution)/shard_map/ppermute | solution.py:37
  56.4 1.4 %collective-permute-done.9.high_2 = f32[32,128]{1,0:T(8,128)S(1)} collective-permute-done((f32[32,128]{1,0:T(8,128)S(1)}, f32[32,128]{1,0:T(8,128)S(1)}, u32[]{:S(2)}, u32[]{:S(2)}) %collective-permute-start.9) | collective-permute-done | bytes 16416 | tf_op jit(solution)/shard_map/ppermute | solution.py:37
  57.8 0.2 shard_map.77
  58.0 2.2 %collective-permute-start.10 = (f32[72,128]{1,0:T(8,128)S(1)}, f32[72,128]{1,0:T(8,128)S(1)}, u32[]{:S(2)}, u32[]{:S(2)}) collective-permute-start(f32[72,128]{1,0:T(8,128)S(1)} %get-tuple-element.50), channel_id=1, source_target_pairs={{0,8},{8,16},{16,24},{24,0},{1,9},{9,17},{17,25},{25,1},{2,10},{10... | collective-permute-start | bytes 110600 | tf_op jit(solution)/shard_map/ppermute | solution.py:37
  60.2 3.7 %collective-permute-start.11 = (f32[72,128]{1,0:T(8,128)S(1)}, f32[72,128]{1,0:T(8,128)S(1)}, u32[]{:S(2)}, u32[]{:S(2)}) collective-permute-start(f32[72,128]{1,0:T(8,128)S(1)} %get-tuple-element.51), channel_id=1, source_target_pairs={{0,24},{8,0},{16,8},{24,16},{1,25},{9,1},{17,9},{25,17},{2,26},{10... | collective-permute-start | bytes 110600 | tf_op jit(solution)/shard_map/ppermute | solution.py:37
  63.9 3.4 %collective-permute-done.11.high = f32[72,128]{1,0:T(8,128)S(1)} collective-permute-done((f32[72,128]{1,0:T(8,128)S(1)}, f32[72,128]{1,0:T(8,128)S(1)}, u32[]{:S(2)}, u32[]{:S(2)}) %collective-permute-start.11) | collective-permute-done | bytes 36896 | tf_op jit(solution)/shard_map/ppermute | solution.py:37
  67.3 1.1 %shard_map.78 = (f32[3,8,16,128]{3,2,1,0:T(8,128)}, f32[8,16,128]{2,1,0:T(8,128)}) custom-call(f32[3,8,16,128]{3,2,1,0:T(8,128)S(1)} %get-tuple-element.38.moved, f32[10,24,256]{2,1,0:T(8,128)S(1)} %get-tuple-element.47.fine, f32[6,16,128]{2,1,0:T(8,128)S(1)} %get-tuple-element.48.middle, f32[4,16,128]{2,1,0:T(8,128)S(1)} %get-tuple-element.49.coarse, ...), custom_call_target="tpu_custom_call" | custom-call | tf_op jit(solution)/shard_map/pallas_call | solution.py:572
  (11 shorter events, 0.1 us)
Async XLA Ops:
  0.6 0.9 %copy-start = (f32[3,8,16,128]{3,2,1,0:T(8,128)S(1)}, f32[3,8,16,128]{3,2,1,0:T(8,128)}, u32[]{:S(2)}) copy-start(f32[3,8,16,128]{3,2,1,0:T(8,128)} %velocity.5) | copy-start | bytes 589828
  1.6 0.8 %copy-start.1 = (f32[8,16,128]{2,1,0:T(8,128)S(1)}, f32[8,16,128]{2,1,0:T(8,128)}, u32[]{:S(2)}) copy-start(f32[8,16,128]{2,1,0:T(8,128)} %density.5) | copy-start | bytes 196612
  2.4 13.5 %copy-start.2 = (s32[3,8,16,128]{3,2,1,0:T(8,128)S(1)}, s32[3,8,16,128]{3,2,1,0:T(8,128)}, u32[]{:S(2)}) copy-start(s32[3,8,16,128]{3,2,1,0:T(8,128)} %param.7) | copy-start | bytes 589828
  2.4 17.1 %collective-permute-start = (f32[4,4,16,128]{3,2,1,0:T(8,128)S(1)}, f32[4,4,16,128]{3,2,1,0:T(8,128)S(1)}, u32[]{:S(2)}, u32[]{:S(2)}) collective-permute-start(f32[4,4,16,128]{3,2,1,0:T(8,128)S(1)} %get-tuple-element.31), channel_id=1, source_target_pairs={{0,32},{32,64},{64,96},{96,128},{128,160},{160,192},{192,224},{224... | collective-permute-start | bytes 393224 | tf_op jit(solution)/shard_map/ppermute | solution.py:37
  6.4 13.1 %collective-permute-start.1 = (f32[4,4,16,128]{3,2,1,0:T(8,128)S(1)}, f32[4,4,16,128]{3,2,1,0:T(8,128)S(1)}, u32[]{:S(2)}, u32[]{:S(2)}) collective-permute-start(f32[4,4,16,128]{3,2,1,0:T(8,128)S(1)} %get-tuple-element.32), channel_id=1, source_target_pairs={{0,480},{32,0},{64,32},{96,64},{128,96},{160,128},{192,160},{224,1... | collective-permute-start | bytes 393224 | tf_op jit(solution)/shard_map/ppermute | solution.py:37
  19.6 8.5 %collective-permute-start.2 = (f32[4,8,8,128]{3,2,1,0:T(8,128)S(1)}, f32[4,8,8,128]{3,2,1,0:T(8,128)S(1)}, u32[]{:S(2)}, u32[]{:S(2)}) collective-permute-start(f32[4,8,8,128]{3,2,1,0:T(8,128)S(1)} %get-tuple-element.33), channel_id=1, source_target_pairs={{0,8},{8,16},{16,24},{24,0},{1,9},{9,17},{17,25},{25,1},{2,10},{10... | collective-permute-start | bytes 393224 | tf_op jit(solution)/shard_map/ppermute | solution.py:37
  22.0 8.1 %collective-permute-start.3 = (f32[4,8,8,128]{3,2,1,0:T(8,128)S(1)}, f32[4,8,8,128]{3,2,1,0:T(8,128)S(1)}, u32[]{:S(2)}, u32[]{:S(2)}) collective-permute-start(f32[4,8,8,128]{3,2,1,0:T(8,128)S(1)} %get-tuple-element.34), channel_id=1, source_target_pairs={{0,24},{8,0},{16,8},{24,16},{1,25},{9,1},{17,9},{25,17},{2,26},{10... | collective-permute-start | bytes 393224 | tf_op jit(solution)/shard_map/ppermute | solution.py:37
  30.2 6.3 %collective-permute-start.4 = (f32[384,128]{1,0:T(8,128)S(1)}, f32[384,128]{1,0:T(8,128)S(1)}, u32[]{:S(2)}, u32[]{:S(2)}) collective-permute-start(f32[384,128]{1,0:T(8,128)S(1)} %get-tuple-element.36), channel_id=1, source_target_pairs={{0,1},{1,2},{2,3},{3,4},{4,5},{5,6},{6,7},{7,0},{8,9},{9,10},{10,1... | collective-permute-start | bytes 589832 | tf_op jit(solution)/shard_map/ppermute | solution.py:37
  30.2 6.3 %collective-permute-start.5 = (f32[384,128]{1,0:T(8,128)S(1)}, f32[384,128]{1,0:T(8,128)S(1)}, u32[]{:S(2)}, u32[]{:S(2)}) collective-permute-start(f32[384,128]{1,0:T(8,128)S(1)} %get-tuple-element.37), channel_id=1, source_target_pairs={{0,7},{1,0},{2,1},{3,2},{4,3},{5,4},{6,5},{7,6},{8,15},{9,8},{10,9... | collective-permute-start | bytes 589832 | tf_op jit(solution)/shard_map/ppermute | solution.py:37
  41.4 16.5 %collective-permute-start.6 = (f32[160,128]{1,0:T(8,128)S(1)}, f32[160,128]{1,0:T(8,128)S(1)}, u32[]{:S(2)}, u32[]{:S(2)}) collective-permute-start(f32[160,128]{1,0:T(8,128)S(1)} %get-tuple-element.43), channel_id=1, source_target_pairs={{0,32},{32,64},{64,96},{96,128},{128,160},{160,192},{192,224},{224... | collective-permute-start | bytes 245768 | tf_op jit(solution)/shard_map/ppermute | solution.py:37
  43.3 14.5 %collective-permute-start.7 = (f32[160,128]{1,0:T(8,128)S(1)}, f32[160,128]{1,0:T(8,128)S(1)}, u32[]{:S(2)}, u32[]{:S(2)}) collective-permute-start(f32[160,128]{1,0:T(8,128)S(1)} %get-tuple-element.44), channel_id=1, source_target_pairs={{0,480},{32,0},{64,32},{96,64},{128,96},{160,128},{192,160},{224,1... | collective-permute-start | bytes 245768 | tf_op jit(solution)/shard_map/ppermute | solution.py:37
  48.4 8.0 %collective-permute-start.8 = (f32[32,128]{1,0:T(8,128)S(1)}, f32[32,128]{1,0:T(8,128)S(1)}, u32[]{:S(2)}, u32[]{:S(2)}) collective-permute-start(f32[32,128]{1,0:T(8,128)S(1)} %get-tuple-element.45), channel_id=1, source_target_pairs={{0,64},{32,96},{64,128},{96,160},{128,192},{160,224},{192,256},{22... | collective-permute-start | bytes 49160 | tf_op jit(solution)/shard_map/ppermute | solution.py:37
  50.4 7.5 %collective-permute-start.9 = (f32[32,128]{1,0:T(8,128)S(1)}, f32[32,128]{1,0:T(8,128)S(1)}, u32[]{:S(2)}, u32[]{:S(2)}) collective-permute-start(f32[32,128]{1,0:T(8,128)S(1)} %get-tuple-element.46), channel_id=1, source_target_pairs={{0,448},{32,480},{64,0},{96,32},{128,64},{160,96},{192,128},{224,1... | collective-permute-start | bytes 49160 | tf_op jit(solution)/shard_map/ppermute | solution.py:37
  58.0 5.9 %collective-permute-start.10 = (f32[72,128]{1,0:T(8,128)S(1)}, f32[72,128]{1,0:T(8,128)S(1)}, u32[]{:S(2)}, u32[]{:S(2)}) collective-permute-start(f32[72,128]{1,0:T(8,128)S(1)} %get-tuple-element.50), channel_id=1, source_target_pairs={{0,8},{8,16},{16,24},{24,0},{1,9},{9,17},{17,25},{25,1},{2,10},{10... | collective-permute-start | bytes 110600 | tf_op jit(solution)/shard_map/ppermute | solution.py:37
  60.2 7.1 %collective-permute-start.11 = (f32[72,128]{1,0:T(8,128)S(1)}, f32[72,128]{1,0:T(8,128)S(1)}, u32[]{:S(2)}, u32[]{:S(2)}) collective-permute-start(f32[72,128]{1,0:T(8,128)S(1)} %get-tuple-element.51), channel_id=1, source_target_pairs={{0,24},{8,0},{16,8},{24,16},{1,25},{9,1},{17,9},{25,17},{2,26},{10... | collective-permute-start | bytes 110600 | tf_op jit(solution)/shard_map/ppermute | solution.py:37

commit v6 on v5

--- a/solution.py
+++ b/solution.py
@@ -37,21 +37,18 @@
     return lax.ppermute(value, axis, [(i, (i + step) % count) for i in range(count)])
 
 
-def pack_kernel(velocity, density, low_planes, high_planes):
+def pack_kernel(fields, low_planes, high_planes):
+    low_planes[...] = fields[:, 0:4]
+    high_planes[...] = fields[:, 4:8]
+
+
+def own_kernel(fields, code, fields_t, code_t):
     for f in range(4):
-        field = velocity[f] if f < 3 else density[...]
-        low_planes[f] = field[0:4]
-        high_planes[f] = field[4:8]
-
-
-def own_kernel(velocity, density, code, fields_t, code_t):
-    for a in range(3):
-        fields_t[a] = velocity[a].reshape(128, 128).T
-    fields_t[3] = density[...].reshape(128, 128).T
+        fields_t[f] = fields[f].reshape(128, 128).T
     code_t[...] = code[...].reshape(128, 128).T.astype(jnp.int32)
 
 
-def rows_kernel(velocity, density, low, high, after, to_low, to_high):
+def rows_kernel(fields, low, high, after, to_low, to_high):
     inside = inside_grid()
     for f in range(4):
         for pair in range(8):
@@ -61,10 +58,8 @@
                     rows = low[f, plane] * inside[0]
                 elif plane >= 12:
                     rows = high[f, plane - 12] * inside[1]
-                elif f < 3:
-                    rows = velocity[f, plane - 4]
                 else:
-                    rows = density[plane - 4]
+                    rows = fields[f, plane - 4]
                 to_low[f, pair, 4 * half : 4 * half + 4] = rows[0:4]
                 to_high[f, pair, 4 * half : 4 * half + 4] = rows[12:16]
 
@@ -164,11 +159,36 @@
     lax.fori_loop(1, 15, tile, 0, unroll=7)
 
 
+def ends_kernel(code_t, rows_t, before, fields_t, planes_t, after, padded):
+    group_kernel(2, code_t, rows_t, before, after)
+    none = jnp.zeros((8, 128), jnp.float32)
+    for f in range(4):
+        for group, source in enumerate((fields_t, planes_t, rows_t)):
+            padded[0, f, group, 0:8] = none
+            padded[0, f, group, 8:24] = source[f, 0:16]
+            padded[1, f, group, 0:16] = source[f, 112:128]
+            padded[1, f, group, 16:24] = none
+    for end, start in ((0, 0), (1, 120)):
+        code = code_t[start : start + 8]
+        by_shift = weights_z(code, range(9))
+        sums = [none] * 4
+        for at, weights in corners_of(code):
+            for group in range(3):
+                parts = gathered(
+                    at, by_shift, lambda f, dz: padded[end, f, group, 4 + dz : 12 + dz]
+                )
+                for f in range(4):
+                    sums[f] = sums[f] + weights[group] * parts[f]
+        for f in range(4):
+            after[f, start : start + 8] = sums[f]
+
+
 def edges_kernel(
     code_t, sums_t, fields_t, planes_t, rows_t, low, high,
-    moved, density, beyond, moved_t, beyond_t, padded, codes,
+    moved, density, beyond, moved_t, beyond_t, padded, codes, only_past,
 ):
     inside = inside_grid()
+    none = jnp.zeros((8, 128), jnp.float32)
     for f in range(4):
         for group, source in enumerate((fields_t, planes_t, rows_t)):
             at = 24 * (3 * f + group)
@@ -176,21 +196,20 @@
             padded[0, f, group, 24:40] = source[f, 0:16]
             padded[1, f, group, 0:16] = source[f, 112:128]
             padded[1, f, group, 16:40] = high[at : at + 24] * inside[5]
+            only_past[0, f, group, 0:8] = low[at + 16 : at + 24] * inside[4]
+            only_past[0, f, group, 8:16] = none
+            only_past[1, f, group, 0:8] = none
+            only_past[1, f, group, 8:16] = high[at : at + 8] * inside[5]
     for end, got in ((0, low), (1, high)):
         code = jnp.zeros((16, 128), jnp.int32)
         for k in range(6):
             code = code + (got[288 + 16 * k : 304 + 16 * k].astype(jnp.int32) << (3 * k))
-        if end == 0:
-            codes[0, 0:16] = code
-            codes[0, 16:24] = code_t[0:8]
-        else:
-            codes[1, 0:8] = code_t[120:128]
-            codes[1, 8:24] = code
+        codes[end] = code
     for f in range(4):
         moved_t[f] = sums_t[f]
 
-    def moved_tile(end, start, count):
-        code = codes[end, pl.ds(start, 8), :]
+    def moved_tile(end, half, start, count):
+        code = codes[end, pl.ds(pl.multiple_of(8 * half, 8), 8), :]
         by_shift = weights_z(code, range(9))
         sums = [jnp.zeros((8, 128), jnp.float32)] * count
         for at, weights in corners_of(code):
@@ -205,21 +224,28 @@
                     sums[f] = sums[f] + weights[group] * parts[f]
         return sums
 
-    def inner(end, carry):
-        sums = moved_tile(end, pl.multiple_of(16 * (1 - end), 8), 4)
+    for end, start, first, shifts in ((0, 0, 4, range(0, 4)), (1, 120, 1, range(5, 9))):
+        code = code_t[start : start + 8]
+        by_shift = weights_z(code, shifts)
+        sums = [sums_t[f, start : start + 8] for f in range(4)]
+        for at, weights in corners_of(code):
+            for group in range(3):
+                parts = gathered(
+                    at, by_shift, lambda f, k: only_past[end, f, group, first + k : first + k + 8]
+                )
+                for f in range(4):
+                    sums[f] = sums[f] + weights[group] * parts[f]
         for f in range(4):
-            moved_t[f, pl.ds(pl.multiple_of(120 * end, 8), 8), :] = sums[f]
-        return carry
+            moved_t[f, start : start + 8] = sums[f]
 
     def outer(step, carry):
         end, half = step // 2, step % 2
-        sums = moved_tile(end, pl.multiple_of(8 * (end + half), 8), 3)
+        sums = moved_tile(end, half, pl.multiple_of(8 * (end + half), 8), 3)
         flag = jnp.where(end == 0, inside[4], inside[5])
         for f in range(3):
             beyond_t[f, pl.ds(pl.multiple_of(112 * (1 - end) + 8 * half, 8), 8), :] = sums[f] * flag
         return carry
 
-    lax.fori_loop(0, 2, inner, 0, unroll=2)
     for f in range(3):
         beyond_t[f] = jnp.zeros((128, 128), jnp.float32)
     lax.fori_loop(0, 4, outer, 0, unroll=2)
@@ -238,21 +264,18 @@
         return call(kernel, [turned], inputs=len(values))(*values)[0]
 
     planes = ((4, 4, 16, 128), f32)
-    low_planes, high_planes = call(pack_kernel, [planes, planes], inputs=2)(
-        velocity, density
-    )
+    fields = jnp.concatenate([velocity, density[None]], axis=0)
+    low_planes, high_planes = call(pack_kernel, [planes, planes], inputs=1)(fields)
     low = shift_ring(high_planes, "gx", 1)
     high = shift_ring(low_planes, "gx", -1)
     code = (offsets[0] + 4) + (offsets[1] + 4) * 8 + (offsets[2] + 4) * 64
     code = code + eighths[0] * 512 + eighths[1] * 4096 + eighths[2] * 32768
-    fields_t, code_t = call(own_kernel, [turned, ((128, 128), jnp.int32)], inputs=3)(
-        velocity, density, code.astype(f32)
+    fields_t, code_t = call(own_kernel, [turned, ((128, 128), jnp.int32)], inputs=2)(
+        fields, code.astype(f32)
     )
     sums_t = gather(0, code_t, fields_t)
     strip = ((4, 8, 8, 128), f32)
-    to_low, to_high = call(rows_kernel, [strip, strip], inputs=5)(
-        velocity, density, low, high, sums_t
-    )
+    to_low, to_high = call(rows_kernel, [strip, strip], inputs=4)(fields, low, high, sums_t)
     rows_low = shift_ring(to_high, "gy", 1)
     rows_high = shift_ring(to_low, "gy", -1)
     (planes_t,) = call(planes_kernel, [turned], inputs=2)(low, high)
@@ -263,12 +286,16 @@
     )(fields_t, planes_t, code_t, rows_low, rows_high, sums_t)
     columns_low = shift_ring(to_high, "gz", 1)
     columns_high = shift_ring(to_low, "gz", -1)
-    sums_t = gather(2, code_t, rows_t, sums_t)
+    scratch = [pltpu.VMEM((2, 4, 3, 24, 128), f32)]
+    (sums_t,) = call(ends_kernel, [turned], scratch, inputs=5)(
+        code_t, rows_t, sums_t, fields_t, planes_t
+    )
     scratch = [
         pltpu.VMEM((4, 128, 128), f32),
         pltpu.VMEM((3, 128, 128), f32),
         pltpu.VMEM((2, 4, 3, 40, 128), f32),
-        pltpu.VMEM((2, 24, 128), jnp.int32),
+        pltpu.VMEM((2, 16, 128), jnp.int32),
+        pltpu.VMEM((2, 4, 3, 16, 128), f32),
     ]
     block = ((3, 8, 16, 128), f32)
     return call(

time: 68.9 us -> 67.3 us (0.977)
  local copies, waits for them, and re-layouts: 1.76 us -> 0.01 us
  waiting for transfers between devices: 7.67 us -> 6.82 us
    pallas_call x3 -> x4, Pallas kernels: 0.22 us -> 3.71 us  [the longest x1 3.49 us: advect(): call(ends_kernel, [turned], scratch, inputs=5)]
    pallas_call x3 -> x2, Pallas kernels: 7.42 us -> 4.95 us  [gather(): return call(kernel, [turned], inputs=len(values))(*values)[0]]
    unnamed x6 -> x4, local copies, waits for them, and re-layouts: 1.76 us -> 0.01 us
    concatenate x0 -> x1, other arithmetic: none -> 1.02 us  [advect(): fields = jnp.concatenate([velocity, density[None]], axis=0)]
    convert_element_type x1, other arithmetic: 0.94 us -> 0.04 us  [advect(): code.astype(f32)]
    ppermute x12, waiting for transfers between devices: 7.67 us -> 6.82 us  [shift_ring(): lax.ppermute(value, axis, [(i, (i + step) % count) for i in range(count)])]
  transfers between devices with their start and end apart: 12 -> 12, of which waited for: 4 -> 3; matrix products, arithmetic and copies ran while one was open for 1% -> 0% of each run, Pallas kernels for 11% -> 13%
where the time goes in v6:
time: 67.3 us; the launch traced here: 66.9 us
  starting transfers between devices  43.6 us (65%)
  Pallas kernels  14.6 us (22%)
  waiting for transfers between devices  6.82 us (10%)
  other arithmetic  1.06 us (2%)
  between operations  0.86 us (1%)
    ppermute x12, starting transfers between devices, shift_ring(): lax.ppermute(value, axis, [(i, (i + step) % count) for i in range(count)])  43.6 us
    ppermute x12, waiting for transfers between devices, shift_ring(): lax.ppermute(value, axis, [(i, (i + step) % count) for i in range(count)])  6.82 us
    pallas_call x2, Pallas kernels, gather(): return call(kernel, [turned], inputs=len(values))(*values)[0]  4.95 us
    pallas_call x1, Pallas kernels, advect(): call(ends_kernel, [turned], scratch, inputs=5)  3.49 us
    pallas_call x1, Pallas kernels, advect(): call(edges_kernel, [block, ((8, 16, 128), f32), block], scratch, inputs=7)  2.95 us
    pallas_call x1, Pallas kernels, project(): call(levels_kernel, [side, side, side_2, side_2] + held, halves, inputs=2)  1.43 us
  transfers between devices with their start and end apart: 12, of which 3 were waited for; matrix products, arithmetic and copies ran while one was open for 0% of the time, Pallas kernels for 13%

profile of v6, /device:TPU:6, one launch (start us, length us, event | category | flops | bytes accessed | tf_op | source)
XLA Modules:
  0.0 66.9 jit_solution(3876514075602813819)
XLA Ops:
  0.6 1.0 %pad_maximum_fusion.fields = f32[4,8,16,128]{3,2,1,0:T(8,128)S(1)} fusion(f32[1,8,16,128]{3,2,1,0:T(8,128)} %bitcast.3, f32[3,8,16,128]{3,2,1,0:T(8,128)} %param.4), kind=kLoop, calls=%fused_computation | loop fusion | flops 65536 | bytes 524288 | tf_op jit(solution)/shard_map/concatenate | solution.py:267
  1.7 0.0 copy-start
  1.7 4.0 %collective-permute-start = (f32[4,4,16,128]{3,2,1,0:T(8,128)S(1)}, f32[4,4,16,128]{3,2,1,0:T(8,128)S(1)}, u32[]{:S(2)}, u32[]{:S(2)}) collective-permute-start(f32[4,4,16,128]{3,2,1,0:T(8,128)S(1)} %get-tuple-element.31), channel_id=1, source_target_pairs={{0,32},{32,64},{64,96},{96,128},{128,160},{160,192},{192,224},{224... | collective-permute-start | bytes 393224 | tf_op jit(solution)/shard_map/ppermute | solution.py:37
  5.7 9.5 %collective-permute-start.1 = (f32[4,4,16,128]{3,2,1,0:T(8,128)S(1)}, f32[4,4,16,128]{3,2,1,0:T(8,128)S(1)}, u32[]{:S(2)}, u32[]{:S(2)}) collective-permute-start(f32[4,4,16,128]{3,2,1,0:T(8,128)S(1)} %get-tuple-element.32), channel_id=1, source_target_pairs={{0,480},{32,0},{64,32},{96,64},{128,96},{160,128},{192,160},{224,1... | collective-permute-start | bytes 393224 | tf_op jit(solution)/shard_map/ppermute | solution.py:37
  15.2 0.2 shard_map.67
  15.4 2.5 %shard_map.70.after.refs_0_ = f32[4,128,128]{2,1,0:T(8,128)S(1)} custom-call(s32[128,128]{1,0:T(8,128)S(1)} %get-tuple-element.29.code_t, f32[4,128,128]{2,1,0:T(8,128)S(1)} %get-tuple-element.30.source_t.fields_t), custom_call_target="tpu_custom_call" | custom-call | tf_op jit(solution)/shard_map/pallas_call | solution.py:264
  17.9 0.0 collective-permute-done.low
  17.9 0.0 collective-permute-done.1.high
  17.9 2.4 %collective-permute-start.2 = (f32[4,8,8,128]{3,2,1,0:T(8,128)S(1)}, f32[4,8,8,128]{3,2,1,0:T(8,128)S(1)}, u32[]{:S(2)}, u32[]{:S(2)}) collective-permute-start(f32[4,8,8,128]{3,2,1,0:T(8,128)S(1)} %get-tuple-element.33), channel_id=1, source_target_pairs={{0,8},{8,16},{16,24},{24,0},{1,9},{9,17},{17,25},{25,1},{2,10},{10... | collective-permute-start | bytes 393224 | tf_op jit(solution)/shard_map/ppermute | solution.py:37
  20.3 3.5 %collective-permute-start.3 = (f32[4,8,8,128]{3,2,1,0:T(8,128)S(1)}, f32[4,8,8,128]{3,2,1,0:T(8,128)S(1)}, u32[]{:S(2)}, u32[]{:S(2)}) collective-permute-start(f32[4,8,8,128]{3,2,1,0:T(8,128)S(1)} %get-tuple-element.34), channel_id=1, source_target_pairs={{0,24},{8,0},{16,8},{24,16},{1,25},{9,1},{17,9},{25,17},{2,26},{10... | collective-permute-start | bytes 393224 | tf_op jit(solution)/shard_map/ppermute | solution.py:37
  23.8 0.1 shard_map.69.source_t.planes_t
  23.9 2.5 %shard_map.72.after.before = f32[4,128,128]{2,1,0:T(8,128)S(1)} custom-call(s32[128,128]{1,0:T(8,128)S(1)} %get-tuple-element.29.code_t, f32[4,128,128]{2,1,0:T(8,128)S(1)} %shard_map.69.source_t.planes_t, f32[4,128,128]{2,1,0:T(8,128)S(1)} %shard_map.70.after.refs_0_), custom_call_target="tpu_custom_call" | custom-call | tf_op jit(solution)/shard_map/pallas_call | solution.py:264
  26.4 0.0 collective-permute-done.2.low
  26.4 2.0 %collective-permute-done.3.high = f32[4,8,8,128]{3,2,1,0:T(8,128)S(1)} collective-permute-done((f32[4,8,8,128]{3,2,1,0:T(8,128)S(1)}, f32[4,8,8,128]{3,2,1,0:T(8,128)S(1)}, u32[]{:S(2)}, u32[]{:S(2)}) %collective-permute-start.3) | collective-permute-done | bytes 131104 | tf_op jit(solution)/shard_map/ppermute | solution.py:37
  28.4 0.1 shard_map.73
  28.6 0.0 collective-permute-start.4
  28.6 2.9 %collective-permute-start.5 = (f32[384,128]{1,0:T(8,128)S(1)}, f32[384,128]{1,0:T(8,128)S(1)}, u32[]{:S(2)}, u32[]{:S(2)}) collective-permute-start(f32[384,128]{1,0:T(8,128)S(1)} %get-tuple-element.37), channel_id=1, source_target_pairs={{0,7},{1,0},{2,1},{3,2},{4,3},{5,4},{6,5},{7,6},{8,15},{9,8},{10,9... | collective-permute-start | bytes 589832 | tf_op jit(solution)/shard_map/ppermute | solution.py:37
  31.5 3.5 %shard_map.74.sums_t = f32[4,128,128]{2,1,0:T(8,128)S(1)} custom-call(s32[128,128]{1,0:T(8,128)S(1)} %get-tuple-element.29.code_t, f32[4,128,128]{2,1,0:T(8,128)S(1)} %get-tuple-element.35.rows_t, f32[4,128,128]{2,1,0:T(8,128)S(1)} %shard_map.72.after.before, f32[4,128,128]{2,1,0:T(8,128)S(1)} %get-tuple-element.30.source_t.fields_t, ...), custom_call_target="tpu_custom_call" | custom-call | tf_op jit(solution)/shard_map/pallas_call | solution.py:290
  35.0 0.0 collective-permute-done.5.high
  35.0 3.0 %shard_map.75 = (f32[3,8,16,128]{3,2,1,0:T(8,128)S(1)}, f32[8,16,128]{2,1,0:T(8,128)}, f32[3,8,16,128]{3,2,1,0:T(8,128)S(1)}) custom-call(s32[128,128]{1,0:T(8,128)S(1)} %get-tuple-element.29.code_t, f32[4,128,128]{2,1,0:T(8,128)S(1)} %shard_map.74.sums_t, f32[4,128,128]{2,1,0:T(8,128)S(1)} %get-tuple-element.30.source_t.fields_t, ...), custom_call_target="tpu_custom_call" | custom-call | tf_op jit(solution)/shard_map/pallas_call | solution.py:301
  38.0 1.4 %shard_map.76 = (f32[160,128]{1,0:T(8,128)S(1)}, f32[160,128]{1,0:T(8,128)S(1)}, f32[32,128]{1,0:T(8,128)S(1)}, f32[32,128]{1,0:T(8,128)S(1)}, f32[10,24,256]{2,...) custom-call(f32[3,8,16,128]{3,2,1,0:T(8,128)S(1)} %get-tuple-element.38.moved, ...), custom_call_target="tpu_custom_call" | custom-call | tf_op jit(solution)/shard_map/pallas_call | solution.py:586
  39.4 1.9 %collective-permute-start.6 = (f32[160,128]{1,0:T(8,128)S(1)}, f32[160,128]{1,0:T(8,128)S(1)}, u32[]{:S(2)}, u32[]{:S(2)}) collective-permute-start(f32[160,128]{1,0:T(8,128)S(1)} %get-tuple-element.43), channel_id=1, source_target_pairs={{0,32},{32,64},{64,96},{96,128},{128,160},{160,192},{192,224},{224... | collective-permute-start | bytes 245768 | tf_op jit(solution)/shard_map/ppermute | solution.py:37
  41.4 5.6 %collective-permute-start.7 = (f32[160,128]{1,0:T(8,128)S(1)}, f32[160,128]{1,0:T(8,128)S(1)}, u32[]{:S(2)}, u32[]{:S(2)}) collective-permute-start(f32[160,128]{1,0:T(8,128)S(1)} %get-tuple-element.44), channel_id=1, source_target_pairs={{0,480},{32,0},{64,32},{96,64},{128,96},{160,128},{192,160},{224,1... | collective-permute-start | bytes 245768 | tf_op jit(solution)/shard_map/ppermute | solution.py:37
  47.0 1.9 %collective-permute-start.8 = (f32[32,128]{1,0:T(8,128)S(1)}, f32[32,128]{1,0:T(8,128)S(1)}, u32[]{:S(2)}, u32[]{:S(2)}) collective-permute-start(f32[32,128]{1,0:T(8,128)S(1)} %get-tuple-element.45), channel_id=1, source_target_pairs={{0,64},{32,96},{64,128},{96,160},{128,192},{160,224},{192,256},{22... | collective-permute-start | bytes 49160 | tf_op jit(solution)/shard_map/ppermute | solution.py:37
  48.9 6.0 %collective-permute-start.9 = (f32[32,128]{1,0:T(8,128)S(1)}, f32[32,128]{1,0:T(8,128)S(1)}, u32[]{:S(2)}, u32[]{:S(2)}) collective-permute-start(f32[32,128]{1,0:T(8,128)S(1)} %get-tuple-element.46), channel_id=1, source_target_pairs={{0,448},{32,480},{64,0},{96,32},{128,64},{160,96},{192,128},{224,1... | collective-permute-start | bytes 49160 | tf_op jit(solution)/shard_map/ppermute | solution.py:37
  54.9 1.4 %collective-permute-done.9.high_2 = f32[32,128]{1,0:T(8,128)S(1)} collective-permute-done((f32[32,128]{1,0:T(8,128)S(1)}, f32[32,128]{1,0:T(8,128)S(1)}, u32[]{:S(2)}, u32[]{:S(2)}) %collective-permute-start.9) | collective-permute-done | bytes 16416 | tf_op jit(solution)/shard_map/ppermute | solution.py:37
  56.4 0.2 shard_map.77
  56.6 2.2 %collective-permute-start.10 = (f32[72,128]{1,0:T(8,128)S(1)}, f32[72,128]{1,0:T(8,128)S(1)}, u32[]{:S(2)}, u32[]{:S(2)}) collective-permute-start(f32[72,128]{1,0:T(8,128)S(1)} %get-tuple-element.50), channel_id=1, source_target_pairs={{0,8},{8,16},{16,24},{24,0},{1,9},{9,17},{17,25},{25,1},{2,10},{10... | collective-permute-start | bytes 110600 | tf_op jit(solution)/shard_map/ppermute | solution.py:37
  58.7 3.7 %collective-permute-start.11 = (f32[72,128]{1,0:T(8,128)S(1)}, f32[72,128]{1,0:T(8,128)S(1)}, u32[]{:S(2)}, u32[]{:S(2)}) collective-permute-start(f32[72,128]{1,0:T(8,128)S(1)} %get-tuple-element.51), channel_id=1, source_target_pairs={{0,24},{8,0},{16,8},{24,16},{1,25},{9,1},{17,9},{25,17},{2,26},{10... | collective-permute-start | bytes 110600 | tf_op jit(solution)/shard_map/ppermute | solution.py:37
  62.4 0.0 collective-permute-done.10.low
  62.4 3.4 %collective-permute-done.11.high = f32[72,128]{1,0:T(8,128)S(1)} collective-permute-done((f32[72,128]{1,0:T(8,128)S(1)}, f32[72,128]{1,0:T(8,128)S(1)}, u32[]{:S(2)}, u32[]{:S(2)}) %collective-permute-start.11) | collective-permute-done | bytes 36896 | tf_op jit(solution)/shard_map/ppermute | solution.py:37
  65.8 1.1 %shard_map.78 = (f32[3,8,16,128]{3,2,1,0:T(8,128)}, f32[8,16,128]{2,1,0:T(8,128)}) custom-call(f32[3,8,16,128]{3,2,1,0:T(8,128)S(1)} %get-tuple-element.38.moved, f32[10,24,256]{2,1,0:T(8,128)S(1)} %get-tuple-element.47.fine, f32[6,16,128]{2,1,0:T(8,128)S(1)} %get-tuple-element.48.middle, f32[4,16,128]{2,1,0:T(8,128)S(1)} %get-tuple-element.49.coarse, ...), custom_call_target="tpu_custom_call" | custom-call | tf_op jit(solution)/shard_map/pallas_call | solution.py:599
  (10 shorter events, 0.1 us)
Async XLA Ops:
  0.6 14.5 %copy-start.1 = (s32[3,8,16,128]{3,2,1,0:T(8,128)S(1)}, s32[3,8,16,128]{3,2,1,0:T(8,128)}, u32[]{:S(2)}) copy-start(s32[3,8,16,128]{3,2,1,0:T(8,128)} %param.6) | copy-start | bytes 589828
  1.7 13.5 %copy-start = (s32[3,8,16,128]{3,2,1,0:T(8,128)S(1)}, s32[3,8,16,128]{3,2,1,0:T(8,128)}, u32[]{:S(2)}) copy-start(s32[3,8,16,128]{3,2,1,0:T(8,128)} %param.7) | copy-start | bytes 589828
  1.7 16.2 %collective-permute-start = (f32[4,4,16,128]{3,2,1,0:T(8,128)S(1)}, f32[4,4,16,128]{3,2,1,0:T(8,128)S(1)}, u32[]{:S(2)}, u32[]{:S(2)}) collective-permute-start(f32[4,4,16,128]{3,2,1,0:T(8,128)S(1)} %get-tuple-element.31), channel_id=1, source_target_pairs={{0,32},{32,64},{64,96},{96,128},{128,160},{160,192},{192,224},{224... | collective-permute-start | bytes 393224 | tf_op jit(solution)/shard_map/ppermute | solution.py:37
  5.7 12.2 %collective-permute-start.1 = (f32[4,4,16,128]{3,2,1,0:T(8,128)S(1)}, f32[4,4,16,128]{3,2,1,0:T(8,128)S(1)}, u32[]{:S(2)}, u32[]{:S(2)}) collective-permute-start(f32[4,4,16,128]{3,2,1,0:T(8,128)S(1)} %get-tuple-element.32), channel_id=1, source_target_pairs={{0,480},{32,0},{64,32},{96,64},{128,96},{160,128},{192,160},{224,1... | collective-permute-start | bytes 393224 | tf_op jit(solution)/shard_map/ppermute | solution.py:37
  17.9 8.5 %collective-permute-start.2 = (f32[4,8,8,128]{3,2,1,0:T(8,128)S(1)}, f32[4,8,8,128]{3,2,1,0:T(8,128)S(1)}, u32[]{:S(2)}, u32[]{:S(2)}) collective-permute-start(f32[4,8,8,128]{3,2,1,0:T(8,128)S(1)} %get-tuple-element.33), channel_id=1, source_target_pairs={{0,8},{8,16},{16,24},{24,0},{1,9},{9,17},{17,25},{25,1},{2,10},{10... | collective-permute-start | bytes 393224 | tf_op jit(solution)/shard_map/ppermute | solution.py:37
  20.3 8.1 %collective-permute-start.3 = (f32[4,8,8,128]{3,2,1,0:T(8,128)S(1)}, f32[4,8,8,128]{3,2,1,0:T(8,128)S(1)}, u32[]{:S(2)}, u32[]{:S(2)}) collective-permute-start(f32[4,8,8,128]{3,2,1,0:T(8,128)S(1)} %get-tuple-element.34), channel_id=1, source_target_pairs={{0,24},{8,0},{16,8},{24,16},{1,25},{9,1},{17,9},{25,17},{2,26},{10... | collective-permute-start | bytes 393224 | tf_op jit(solution)/shard_map/ppermute | solution.py:37
  28.6 6.5 %collective-permute-start.4 = (f32[384,128]{1,0:T(8,128)S(1)}, f32[384,128]{1,0:T(8,128)S(1)}, u32[]{:S(2)}, u32[]{:S(2)}) collective-permute-start(f32[384,128]{1,0:T(8,128)S(1)} %get-tuple-element.36), channel_id=1, source_target_pairs={{0,1},{1,2},{2,3},{3,4},{4,5},{5,6},{6,7},{7,0},{8,9},{9,10},{10,1... | collective-permute-start | bytes 589832 | tf_op jit(solution)/shard_map/ppermute | solution.py:37
  28.6 6.4 %collective-permute-start.5 = (f32[384,128]{1,0:T(8,128)S(1)}, f32[384,128]{1,0:T(8,128)S(1)}, u32[]{:S(2)}, u32[]{:S(2)}) collective-permute-start(f32[384,128]{1,0:T(8,128)S(1)} %get-tuple-element.37), channel_id=1, source_target_pairs={{0,7},{1,0},{2,1},{3,2},{4,3},{5,4},{6,5},{7,6},{8,15},{9,8},{10,9... | collective-permute-start | bytes 589832 | tf_op jit(solution)/shard_map/ppermute | solution.py:37
  39.4 16.9 %collective-permute-start.6 = (f32[160,128]{1,0:T(8,128)S(1)}, f32[160,128]{1,0:T(8,128)S(1)}, u32[]{:S(2)}, u32[]{:S(2)}) collective-permute-start(f32[160,128]{1,0:T(8,128)S(1)} %get-tuple-element.43), channel_id=1, source_target_pairs={{0,32},{32,64},{64,96},{96,128},{128,160},{160,192},{192,224},{224... | collective-permute-start | bytes 245768 | tf_op jit(solution)/shard_map/ppermute | solution.py:37
  41.4 15.0 %collective-permute-start.7 = (f32[160,128]{1,0:T(8,128)S(1)}, f32[160,128]{1,0:T(8,128)S(1)}, u32[]{:S(2)}, u32[]{:S(2)}) collective-permute-start(f32[160,128]{1,0:T(8,128)S(1)} %get-tuple-element.44), channel_id=1, source_target_pairs={{0,480},{32,0},{64,32},{96,64},{128,96},{160,128},{192,160},{224,1... | collective-permute-start | bytes 245768 | tf_op jit(solution)/shard_map/ppermute | solution.py:37
  47.0 8.0 %collective-permute-start.8 = (f32[32,128]{1,0:T(8,128)S(1)}, f32[32,128]{1,0:T(8,128)S(1)}, u32[]{:S(2)}, u32[]{:S(2)}) collective-permute-start(f32[32,128]{1,0:T(8,128)S(1)} %get-tuple-element.45), channel_id=1, source_target_pairs={{0,64},{32,96},{64,128},{96,160},{128,192},{160,224},{192,256},{22... | collective-permute-start | bytes 49160 | tf_op jit(solution)/shard_map/ppermute | solution.py:37
  48.9 7.5 %collective-permute-start.9 = (f32[32,128]{1,0:T(8,128)S(1)}, f32[32,128]{1,0:T(8,128)S(1)}, u32[]{:S(2)}, u32[]{:S(2)}) collective-permute-start(f32[32,128]{1,0:T(8,128)S(1)} %get-tuple-element.46), channel_id=1, source_target_pairs={{0,448},{32,480},{64,0},{96,32},{128,64},{160,96},{192,128},{224,1... | collective-permute-start | bytes 49160 | tf_op jit(solution)/shard_map/ppermute | solution.py:37
  56.6 5.9 %collective-permute-start.10 = (f32[72,128]{1,0:T(8,128)S(1)}, f32[72,128]{1,0:T(8,128)S(1)}, u32[]{:S(2)}, u32[]{:S(2)}) collective-permute-start(f32[72,128]{1,0:T(8,128)S(1)} %get-tuple-element.50), channel_id=1, source_target_pairs={{0,8},{8,16},{16,24},{24,0},{1,9},{9,17},{17,25},{25,1},{2,10},{10... | collective-permute-start | bytes 110600 | tf_op jit(solution)/shard_map/ppermute | solution.py:37
  58.7 7.1 %collective-permute-start.11 = (f32[72,128]{1,0:T(8,128)S(1)}, f32[72,128]{1,0:T(8,128)S(1)}, u32[]{:S(2)}, u32[]{:S(2)}) collective-permute-start(f32[72,128]{1,0:T(8,128)S(1)} %get-tuple-element.51), channel_id=1, source_target_pairs={{0,24},{8,0},{16,8},{24,16},{1,25},{9,1},{17,9},{25,17},{2,26},{10... | collective-permute-start | bytes 110600 | tf_op jit(solution)/shard_map/ppermute | solution.py:37

commit v7 on v6

--- a/solution.py
+++ b/solution.py
@@ -1,4 +1,5 @@
 import functools
+import itertools
 
 import jax
 import jax.numpy as jnp
@@ -37,9 +38,41 @@
     return lax.ppermute(value, axis, [(i, (i + step) % count) for i in range(count)])
 
 
-def pack_kernel(fields, low_planes, high_planes):
-    low_planes[...] = fields[:, 0:4]
-    high_planes[...] = fields[:, 4:8]
+def shift_split(value, axis, step):
+    axes = ("gx", "gy", "gz")
+    counts = [lax.axis_size(name) for name in axes]
+    pairs = []
+    for source, place in enumerate(itertools.product(*[range(count) for count in counts])):
+        goal = list(place)
+        a = axes.index(axis)
+        goal[a] = (goal[a] + (step if place[2] % 2 == 0 else -step)) % counts[a]
+        pairs.append((source, (goal[0] * counts[1] + goal[1]) * counts[2] + goal[2]))
+    return lax.ppermute(value, axes, pairs)
+
+
+def second_core():
+    return lax.axis_index("gz") % 2 == 1
+
+
+class Either:
+    def __init__(self, first, second):
+        self.first, self.second = first, second
+
+    def __getitem__(self, index):
+        return jnp.where(second_core(), self.second[index], self.first[index])
+
+
+def by_direction(first, second):
+    return Either(first, second), Either(second, first)
+
+
+def give(first, second, low, high):
+    first[...] = jnp.where(second_core(), low[...], high[...])
+    second[...] = jnp.where(second_core(), high[...], low[...])
+
+
+def pack_kernel(fields, first, second):
+    give(first, second, fields[:, 0:4], fields[:, 4:8])
 
 
 def own_kernel(fields, code, fields_t, code_t):
@@ -48,8 +81,9 @@
     code_t[...] = code[...].reshape(128, 128).T.astype(jnp.int32)
 
 
-def rows_kernel(fields, low, high, after, to_low, to_high):
+def rows_kernel(fields, first, second, after, to_first, to_second, to_low, to_high):
     inside = inside_grid()
+    low, high = by_direction(first, second)
     for f in range(4):
         for pair in range(8):
             for half in range(2):
@@ -62,10 +96,12 @@
                     rows = fields[f, plane - 4]
                 to_low[f, pair, 4 * half : 4 * half + 4] = rows[0:4]
                 to_high[f, pair, 4 * half : 4 * half + 4] = rows[12:16]
-
-
-def planes_kernel(low, high, planes_t):
+    give(to_first, to_second, to_low, to_high)
+
+
+def planes_kernel(first, second, planes_t):
     inside = inside_grid()
+    low, high = by_direction(first, second)
     for f in range(4):
         both = jnp.concatenate(
             [low[f].reshape(64, 128) * inside[0], high[f].reshape(64, 128) * inside[1]], axis=0
@@ -73,8 +109,9 @@
         planes_t[f] = both.T
 
 
-def columns_kernel(fields_t, planes_t, code_t, low, high, after, rows_t, to_low, to_high):
+def columns_kernel(fields_t, planes_t, code_t, first, second, after, rows_t, to_low, to_high):
     inside = inside_grid()
+    low, high = by_direction(first, second)
     for f in range(4):
         both = jnp.concatenate(
             [low[f].reshape(64, 128) * inside[2], high[f].reshape(64, 128) * inside[3]], axis=0
@@ -265,9 +302,9 @@
 
     planes = ((4, 4, 16, 128), f32)
     fields = jnp.concatenate([velocity, density[None]], axis=0)
-    low_planes, high_planes = call(pack_kernel, [planes, planes], inputs=1)(fields)
-    low = shift_ring(high_planes, "gx", 1)
-    high = shift_ring(low_planes, "gx", -1)
+    first, second = call(pack_kernel, [planes, planes], inputs=1)(fields)
+    first = shift_split(first, "gx", 1)
+    second = shift_split(second, "gx", -1)
     code = (offsets[0] + 4) + (offsets[1] + 4) * 8 + (offsets[2] + 4) * 64
     code = code + eighths[0] * 512 + eighths[1] * 4096 + eighths[2] * 32768
     fields_t, code_t = call(own_kernel, [turned, ((128, 128), jnp.int32)], inputs=2)(
@@ -275,15 +312,18 @@
     )
     sums_t = gather(0, code_t, fields_t)
     strip = ((4, 8, 8, 128), f32)
-    to_low, to_high = call(rows_kernel, [strip, strip], inputs=4)(fields, low, high, sums_t)
-    rows_low = shift_ring(to_high, "gy", 1)
-    rows_high = shift_ring(to_low, "gy", -1)
-    (planes_t,) = call(planes_kernel, [turned], inputs=2)(low, high)
+    scratch = [pltpu.VMEM(*strip)] * 2
+    to_first, to_second = call(rows_kernel, [strip, strip], scratch, inputs=4)(
+        fields, first, second, sums_t
+    )
+    rows_first = shift_split(to_first, "gy", 1)
+    rows_second = shift_split(to_second, "gy", -1)
+    (planes_t,) = call(planes_kernel, [turned], inputs=2)(first, second)
     sums_t = gather(1, code_t, planes_t, sums_t)
     edge = ((384, 128), f32)
     rows_t, to_low, to_high = call(
         columns_kernel, [turned, edge, edge], inputs=6
-    )(fields_t, planes_t, code_t, rows_low, rows_high, sums_t)
+    )(fields_t, planes_t, code_t, rows_first, rows_second, sums_t)
     columns_low = shift_ring(to_high, "gz", 1)
     columns_high = shift_ring(to_low, "gz", -1)
     scratch = [pltpu.VMEM((2, 4, 3, 24, 128), f32)]
@@ -407,7 +447,8 @@
 
 
 def levels_kernel(
-    moved, beyond, to_low, to_high, to_low_2, to_high_2, fine, middle, coarse, halves
+    moved, beyond, first, second_, first_2, second_2_, fine, middle, coarse, halves,
+    to_low, to_high, to_low_2, to_high_2,
 ):
     inside = inside_grid()
     def spread(a):
@@ -450,6 +491,8 @@
     for k in range(2):
         to_high_2[16 * k : 16 * k + 16] = second_2[6 + k]
         to_low_2[16 * k : 16 * k + 16] = second_2[k]
+    give(first, second_, to_low, to_high)
+    give(first_2, second_2_, to_low_2, to_high_2)
 
 
 def near_end(lane):
@@ -464,9 +507,12 @@
 
 
 def planes_sum_kernel(
-    fine, middle, coarse, low, high, low_2, high_2, to_low, to_high, fine_o, middle_o, coarse_o
+    fine, middle, coarse, first, second, first_2, second_2, to_first, to_second,
+    fine_o, middle_o, coarse_o, to_low, to_high,
 ):
     inside = inside_grid()
+    low, high = by_direction(first, second)
+    low_2, high_2 = by_direction(first_2, second_2)
     f = [fine[k] for k in range(10)]
     m = [middle[k] for k in range(6)]
     c = [coarse[k] for k in range(4)]
@@ -504,6 +550,7 @@
             if k < 4:
                 rows = rows + roll(roll(c[k], -at_2, 0)[0:8], 80, 1)
             out[48 + 4 * k : 52 + 4 * k] = rows[0:4]
+    give(to_first, to_second, to_low, to_high)
 
 
 def four_lanes(rows):
@@ -512,9 +559,10 @@
 
 
 def pressure_kernel(
-    moved, fine, middle, coarse, low, high, velocity, pressure, halves
+    moved, fine, middle, coarse, first, second, velocity, pressure, halves
 ):
     inside = inside_grid()
+    low, high = by_direction(first, second)
     f = [fine[k] for k in range(10)]
     m = [middle[k] for k in range(6)]
     c = [coarse[k] for k in range(4)]
@@ -583,25 +631,26 @@
     held = [((10, 24, 256), f32), ((6, 16, 128), f32), ((4, 16, 128), f32)]
     halves = [pltpu.VMEM((2, 8, 32, 128), f32)]
     side, side_2 = ((160, 128), f32), ((32, 128), f32)
-    to_low, to_high, to_low_2, to_high_2, *sums = call(
-        levels_kernel, [side, side, side_2, side_2] + held, halves, inputs=2
+    scratch = halves + [pltpu.VMEM(*side)] * 2 + [pltpu.VMEM(*side_2)] * 2
+    first, second, first_2, second_2, *sums = call(
+        levels_kernel, [side, side, side_2, side_2] + held, scratch, inputs=2
     )(moved, beyond)
-    low = shift_ring(to_high, "gx", 1)
-    high = shift_ring(to_low, "gx", -1)
-    low_2 = shift_ring(to_high_2, "gx", 2)
-    high_2 = shift_ring(to_low_2, "gx", -2)
+    first = shift_split(first, "gx", 1)
+    second = shift_split(second, "gx", -1)
+    first_2 = shift_split(first_2, "gx", 2)
+    second_2 = shift_split(second_2, "gx", -2)
     side = ((72, 128), f32)
-    to_low, to_high, *sums = call(
-        planes_sum_kernel, [side, side] + held, inputs=7
-    )(*sums, low, high, low_2, high_2)
-    low = shift_ring(to_high, "gy", 1)
-    high = shift_ring(to_low, "gy", -1)
+    first, second, *sums = call(
+        planes_sum_kernel, [side, side] + held, [pltpu.VMEM(*side)] * 2, inputs=7
+    )(*sums, first, second, first_2, second_2)
+    first = shift_split(first, "gy", 1)
+    second = shift_split(second, "gy", -1)
     return call(
         pressure_kernel,
         [((3, 8, 16, 128), f32), ((8, 16, 128), f32)],
         halves,
         inputs=6,
-    )(moved, *sums, low, high)
+    )(moved, *sums, first, second)
 
 
 def body(velocity, density, offsets, eighths):

time: 67.3 us -> 70 us (1.040)
  waiting for transfers between devices: 6.82 us -> 8.53 us
    ppermute x0 -> x10, starting transfers between devices: none -> 40.8 us  [shift_split(): return lax.ppermute(value, axes, pairs)]
    ppermute x12 -> x2, starting transfers between devices: 43.6 us -> 3.16 us  [shift_ring(): lax.ppermute(value, axis, [(i, (i + step) % count) for i in range(count)])]
    ppermute x0 -> x10, waiting for transfers between devices: none -> 8.53 us  [shift_split(): return lax.ppermute(value, axes, pairs)]
    ppermute x12 -> x2, waiting for transfers between devices: 6.82 us -> 0.01 us  [shift_ring(): lax.ppermute(value, axis, [(i, (i + step) % count) for i in range(count)])]
where the time goes in v7:
time: 70 us; the launch traced here: 69 us
  starting transfers between devices  43.9 us (63%)
  Pallas kernels  14.6 us (21%)
  waiting for transfers between devices  8.53 us (12%)
  other arithmetic  1.06 us (2%)
  between operations  0.86 us (1%)
    ppermute x10, starting transfers between devices, shift_split(): return lax.ppermute(value, axes, pairs)  40.8 us
    ppermute x10, waiting for transfers between devices, shift_split(): return lax.ppermute(value, axes, pairs)  8.53 us
    pallas_call x2, Pallas kernels, gather(): return call(kernel, [turned], inputs=len(values))(*values)[0]  4.95 us
    pallas_call x1, Pallas kernels, advect(): call(ends_kernel, [turned], scratch, inputs=5)  3.49 us
    ppermute x2, starting transfers between devices, shift_ring(): lax.ppermute(value, axis, [(i, (i + step) % count) for i in range(count)])  3.16 us
    pallas_call x1, Pallas kernels, advect(): call(edges_kernel, [block, ((8, 16, 128), f32), block], scratch, inputs=7)  2.95 us
    pallas_call x1, Pallas kernels, project(): call(levels_kernel, [side, side, side_2, side_2] + held, scratch, inputs=2)  1.44 us
  transfers between devices with their start and end apart: 12, of which 3 were waited for; matrix products, arithmetic and copies ran while one was open for 0% of the time, Pallas kernels for 13%

profile of v7, /device:TPU:6, one launch (start us, length us, event | category | flops | bytes accessed | tf_op | source)
XLA Modules:
  0.0 69.0 jit_solution(6409415879870374731)
XLA Ops:
  0.6 1.0 %pad_maximum_fusion.fields = f32[4,8,16,128]{3,2,1,0:T(8,128)S(1)} fusion(f32[1,8,16,128]{3,2,1,0:T(8,128)} %bitcast.3, f32[3,8,16,128]{3,2,1,0:T(8,128)} %param.4), kind=kLoop, calls=%fused_computation | loop fusion | flops 65536 | bytes 524288 | tf_op jit(solution)/shard_map/concatenate | solution.py:304
  1.7 0.0 copy-start
  1.7 4.0 %collective-permute-start = (f32[4,4,16,128]{3,2,1,0:T(8,128)S(1)}, f32[4,4,16,128]{3,2,1,0:T(8,128)S(1)}, u32[]{:S(2)}, u32[]{:S(2)}) collective-permute-start(f32[4,4,16,128]{3,2,1,0:T(8,128)S(1)} %get-tuple-element.31), channel_id=1, source_target_pairs={{0,32},{1,481},{2,34},{3,483},{4,36},{5,485},{6,38},{7,487},{8,40}... | collective-permute-start | bytes 393224 | tf_op jit(solution)/shard_map/ppermute | solution.py:50
  5.7 9.5 %collective-permute-start.1 = (f32[4,4,16,128]{3,2,1,0:T(8,128)S(1)}, f32[4,4,16,128]{3,2,1,0:T(8,128)S(1)}, u32[]{:S(2)}, u32[]{:S(2)}) collective-permute-start(f32[4,4,16,128]{3,2,1,0:T(8,128)S(1)} %get-tuple-element.32), channel_id=1, source_target_pairs={{0,480},{1,33},{2,482},{3,35},{4,484},{5,37},{6,486},{7,39},{8,488... | collective-permute-start | bytes 393224 | tf_op jit(solution)/shard_map/ppermute | solution.py:50
  15.2 0.2 shard_map.67
  15.4 2.5 %shard_map.70.after.refs_0_ = f32[4,128,128]{2,1,0:T(8,128)S(1)} custom-call(s32[128,128]{1,0:T(8,128)S(1)} %get-tuple-element.29.code_t, f32[4,128,128]{2,1,0:T(8,128)S(1)} %get-tuple-element.30.source_t.fields_t), custom_call_target="tpu_custom_call" | custom-call | tf_op jit(solution)/shard_map/pallas_call | solution.py:301
  17.9 0.0 collective-permute-done.first
  17.9 0.0 collective-permute-done.1.second
  17.9 0.1 shard_map.71
  18.0 2.4 %collective-permute-start.2 = (f32[4,8,8,128]{3,2,1,0:T(8,128)S(1)}, f32[4,8,8,128]{3,2,1,0:T(8,128)S(1)}, u32[]{:S(2)}, u32[]{:S(2)}) collective-permute-start(f32[4,8,8,128]{3,2,1,0:T(8,128)S(1)} %get-tuple-element.33), channel_id=1, source_target_pairs={{0,8},{1,25},{2,10},{3,27},{4,12},{5,29},{6,14},{7,31},{8,16},{9,1... | collective-permute-start | bytes 393224 | tf_op jit(solution)/shard_map/ppermute | solution.py:50
  20.4 3.5 %collective-permute-start.3 = (f32[4,8,8,128]{3,2,1,0:T(8,128)S(1)}, f32[4,8,8,128]{3,2,1,0:T(8,128)S(1)}, u32[]{:S(2)}, u32[]{:S(2)}) collective-permute-start(f32[4,8,8,128]{3,2,1,0:T(8,128)S(1)} %get-tuple-element.34), channel_id=1, source_target_pairs={{0,24},{1,9},{2,26},{3,11},{4,28},{5,13},{6,30},{7,15},{8,0},{9,17... | collective-permute-start | bytes 393224 | tf_op jit(solution)/shard_map/ppermute | solution.py:50
  23.8 0.1 shard_map.69.source_t.planes_t
  24.0 2.5 %shard_map.72.after.before = f32[4,128,128]{2,1,0:T(8,128)S(1)} custom-call(s32[128,128]{1,0:T(8,128)S(1)} %get-tuple-element.29.code_t, f32[4,128,128]{2,1,0:T(8,128)S(1)} %shard_map.69.source_t.planes_t, f32[4,128,128]{2,1,0:T(8,128)S(1)} %shard_map.70.after.refs_0_), custom_call_target="tpu_custom_call" | custom-call | tf_op jit(solution)/shard_map/pallas_call | solution.py:301
  26.5 2.0 %collective-permute-done.3.second = f32[4,8,8,128]{3,2,1,0:T(8,128)S(1)} collective-permute-done((f32[4,8,8,128]{3,2,1,0:T(8,128)S(1)}, f32[4,8,8,128]{3,2,1,0:T(8,128)S(1)}, u32[]{:S(2)}, u32[]{:S(2)}) %collective-permute-start.3) | collective-permute-done | bytes 131104 | tf_op jit(solution)/shard_map/ppermute | solution.py:50
  28.4 0.1 shard_map.73
  28.6 0.5 collective-permute-start.4
  29.1 2.6 %collective-permute-start.5 = (f32[384,128]{1,0:T(8,128)S(1)}, f32[384,128]{1,0:T(8,128)S(1)}, u32[]{:S(2)}, u32[]{:S(2)}) collective-permute-start(f32[384,128]{1,0:T(8,128)S(1)} %get-tuple-element.37), channel_id=1, source_target_pairs={{0,7},{1,0},{2,1},{3,2},{4,3},{5,4},{6,5},{7,6},{8,15},{9,8},{10,9... | collective-permute-start | bytes 589832 | tf_op jit(solution)/shard_map/ppermute | solution.py:38
  31.8 3.5 %shard_map.74.sums_t = f32[4,128,128]{2,1,0:T(8,128)S(1)} custom-call(s32[128,128]{1,0:T(8,128)S(1)} %get-tuple-element.29.code_t, f32[4,128,128]{2,1,0:T(8,128)S(1)} %get-tuple-element.35.rows_t, f32[4,128,128]{2,1,0:T(8,128)S(1)} %shard_map.72.after.before, f32[4,128,128]{2,1,0:T(8,128)S(1)} %get-tuple-element.30.source_t.fields_t, ...), custom_call_target="tpu_custom_call" | custom-call | tf_op jit(solution)/shard_map/pallas_call | solution.py:330
  35.3 0.0 collective-permute-done.4.low
  35.3 3.0 %shard_map.75 = (f32[3,8,16,128]{3,2,1,0:T(8,128)S(1)}, f32[8,16,128]{2,1,0:T(8,128)}, f32[3,8,16,128]{3,2,1,0:T(8,128)S(1)}) custom-call(s32[128,128]{1,0:T(8,128)S(1)} %get-tuple-element.29.code_t, f32[4,128,128]{2,1,0:T(8,128)S(1)} %shard_map.74.sums_t, f32[4,128,128]{2,1,0:T(8,128)S(1)} %get-tuple-element.30.source_t.fields_t, ...), custom_call_target="tpu_custom_call" | custom-call | tf_op jit(solution)/shard_map/pallas_call | solution.py:341
  38.2 1.4 %shard_map.76 = (f32[160,128]{1,0:T(8,128)S(1)}, f32[160,128]{1,0:T(8,128)S(1)}, f32[32,128]{1,0:T(8,128)S(1)}, f32[32,128]{1,0:T(8,128)S(1)}, f32[10,24,256]{2,...) custom-call(f32[3,8,16,128]{3,2,1,0:T(8,128)S(1)} %get-tuple-element.38.moved, ...), custom_call_target="tpu_custom_call" | custom-call | tf_op jit(solution)/shard_map/pallas_call | solution.py:635
  39.7 1.9 %collective-permute-start.6 = (f32[160,128]{1,0:T(8,128)S(1)}, f32[160,128]{1,0:T(8,128)S(1)}, u32[]{:S(2)}, u32[]{:S(2)}) collective-permute-start(f32[160,128]{1,0:T(8,128)S(1)} %get-tuple-element.43), channel_id=1, source_target_pairs={{0,32},{1,481},{2,34},{3,483},{4,36},{5,485},{6,38},{7,487},{8,40}... | collective-permute-start | bytes 245768 | tf_op jit(solution)/shard_map/ppermute | solution.py:50
  41.6 5.1 %collective-permute-start.7 = (f32[160,128]{1,0:T(8,128)S(1)}, f32[160,128]{1,0:T(8,128)S(1)}, u32[]{:S(2)}, u32[]{:S(2)}) collective-permute-start(f32[160,128]{1,0:T(8,128)S(1)} %get-tuple-element.44), channel_id=1, source_target_pairs={{0,480},{1,33},{2,482},{3,35},{4,484},{5,37},{6,486},{7,39},{8,488... | collective-permute-start | bytes 245768 | tf_op jit(solution)/shard_map/ppermute | solution.py:50
  46.7 1.9 %collective-permute-start.8 = (f32[32,128]{1,0:T(8,128)S(1)}, f32[32,128]{1,0:T(8,128)S(1)}, u32[]{:S(2)}, u32[]{:S(2)}) collective-permute-start(f32[32,128]{1,0:T(8,128)S(1)} %get-tuple-element.45), channel_id=1, source_target_pairs={{0,64},{1,449},{2,66},{3,451},{4,68},{5,453},{6,70},{7,455},{8,72}... | collective-permute-start | bytes 49160 | tf_op jit(solution)/shard_map/ppermute | solution.py:50
  48.7 6.0 %collective-permute-start.9 = (f32[32,128]{1,0:T(8,128)S(1)}, f32[32,128]{1,0:T(8,128)S(1)}, u32[]{:S(2)}, u32[]{:S(2)}) collective-permute-start(f32[32,128]{1,0:T(8,128)S(1)} %get-tuple-element.46), channel_id=1, source_target_pairs={{0,448},{1,65},{2,450},{3,67},{4,452},{5,69},{6,454},{7,71},{8,456... | collective-permute-start | bytes 49160 | tf_op jit(solution)/shard_map/ppermute | solution.py:50
  54.7 0.0 collective-permute-done.8.first_2
  54.7 1.4 %collective-permute-done.9.second_2 = f32[32,128]{1,0:T(8,128)S(1)} collective-permute-done((f32[32,128]{1,0:T(8,128)S(1)}, f32[32,128]{1,0:T(8,128)S(1)}, u32[]{:S(2)}, u32[]{:S(2)}) %collective-permute-start.9) | collective-permute-done | bytes 16416 | tf_op jit(solution)/shard_map/ppermute | solution.py:50
  56.1 0.2 shard_map.77
  56.3 4.5 %collective-permute-start.10 = (f32[72,128]{1,0:T(8,128)S(1)}, f32[72,128]{1,0:T(8,128)S(1)}, u32[]{:S(2)}, u32[]{:S(2)}) collective-permute-start(f32[72,128]{1,0:T(8,128)S(1)} %get-tuple-element.50), channel_id=1, source_target_pairs={{0,8},{1,25},{2,10},{3,27},{4,12},{5,29},{6,14},{7,31},{8,16},{9,1... | collective-permute-start | bytes 110600 | tf_op jit(solution)/shard_map/ppermute | solution.py:50
  60.9 1.9 %collective-permute-start.11 = (f32[72,128]{1,0:T(8,128)S(1)}, f32[72,128]{1,0:T(8,128)S(1)}, u32[]{:S(2)}, u32[]{:S(2)}) collective-permute-start(f32[72,128]{1,0:T(8,128)S(1)} %get-tuple-element.51), channel_id=1, source_target_pairs={{0,24},{1,9},{2,26},{3,11},{4,28},{5,13},{6,30},{7,15},{8,0},{9,17... | collective-permute-start | bytes 110600 | tf_op jit(solution)/shard_map/ppermute | solution.py:50
  62.8 5.1 %collective-permute-done.11.second = f32[72,128]{1,0:T(8,128)S(1)} collective-permute-done((f32[72,128]{1,0:T(8,128)S(1)}, f32[72,128]{1,0:T(8,128)S(1)}, u32[]{:S(2)}, u32[]{:S(2)}) %collective-permute-start.11) | collective-permute-done | bytes 36896 | tf_op jit(solution)/shard_map/ppermute | solution.py:50
  67.9 1.1 %shard_map.78 = (f32[3,8,16,128]{3,2,1,0:T(8,128)}, f32[8,16,128]{2,1,0:T(8,128)}) custom-call(f32[3,8,16,128]{3,2,1,0:T(8,128)S(1)} %get-tuple-element.38.moved, f32[10,24,256]{2,1,0:T(8,128)S(1)} %get-tuple-element.47.fine, f32[6,16,128]{2,1,0:T(8,128)S(1)} %get-tuple-element.48.middle, f32[4,16,128]{2,1,0:T(8,128)S(1)} %get-tuple-element.49.coarse, ...), custom_call_target="tpu_custom_call" | custom-call | tf_op jit(solution)/shard_map/pallas_call | solution.py:648
  (10 shorter events, 0.1 us)
Async XLA Ops:
  0.6 14.6 %copy-start.1 = (s32[3,8,16,128]{3,2,1,0:T(8,128)S(1)}, s32[3,8,16,128]{3,2,1,0:T(8,128)}, u32[]{:S(2)}) copy-start(s32[3,8,16,128]{3,2,1,0:T(8,128)} %param.6) | copy-start | bytes 589828
  1.7 13.5 %copy-start = (s32[3,8,16,128]{3,2,1,0:T(8,128)S(1)}, s32[3,8,16,128]{3,2,1,0:T(8,128)}, u32[]{:S(2)}) copy-start(s32[3,8,16,128]{3,2,1,0:T(8,128)} %param.7) | copy-start | bytes 589828
  1.7 16.2 %collective-permute-start = (f32[4,4,16,128]{3,2,1,0:T(8,128)S(1)}, f32[4,4,16,128]{3,2,1,0:T(8,128)S(1)}, u32[]{:S(2)}, u32[]{:S(2)}) collective-permute-start(f32[4,4,16,128]{3,2,1,0:T(8,128)S(1)} %get-tuple-element.31), channel_id=1, source_target_pairs={{0,32},{1,481},{2,34},{3,483},{4,36},{5,485},{6,38},{7,487},{8,40}... | collective-permute-start | bytes 393224 | tf_op jit(solution)/shard_map/ppermute | solution.py:50
  5.7 12.2 %collective-permute-start.1 = (f32[4,4,16,128]{3,2,1,0:T(8,128)S(1)}, f32[4,4,16,128]{3,2,1,0:T(8,128)S(1)}, u32[]{:S(2)}, u32[]{:S(2)}) collective-permute-start(f32[4,4,16,128]{3,2,1,0:T(8,128)S(1)} %get-tuple-element.32), channel_id=1, source_target_pairs={{0,480},{1,33},{2,482},{3,35},{4,484},{5,37},{6,486},{7,39},{8,488... | collective-permute-start | bytes 393224 | tf_op jit(solution)/shard_map/ppermute | solution.py:50
  18.0 8.5 %collective-permute-start.2 = (f32[4,8,8,128]{3,2,1,0:T(8,128)S(1)}, f32[4,8,8,128]{3,2,1,0:T(8,128)S(1)}, u32[]{:S(2)}, u32[]{:S(2)}) collective-permute-start(f32[4,8,8,128]{3,2,1,0:T(8,128)S(1)} %get-tuple-element.33), channel_id=1, source_target_pairs={{0,8},{1,25},{2,10},{3,27},{4,12},{5,29},{6,14},{7,31},{8,16},{9,1... | collective-permute-start | bytes 393224 | tf_op jit(solution)/shard_map/ppermute | solution.py:50
  20.4 8.1 %collective-permute-start.3 = (f32[4,8,8,128]{3,2,1,0:T(8,128)S(1)}, f32[4,8,8,128]{3,2,1,0:T(8,128)S(1)}, u32[]{:S(2)}, u32[]{:S(2)}) collective-permute-start(f32[4,8,8,128]{3,2,1,0:T(8,128)S(1)} %get-tuple-element.34), channel_id=1, source_target_pairs={{0,24},{1,9},{2,26},{3,11},{4,28},{5,13},{6,30},{7,15},{8,0},{9,17... | collective-permute-start | bytes 393224 | tf_op jit(solution)/shard_map/ppermute | solution.py:50
  28.6 6.7 %collective-permute-start.4 = (f32[384,128]{1,0:T(8,128)S(1)}, f32[384,128]{1,0:T(8,128)S(1)}, u32[]{:S(2)}, u32[]{:S(2)}) collective-permute-start(f32[384,128]{1,0:T(8,128)S(1)} %get-tuple-element.36), channel_id=1, source_target_pairs={{0,1},{1,2},{2,3},{3,4},{4,5},{5,6},{6,7},{7,0},{8,9},{9,10},{10,1... | collective-permute-start | bytes 589832 | tf_op jit(solution)/shard_map/ppermute | solution.py:38
  29.1 6.1 %collective-permute-start.5 = (f32[384,128]{1,0:T(8,128)S(1)}, f32[384,128]{1,0:T(8,128)S(1)}, u32[]{:S(2)}, u32[]{:S(2)}) collective-permute-start(f32[384,128]{1,0:T(8,128)S(1)} %get-tuple-element.37), channel_id=1, source_target_pairs={{0,7},{1,0},{2,1},{3,2},{4,3},{5,4},{6,5},{7,6},{8,15},{9,8},{10,9... | collective-permute-start | bytes 589832 | tf_op jit(solution)/shard_map/ppermute | solution.py:38
  39.7 16.5 %collective-permute-start.6 = (f32[160,128]{1,0:T(8,128)S(1)}, f32[160,128]{1,0:T(8,128)S(1)}, u32[]{:S(2)}, u32[]{:S(2)}) collective-permute-start(f32[160,128]{1,0:T(8,128)S(1)} %get-tuple-element.43), channel_id=1, source_target_pairs={{0,32},{1,481},{2,34},{3,483},{4,36},{5,485},{6,38},{7,487},{8,40}... | collective-permute-start | bytes 245768 | tf_op jit(solution)/shard_map/ppermute | solution.py:50
  41.6 14.5 %collective-permute-start.7 = (f32[160,128]{1,0:T(8,128)S(1)}, f32[160,128]{1,0:T(8,128)S(1)}, u32[]{:S(2)}, u32[]{:S(2)}) collective-permute-start(f32[160,128]{1,0:T(8,128)S(1)} %get-tuple-element.44), channel_id=1, source_target_pairs={{0,480},{1,33},{2,482},{3,35},{4,484},{5,37},{6,486},{7,39},{8,488... | collective-permute-start | bytes 245768 | tf_op jit(solution)/shard_map/ppermute | solution.py:50
  46.7 8.0 %collective-permute-start.8 = (f32[32,128]{1,0:T(8,128)S(1)}, f32[32,128]{1,0:T(8,128)S(1)}, u32[]{:S(2)}, u32[]{:S(2)}) collective-permute-start(f32[32,128]{1,0:T(8,128)S(1)} %get-tuple-element.45), channel_id=1, source_target_pairs={{0,64},{1,449},{2,66},{3,451},{4,68},{5,453},{6,70},{7,455},{8,72}... | collective-permute-start | bytes 49160 | tf_op jit(solution)/shard_map/ppermute | solution.py:50
  48.7 7.5 %collective-permute-start.9 = (f32[32,128]{1,0:T(8,128)S(1)}, f32[32,128]{1,0:T(8,128)S(1)}, u32[]{:S(2)}, u32[]{:S(2)}) collective-permute-start(f32[32,128]{1,0:T(8,128)S(1)} %get-tuple-element.46), channel_id=1, source_target_pairs={{0,448},{1,65},{2,450},{3,67},{4,452},{5,69},{6,454},{7,71},{8,456... | collective-permute-start | bytes 49160 | tf_op jit(solution)/shard_map/ppermute | solution.py:50
  56.3 6.5 %collective-permute-start.10 = (f32[72,128]{1,0:T(8,128)S(1)}, f32[72,128]{1,0:T(8,128)S(1)}, u32[]{:S(2)}, u32[]{:S(2)}) collective-permute-start(f32[72,128]{1,0:T(8,128)S(1)} %get-tuple-element.50), channel_id=1, source_target_pairs={{0,8},{1,25},{2,10},{3,27},{4,12},{5,29},{6,14},{7,31},{8,16},{9,1... | collective-permute-start | bytes 110600 | tf_op jit(solution)/shard_map/ppermute | solution.py:50
  60.9 7.1 %collective-permute-start.11 = (f32[72,128]{1,0:T(8,128)S(1)}, f32[72,128]{1,0:T(8,128)S(1)}, u32[]{:S(2)}, u32[]{:S(2)}) collective-permute-start(f32[72,128]{1,0:T(8,128)S(1)} %get-tuple-element.51), channel_id=1, source_target_pairs={{0,24},{1,9},{2,26},{3,11},{4,28},{5,13},{6,30},{7,15},{8,0},{9,17... | collective-permute-start | bytes 110600 | tf_op jit(solution)/shard_map/ppermute | solution.py:50

commit v8 on v6

--- a/solution.py
+++ b/solution.py
@@ -145,14 +145,14 @@
         start = pl.multiple_of(step * 8, 8)
         code = code_t[pl.ds(start, 8), :]
         by_shift = weights_z(code, range(9))
-        sums = [before[0][f, pl.ds(start, 8), :] if before else none for f in range(4)]
+        sums = [before[0][f, pl.ds(start, 8), :] if before else none for f in range(3)]
         for at, weights in corners_of(code):
             parts = gathered(
-                at, by_shift, lambda f, dz: source_t[f, pl.ds(start + (dz - 4), 8), :]
+                at, by_shift, lambda f, dz: source_t[f, pl.ds(start + (dz - 4), 8), :], 3
             )
-            for f in range(4):
+            for f in range(3):
                 sums[f] = sums[f] + weights[group] * parts[f]
-        for f in range(4):
+        for f in range(3):
             after[f, pl.ds(start, 8), :] = sums[f]
         return carry
 
@@ -162,7 +162,7 @@
 def ends_kernel(code_t, rows_t, before, fields_t, planes_t, after, padded):
     group_kernel(2, code_t, rows_t, before, after)
     none = jnp.zeros((8, 128), jnp.float32)
-    for f in range(4):
+    for f in range(3):
         for group, source in enumerate((fields_t, planes_t, rows_t)):
             padded[0, f, group, 0:8] = none
             padded[0, f, group, 8:24] = source[f, 0:16]
@@ -171,25 +171,25 @@
     for end, start in ((0, 0), (1, 120)):
         code = code_t[start : start + 8]
         by_shift = weights_z(code, range(9))
-        sums = [none] * 4
+        sums = [none] * 3
         for at, weights in corners_of(code):
             for group in range(3):
                 parts = gathered(
-                    at, by_shift, lambda f, dz: padded[end, f, group, 4 + dz : 12 + dz]
+                    at, by_shift, lambda f, dz: padded[end, f, group, 4 + dz : 12 + dz], 3
                 )
-                for f in range(4):
+                for f in range(3):
                     sums[f] = sums[f] + weights[group] * parts[f]
-        for f in range(4):
+        for f in range(3):
             after[f, start : start + 8] = sums[f]
 
 
 def edges_kernel(
     code_t, sums_t, fields_t, planes_t, rows_t, low, high,
-    moved, density, beyond, moved_t, beyond_t, padded, codes, only_past,
+    moved, beyond, moved_t, beyond_t, padded, codes, only_past,
 ):
     inside = inside_grid()
     none = jnp.zeros((8, 128), jnp.float32)
-    for f in range(4):
+    for f in range(3):
         for group, source in enumerate((fields_t, planes_t, rows_t)):
             at = 24 * (3 * f + group)
             padded[0, f, group, 0:24] = low[at : at + 24] * inside[4]
@@ -205,7 +205,7 @@
         for k in range(6):
             code = code + (got[288 + 16 * k : 304 + 16 * k].astype(jnp.int32) << (3 * k))
         codes[end] = code
-    for f in range(4):
+    for f in range(3):
         moved_t[f] = sums_t[f]
 
     def moved_tile(end, half, start, count):
@@ -227,15 +227,18 @@
     for end, start, first, shifts in ((0, 0, 4, range(0, 4)), (1, 120, 1, range(5, 9))):
         code = code_t[start : start + 8]
         by_shift = weights_z(code, shifts)
-        sums = [sums_t[f, start : start + 8] for f in range(4)]
+        sums = [sums_t[f, start : start + 8] for f in range(3)]
         for at, weights in corners_of(code):
             for group in range(3):
                 parts = gathered(
-                    at, by_shift, lambda f, k: only_past[end, f, group, first + k : first + k + 8]
+                    at,
+                    by_shift,
+                    lambda f, k: only_past[end, f, group, first + k : first + k + 8],
+                    3,
                 )
-                for f in range(4):
+                for f in range(3):
                     sums[f] = sums[f] + weights[group] * parts[f]
-        for f in range(4):
+        for f in range(3):
             moved_t[f, start : start + 8] = sums[f]
 
     def outer(step, carry):
@@ -252,16 +255,43 @@
     for f in range(3):
         moved[f] = moved_t[f].T.reshape(8, 16, 128)
         beyond[f] = beyond_t[f].T.reshape(8, 16, 128)
-    density[...] = moved_t[3].T.reshape(8, 16, 128)
+
+
+def density_kernel(code_t, fields_t, planes_t, rows_t, low, high, after, density, done, padded, moved_t):
+    inside = inside_grid()
+    for group, source in enumerate((fields_t, planes_t, rows_t)):
+        at = 24 * (9 + group)
+        padded[group, 0:8] = low[at + 16 : at + 24] * inside[4]
+        padded[group, 8:136] = source[3]
+        padded[group, 136:144] = high[at : at + 8] * inside[5]
+
+    def tile(step, carry):
+        start = pl.multiple_of(step * 8, 8)
+        code = code_t[pl.ds(start, 8), :]
+        by_shift = weights_z(code, range(9))
+        total = jnp.zeros((8, 128), jnp.float32)
+        for at, weights in corners_of(code):
+            for group in range(3):
+                (part,) = gathered(
+                    at, by_shift, lambda f, dz: padded[group, pl.ds(start + (4 + dz), 8), :], 1
+                )
+                total = total + weights[group] * part
+        moved_t[pl.ds(start, 8), :] = total
+        return carry
+
+    lax.fori_loop(0, 16, tile, 0, unroll=4)
+    density[...] = moved_t[...].T.reshape(8, 16, 128)
+    done[...] = moved_t[0:8]
 
 
 def advect(velocity, density, offsets, eighths):
     f32 = jnp.float32
     turned = ((4, 128, 128), f32)
+    three = ((3, 128, 128), f32)
 
     def gather(group, *values):
         kernel = functools.partial(group_kernel, group)
-        return call(kernel, [turned], inputs=len(values))(*values)[0]
+        return call(kernel, [three], inputs=len(values))(*values)[0]
 
     planes = ((4, 4, 16, 128), f32)
     fields = jnp.concatenate([velocity, density[None]], axis=0)
@@ -286,21 +316,23 @@
     )(fields_t, planes_t, code_t, rows_low, rows_high, sums_t)
     columns_low = shift_ring(to_high, "gz", 1)
     columns_high = shift_ring(to_low, "gz", -1)
-    scratch = [pltpu.VMEM((2, 4, 3, 24, 128), f32)]
-    (sums_t,) = call(ends_kernel, [turned], scratch, inputs=5)(
+    scratch = [pltpu.VMEM((2, 3, 3, 24, 128), f32)]
+    (sums_t,) = call(ends_kernel, [three], scratch, inputs=5)(
         code_t, rows_t, sums_t, fields_t, planes_t
     )
     scratch = [
-        pltpu.VMEM((4, 128, 128), f32),
         pltpu.VMEM((3, 128, 128), f32),
-        pltpu.VMEM((2, 4, 3, 40, 128), f32),
+        pltpu.VMEM((3, 128, 128), f32),
+        pltpu.VMEM((2, 3, 3, 40, 128), f32),
         pltpu.VMEM((2, 16, 128), jnp.int32),
-        pltpu.VMEM((2, 4, 3, 16, 128), f32),
+        pltpu.VMEM((2, 3, 3, 16, 128), f32),
     ]
     block = ((3, 8, 16, 128), f32)
-    return call(
-        edges_kernel, [block, ((8, 16, 128), f32), block], scratch, inputs=7
-    )(code_t, sums_t, fields_t, planes_t, rows_t, columns_low, columns_high)
+    sources = (fields_t, planes_t, rows_t, columns_low, columns_high)
+    moved, beyond = call(edges_kernel, [block, block], scratch, inputs=7)(
+        code_t, sums_t, *sources
+    )
+    return moved, beyond, (code_t,) + sources
 
 
 def roll(value, shift, dim):
@@ -512,7 +544,7 @@
 
 
 def pressure_kernel(
-    moved, fine, middle, coarse, low, high, velocity, pressure, halves
+    moved, fine, middle, coarse, low, high, after, velocity, pressure, halves
 ):
     inside = inside_grid()
     f = [fine[k] for k in range(10)]
@@ -578,7 +610,7 @@
         velocity[2, k] = moved[2, k] - 0.5 * slope[:, 0:128]
 
 
-def project(moved, beyond):
+def project(moved, beyond, *sources):
     f32 = jnp.float32
     held = [((10, 24, 256), f32), ((6, 16, 128), f32), ((4, 16, 128), f32)]
     halves = [pltpu.VMEM((2, 8, 32, 128), f32)]
@@ -596,18 +628,22 @@
     )(*sums, low, high, low_2, high_2)
     low = shift_ring(to_high, "gy", 1)
     high = shift_ring(to_low, "gy", -1)
-    return call(
+    scratch = [pltpu.VMEM((3, 144, 128), f32), pltpu.VMEM((128, 128), f32)]
+    density, done = call(
+        density_kernel, [((8, 16, 128), f32), ((8, 128), f32)], scratch, inputs=7
+    )(*sources, sums[-1])
+    velocity, pressure = call(
         pressure_kernel,
         [((3, 8, 16, 128), f32), ((8, 16, 128), f32)],
         halves,
-        inputs=6,
-    )(moved, *sums, low, high)
+        inputs=7,
+    )(moved, *sums, low, high, done)
+    return velocity, density, pressure
 
 
 def body(velocity, density, offsets, eighths):
-    moved, new_density, past = advect(velocity, density, offsets, eighths)
-    new_velocity, pressure = project(moved, past)
-    return new_velocity, new_density, pressure
+    moved, past, sources = advect(velocity, density, offsets, eighths)
+    return project(moved, past, *sources)
 
 
 def solution(mesh):

time: 67.3 us -> 66.6 us (0.990)
  waiting for transfers between devices: 6.82 us -> 5.41 us
    ppermute x12, waiting for transfers between devices: 6.82 us -> 5.41 us  [shift_ring(): lax.ppermute(value, axis, [(i, (i + step) % count) for i in range(count)])]
    pallas_call x4 -> x5, Pallas kernels: 11.4 us -> 11.9 us  [the longest x2 3.88 us: gather(): return call(kernel, [three], inputs=len(values))(*values)[0]]
  transfers between devices with their start and end apart: 12 -> 12, of which waited for: 3 -> 5; matrix products, arithmetic and copies ran while one was open for 0% -> 0% of each run, Pallas kernels for 13% -> 15%
where the time goes in v8:
time: 66.6 us; the launch traced here: 66 us
  starting transfers between devices  43.6 us (65%)
  Pallas kernels  15.1 us (23%)
  waiting for transfers between devices  5.41 us (8%)
  other arithmetic  1.06 us (2%)
  between operations  0.84 us (1%)
    ppermute x12, starting transfers between devices, shift_ring(): lax.ppermute(value, axis, [(i, (i + step) % count) for i in range(count)])  43.6 us
    ppermute x12, waiting for transfers between devices, shift_ring(): lax.ppermute(value, axis, [(i, (i + step) % count) for i in range(count)])  5.41 us
    pallas_call x2, Pallas kernels, gather(): return call(kernel, [three], inputs=len(values))(*values)[0]  3.88 us
    pallas_call x1, Pallas kernels, project(): call(density_kernel, [((8, 16, 128), f32), ((8, 128), f32)], scratch, inp...  3.1 us
    pallas_call x1, Pallas kernels, advect(): call(ends_kernel, [three], scratch, inputs=5)  2.71 us
    pallas_call x1, Pallas kernels, advect(): call(edges_kernel, [block, block], scratch, inputs=7)  2.2 us
    pallas_call x1, Pallas kernels, project(): call(levels_kernel, [side, side, side_2, side_2] + held, halves, inputs=2)  1.43 us
  transfers between devices with their start and end apart: 12, of which 5 were waited for; matrix products, arithmetic and copies ran while one was open for 0% of the time, Pallas kernels for 15%

profile of v8, /device:TPU:6, one launch (start us, length us, event | category | flops | bytes accessed | tf_op | source)
XLA Modules:
  0.0 66.0 jit_solution(6134271508955994791)
XLA Ops:
  0.6 1.0 %pad_maximum_fusion.fields = f32[4,8,16,128]{3,2,1,0:T(8,128)S(1)} fusion(f32[1,8,16,128]{3,2,1,0:T(8,128)} %bitcast.3, f32[3,8,16,128]{3,2,1,0:T(8,128)} %param.4), kind=kLoop, calls=%fused_computation | loop fusion | flops 65536 | bytes 524288 | tf_op jit(solution)/shard_map/concatenate | solution.py:297
  1.7 0.0 copy-start
  1.7 4.0 %collective-permute-start = (f32[4,4,16,128]{3,2,1,0:T(8,128)S(1)}, f32[4,4,16,128]{3,2,1,0:T(8,128)S(1)}, u32[]{:S(2)}, u32[]{:S(2)}) collective-permute-start(f32[4,4,16,128]{3,2,1,0:T(8,128)S(1)} %get-tuple-element.32), channel_id=1, source_target_pairs={{0,32},{32,64},{64,96},{96,128},{128,160},{160,192},{192,224},{224... | collective-permute-start | bytes 393224 | tf_op jit(solution)/shard_map/ppermute | solution.py:37
  5.7 9.5 %collective-permute-start.1 = (f32[4,4,16,128]{3,2,1,0:T(8,128)S(1)}, f32[4,4,16,128]{3,2,1,0:T(8,128)S(1)}, u32[]{:S(2)}, u32[]{:S(2)}) collective-permute-start(f32[4,4,16,128]{3,2,1,0:T(8,128)S(1)} %get-tuple-element.33), channel_id=1, source_target_pairs={{0,480},{32,0},{64,32},{96,64},{128,96},{160,128},{192,160},{224,1... | collective-permute-start | bytes 393224 | tf_op jit(solution)/shard_map/ppermute | solution.py:37
  15.2 0.2 shard_map.67
  15.4 1.9 %shard_map.70.after.refs_0_ = f32[3,128,128]{2,1,0:T(8,128)S(1)} custom-call(s32[128,128]{1,0:T(8,128)S(1)} %get-tuple-element.30.code_t, f32[4,128,128]{2,1,0:T(8,128)S(1)} %get-tuple-element.31.source_t.fields_t), custom_call_target="tpu_custom_call" | custom-call | tf_op jit(solution)/shard_map/pallas_call | solution.py:294
  17.3 0.0 collective-permute-done.low
  17.4 0.5 collective-permute-done.1.high
  17.9 2.4 %collective-permute-start.2 = (f32[4,8,8,128]{3,2,1,0:T(8,128)S(1)}, f32[4,8,8,128]{3,2,1,0:T(8,128)S(1)}, u32[]{:S(2)}, u32[]{:S(2)}) collective-permute-start(f32[4,8,8,128]{3,2,1,0:T(8,128)S(1)} %get-tuple-element.34), channel_id=1, source_target_pairs={{0,8},{8,16},{16,24},{24,0},{1,9},{9,17},{17,25},{25,1},{2,10},{10... | collective-permute-start | bytes 393224 | tf_op jit(solution)/shard_map/ppermute | solution.py:37
  20.3 3.5 %collective-permute-start.3 = (f32[4,8,8,128]{3,2,1,0:T(8,128)S(1)}, f32[4,8,8,128]{3,2,1,0:T(8,128)S(1)}, u32[]{:S(2)}, u32[]{:S(2)}) collective-permute-start(f32[4,8,8,128]{3,2,1,0:T(8,128)S(1)} %get-tuple-element.35), channel_id=1, source_target_pairs={{0,24},{8,0},{16,8},{24,16},{1,25},{9,1},{17,9},{25,17},{2,26},{10... | collective-permute-start | bytes 393224 | tf_op jit(solution)/shard_map/ppermute | solution.py:37
  23.8 0.1 shard_map.69.source_t.planes_t
  23.9 1.9 %shard_map.72.after.before = f32[3,128,128]{2,1,0:T(8,128)S(1)} custom-call(s32[128,128]{1,0:T(8,128)S(1)} %get-tuple-element.30.code_t, f32[4,128,128]{2,1,0:T(8,128)S(1)} %shard_map.69.source_t.planes_t, f32[3,128,128]{2,1,0:T(8,128)S(1)} %shard_map.70.after.refs_0_), custom_call_target="tpu_custom_call" | custom-call | tf_op jit(solution)/shard_map/pallas_call | solution.py:294
  25.9 2.5 %collective-permute-done.3.high = f32[4,8,8,128]{3,2,1,0:T(8,128)S(1)} collective-permute-done((f32[4,8,8,128]{3,2,1,0:T(8,128)S(1)}, f32[4,8,8,128]{3,2,1,0:T(8,128)S(1)}, u32[]{:S(2)}, u32[]{:S(2)}) %collective-permute-start.3) | collective-permute-done | bytes 131104 | tf_op jit(solution)/shard_map/ppermute | solution.py:37
  28.4 0.1 shard_map.73
  28.6 0.0 collective-permute-start.4
  28.6 2.9 %collective-permute-start.5 = (f32[384,128]{1,0:T(8,128)S(1)}, f32[384,128]{1,0:T(8,128)S(1)}, u32[]{:S(2)}, u32[]{:S(2)}) collective-permute-start(f32[384,128]{1,0:T(8,128)S(1)} %get-tuple-element.38), channel_id=1, source_target_pairs={{0,7},{1,0},{2,1},{3,2},{4,3},{5,4},{6,5},{7,6},{8,15},{9,8},{10,9... | collective-permute-start | bytes 589832 | tf_op jit(solution)/shard_map/ppermute | solution.py:37
  31.5 2.7 %shard_map.74.sums_t = f32[3,128,128]{2,1,0:T(8,128)S(1)} custom-call(s32[128,128]{1,0:T(8,128)S(1)} %get-tuple-element.30.code_t, f32[4,128,128]{2,1,0:T(8,128)S(1)} %get-tuple-element.36.rows_t, f32[3,128,128]{2,1,0:T(8,128)S(1)} %shard_map.72.after.before, f32[4,128,128]{2,1,0:T(8,128)S(1)} %get-tuple-element.31.source_t.fields_t, ...), custom_call_target="tpu_custom_call" | custom-call | tf_op jit(solution)/shard_map/pallas_call | solution.py:320
  34.2 0.6 collective-permute-done.4.low
  34.9 0.0 collective-permute-done.5.high
  34.9 2.2 %shard_map.75 = (f32[3,8,16,128]{3,2,1,0:T(8,128)S(1)}, f32[3,8,16,128]{3,2,1,0:T(8,128)S(1)}) custom-call(s32[128,128]{1,0:T(8,128)S(1)} %get-tuple-element.30.code_t, f32[3,128,128]{2,1,0:T(8,128)S(1)} %shard_map.74.sums_t, f32[4,128,128]{2,1,0:T(8,128)S(1)} %get-tuple-element.31.source_t.fields_t, f32[4,128,128]{2,1,0:T(8,128)S(1)} %shard_map.69.source_t.planes_t, ...), custom_call_target="tpu_custom_call" | custom-call | tf_op jit(solution)/shard_map/pallas_call | solution.py:332
  37.1 1.4 %shard_map.76 = (f32[160,128]{1,0:T(8,128)S(1)}, f32[160,128]{1,0:T(8,128)S(1)}, f32[32,128]{1,0:T(8,128)S(1)}, f32[32,128]{1,0:T(8,128)S(1)}, f32[10,24,256]{2,...) custom-call(f32[3,8,16,128]{3,2,1,0:T(8,128)S(1)} %get-tuple-element.39.moved, ...), custom_call_target="tpu_custom_call" | custom-call | tf_op jit(solution)/shard_map/pallas_call | solution.py:618
  38.5 1.9 %collective-permute-start.6 = (f32[160,128]{1,0:T(8,128)S(1)}, f32[160,128]{1,0:T(8,128)S(1)}, u32[]{:S(2)}, u32[]{:S(2)}) collective-permute-start(f32[160,128]{1,0:T(8,128)S(1)} %get-tuple-element.44), channel_id=1, source_target_pairs={{0,32},{32,64},{64,96},{96,128},{128,160},{160,192},{192,224},{224... | collective-permute-start | bytes 245768 | tf_op jit(solution)/shard_map/ppermute | solution.py:37
  40.4 5.6 %collective-permute-start.7 = (f32[160,128]{1,0:T(8,128)S(1)}, f32[160,128]{1,0:T(8,128)S(1)}, u32[]{:S(2)}, u32[]{:S(2)}) collective-permute-start(f32[160,128]{1,0:T(8,128)S(1)} %get-tuple-element.45), channel_id=1, source_target_pairs={{0,480},{32,0},{64,32},{96,64},{128,96},{160,128},{192,160},{224,1... | collective-permute-start | bytes 245768 | tf_op jit(solution)/shard_map/ppermute | solution.py:37
  46.1 1.9 %collective-permute-start.8 = (f32[32,128]{1,0:T(8,128)S(1)}, f32[32,128]{1,0:T(8,128)S(1)}, u32[]{:S(2)}, u32[]{:S(2)}) collective-permute-start(f32[32,128]{1,0:T(8,128)S(1)} %get-tuple-element.46), channel_id=1, source_target_pairs={{0,64},{32,96},{64,128},{96,160},{128,192},{160,224},{192,256},{22... | collective-permute-start | bytes 49160 | tf_op jit(solution)/shard_map/ppermute | solution.py:37
  48.0 6.0 %collective-permute-start.9 = (f32[32,128]{1,0:T(8,128)S(1)}, f32[32,128]{1,0:T(8,128)S(1)}, u32[]{:S(2)}, u32[]{:S(2)}) collective-permute-start(f32[32,128]{1,0:T(8,128)S(1)} %get-tuple-element.47), channel_id=1, source_target_pairs={{0,448},{32,480},{64,0},{96,32},{128,64},{160,96},{192,128},{224,1... | collective-permute-start | bytes 49160 | tf_op jit(solution)/shard_map/ppermute | solution.py:37
  54.0 1.4 %collective-permute-done.9.high_2 = f32[32,128]{1,0:T(8,128)S(1)} collective-permute-done((f32[32,128]{1,0:T(8,128)S(1)}, f32[32,128]{1,0:T(8,128)S(1)}, u32[]{:S(2)}, u32[]{:S(2)}) %collective-permute-start.9) | collective-permute-done | bytes 16416 | tf_op jit(solution)/shard_map/ppermute | solution.py:37
  55.5 0.2 shard_map.77
  55.7 2.2 %collective-permute-start.10 = (f32[72,128]{1,0:T(8,128)S(1)}, f32[72,128]{1,0:T(8,128)S(1)}, u32[]{:S(2)}, u32[]{:S(2)}) collective-permute-start(f32[72,128]{1,0:T(8,128)S(1)} %get-tuple-element.51), channel_id=1, source_target_pairs={{0,8},{8,16},{16,24},{24,0},{1,9},{9,17},{17,25},{25,1},{2,10},{10... | collective-permute-start | bytes 110600 | tf_op jit(solution)/shard_map/ppermute | solution.py:37
  57.8 3.7 %collective-permute-start.11 = (f32[72,128]{1,0:T(8,128)S(1)}, f32[72,128]{1,0:T(8,128)S(1)}, u32[]{:S(2)}, u32[]{:S(2)}) collective-permute-start(f32[72,128]{1,0:T(8,128)S(1)} %get-tuple-element.52), channel_id=1, source_target_pairs={{0,24},{8,0},{16,8},{24,16},{1,25},{9,1},{17,9},{25,17},{2,26},{10... | collective-permute-start | bytes 110600 | tf_op jit(solution)/shard_map/ppermute | solution.py:37
  61.5 3.1 %shard_map.78 = (f32[8,16,128]{2,1,0:T(8,128)}, f32[8,128]{1,0:T(8,128)S(1)}) custom-call(s32[128,128]{1,0:T(8,128)S(1)} %get-tuple-element.30.code_t, f32[4,128,128]{2,1,0:T(8,128)S(1)} %get-tuple-element.31.source_t.fields_t, f32[4,128,128]{2,1,0:T(8,128)S(1)} %shard_map.69.source_t.planes_t, f32[4,128,128]{2,1,0:T(8,128)S(1)} %get-tuple-element.36.rows_t, ...), custom_call_target="tpu_custom_call" | custom-call | tf_op jit(solution)/shard_map/pallas_call | solution.py:632
  64.6 0.3 collective-permute-done.11.high
  64.9 1.1 %shard_map.79 = (f32[3,8,16,128]{3,2,1,0:T(8,128)}, f32[8,16,128]{2,1,0:T(8,128)}) custom-call(f32[3,8,16,128]{3,2,1,0:T(8,128)S(1)} %get-tuple-element.39.moved, f32[10,24,256]{2,1,0:T(8,128)S(1)} %get-tuple-element.48.fine, f32[6,16,128]{2,1,0:T(8,128)S(1)} %get-tuple-element.49.middle, f32[4,16,128]{2,1,0:T(8,128)S(1)} %get-tuple-element.50.after.coarse, ...), custom_call_target="tpu_custom_call" | custom-call | tf_op jit(solution)/shard_map/pallas_call | solution.py:635
  (11 shorter events, 0.1 us)
Async XLA Ops:
  0.6 14.5 %copy-start.1 = (s32[3,8,16,128]{3,2,1,0:T(8,128)S(1)}, s32[3,8,16,128]{3,2,1,0:T(8,128)}, u32[]{:S(2)}) copy-start(s32[3,8,16,128]{3,2,1,0:T(8,128)} %param.6) | copy-start | bytes 589828
  1.7 13.5 %copy-start = (s32[3,8,16,128]{3,2,1,0:T(8,128)S(1)}, s32[3,8,16,128]{3,2,1,0:T(8,128)}, u32[]{:S(2)}) copy-start(s32[3,8,16,128]{3,2,1,0:T(8,128)} %param.7) | copy-start | bytes 589828
  1.7 15.7 %collective-permute-start = (f32[4,4,16,128]{3,2,1,0:T(8,128)S(1)}, f32[4,4,16,128]{3,2,1,0:T(8,128)S(1)}, u32[]{:S(2)}, u32[]{:S(2)}) collective-permute-start(f32[4,4,16,128]{3,2,1,0:T(8,128)S(1)} %get-tuple-element.32), channel_id=1, source_target_pairs={{0,32},{32,64},{64,96},{96,128},{128,160},{160,192},{192,224},{224... | collective-permute-start | bytes 393224 | tf_op jit(solution)/shard_map/ppermute | solution.py:37
  5.7 12.2 %collective-permute-start.1 = (f32[4,4,16,128]{3,2,1,0:T(8,128)S(1)}, f32[4,4,16,128]{3,2,1,0:T(8,128)S(1)}, u32[]{:S(2)}, u32[]{:S(2)}) collective-permute-start(f32[4,4,16,128]{3,2,1,0:T(8,128)S(1)} %get-tuple-element.33), channel_id=1, source_target_pairs={{0,480},{32,0},{64,32},{96,64},{128,96},{160,128},{192,160},{224,1... | collective-permute-start | bytes 393224 | tf_op jit(solution)/shard_map/ppermute | solution.py:37
  17.9 7.9 %collective-permute-start.2 = (f32[4,8,8,128]{3,2,1,0:T(8,128)S(1)}, f32[4,8,8,128]{3,2,1,0:T(8,128)S(1)}, u32[]{:S(2)}, u32[]{:S(2)}) collective-permute-start(f32[4,8,8,128]{3,2,1,0:T(8,128)S(1)} %get-tuple-element.34), channel_id=1, source_target_pairs={{0,8},{8,16},{16,24},{24,0},{1,9},{9,17},{17,25},{25,1},{2,10},{10... | collective-permute-start | bytes 393224 | tf_op jit(solution)/shard_map/ppermute | solution.py:37
  20.3 8.1 %collective-permute-start.3 = (f32[4,8,8,128]{3,2,1,0:T(8,128)S(1)}, f32[4,8,8,128]{3,2,1,0:T(8,128)S(1)}, u32[]{:S(2)}, u32[]{:S(2)}) collective-permute-start(f32[4,8,8,128]{3,2,1,0:T(8,128)S(1)} %get-tuple-element.35), channel_id=1, source_target_pairs={{0,24},{8,0},{16,8},{24,16},{1,25},{9,1},{17,9},{25,17},{2,26},{10... | collective-permute-start | bytes 393224 | tf_op jit(solution)/shard_map/ppermute | solution.py:37
  28.6 6.3 %collective-permute-start.4 = (f32[384,128]{1,0:T(8,128)S(1)}, f32[384,128]{1,0:T(8,128)S(1)}, u32[]{:S(2)}, u32[]{:S(2)}) collective-permute-start(f32[384,128]{1,0:T(8,128)S(1)} %get-tuple-element.37), channel_id=1, source_target_pairs={{0,1},{1,2},{2,3},{3,4},{4,5},{5,6},{6,7},{7,0},{8,9},{9,10},{10,1... | collective-permute-start | bytes 589832 | tf_op jit(solution)/shard_map/ppermute | solution.py:37
  28.6 6.3 %collective-permute-start.5 = (f32[384,128]{1,0:T(8,128)S(1)}, f32[384,128]{1,0:T(8,128)S(1)}, u32[]{:S(2)}, u32[]{:S(2)}) collective-permute-start(f32[384,128]{1,0:T(8,128)S(1)} %get-tuple-element.38), channel_id=1, source_target_pairs={{0,7},{1,0},{2,1},{3,2},{4,3},{5,4},{6,5},{7,6},{8,15},{9,8},{10,9... | collective-permute-start | bytes 589832 | tf_op jit(solution)/shard_map/ppermute | solution.py:37
  38.5 16.9 %collective-permute-start.6 = (f32[160,128]{1,0:T(8,128)S(1)}, f32[160,128]{1,0:T(8,128)S(1)}, u32[]{:S(2)}, u32[]{:S(2)}) collective-permute-start(f32[160,128]{1,0:T(8,128)S(1)} %get-tuple-element.44), channel_id=1, source_target_pairs={{0,32},{32,64},{64,96},{96,128},{128,160},{160,192},{192,224},{224... | collective-permute-start | bytes 245768 | tf_op jit(solution)/shard_map/ppermute | solution.py:37
  40.4 15.0 %collective-permute-start.7 = (f32[160,128]{1,0:T(8,128)S(1)}, f32[160,128]{1,0:T(8,128)S(1)}, u32[]{:S(2)}, u32[]{:S(2)}) collective-permute-start(f32[160,128]{1,0:T(8,128)S(1)} %get-tuple-element.45), channel_id=1, source_target_pairs={{0,480},{32,0},{64,32},{96,64},{128,96},{160,128},{192,160},{224,1... | collective-permute-start | bytes 245768 | tf_op jit(solution)/shard_map/ppermute | solution.py:37
  46.1 8.0 %collective-permute-start.8 = (f32[32,128]{1,0:T(8,128)S(1)}, f32[32,128]{1,0:T(8,128)S(1)}, u32[]{:S(2)}, u32[]{:S(2)}) collective-permute-start(f32[32,128]{1,0:T(8,128)S(1)} %get-tuple-element.46), channel_id=1, source_target_pairs={{0,64},{32,96},{64,128},{96,160},{128,192},{160,224},{192,256},{22... | collective-permute-start | bytes 49160 | tf_op jit(solution)/shard_map/ppermute | solution.py:37
  48.0 7.5 %collective-permute-start.9 = (f32[32,128]{1,0:T(8,128)S(1)}, f32[32,128]{1,0:T(8,128)S(1)}, u32[]{:S(2)}, u32[]{:S(2)}) collective-permute-start(f32[32,128]{1,0:T(8,128)S(1)} %get-tuple-element.47), channel_id=1, source_target_pairs={{0,448},{32,480},{64,0},{96,32},{128,64},{160,96},{192,128},{224,1... | collective-permute-start | bytes 49160 | tf_op jit(solution)/shard_map/ppermute | solution.py:37
  55.7 9.0 %collective-permute-start.10 = (f32[72,128]{1,0:T(8,128)S(1)}, f32[72,128]{1,0:T(8,128)S(1)}, u32[]{:S(2)}, u32[]{:S(2)}) collective-permute-start(f32[72,128]{1,0:T(8,128)S(1)} %get-tuple-element.51), channel_id=1, source_target_pairs={{0,8},{8,16},{16,24},{24,0},{1,9},{9,17},{17,25},{25,1},{2,10},{10... | collective-permute-start | bytes 110600 | tf_op jit(solution)/shard_map/ppermute | solution.py:37
  57.8 7.1 %collective-permute-start.11 = (f32[72,128]{1,0:T(8,128)S(1)}, f32[72,128]{1,0:T(8,128)S(1)}, u32[]{:S(2)}, u32[]{:S(2)}) collective-permute-start(f32[72,128]{1,0:T(8,128)S(1)} %get-tuple-element.52), channel_id=1, source_target_pairs={{0,24},{8,0},{16,8},{24,16},{1,25},{9,1},{17,9},{25,17},{2,26},{10... | collective-permute-start | bytes 110600 | tf_op jit(solution)/shard_map/ppermute | solution.py:37

commit v9 on v8

--- a/solution.py
+++ b/solution.py
@@ -257,7 +257,20 @@
         beyond[f] = beyond_t[f].T.reshape(8, 16, 128)
 
 
-def density_kernel(code_t, fields_t, planes_t, rows_t, low, high, after, density, done, padded, moved_t):
+def low_density_kernel(code_t, fields_t, planes_t, rows_t, low, high, after, half_t, padded):
+    density_tiles(0, code_t, fields_t, planes_t, rows_t, low, high, half_t, padded)
+
+
+def density_kernel(
+    code_t, fields_t, planes_t, rows_t, low, high, half_t, after, density, done, padded, moved_t
+):
+    density_tiles(8, code_t, fields_t, planes_t, rows_t, low, high, moved_t, padded)
+    done[...] = moved_t[0:8]
+    whole = jnp.concatenate([half_t[...], moved_t[...]], axis=0)
+    density[...] = whole.T.reshape(8, 16, 128)
+
+
+def density_tiles(first, code_t, fields_t, planes_t, rows_t, low, high, moved_t, padded):
     inside = inside_grid()
     for group, source in enumerate((fields_t, planes_t, rows_t)):
         at = 24 * (9 + group)
@@ -276,12 +289,10 @@
                     at, by_shift, lambda f, dz: padded[group, pl.ds(start + (4 + dz), 8), :], 1
                 )
                 total = total + weights[group] * part
-        moved_t[pl.ds(start, 8), :] = total
+        moved_t[pl.ds(pl.multiple_of(start - 8 * first, 8), 8), :] = total
         return carry
 
-    lax.fori_loop(0, 16, tile, 0, unroll=4)
-    density[...] = moved_t[...].T.reshape(8, 16, 128)
-    done[...] = moved_t[0:8]
+    lax.fori_loop(first, first + 8, tile, 0, unroll=4)
 
 
 def advect(velocity, density, offsets, eighths):
@@ -496,7 +507,8 @@
 
 
 def planes_sum_kernel(
-    fine, middle, coarse, low, high, low_2, high_2, to_low, to_high, fine_o, middle_o, coarse_o
+    fine, middle, coarse, low, high, low_2, high_2, after, to_low, to_high,
+    fine_o, middle_o, coarse_o,
 ):
     inside = inside_grid()
     f = [fine[k] for k in range(10)]
@@ -622,16 +634,20 @@
     high = shift_ring(to_low, "gx", -1)
     low_2 = shift_ring(to_high_2, "gx", 2)
     high_2 = shift_ring(to_low_2, "gx", -2)
+    padded = pltpu.VMEM((3, 144, 128), f32)
+    (half_t,) = call(low_density_kernel, [((64, 128), f32)], [padded], inputs=7)(
+        *sources, sums[-1]
+    )
     side = ((72, 128), f32)
     to_low, to_high, *sums = call(
-        planes_sum_kernel, [side, side] + held, inputs=7
-    )(*sums, low, high, low_2, high_2)
+        planes_sum_kernel, [side, side] + held, inputs=8
+    )(*sums, low, high, low_2, high_2, half_t)
     low = shift_ring(to_high, "gy", 1)
     high = shift_ring(to_low, "gy", -1)
-    scratch = [pltpu.VMEM((3, 144, 128), f32), pltpu.VMEM((128, 128), f32)]
+    scratch = [padded, pltpu.VMEM((64, 128), f32)]
     density, done = call(
-        density_kernel, [((8, 16, 128), f32), ((8, 128), f32)], scratch, inputs=7
-    )(*sources, sums[-1])
+        density_kernel, [((8, 16, 128), f32), ((8, 128), f32)], scratch, inputs=8
+    )(*sources, half_t, sums[-1])
     velocity, pressure = call(
         pressure_kernel,
         [((3, 8, 16, 128), f32), ((8, 16, 128), f32)],

time: 66.6 us -> 66.4 us (level)
    pallas_call x1, Pallas kernels: 3.1 us -> 1.91 us  [project(): call(density_kernel, [((8, 16, 128), f32), ((8, 128), f32)], scratch, inp...]
    pallas_call x1 -> x2, Pallas kernels: 0.19 us -> 1.38 us  [the longest x1 1.19 us: project(): call(low_density_kernel, [((64, 128), f32)], [padded], inputs=7)]
where the time goes in v9:
time: 66.4 us; the launch traced here: 66 us
  starting transfers between devices  43.6 us (66%)
  Pallas kernels  15.1 us (23%)
  waiting for transfers between devices  5.41 us (8%)
  other arithmetic  1.06 us (2%)
  between operations  0.85 us (1%)
    ppermute x12, starting transfers between devices, shift_ring(): lax.ppermute(value, axis, [(i, (i + step) % count) for i in range(count)])  43.6 us
    ppermute x12, waiting for transfers between devices, shift_ring(): lax.ppermute(value, axis, [(i, (i + step) % count) for i in range(count)])  5.41 us
    pallas_call x2, Pallas kernels, gather(): return call(kernel, [three], inputs=len(values))(*values)[0]  3.88 us
    pallas_call x1, Pallas kernels, advect(): call(ends_kernel, [three], scratch, inputs=5)  2.71 us
    pallas_call x1, Pallas kernels, advect(): call(edges_kernel, [block, block], scratch, inputs=7)  2.2 us
    pallas_call x1, Pallas kernels, project(): call(density_kernel, [((8, 16, 128), f32), ((8, 128), f32)], scratch, inp...  1.91 us
    pallas_call x1, Pallas kernels, project(): call(levels_kernel, [side, side, side_2, side_2] + held, halves, inputs=2)  1.43 us
  transfers between devices with their start and end apart: 12, of which 5 were waited for; matrix products, arithmetic and copies ran while one was open for 0% of the time, Pallas kernels for 15%

profile of v9, /device:TPU:6, one launch (start us, length us, event | category | flops | bytes accessed | tf_op | source)
XLA Modules:
  0.0 66.0 jit_solution(6397209162946870043)
XLA Ops:
  0.6 1.0 %pad_maximum_fusion.fields = f32[4,8,16,128]{3,2,1,0:T(8,128)S(1)} fusion(f32[1,8,16,128]{3,2,1,0:T(8,128)} %bitcast.3, f32[3,8,16,128]{3,2,1,0:T(8,128)} %param.4), kind=kLoop, calls=%fused_computation | loop fusion | flops 65536 | bytes 524288 | tf_op jit(solution)/shard_map/concatenate | solution.py:308
  1.7 0.0 copy-start
  1.7 4.0 %collective-permute-start = (f32[4,4,16,128]{3,2,1,0:T(8,128)S(1)}, f32[4,4,16,128]{3,2,1,0:T(8,128)S(1)}, u32[]{:S(2)}, u32[]{:S(2)}) collective-permute-start(f32[4,4,16,128]{3,2,1,0:T(8,128)S(1)} %get-tuple-element.32), channel_id=1, source_target_pairs={{0,32},{32,64},{64,96},{96,128},{128,160},{160,192},{192,224},{224... | collective-permute-start | bytes 393224 | tf_op jit(solution)/shard_map/ppermute | solution.py:37
  5.7 9.5 %collective-permute-start.1 = (f32[4,4,16,128]{3,2,1,0:T(8,128)S(1)}, f32[4,4,16,128]{3,2,1,0:T(8,128)S(1)}, u32[]{:S(2)}, u32[]{:S(2)}) collective-permute-start(f32[4,4,16,128]{3,2,1,0:T(8,128)S(1)} %get-tuple-element.33), channel_id=1, source_target_pairs={{0,480},{32,0},{64,32},{96,64},{128,96},{160,128},{192,160},{224,1... | collective-permute-start | bytes 393224 | tf_op jit(solution)/shard_map/ppermute | solution.py:37
  15.2 0.2 shard_map.67
  15.4 1.9 %shard_map.70.after.refs_0_ = f32[3,128,128]{2,1,0:T(8,128)S(1)} custom-call(s32[128,128]{1,0:T(8,128)S(1)} %get-tuple-element.30.code_t, f32[4,128,128]{2,1,0:T(8,128)S(1)} %get-tuple-element.31.source_t.fields_t), custom_call_target="tpu_custom_call" | custom-call | tf_op jit(solution)/shard_map/pallas_call | solution.py:305
  17.3 0.0 collective-permute-done.low
  17.4 0.5 collective-permute-done.1.high
  17.9 2.4 %collective-permute-start.2 = (f32[4,8,8,128]{3,2,1,0:T(8,128)S(1)}, f32[4,8,8,128]{3,2,1,0:T(8,128)S(1)}, u32[]{:S(2)}, u32[]{:S(2)}) collective-permute-start(f32[4,8,8,128]{3,2,1,0:T(8,128)S(1)} %get-tuple-element.34), channel_id=1, source_target_pairs={{0,8},{8,16},{16,24},{24,0},{1,9},{9,17},{17,25},{25,1},{2,10},{10... | collective-permute-start | bytes 393224 | tf_op jit(solution)/shard_map/ppermute | solution.py:37
  20.3 3.5 %collective-permute-start.3 = (f32[4,8,8,128]{3,2,1,0:T(8,128)S(1)}, f32[4,8,8,128]{3,2,1,0:T(8,128)S(1)}, u32[]{:S(2)}, u32[]{:S(2)}) collective-permute-start(f32[4,8,8,128]{3,2,1,0:T(8,128)S(1)} %get-tuple-element.35), channel_id=1, source_target_pairs={{0,24},{8,0},{16,8},{24,16},{1,25},{9,1},{17,9},{25,17},{2,26},{10... | collective-permute-start | bytes 393224 | tf_op jit(solution)/shard_map/ppermute | solution.py:37
  23.8 0.1 shard_map.69.source_t.planes_t
  23.9 1.9 %shard_map.72.after.before = f32[3,128,128]{2,1,0:T(8,128)S(1)} custom-call(s32[128,128]{1,0:T(8,128)S(1)} %get-tuple-element.30.code_t, f32[4,128,128]{2,1,0:T(8,128)S(1)} %shard_map.69.source_t.planes_t, f32[3,128,128]{2,1,0:T(8,128)S(1)} %shard_map.70.after.refs_0_), custom_call_target="tpu_custom_call" | custom-call | tf_op jit(solution)/shard_map/pallas_call | solution.py:305
  25.9 2.5 %collective-permute-done.3.high = f32[4,8,8,128]{3,2,1,0:T(8,128)S(1)} collective-permute-done((f32[4,8,8,128]{3,2,1,0:T(8,128)S(1)}, f32[4,8,8,128]{3,2,1,0:T(8,128)S(1)}, u32[]{:S(2)}, u32[]{:S(2)}) %collective-permute-start.3) | collective-permute-done | bytes 131104 | tf_op jit(solution)/shard_map/ppermute | solution.py:37
  28.4 0.1 shard_map.73
  28.6 0.0 collective-permute-start.4
  28.6 2.9 %collective-permute-start.5 = (f32[384,128]{1,0:T(8,128)S(1)}, f32[384,128]{1,0:T(8,128)S(1)}, u32[]{:S(2)}, u32[]{:S(2)}) collective-permute-start(f32[384,128]{1,0:T(8,128)S(1)} %get-tuple-element.38), channel_id=1, source_target_pairs={{0,7},{1,0},{2,1},{3,2},{4,3},{5,4},{6,5},{7,6},{8,15},{9,8},{10,9... | collective-permute-start | bytes 589832 | tf_op jit(solution)/shard_map/ppermute | solution.py:37
  31.5 2.7 %shard_map.74.sums_t = f32[3,128,128]{2,1,0:T(8,128)S(1)} custom-call(s32[128,128]{1,0:T(8,128)S(1)} %get-tuple-element.30.code_t, f32[4,128,128]{2,1,0:T(8,128)S(1)} %get-tuple-element.36.rows_t, f32[3,128,128]{2,1,0:T(8,128)S(1)} %shard_map.72.after.before, f32[4,128,128]{2,1,0:T(8,128)S(1)} %get-tuple-element.31.source_t.fields_t, ...), custom_call_target="tpu_custom_call" | custom-call | tf_op jit(solution)/shard_map/pallas_call | solution.py:331
  34.2 0.6 collective-permute-done.4.low
  34.9 2.2 %shard_map.75 = (f32[3,8,16,128]{3,2,1,0:T(8,128)S(1)}, f32[3,8,16,128]{3,2,1,0:T(8,128)S(1)}) custom-call(s32[128,128]{1,0:T(8,128)S(1)} %get-tuple-element.30.code_t, f32[3,128,128]{2,1,0:T(8,128)S(1)} %shard_map.74.sums_t, f32[4,128,128]{2,1,0:T(8,128)S(1)} %get-tuple-element.31.source_t.fields_t, f32[4,128,128]{2,1,0:T(8,128)S(1)} %shard_map.69.source_t.planes_t, ...), custom_call_target="tpu_custom_call" | custom-call | tf_op jit(solution)/shard_map/pallas_call | solution.py:343
  37.1 1.4 %shard_map.76 = (f32[160,128]{1,0:T(8,128)S(1)}, f32[160,128]{1,0:T(8,128)S(1)}, f32[32,128]{1,0:T(8,128)S(1)}, f32[32,128]{1,0:T(8,128)S(1)}, f32[10,24,256]{2,...) custom-call(f32[3,8,16,128]{3,2,1,0:T(8,128)S(1)} %get-tuple-element.39.moved, ...), custom_call_target="tpu_custom_call" | custom-call | tf_op jit(solution)/shard_map/pallas_call | solution.py:630
  38.5 1.9 %collective-permute-start.6 = (f32[160,128]{1,0:T(8,128)S(1)}, f32[160,128]{1,0:T(8,128)S(1)}, u32[]{:S(2)}, u32[]{:S(2)}) collective-permute-start(f32[160,128]{1,0:T(8,128)S(1)} %get-tuple-element.44), channel_id=1, source_target_pairs={{0,32},{32,64},{64,96},{96,128},{128,160},{160,192},{192,224},{224... | collective-permute-start | bytes 245768 | tf_op jit(solution)/shard_map/ppermute | solution.py:37
  40.4 5.6 %collective-permute-start.7 = (f32[160,128]{1,0:T(8,128)S(1)}, f32[160,128]{1,0:T(8,128)S(1)}, u32[]{:S(2)}, u32[]{:S(2)}) collective-permute-start(f32[160,128]{1,0:T(8,128)S(1)} %get-tuple-element.45), channel_id=1, source_target_pairs={{0,480},{32,0},{64,32},{96,64},{128,96},{160,128},{192,160},{224,1... | collective-permute-start | bytes 245768 | tf_op jit(solution)/shard_map/ppermute | solution.py:37
  46.1 1.9 %collective-permute-start.8 = (f32[32,128]{1,0:T(8,128)S(1)}, f32[32,128]{1,0:T(8,128)S(1)}, u32[]{:S(2)}, u32[]{:S(2)}) collective-permute-start(f32[32,128]{1,0:T(8,128)S(1)} %get-tuple-element.46), channel_id=1, source_target_pairs={{0,64},{32,96},{64,128},{96,160},{128,192},{160,224},{192,256},{22... | collective-permute-start | bytes 49160 | tf_op jit(solution)/shard_map/ppermute | solution.py:37
  48.0 6.0 %collective-permute-start.9 = (f32[32,128]{1,0:T(8,128)S(1)}, f32[32,128]{1,0:T(8,128)S(1)}, u32[]{:S(2)}, u32[]{:S(2)}) collective-permute-start(f32[32,128]{1,0:T(8,128)S(1)} %get-tuple-element.47), channel_id=1, source_target_pairs={{0,448},{32,480},{64,0},{96,32},{128,64},{160,96},{192,128},{224,1... | collective-permute-start | bytes 49160 | tf_op jit(solution)/shard_map/ppermute | solution.py:37
  54.0 1.2 %shard_map.77.after.half_t = f32[64,128]{1,0:T(8,128)S(1)} custom-call(s32[128,128]{1,0:T(8,128)S(1)} %get-tuple-element.30.code_t, f32[4,128,128]{2,1,0:T(8,128)S(1)} %get-tuple-element.31.source_t.fields_t, f32[4,128,128]{2,1,0:T(8,128)S(1)} %shard_map.69.source_t.planes_t, f32[4,128,128]{2,1,0:T(8,128)S(1)} %get-tuple-element.36.rows_t, ...), custom_call_target="tpu_custom_call" | custom-call | tf_op jit(solution)/shard_map/pallas_call | solution.py:638
  55.2 0.2 collective-permute-done.9.high_2
  55.4 0.2 shard_map.78
  55.6 2.2 %collective-permute-start.10 = (f32[72,128]{1,0:T(8,128)S(1)}, f32[72,128]{1,0:T(8,128)S(1)}, u32[]{:S(2)}, u32[]{:S(2)}) collective-permute-start(f32[72,128]{1,0:T(8,128)S(1)} %get-tuple-element.51), channel_id=1, source_target_pairs={{0,8},{8,16},{16,24},{24,0},{1,9},{9,17},{17,25},{25,1},{2,10},{10... | collective-permute-start | bytes 110600 | tf_op jit(solution)/shard_map/ppermute | solution.py:37
  57.8 3.7 %collective-permute-start.11 = (f32[72,128]{1,0:T(8,128)S(1)}, f32[72,128]{1,0:T(8,128)S(1)}, u32[]{:S(2)}, u32[]{:S(2)}) collective-permute-start(f32[72,128]{1,0:T(8,128)S(1)} %get-tuple-element.52), channel_id=1, source_target_pairs={{0,24},{8,0},{16,8},{24,16},{1,25},{9,1},{17,9},{25,17},{2,26},{10... | collective-permute-start | bytes 110600 | tf_op jit(solution)/shard_map/ppermute | solution.py:37
  61.5 1.9 %shard_map.79 = (f32[8,16,128]{2,1,0:T(8,128)}, f32[8,128]{1,0:T(8,128)S(1)}) custom-call(s32[128,128]{1,0:T(8,128)S(1)} %get-tuple-element.30.code_t, f32[4,128,128]{2,1,0:T(8,128)S(1)} %get-tuple-element.31.source_t.fields_t, f32[4,128,128]{2,1,0:T(8,128)S(1)} %shard_map.69.source_t.planes_t, f32[4,128,128]{2,1,0:T(8,128)S(1)} %get-tuple-element.36.rows_t, ...), custom_call_target="tpu_custom_call" | custom-call | tf_op jit(solution)/shard_map/pallas_call | solution.py:648
  63.4 1.5 %collective-permute-done.11.high = f32[72,128]{1,0:T(8,128)S(1)} collective-permute-done((f32[72,128]{1,0:T(8,128)S(1)}, f32[72,128]{1,0:T(8,128)S(1)}, u32[]{:S(2)}, u32[]{:S(2)}) %collective-permute-start.11) | collective-permute-done | bytes 36896 | tf_op jit(solution)/shard_map/ppermute | solution.py:37
  64.9 1.1 %shard_map.80 = (f32[3,8,16,128]{3,2,1,0:T(8,128)}, f32[8,16,128]{2,1,0:T(8,128)}) custom-call(f32[3,8,16,128]{3,2,1,0:T(8,128)S(1)} %get-tuple-element.39.moved, f32[10,24,256]{2,1,0:T(8,128)S(1)} %get-tuple-element.48.fine, f32[6,16,128]{2,1,0:T(8,128)S(1)} %get-tuple-element.49.middle, f32[4,16,128]{2,1,0:T(8,128)S(1)} %get-tuple-element.50.after.coarse, ...), custom_call_target="tpu_custom_call" | custom-call | tf_op jit(solution)/shard_map/pallas_call | solution.py:651
  (12 shorter events, 0.1 us)
Async XLA Ops:
  0.6 14.5 %copy-start.1 = (s32[3,8,16,128]{3,2,1,0:T(8,128)S(1)}, s32[3,8,16,128]{3,2,1,0:T(8,128)}, u32[]{:S(2)}) copy-start(s32[3,8,16,128]{3,2,1,0:T(8,128)} %param.6) | copy-start | bytes 589828
  1.7 13.5 %copy-start = (s32[3,8,16,128]{3,2,1,0:T(8,128)S(1)}, s32[3,8,16,128]{3,2,1,0:T(8,128)}, u32[]{:S(2)}) copy-start(s32[3,8,16,128]{3,2,1,0:T(8,128)} %param.7) | copy-start | bytes 589828
  1.7 15.7 %collective-permute-start = (f32[4,4,16,128]{3,2,1,0:T(8,128)S(1)}, f32[4,4,16,128]{3,2,1,0:T(8,128)S(1)}, u32[]{:S(2)}, u32[]{:S(2)}) collective-permute-start(f32[4,4,16,128]{3,2,1,0:T(8,128)S(1)} %get-tuple-element.32), channel_id=1, source_target_pairs={{0,32},{32,64},{64,96},{96,128},{128,160},{160,192},{192,224},{224... | collective-permute-start | bytes 393224 | tf_op jit(solution)/shard_map/ppermute | solution.py:37
  5.7 12.2 %collective-permute-start.1 = (f32[4,4,16,128]{3,2,1,0:T(8,128)S(1)}, f32[4,4,16,128]{3,2,1,0:T(8,128)S(1)}, u32[]{:S(2)}, u32[]{:S(2)}) collective-permute-start(f32[4,4,16,128]{3,2,1,0:T(8,128)S(1)} %get-tuple-element.33), channel_id=1, source_target_pairs={{0,480},{32,0},{64,32},{96,64},{128,96},{160,128},{192,160},{224,1... | collective-permute-start | bytes 393224 | tf_op jit(solution)/shard_map/ppermute | solution.py:37
  17.9 7.9 %collective-permute-start.2 = (f32[4,8,8,128]{3,2,1,0:T(8,128)S(1)}, f32[4,8,8,128]{3,2,1,0:T(8,128)S(1)}, u32[]{:S(2)}, u32[]{:S(2)}) collective-permute-start(f32[4,8,8,128]{3,2,1,0:T(8,128)S(1)} %get-tuple-element.34), channel_id=1, source_target_pairs={{0,8},{8,16},{16,24},{24,0},{1,9},{9,17},{17,25},{25,1},{2,10},{10... | collective-permute-start | bytes 393224 | tf_op jit(solution)/shard_map/ppermute | solution.py:37
  20.3 8.1 %collective-permute-start.3 = (f32[4,8,8,128]{3,2,1,0:T(8,128)S(1)}, f32[4,8,8,128]{3,2,1,0:T(8,128)S(1)}, u32[]{:S(2)}, u32[]{:S(2)}) collective-permute-start(f32[4,8,8,128]{3,2,1,0:T(8,128)S(1)} %get-tuple-element.35), channel_id=1, source_target_pairs={{0,24},{8,0},{16,8},{24,16},{1,25},{9,1},{17,9},{25,17},{2,26},{10... | collective-permute-start | bytes 393224 | tf_op jit(solution)/shard_map/ppermute | solution.py:37
  28.6 6.3 %collective-permute-start.4 = (f32[384,128]{1,0:T(8,128)S(1)}, f32[384,128]{1,0:T(8,128)S(1)}, u32[]{:S(2)}, u32[]{:S(2)}) collective-permute-start(f32[384,128]{1,0:T(8,128)S(1)} %get-tuple-element.37), channel_id=1, source_target_pairs={{0,1},{1,2},{2,3},{3,4},{4,5},{5,6},{6,7},{7,0},{8,9},{9,10},{10,1... | collective-permute-start | bytes 589832 | tf_op jit(solution)/shard_map/ppermute | solution.py:37
  28.6 6.3 %collective-permute-start.5 = (f32[384,128]{1,0:T(8,128)S(1)}, f32[384,128]{1,0:T(8,128)S(1)}, u32[]{:S(2)}, u32[]{:S(2)}) collective-permute-start(f32[384,128]{1,0:T(8,128)S(1)} %get-tuple-element.38), channel_id=1, source_target_pairs={{0,7},{1,0},{2,1},{3,2},{4,3},{5,4},{6,5},{7,6},{8,15},{9,8},{10,9... | collective-permute-start | bytes 589832 | tf_op jit(solution)/shard_map/ppermute | solution.py:37
  38.5 16.9 %collective-permute-start.6 = (f32[160,128]{1,0:T(8,128)S(1)}, f32[160,128]{1,0:T(8,128)S(1)}, u32[]{:S(2)}, u32[]{:S(2)}) collective-permute-start(f32[160,128]{1,0:T(8,128)S(1)} %get-tuple-element.44), channel_id=1, source_target_pairs={{0,32},{32,64},{64,96},{96,128},{128,160},{160,192},{192,224},{224... | collective-permute-start | bytes 245768 | tf_op jit(solution)/shard_map/ppermute | solution.py:37
  40.4 15.0 %collective-permute-start.7 = (f32[160,128]{1,0:T(8,128)S(1)}, f32[160,128]{1,0:T(8,128)S(1)}, u32[]{:S(2)}, u32[]{:S(2)}) collective-permute-start(f32[160,128]{1,0:T(8,128)S(1)} %get-tuple-element.45), channel_id=1, source_target_pairs={{0,480},{32,0},{64,32},{96,64},{128,96},{160,128},{192,160},{224,1... | collective-permute-start | bytes 245768 | tf_op jit(solution)/shard_map/ppermute | solution.py:37
  46.1 9.2 %collective-permute-start.8 = (f32[32,128]{1,0:T(8,128)S(1)}, f32[32,128]{1,0:T(8,128)S(1)}, u32[]{:S(2)}, u32[]{:S(2)}) collective-permute-start(f32[32,128]{1,0:T(8,128)S(1)} %get-tuple-element.46), channel_id=1, source_target_pairs={{0,64},{32,96},{64,128},{96,160},{128,192},{160,224},{192,256},{22... | collective-permute-start | bytes 49160 | tf_op jit(solution)/shard_map/ppermute | solution.py:37
  48.0 7.5 %collective-permute-start.9 = (f32[32,128]{1,0:T(8,128)S(1)}, f32[32,128]{1,0:T(8,128)S(1)}, u32[]{:S(2)}, u32[]{:S(2)}) collective-permute-start(f32[32,128]{1,0:T(8,128)S(1)} %get-tuple-element.47), channel_id=1, source_target_pairs={{0,448},{32,480},{64,0},{96,32},{128,64},{160,96},{192,128},{224,1... | collective-permute-start | bytes 49160 | tf_op jit(solution)/shard_map/ppermute | solution.py:37
  55.6 7.8 %collective-permute-start.10 = (f32[72,128]{1,0:T(8,128)S(1)}, f32[72,128]{1,0:T(8,128)S(1)}, u32[]{:S(2)}, u32[]{:S(2)}) collective-permute-start(f32[72,128]{1,0:T(8,128)S(1)} %get-tuple-element.51), channel_id=1, source_target_pairs={{0,8},{8,16},{16,24},{24,0},{1,9},{9,17},{17,25},{25,1},{2,10},{10... | collective-permute-start | bytes 110600 | tf_op jit(solution)/shard_map/ppermute | solution.py:37
  57.8 7.1 %collective-permute-start.11 = (f32[72,128]{1,0:T(8,128)S(1)}, f32[72,128]{1,0:T(8,128)S(1)}, u32[]{:S(2)}, u32[]{:S(2)}) collective-permute-start(f32[72,128]{1,0:T(8,128)S(1)} %get-tuple-element.52), channel_id=1, source_target_pairs={{0,24},{8,0},{16,8},{24,16},{1,25},{9,1},{17,9},{25,17},{2,26},{10... | collective-permute-start | bytes 110600 | tf_op jit(solution)/shard_map/ppermute | solution.py:37

commit v10 on v9

--- a/solution.py
+++ b/solution.py
@@ -630,10 +630,10 @@
     to_low, to_high, to_low_2, to_high_2, *sums = call(
         levels_kernel, [side, side, side_2, side_2] + held, halves, inputs=2
     )(moved, beyond)
+    low_2 = shift_ring(to_high_2, "gx", 2)
+    high_2 = shift_ring(to_low_2, "gx", -2)
     low = shift_ring(to_high, "gx", 1)
     high = shift_ring(to_low, "gx", -1)
-    low_2 = shift_ring(to_high_2, "gx", 2)
-    high_2 = shift_ring(to_low_2, "gx", -2)
     padded = pltpu.VMEM((3, 144, 128), f32)
     (half_t,) = call(low_density_kernel, [((64, 128), f32)], [padded], inputs=7)(
         *sources, sums[-1]

time: 66.4 us -> 66.4 us (level)
  no operation moved by 1% of the time
where the time goes in v10:
time: 66.4 us; the launch traced here: 66 us
  starting transfers between devices  43.6 us (66%)
  Pallas kernels  15.1 us (23%)
  waiting for transfers between devices  5.41 us (8%)
  other arithmetic  1.06 us (2%)
  between operations  0.85 us (1%)
    ppermute x12, starting transfers between devices, shift_ring(): lax.ppermute(value, axis, [(i, (i + step) % count) for i in range(count)])  43.6 us
    ppermute x12, waiting for transfers between devices, shift_ring(): lax.ppermute(value, axis, [(i, (i + step) % count) for i in range(count)])  5.41 us
    pallas_call x2, Pallas kernels, gather(): return call(kernel, [three], inputs=len(values))(*values)[0]  3.88 us
    pallas_call x1, Pallas kernels, advect(): call(ends_kernel, [three], scratch, inputs=5)  2.71 us
    pallas_call x1, Pallas kernels, advect(): call(edges_kernel, [block, block], scratch, inputs=7)  2.2 us
    pallas_call x1, Pallas kernels, project(): call(density_kernel, [((8, 16, 128), f32), ((8, 128), f32)], scratch, inp...  1.91 us
    pallas_call x1, Pallas kernels, project(): call(levels_kernel, [side, side, side_2, side_2] + held, halves, inputs=2)  1.43 us
  transfers between devices with their start and end apart: 12, of which 5 were waited for; matrix products, arithmetic and copies ran while one was open for 0% of the time, Pallas kernels for 15%

profile of v10, /device:TPU:6, one launch (start us, length us, event | category | flops | bytes accessed | tf_op | source)
XLA Modules:
  0.0 66.0 jit_solution(6397209162946870043)
XLA Ops:
  0.6 1.0 %pad_maximum_fusion.fields = f32[4,8,16,128]{3,2,1,0:T(8,128)S(1)} fusion(f32[1,8,16,128]{3,2,1,0:T(8,128)} %bitcast.3, f32[3,8,16,128]{3,2,1,0:T(8,128)} %param.4), kind=kLoop, calls=%fused_computation | loop fusion | flops 65536 | bytes 524288 | tf_op jit(solution)/shard_map/concatenate | solution.py:308
  1.7 0.0 copy-start
  1.7 4.0 %collective-permute-start = (f32[4,4,16,128]{3,2,1,0:T(8,128)S(1)}, f32[4,4,16,128]{3,2,1,0:T(8,128)S(1)}, u32[]{:S(2)}, u32[]{:S(2)}) collective-permute-start(f32[4,4,16,128]{3,2,1,0:T(8,128)S(1)} %get-tuple-element.32), channel_id=1, source_target_pairs={{0,32},{32,64},{64,96},{96,128},{128,160},{160,192},{192,224},{224... | collective-permute-start | bytes 393224 | tf_op jit(solution)/shard_map/ppermute | solution.py:37
  5.7 9.5 %collective-permute-start.1 = (f32[4,4,16,128]{3,2,1,0:T(8,128)S(1)}, f32[4,4,16,128]{3,2,1,0:T(8,128)S(1)}, u32[]{:S(2)}, u32[]{:S(2)}) collective-permute-start(f32[4,4,16,128]{3,2,1,0:T(8,128)S(1)} %get-tuple-element.33), channel_id=1, source_target_pairs={{0,480},{32,0},{64,32},{96,64},{128,96},{160,128},{192,160},{224,1... | collective-permute-start | bytes 393224 | tf_op jit(solution)/shard_map/ppermute | solution.py:37
  15.2 0.2 shard_map.67
  15.4 1.9 %shard_map.70.after.refs_0_ = f32[3,128,128]{2,1,0:T(8,128)S(1)} custom-call(s32[128,128]{1,0:T(8,128)S(1)} %get-tuple-element.30.code_t, f32[4,128,128]{2,1,0:T(8,128)S(1)} %get-tuple-element.31.source_t.fields_t), custom_call_target="tpu_custom_call" | custom-call | tf_op jit(solution)/shard_map/pallas_call | solution.py:305
  17.3 0.0 collective-permute-done.low
  17.4 0.5 collective-permute-done.1.high
  17.9 2.4 %collective-permute-start.2 = (f32[4,8,8,128]{3,2,1,0:T(8,128)S(1)}, f32[4,8,8,128]{3,2,1,0:T(8,128)S(1)}, u32[]{:S(2)}, u32[]{:S(2)}) collective-permute-start(f32[4,8,8,128]{3,2,1,0:T(8,128)S(1)} %get-tuple-element.34), channel_id=1, source_target_pairs={{0,8},{8,16},{16,24},{24,0},{1,9},{9,17},{17,25},{25,1},{2,10},{10... | collective-permute-start | bytes 393224 | tf_op jit(solution)/shard_map/ppermute | solution.py:37
  20.3 3.5 %collective-permute-start.3 = (f32[4,8,8,128]{3,2,1,0:T(8,128)S(1)}, f32[4,8,8,128]{3,2,1,0:T(8,128)S(1)}, u32[]{:S(2)}, u32[]{:S(2)}) collective-permute-start(f32[4,8,8,128]{3,2,1,0:T(8,128)S(1)} %get-tuple-element.35), channel_id=1, source_target_pairs={{0,24},{8,0},{16,8},{24,16},{1,25},{9,1},{17,9},{25,17},{2,26},{10... | collective-permute-start | bytes 393224 | tf_op jit(solution)/shard_map/ppermute | solution.py:37
  23.8 0.1 shard_map.69.source_t.planes_t
  23.9 1.9 %shard_map.72.after.before = f32[3,128,128]{2,1,0:T(8,128)S(1)} custom-call(s32[128,128]{1,0:T(8,128)S(1)} %get-tuple-element.30.code_t, f32[4,128,128]{2,1,0:T(8,128)S(1)} %shard_map.69.source_t.planes_t, f32[3,128,128]{2,1,0:T(8,128)S(1)} %shard_map.70.after.refs_0_), custom_call_target="tpu_custom_call" | custom-call | tf_op jit(solution)/shard_map/pallas_call | solution.py:305
  25.9 2.5 %collective-permute-done.3.high = f32[4,8,8,128]{3,2,1,0:T(8,128)S(1)} collective-permute-done((f32[4,8,8,128]{3,2,1,0:T(8,128)S(1)}, f32[4,8,8,128]{3,2,1,0:T(8,128)S(1)}, u32[]{:S(2)}, u32[]{:S(2)}) %collective-permute-start.3) | collective-permute-done | bytes 131104 | tf_op jit(solution)/shard_map/ppermute | solution.py:37
  28.4 0.1 shard_map.73
  28.6 0.0 collective-permute-start.4
  28.6 2.9 %collective-permute-start.5 = (f32[384,128]{1,0:T(8,128)S(1)}, f32[384,128]{1,0:T(8,128)S(1)}, u32[]{:S(2)}, u32[]{:S(2)}) collective-permute-start(f32[384,128]{1,0:T(8,128)S(1)} %get-tuple-element.38), channel_id=1, source_target_pairs={{0,7},{1,0},{2,1},{3,2},{4,3},{5,4},{6,5},{7,6},{8,15},{9,8},{10,9... | collective-permute-start | bytes 589832 | tf_op jit(solution)/shard_map/ppermute | solution.py:37
  31.5 2.7 %shard_map.74.sums_t = f32[3,128,128]{2,1,0:T(8,128)S(1)} custom-call(s32[128,128]{1,0:T(8,128)S(1)} %get-tuple-element.30.code_t, f32[4,128,128]{2,1,0:T(8,128)S(1)} %get-tuple-element.36.rows_t, f32[3,128,128]{2,1,0:T(8,128)S(1)} %shard_map.72.after.before, f32[4,128,128]{2,1,0:T(8,128)S(1)} %get-tuple-element.31.source_t.fields_t, ...), custom_call_target="tpu_custom_call" | custom-call | tf_op jit(solution)/shard_map/pallas_call | solution.py:331
  34.2 0.6 collective-permute-done.4.low
  34.9 2.2 %shard_map.75 = (f32[3,8,16,128]{3,2,1,0:T(8,128)S(1)}, f32[3,8,16,128]{3,2,1,0:T(8,128)S(1)}) custom-call(s32[128,128]{1,0:T(8,128)S(1)} %get-tuple-element.30.code_t, f32[3,128,128]{2,1,0:T(8,128)S(1)} %shard_map.74.sums_t, f32[4,128,128]{2,1,0:T(8,128)S(1)} %get-tuple-element.31.source_t.fields_t, f32[4,128,128]{2,1,0:T(8,128)S(1)} %shard_map.69.source_t.planes_t, ...), custom_call_target="tpu_custom_call" | custom-call | tf_op jit(solution)/shard_map/pallas_call | solution.py:343
  37.1 1.4 %shard_map.76 = (f32[160,128]{1,0:T(8,128)S(1)}, f32[160,128]{1,0:T(8,128)S(1)}, f32[32,128]{1,0:T(8,128)S(1)}, f32[32,128]{1,0:T(8,128)S(1)}, f32[10,24,256]{2,...) custom-call(f32[3,8,16,128]{3,2,1,0:T(8,128)S(1)} %get-tuple-element.39.moved, ...), custom_call_target="tpu_custom_call" | custom-call | tf_op jit(solution)/shard_map/pallas_call | solution.py:630
  38.5 1.9 %collective-permute-start.6 = (f32[160,128]{1,0:T(8,128)S(1)}, f32[160,128]{1,0:T(8,128)S(1)}, u32[]{:S(2)}, u32[]{:S(2)}) collective-permute-start(f32[160,128]{1,0:T(8,128)S(1)} %get-tuple-element.44), channel_id=1, source_target_pairs={{0,32},{32,64},{64,96},{96,128},{128,160},{160,192},{192,224},{224... | collective-permute-start | bytes 245768 | tf_op jit(solution)/shard_map/ppermute | solution.py:37
  40.4 5.6 %collective-permute-start.7 = (f32[160,128]{1,0:T(8,128)S(1)}, f32[160,128]{1,0:T(8,128)S(1)}, u32[]{:S(2)}, u32[]{:S(2)}) collective-permute-start(f32[160,128]{1,0:T(8,128)S(1)} %get-tuple-element.45), channel_id=1, source_target_pairs={{0,480},{32,0},{64,32},{96,64},{128,96},{160,128},{192,160},{224,1... | collective-permute-start | bytes 245768 | tf_op jit(solution)/shard_map/ppermute | solution.py:37
  46.1 1.9 %collective-permute-start.8 = (f32[32,128]{1,0:T(8,128)S(1)}, f32[32,128]{1,0:T(8,128)S(1)}, u32[]{:S(2)}, u32[]{:S(2)}) collective-permute-start(f32[32,128]{1,0:T(8,128)S(1)} %get-tuple-element.46), channel_id=1, source_target_pairs={{0,64},{32,96},{64,128},{96,160},{128,192},{160,224},{192,256},{22... | collective-permute-start | bytes 49160 | tf_op jit(solution)/shard_map/ppermute | solution.py:37
  48.0 6.0 %collective-permute-start.9 = (f32[32,128]{1,0:T(8,128)S(1)}, f32[32,128]{1,0:T(8,128)S(1)}, u32[]{:S(2)}, u32[]{:S(2)}) collective-permute-start(f32[32,128]{1,0:T(8,128)S(1)} %get-tuple-element.47), channel_id=1, source_target_pairs={{0,448},{32,480},{64,0},{96,32},{128,64},{160,96},{192,128},{224,1... | collective-permute-start | bytes 49160 | tf_op jit(solution)/shard_map/ppermute | solution.py:37
  54.0 1.2 %shard_map.77.after.half_t = f32[64,128]{1,0:T(8,128)S(1)} custom-call(s32[128,128]{1,0:T(8,128)S(1)} %get-tuple-element.30.code_t, f32[4,128,128]{2,1,0:T(8,128)S(1)} %get-tuple-element.31.source_t.fields_t, f32[4,128,128]{2,1,0:T(8,128)S(1)} %shard_map.69.source_t.planes_t, f32[4,128,128]{2,1,0:T(8,128)S(1)} %get-tuple-element.36.rows_t, ...), custom_call_target="tpu_custom_call" | custom-call | tf_op jit(solution)/shard_map/pallas_call | solution.py:638
  55.2 0.2 collective-permute-done.9.high_2
  55.4 0.2 shard_map.78
  55.6 2.2 %collective-permute-start.10 = (f32[72,128]{1,0:T(8,128)S(1)}, f32[72,128]{1,0:T(8,128)S(1)}, u32[]{:S(2)}, u32[]{:S(2)}) collective-permute-start(f32[72,128]{1,0:T(8,128)S(1)} %get-tuple-element.51), channel_id=1, source_target_pairs={{0,8},{8,16},{16,24},{24,0},{1,9},{9,17},{17,25},{25,1},{2,10},{10... | collective-permute-start | bytes 110600 | tf_op jit(solution)/shard_map/ppermute | solution.py:37
  57.8 3.7 %collective-permute-start.11 = (f32[72,128]{1,0:T(8,128)S(1)}, f32[72,128]{1,0:T(8,128)S(1)}, u32[]{:S(2)}, u32[]{:S(2)}) collective-permute-start(f32[72,128]{1,0:T(8,128)S(1)} %get-tuple-element.52), channel_id=1, source_target_pairs={{0,24},{8,0},{16,8},{24,16},{1,25},{9,1},{17,9},{25,17},{2,26},{10... | collective-permute-start | bytes 110600 | tf_op jit(solution)/shard_map/ppermute | solution.py:37
  61.5 1.9 %shard_map.79 = (f32[8,16,128]{2,1,0:T(8,128)}, f32[8,128]{1,0:T(8,128)S(1)}) custom-call(s32[128,128]{1,0:T(8,128)S(1)} %get-tuple-element.30.code_t, f32[4,128,128]{2,1,0:T(8,128)S(1)} %get-tuple-element.31.source_t.fields_t, f32[4,128,128]{2,1,0:T(8,128)S(1)} %shard_map.69.source_t.planes_t, f32[4,128,128]{2,1,0:T(8,128)S(1)} %get-tuple-element.36.rows_t, ...), custom_call_target="tpu_custom_call" | custom-call | tf_op jit(solution)/shard_map/pallas_call | solution.py:648
  63.4 1.5 %collective-permute-done.11.high = f32[72,128]{1,0:T(8,128)S(1)} collective-permute-done((f32[72,128]{1,0:T(8,128)S(1)}, f32[72,128]{1,0:T(8,128)S(1)}, u32[]{:S(2)}, u32[]{:S(2)}) %collective-permute-start.11) | collective-permute-done | bytes 36896 | tf_op jit(solution)/shard_map/ppermute | solution.py:37
  64.9 1.1 %shard_map.80 = (f32[3,8,16,128]{3,2,1,0:T(8,128)}, f32[8,16,128]{2,1,0:T(8,128)}) custom-call(f32[3,8,16,128]{3,2,1,0:T(8,128)S(1)} %get-tuple-element.39.moved, f32[10,24,256]{2,1,0:T(8,128)S(1)} %get-tuple-element.48.fine, f32[6,16,128]{2,1,0:T(8,128)S(1)} %get-tuple-element.49.middle, f32[4,16,128]{2,1,0:T(8,128)S(1)} %get-tuple-element.50.after.coarse, ...), custom_call_target="tpu_custom_call" | custom-call | tf_op jit(solution)/shard_map/pallas_call | solution.py:651
  (12 shorter events, 0.1 us)
Async XLA Ops:
  0.6 14.5 %copy-start.1 = (s32[3,8,16,128]{3,2,1,0:T(8,128)S(1)}, s32[3,8,16,128]{3,2,1,0:T(8,128)}, u32[]{:S(2)}) copy-start(s32[3,8,16,128]{3,2,1,0:T(8,128)} %param.6) | copy-start | bytes 589828
  1.7 13.5 %copy-start = (s32[3,8,16,128]{3,2,1,0:T(8,128)S(1)}, s32[3,8,16,128]{3,2,1,0:T(8,128)}, u32[]{:S(2)}) copy-start(s32[3,8,16,128]{3,2,1,0:T(8,128)} %param.7) | copy-start | bytes 589828
  1.7 15.7 %collective-permute-start = (f32[4,4,16,128]{3,2,1,0:T(8,128)S(1)}, f32[4,4,16,128]{3,2,1,0:T(8,128)S(1)}, u32[]{:S(2)}, u32[]{:S(2)}) collective-permute-start(f32[4,4,16,128]{3,2,1,0:T(8,128)S(1)} %get-tuple-element.32), channel_id=1, source_target_pairs={{0,32},{32,64},{64,96},{96,128},{128,160},{160,192},{192,224},{224... | collective-permute-start | bytes 393224 | tf_op jit(solution)/shard_map/ppermute | solution.py:37
  5.7 12.2 %collective-permute-start.1 = (f32[4,4,16,128]{3,2,1,0:T(8,128)S(1)}, f32[4,4,16,128]{3,2,1,0:T(8,128)S(1)}, u32[]{:S(2)}, u32[]{:S(2)}) collective-permute-start(f32[4,4,16,128]{3,2,1,0:T(8,128)S(1)} %get-tuple-element.33), channel_id=1, source_target_pairs={{0,480},{32,0},{64,32},{96,64},{128,96},{160,128},{192,160},{224,1... | collective-permute-start | bytes 393224 | tf_op jit(solution)/shard_map/ppermute | solution.py:37
  17.9 7.9 %collective-permute-start.2 = (f32[4,8,8,128]{3,2,1,0:T(8,128)S(1)}, f32[4,8,8,128]{3,2,1,0:T(8,128)S(1)}, u32[]{:S(2)}, u32[]{:S(2)}) collective-permute-start(f32[4,8,8,128]{3,2,1,0:T(8,128)S(1)} %get-tuple-element.34), channel_id=1, source_target_pairs={{0,8},{8,16},{16,24},{24,0},{1,9},{9,17},{17,25},{25,1},{2,10},{10... | collective-permute-start | bytes 393224 | tf_op jit(solution)/shard_map/ppermute | solution.py:37
  20.3 8.1 %collective-permute-start.3 = (f32[4,8,8,128]{3,2,1,0:T(8,128)S(1)}, f32[4,8,8,128]{3,2,1,0:T(8,128)S(1)}, u32[]{:S(2)}, u32[]{:S(2)}) collective-permute-start(f32[4,8,8,128]{3,2,1,0:T(8,128)S(1)} %get-tuple-element.35), channel_id=1, source_target_pairs={{0,24},{8,0},{16,8},{24,16},{1,25},{9,1},{17,9},{25,17},{2,26},{10... | collective-permute-start | bytes 393224 | tf_op jit(solution)/shard_map/ppermute | solution.py:37
  28.6 6.3 %collective-permute-start.4 = (f32[384,128]{1,0:T(8,128)S(1)}, f32[384,128]{1,0:T(8,128)S(1)}, u32[]{:S(2)}, u32[]{:S(2)}) collective-permute-start(f32[384,128]{1,0:T(8,128)S(1)} %get-tuple-element.37), channel_id=1, source_target_pairs={{0,1},{1,2},{2,3},{3,4},{4,5},{5,6},{6,7},{7,0},{8,9},{9,10},{10,1... | collective-permute-start | bytes 589832 | tf_op jit(solution)/shard_map/ppermute | solution.py:37
  28.6 6.3 %collective-permute-start.5 = (f32[384,128]{1,0:T(8,128)S(1)}, f32[384,128]{1,0:T(8,128)S(1)}, u32[]{:S(2)}, u32[]{:S(2)}) collective-permute-start(f32[384,128]{1,0:T(8,128)S(1)} %get-tuple-element.38), channel_id=1, source_target_pairs={{0,7},{1,0},{2,1},{3,2},{4,3},{5,4},{6,5},{7,6},{8,15},{9,8},{10,9... | collective-permute-start | bytes 589832 | tf_op jit(solution)/shard_map/ppermute | solution.py:37
  38.5 16.9 %collective-permute-start.6 = (f32[160,128]{1,0:T(8,128)S(1)}, f32[160,128]{1,0:T(8,128)S(1)}, u32[]{:S(2)}, u32[]{:S(2)}) collective-permute-start(f32[160,128]{1,0:T(8,128)S(1)} %get-tuple-element.44), channel_id=1, source_target_pairs={{0,32},{32,64},{64,96},{96,128},{128,160},{160,192},{192,224},{224... | collective-permute-start | bytes 245768 | tf_op jit(solution)/shard_map/ppermute | solution.py:37
  40.4 15.0 %collective-permute-start.7 = (f32[160,128]{1,0:T(8,128)S(1)}, f32[160,128]{1,0:T(8,128)S(1)}, u32[]{:S(2)}, u32[]{:S(2)}) collective-permute-start(f32[160,128]{1,0:T(8,128)S(1)} %get-tuple-element.45), channel_id=1, source_target_pairs={{0,480},{32,0},{64,32},{96,64},{128,96},{160,128},{192,160},{224,1... | collective-permute-start | bytes 245768 | tf_op jit(solution)/shard_map/ppermute | solution.py:37
  46.1 9.2 %collective-permute-start.8 = (f32[32,128]{1,0:T(8,128)S(1)}, f32[32,128]{1,0:T(8,128)S(1)}, u32[]{:S(2)}, u32[]{:S(2)}) collective-permute-start(f32[32,128]{1,0:T(8,128)S(1)} %get-tuple-element.46), channel_id=1, source_target_pairs={{0,64},{32,96},{64,128},{96,160},{128,192},{160,224},{192,256},{22... | collective-permute-start | bytes 49160 | tf_op jit(solution)/shard_map/ppermute | solution.py:37
  48.0 7.5 %collective-permute-start.9 = (f32[32,128]{1,0:T(8,128)S(1)}, f32[32,128]{1,0:T(8,128)S(1)}, u32[]{:S(2)}, u32[]{:S(2)}) collective-permute-start(f32[32,128]{1,0:T(8,128)S(1)} %get-tuple-element.47), channel_id=1, source_target_pairs={{0,448},{32,480},{64,0},{96,32},{128,64},{160,96},{192,128},{224,1... | collective-permute-start | bytes 49160 | tf_op jit(solution)/shard_map/ppermute | solution.py:37
  55.6 7.8 %collective-permute-start.10 = (f32[72,128]{1,0:T(8,128)S(1)}, f32[72,128]{1,0:T(8,128)S(1)}, u32[]{:S(2)}, u32[]{:S(2)}) collective-permute-start(f32[72,128]{1,0:T(8,128)S(1)} %get-tuple-element.51), channel_id=1, source_target_pairs={{0,8},{8,16},{16,24},{24,0},{1,9},{9,17},{17,25},{25,1},{2,10},{10... | collective-permute-start | bytes 110600 | tf_op jit(solution)/shard_map/ppermute | solution.py:37
  57.8 7.1 %collective-permute-start.11 = (f32[72,128]{1,0:T(8,128)S(1)}, f32[72,128]{1,0:T(8,128)S(1)}, u32[]{:S(2)}, u32[]{:S(2)}) collective-permute-start(f32[72,128]{1,0:T(8,128)S(1)} %get-tuple-element.52), channel_id=1, source_target_pairs={{0,24},{8,0},{16,8},{24,16},{1,25},{9,1},{17,9},{25,17},{2,26},{10... | collective-permute-start | bytes 110600 | tf_op jit(solution)/shard_map/ppermute | solution.py:37
